TPU v7x, 32 devices: a whole 2x2x4 slice. The times are simulated.
32 devices in a mesh: row: 8 (over y, x, core), col: 4 (over z).
Axes of the slice: x: 2, y: 2, z: 4, core: 2. Of those that a mesh axis runs over, the one named last changes fastest.
Arguments:
- features: bfloat16 [8192, 128], P(('row', 'col')), may hold values from -6 to 6
- degree: int32 [8192], P(('row', 'col')), may hold values from 1 to 256
- weight: bfloat16 [128, 128], replicated, may hold values from -0.5 to 0.5
- bias: float32 [128], replicated, may hold values from -3 to 3
- cotangent: bfloat16 [8192, 128], P(('row', 'col')), may hold values from -8 to 8
- tile_rows: int32 [8, 4, 128], P('row', 'col'), may hold values from 0 to 7
- tile_cols: int32 [8, 4, 128], P('row', 'col'), may hold values from 0 to 15
- tile_count: int32 [8, 4, 1], P('row', 'col'), may hold values from 32 to 128, as said below
- tile_codes: int32 [8, 4, 128, 256], P('row', 'col'), may hold values from 0 to 4095
Outputs:
- hidden: bfloat16 [8192, 128], P(('row', 'col'))
- grad_features: bfloat16 [8192, 128], P(('row', 'col'))
- grad_weight: float32 [128, 128], replicated
- grad_bias: float32 [128], replicated
Inputs may be any that keep to these rules, and one draw needn't show every extreme that they name: Only the first tile_count slots of a block are live; on some block the count is exactly 128. `tile_rows`: A tile position may repeat within a block; repeated tiles add.
All inputs are finite; a program needn't handle non-finite values.
Results may differ from a plain program's by a relative error of at most 0.019.
Values may be sent and summed in bfloat16 or wider, within the bound.
No kernel may reach another device: no remote copies, remote signals or barrier semaphores. Data moves between devices by JAX's collectives and lax.ppermute only.
A program may use at most 64 MiB of HBM per device.

v0:
```python
import math

import jax
import jax.numpy as jnp
from jax import lax
from jax.sharding import PartitionSpec as P

BLOCK = 16


def tile_mask(code_block, living):
    tile_side = code_block.shape[1] // 2
    row_code = code_block[:, :tile_side][:, :, None]
    col_code = code_block[:, tile_side:][:, None, :]
    hashed = (row_code * col_code + row_code + 3 * col_code) % 4093
    return ((hashed < 64) & living[:, None, None]).astype(jnp.bfloat16)


def accumulate(codes_dev, rows_dev, cols_dev, count_dev, source, out_tiles, backward):
    tile_side = source.shape[1]
    width_feat = source.shape[2]

    def block_step(block_id, summed):
        slot_start = block_id * BLOCK
        code_block = lax.dynamic_slice_in_dim(codes_dev, slot_start, BLOCK, 0)
        row_block = lax.dynamic_slice_in_dim(rows_dev, slot_start, BLOCK, 0)
        col_block = lax.dynamic_slice_in_dim(cols_dev, slot_start, BLOCK, 0)
        slot_ids = slot_start + jnp.arange(BLOCK, dtype=jnp.int32)
        target = col_block if backward else row_block
        anchor = row_block if backward else col_block
        living = slot_ids < count_dev
        keep = tile_mask(code_block, living)
        picked = jnp.take(source, anchor, axis=0)
        if backward:
            product = jnp.einsum("tij,tif->tjf", keep, picked, preferred_element_type=jnp.float32)
        else:
            product = jnp.einsum("tij,tjf->tif", keep, picked, preferred_element_type=jnp.float32)
        return summed.at[target].add(product)

    start_sum = jnp.zeros((out_tiles, tile_side, width_feat), jnp.float32)
    loop_count = codes_dev.shape[0] // BLOCK
    summed = lax.fori_loop(0, loop_count, block_step, start_sum)
    return summed.reshape(out_tiles * tile_side, width_feat)


def dense_part(aggregate, weight, bias, cotangent, inv_root):
    preact = jnp.dot(aggregate, weight, preferred_element_type=jnp.float32) + bias
    hidden = jax.nn.elu(preact).astype(jnp.bfloat16)
    elu_slope = jnp.where(preact > 0, 1.0, jnp.exp(jnp.minimum(preact, 0.0)))
    grad_pre = cotangent.astype(jnp.float32) * elu_slope
    grad_pre_b = grad_pre.astype(jnp.bfloat16)
    grad_weight = lax.dot_general(
        aggregate, grad_pre_b, (((0,), (0,)), ((), ())), preferred_element_type=jnp.float32
    )
    grad_bias = jnp.sum(grad_pre, axis=0)
    grad_agg = jnp.dot(grad_pre_b, weight.T, preferred_element_type=jnp.float32)
    grad_scaled = (inv_root * grad_agg).astype(jnp.bfloat16)
    return (hidden, grad_weight, grad_bias, grad_scaled)


def local(features, degree, weight, bias, cotangent, tile_rows, tile_cols, tile_count, tile_codes):
    codes_dev = tile_codes[0, 0]
    rows_dev = tile_rows[0, 0]
    cols_dev = tile_cols[0, 0]
    count_dev = tile_count[0, 0, 0]
    pieces = features.shape[0]
    width_feat = features.shape[1]
    tile_side = codes_dev.shape[1] // 2
    row_devs = lax.axis_size("row")
    col_devs = lax.axis_size("col")
    grad_scale = 1.0 / math.sqrt(pieces * row_devs * col_devs)
    row_tiles = pieces * col_devs // tile_side
    col_tiles = pieces * row_devs // tile_side
    inv_root = lax.rsqrt(degree.astype(jnp.float32))[:, None]
    scaled = (inv_root * features.astype(jnp.float32)).astype(jnp.bfloat16)
    column_feats = lax.all_gather(scaled, "row", axis=0, tiled=True).reshape(
        col_tiles, tile_side, width_feat
    )
    row_terms = accumulate(codes_dev, rows_dev, cols_dev, count_dev, column_feats, row_tiles, False)
    row_sum = lax.psum(row_terms.astype(jnp.bfloat16), "col").astype(jnp.float32)
    row_cot, row_degree = (
        lax.all_gather(cotangent, "col", axis=0, tiled=True),
        lax.all_gather(degree.astype(jnp.bfloat16), "col", axis=0, tiled=True),
    )
    row_root = lax.rsqrt(row_degree.astype(jnp.float32))[:, None]
    aggregate = (row_root * row_sum).astype(jnp.bfloat16)
    hidden_rows, grad_weight, grad_bias, row_grads = dense_part(
        aggregate, weight, bias, row_cot, row_root
    )
    own_start = lax.axis_index("col") * pieces
    hidden = lax.dynamic_slice_in_dim(hidden_rows, own_start, pieces, 0)
    grad_weight, grad_bias = (
        lax.psum((grad_weight * grad_scale).astype(jnp.bfloat16), "row").astype(jnp.float32),
        lax.psum((grad_bias * grad_scale).astype(jnp.bfloat16), "row").astype(jnp.float32),
    )
    row_sources = row_grads.reshape(row_tiles, tile_side, width_feat)
    col_terms = accumulate(codes_dev, rows_dev, cols_dev, count_dev, row_sources, col_tiles, True)
    grad_sum = lax.psum_scatter(
        col_terms.astype(jnp.bfloat16), "row", scatter_dimension=0, tiled=True
    ).astype(jnp.float32)
    grad_features = (inv_root * grad_sum).astype(jnp.bfloat16)
    return (hidden, grad_features, grad_weight, grad_bias)


def solution(mesh):
    placed = (
        P(("row", "col"), None),
        P(("row", "col")),
        P(),
        P(),
        P(("row", "col"), None),
        P("row", "col", None),
        P("row", "col", None),
        P("row", "col", None),
        P("row", "col", None, None),
    )
    return jax.shard_map(
        local,
        mesh=mesh,
        in_specs=placed,
        out_specs=(P(("row", "col"), None), P(("row", "col"), None), P(), P()),
        check_vma=False,
    )
```

profile of v0, /device:TPU:0, one launch (start us, length us, event | category | flops | bytes accessed | tf_op | source)
XLA Modules:
  0.0 198.0 jit_solution(8774639750551652139)
XLA Ops:
  8.8 11.3 %all_gather.10 = bf16[2048,128]{1,0:T(8,128)(2,1)S(1)} all-gather(bf16[256,128]{1,0:T(8,128)(2,1)S(1)} %multiply_convert_fusion.2), channel_id=1, replica_groups=mesh['row'=8,'col'=4] {'row'}, dimensions={0}, use_global_device_ids=true | all-gather | bytes 589824 | tf_op jit(solution)/shard_map/all_gather | solution.py:76
  20.8 43.5 %while.30 = (s32[]{:T(128)}, f32[8,128,128]{2,1,0:T(8,128)S(1)}, s32[128]{0:T(128)S(1)}, s32[128,256]{1,0:T(8,128)}, s32[]{:T(128)}, /*index=5*/s32[128]{0:T(128...) while((s32[]{:T(128)}, f32[8,128,128]{2,1,0:T(8,128)S(1)}, ...), condition=%wide.region_2.3_spmd, body=%wide.region_0.2_spmd.sunk | while | flops 70519992 | bytes 5837511 | solution.py:42
  23.0 1.6 fusion.58
  28.4 1.6 fusion.58
  33.9 1.6 fusion.58
  39.3 1.6 fusion.58
  44.8 1.6 fusion.58
  50.2 1.6 fusion.58
  55.7 1.6 fusion.58
  61.1 1.6 fusion.58
  65.9 16.0 %all_gather.11 = bf16[1024,128]{1,0:T(8,128)(2,1)S(1)} all-gather(bf16[256,128]{1,0:T(8,128)(2,1)S(1)} %copy-done.3), channel_id=1, replica_groups=mesh['row'=8,'col'=4] {'col'}, dimensions={0}, use_global_device_ids=true | all-gather | bytes 327680 | tf_op jit(solution)/shard_map/all_gather | solution.py:82
  81.9 11.1 %all-gather = bf16[4,1,256]{2,1,0:T(2,128)(2,1)S(1)} all-gather(bf16[1,1,256]{2,1,0:T(2,128)(2,1)S(1)} %reshape.87), channel_id=1, replica_groups=mesh['row'=8,'col'=4] {'col'}, dimensions={0}, use_global_device_ids=true | all-gather | bytes 2560 | tf_op jit(solution)/shard_map/all_gather | solution.py:83
  93.1 9.4 %all-reduce.3.cloned.1.call-done = bf16[1024,128]{1,0:T(8,128)(2,1)} async-done(((bf16[1024,128]{1,0:T(8,128)(2,1)}), bf16[1024,128]{1,0:T(8,128)(2,1)}) %all-reduce.3.cloned.1.call-update) | async-done | bytes 262160 | tf_op jit(solution)/shard_map/psum | solution.py:80
  104.7 49.9 %while.31 = (s32[]{:T(128)}, f32[16,128,128]{2,1,0:T(8,128)S(1)}, s32[128]{0:T(128)S(1)}, s32[128,256]{1,0:T(8,128)}, s32[]{:T(128)}, /*index=5*/s32[128]{0:T(12...) while((s32[]{:T(128)}, f32[16,128,128]{2,1,0:T(8,128)S(1)}, ...), condition=%wide.region_6.7_spmd, body=%wide.region_4.6_spmd.sunk | while | flops 70519992 | bytes 5837511 | solution.py:42
  106.9 2.4 %fusion.61 = f32[16,128,128]{2,1,0:T(8,128)S(1)} fusion(bf16[16,128,128]{2,1,0:T(8,128)(2,1)S(1)} %gather_fusion.1, s32[16,128]{1,0:T(8,128)S(1)} %get-tuple-element.509, s32[16,128]{1,0:T(8,128)S(1)} %get-tuple-element.510, s32[16,128]{1,0:T(8,128)S(1)} %get-tuple-element.511, pred[16]{0:T(512)(128)(4,1)S(1)} %get-tuple-element.512, ...), kind=kOutput, calls=%fused_computation.40.clone.1 | convolution fusion | flops 70254592 | bytes 1597472 | tf_op jit(solution)/shard_map/while/body/eval_jaxpr/tij,tif->tjf/dot_general | solution.py:35
  113.1 2.4 %fusion.61 = f32[16,128,128]{2,1,0:T(8,128)S(1)} fusion(bf16[16,128,128]{2,1,0:T(8,128)(2,1)S(1)} %gather_fusion.1, s32[16,128]{1,0:T(8,128)S(1)} %get-tuple-element.509, s32[16,128]{1,0:T(8,128)S(1)} %get-tuple-element.510, s32[16,128]{1,0:T(8,128)S(1)} %get-tuple-element.511, pred[16]{0:T(512)(128)(4,1)S(1)} %get-tuple-element.512, ...), kind=kOutput, calls=%fused_computation.40.clone.1 | convolution fusion | flops 70254592 | bytes 1597472 | tf_op jit(solution)/shard_map/while/body/eval_jaxpr/tij,tif->tjf/dot_general | solution.py:35
  119.4 2.4 %fusion.61 = f32[16,128,128]{2,1,0:T(8,128)S(1)} fusion(bf16[16,128,128]{2,1,0:T(8,128)(2,1)S(1)} %gather_fusion.1, s32[16,128]{1,0:T(8,128)S(1)} %get-tuple-element.509, s32[16,128]{1,0:T(8,128)S(1)} %get-tuple-element.510, s32[16,128]{1,0:T(8,128)S(1)} %get-tuple-element.511, pred[16]{0:T(512)(128)(4,1)S(1)} %get-tuple-element.512, ...), kind=kOutput, calls=%fused_computation.40.clone.1 | convolution fusion | flops 70254592 | bytes 1597472 | tf_op jit(solution)/shard_map/while/body/eval_jaxpr/tij,tif->tjf/dot_general | solution.py:35
  125.6 2.4 %fusion.61 = f32[16,128,128]{2,1,0:T(8,128)S(1)} fusion(bf16[16,128,128]{2,1,0:T(8,128)(2,1)S(1)} %gather_fusion.1, s32[16,128]{1,0:T(8,128)S(1)} %get-tuple-element.509, s32[16,128]{1,0:T(8,128)S(1)} %get-tuple-element.510, s32[16,128]{1,0:T(8,128)S(1)} %get-tuple-element.511, pred[16]{0:T(512)(128)(4,1)S(1)} %get-tuple-element.512, ...), kind=kOutput, calls=%fused_computation.40.clone.1 | convolution fusion | flops 70254592 | bytes 1597472 | tf_op jit(solution)/shard_map/while/body/eval_jaxpr/tij,tif->tjf/dot_general | solution.py:35
  131.9 2.4 %fusion.61 = f32[16,128,128]{2,1,0:T(8,128)S(1)} fusion(bf16[16,128,128]{2,1,0:T(8,128)(2,1)S(1)} %gather_fusion.1, s32[16,128]{1,0:T(8,128)S(1)} %get-tuple-element.509, s32[16,128]{1,0:T(8,128)S(1)} %get-tuple-element.510, s32[16,128]{1,0:T(8,128)S(1)} %get-tuple-element.511, pred[16]{0:T(512)(128)(4,1)S(1)} %get-tuple-element.512, ...), kind=kOutput, calls=%fused_computation.40.clone.1 | convolution fusion | flops 70254592 | bytes 1597472 | tf_op jit(solution)/shard_map/while/body/eval_jaxpr/tij,tif->tjf/dot_general | solution.py:35
  138.1 2.4 %fusion.61 = f32[16,128,128]{2,1,0:T(8,128)S(1)} fusion(bf16[16,128,128]{2,1,0:T(8,128)(2,1)S(1)} %gather_fusion.1, s32[16,128]{1,0:T(8,128)S(1)} %get-tuple-element.509, s32[16,128]{1,0:T(8,128)S(1)} %get-tuple-element.510, s32[16,128]{1,0:T(8,128)S(1)} %get-tuple-element.511, pred[16]{0:T(512)(128)(4,1)S(1)} %get-tuple-element.512, ...), kind=kOutput, calls=%fused_computation.40.clone.1 | convolution fusion | flops 70254592 | bytes 1597472 | tf_op jit(solution)/shard_map/while/body/eval_jaxpr/tij,tif->tjf/dot_general | solution.py:35
  144.4 2.4 %fusion.61 = f32[16,128,128]{2,1,0:T(8,128)S(1)} fusion(bf16[16,128,128]{2,1,0:T(8,128)(2,1)S(1)} %gather_fusion.1, s32[16,128]{1,0:T(8,128)S(1)} %get-tuple-element.509, s32[16,128]{1,0:T(8,128)S(1)} %get-tuple-element.510, s32[16,128]{1,0:T(8,128)S(1)} %get-tuple-element.511, pred[16]{0:T(512)(128)(4,1)S(1)} %get-tuple-element.512, ...), kind=kOutput, calls=%fused_computation.40.clone.1 | convolution fusion | flops 70254592 | bytes 1597472 | tf_op jit(solution)/shard_map/while/body/eval_jaxpr/tij,tif->tjf/dot_general | solution.py:35
  150.6 2.4 %fusion.61 = f32[16,128,128]{2,1,0:T(8,128)S(1)} fusion(bf16[16,128,128]{2,1,0:T(8,128)(2,1)S(1)} %gather_fusion.1, s32[16,128]{1,0:T(8,128)S(1)} %get-tuple-element.509, s32[16,128]{1,0:T(8,128)S(1)} %get-tuple-element.510, s32[16,128]{1,0:T(8,128)S(1)} %get-tuple-element.511, pred[16]{0:T(512)(128)(4,1)S(1)} %get-tuple-element.512, ...), kind=kOutput, calls=%fused_computation.40.clone.1 | convolution fusion | flops 70254592 | bytes 1597472 | tf_op jit(solution)/shard_map/while/body/eval_jaxpr/tij,tif->tjf/dot_general | solution.py:35
  157.9 23.1 %all-reduce = (bf16[128,128]{1,0:T(8,128)(2,1)S(1)}, bf16[128]{0:T(256)(128)(2,1)S(1)}) all-reduce(bf16[128,128]{1,0:T(8,128)(2,1)S(1)} %fusion.43, bf16[128]{0:T(256)(128)(2,1)S(1)} %multiply_convert_fusion.5), channel_id=1, replica_groups=mesh['row'=8,'col'=4] {'row'}, use_global_device_ids=true, to_apply=%region_8.9 | all-reduce | flops 16512 | bytes 66048 | tf_op jit(solution)/shard_map/psum | solution.py:93
  182.8 6.8 %reduce-scatter.2.cloned.1.call-done = bf16[256,128]{1,0:T(8,128)(2,1)} async-done(((bf16[2048,128]{1,0:T(8,128)(2,1)}), bf16[256,128]{1,0:T(8,128)(2,1)}) %reduce-scatter.2.cloned.1.call-update) | async-done | bytes 65552 | tf_op jit(solution)/shard_map/reduce_scatter | solution.py:98
  (136 shorter events, 73.3 us)
Async XLA Ops:
  7.2 95.3 %copy-start = (bf16[128,128]{1,0:T(8,128)(2,1)S(1)}, bf16[128,128]{1,0:T(8,128)(2,1)}, u32[]{:S(2)}) copy-start(bf16[128,128]{1,0:T(8,128)(2,1)} %param.15) | copy-start | bytes 98308
  7.2 0.7 copy-start.6
  7.2 95.3 %all-reduce.3.cloned.1.call-start = ((), (), s32[]{:S(2)}) async-start(), calls=%async_computation.1 | async-start | bytes 524288 | tf_op jit(solution)/shard_map/psum | solution.py:80
  20.1 0.7 copy-start.4
  20.1 0.7 copy-start.5
  65.1 0.8 copy-start.3
  65.1 124.5 %reduce-scatter.2.cloned.1.call-start = ((), (), s32[]{:S(2)}) async-start(), calls=%async_computation.2 | async-start | bytes 589824 | tf_op jit(solution)/shard_map/reduce_scatter | solution.py:98
  93.0 9.5 %copy-start.8 = (f32[128]{0:T(128)S(1)}, f32[128]{0:T(128)}, u32[]{:S(2)}) copy-start(f32[128]{0:T(128)} %param.16) | copy-start | bytes 1540
  103.8 0.8 copy-start.1
  155.5 1.0 copy-start.2
  156.6 0.9 copy-start.7
Sparse Core Ops, SparseCore 0:
  65.2 37.2 all-reduce.2
  155.7 33.9 reduce-scatter.1
where the time goes:
time: 199 us; the launch traced here: 198 us
  blocking collectives  61.5 us (31%)
  other arithmetic  56.4 us (28%)
  matrix products  34.2 us (17%)
  waiting for transfers between devices  16.3 us (8%)
  local copies, waits for them, and re-layouts  14.8 us (7%)
  between operations  14.1 us (7%)
    scatter-add x16, other arithmetic, block_step(): return summed.at[target].add(product)  25.6 us
    psum x1, blocking collectives, local(): lax.psum((grad_weight * grad_scale).astype(jnp.bfloat16), 'row')  23.1 us
    dot_general x8, matrix products, block_step(): jnp.einsum('tij,tif->tjf', keep, picked, preferred_element_type=jnp.float32)  19.3 us
    all_gather x1, blocking collectives, local(): lax.all_gather(cotangent, 'col', axis=0, tiled=True)  16 us
    dot_general x8, matrix products, block_step(): jnp.einsum('tij,tjf->tif', keep, picked, preferred_element_type=jnp.float32)  12.9 us
    mul x16, other arithmetic, tile_mask(): hashed = (row_code * col_code + row_code + 3 * col_code) % 4093  11.6 us
    and x16, other arithmetic, block_step(): picked = jnp.take(source, anchor, axis=0)  11.6 us
    all_gather x1, blocking collectives, local(): lax.all_gather(scaled, 'row', axis=0, tiled=True)  11.3 us
  transfers between devices with their start and end apart: 2, of which 2 were waited for; matrix products, arithmetic and copies ran while one was open for 1% of the time, Pallas kernels for 0%

commit v1 on v0

--- a/solution.py
+++ b/solution.py
@@ -1,19 +1,27 @@
+import functools
 import math
 
 import jax
 import jax.numpy as jnp
 from jax import lax
+from jax.experimental import pallas as pl
+from jax.experimental.pallas import tpu as pltpu
 from jax.sharding import PartitionSpec as P
 
 BLOCK = 16
+GROUP = 16
+MOD = 4093
+HIT = 64
+DENSE_BYTES = 8 * 2**20
+LIMIT = 16 * 2**20
 
 
 def tile_mask(code_block, living):
     tile_side = code_block.shape[1] // 2
     row_code = code_block[:, :tile_side][:, :, None]
     col_code = code_block[:, tile_side:][:, None, :]
-    hashed = (row_code * col_code + row_code + 3 * col_code) % 4093
-    return ((hashed < 64) & living[:, None, None]).astype(jnp.bfloat16)
+    hashed = (row_code * col_code + row_code + 3 * col_code) % MOD
+    return ((hashed < HIT) & living[:, None, None]).astype(jnp.bfloat16)
 
 
 def accumulate(codes_dev, rows_dev, cols_dev, count_dev, source, out_tiles, backward):
@@ -58,7 +66,9 @@
     return (hidden, grad_weight, grad_bias, grad_scaled)
 
 
-def local(features, degree, weight, bias, cotangent, tile_rows, tile_cols, tile_count, tile_codes):
+def sparse_local(
+    features, degree, weight, bias, cotangent, tile_rows, tile_cols, tile_count, tile_codes
+):
     codes_dev = tile_codes[0, 0]
     rows_dev = tile_rows[0, 0]
     cols_dev = tile_cols[0, 0]
@@ -77,29 +87,324 @@
         col_tiles, tile_side, width_feat
     )
     row_terms = accumulate(codes_dev, rows_dev, cols_dev, count_dev, column_feats, row_tiles, False)
-    row_sum = lax.psum(row_terms.astype(jnp.bfloat16), "col").astype(jnp.float32)
-    row_cot, row_degree = (
-        lax.all_gather(cotangent, "col", axis=0, tiled=True),
-        lax.all_gather(degree.astype(jnp.bfloat16), "col", axis=0, tiled=True),
-    )
-    row_root = lax.rsqrt(row_degree.astype(jnp.float32))[:, None]
-    aggregate = (row_root * row_sum).astype(jnp.bfloat16)
-    hidden_rows, grad_weight, grad_bias, row_grads = dense_part(
-        aggregate, weight, bias, row_cot, row_root
-    )
-    own_start = lax.axis_index("col") * pieces
-    hidden = lax.dynamic_slice_in_dim(hidden_rows, own_start, pieces, 0)
+    row_sum = lax.psum_scatter(
+        row_terms.astype(jnp.bfloat16), "col", scatter_dimension=0, tiled=True
+    ).astype(jnp.float32)
+    aggregate = (inv_root * row_sum).astype(jnp.bfloat16)
+    hidden, grad_weight, grad_bias, grads = dense_part(
+        aggregate, weight, bias, cotangent, inv_root
+    )
     grad_weight, grad_bias = (
-        lax.psum((grad_weight * grad_scale).astype(jnp.bfloat16), "row").astype(jnp.float32),
-        lax.psum((grad_bias * grad_scale).astype(jnp.bfloat16), "row").astype(jnp.float32),
-    )
-    row_sources = row_grads.reshape(row_tiles, tile_side, width_feat)
+        lax.psum((grad_weight * grad_scale).astype(jnp.bfloat16), ("row", "col")),
+        lax.psum((grad_bias * grad_scale).astype(jnp.bfloat16), ("row", "col")),
+    )
+    row_sources = lax.all_gather(grads, "col", axis=0, tiled=True).reshape(
+        row_tiles, tile_side, width_feat
+    )
     col_terms = accumulate(codes_dev, rows_dev, cols_dev, count_dev, row_sources, col_tiles, True)
     grad_sum = lax.psum_scatter(
         col_terms.astype(jnp.bfloat16), "row", scatter_dimension=0, tiled=True
     ).astype(jnp.float32)
     grad_features = (inv_root * grad_sum).astype(jnp.bfloat16)
-    return (hidden, grad_features, grad_weight, grad_bias)
+    return (
+        hidden,
+        grad_features,
+        grad_weight.astype(jnp.float32),
+        grad_bias.astype(jnp.float32),
+    )
+
+
+def swap(value, axis, bits):
+    size = lax.axis_size(axis)
+    return lax.ppermute(value, axis, [(i, i ^ bits) for i in range(size)])
+
+
+def column_of(row):
+    n = row.shape[1]
+    blocks = [
+        jnp.broadcast_to(row[:, k : k + 128], (128, 128)).T for k in range(0, n, 128)
+    ]
+    return jnp.concatenate(blocks, axis=0)
+
+
+def build_kernel(rows_ref, cols_ref, count_ref, codes_ref, block_ref, row_scr, col_scr):
+    slots = codes_ref.shape[0]
+    side = codes_ref.shape[1] // 2
+    block_ref[...] = jnp.zeros_like(block_ref)
+    row_code = codes_ref[:, :side].astype(jnp.float32) + 3.0
+    row_code = jnp.where(row_code > MOD // 2, row_code - MOD, row_code)
+    slot = lax.broadcasted_iota(jnp.int32, (slots, side), 0)
+    row_code = jnp.where(slot < count_ref[0], row_code, 0.0)
+    col_code = codes_ref[:, side:].astype(jnp.float32) + 1.0
+    col_code = jnp.where(col_code > MOD // 2, col_code - MOD, col_code)
+    coarse = 2.0**-12
+    col_scr[...] = col_code * coarse + col_code * (1.0 / MOD - coarse)
+    by_side = row_code.T
+    groups = slots // GROUP
+    for g in range(groups):
+        row_scr[g] = by_side if g == 0 else pltpu.roll(by_side, slots - g * GROUP, axis=1)
+
+    def step(g, carry):
+        row_vals = row_scr[g]
+        col_vals = col_scr[pl.ds(pl.multiple_of(g * GROUP, GROUP), GROUP), :]
+        for t in range(GROUP):
+            s = g * GROUP + t
+            turns = jnp.broadcast_to(row_vals[:, t : t + 1], (side, side)) * jnp.broadcast_to(
+                col_vals[t : t + 1, :], (side, side)
+            )
+            part = turns - jnp.round(turns)
+            middle = 3.0 + (HIT - 1) / 2.0
+            keep = jnp.abs(part - middle / MOD) < (HIT / 2.0) / MOD
+            down = pl.ds(pl.multiple_of(rows_ref[s] * side, side), side)
+            across = pl.ds(pl.multiple_of(cols_ref[s] * side, side), side)
+            block_ref[down, across] += keep.astype(jnp.float32).astype(jnp.bfloat16)
+        return carry
+
+    lax.fori_loop(0, groups, step, 0)
+
+
+def build_block(tile_rows, tile_cols, tile_count, codes, row_nodes, col_nodes):
+    slots, width = codes.shape
+    side = width // 2
+    smem = pl.BlockSpec(memory_space=pltpu.SMEM)
+    vmem = pl.BlockSpec(memory_space=pltpu.VMEM)
+    return pl.pallas_call(
+        build_kernel,
+        out_shape=jax.ShapeDtypeStruct((row_nodes, col_nodes), jnp.bfloat16),
+        in_specs=[smem, smem, smem, vmem],
+        out_specs=vmem,
+        scratch_shapes=[
+            pltpu.VMEM((slots // GROUP, side, slots), jnp.float32),
+            pltpu.VMEM((slots, side), jnp.float32),
+        ],
+        compiler_params=pltpu.CompilerParams(vmem_limit_bytes=LIMIT),
+        cost_estimate=pl.CostEstimate(
+            flops=20 * slots * side * side, bytes_accessed=2**24, transcendentals=0
+        ),
+        name="build_block",
+    )(tile_rows, tile_cols, tile_count, codes)
+
+
+def forward_kernel(n_row, n_col, block_ref, *refs):
+    sources = refs[:n_row]
+    outs = refs[n_row : n_row + n_col]
+    source = refs[n_row + n_col]
+    pieces = sources[0].shape[0]
+    me_row = lax.axis_index("row")
+    me_col = lax.axis_index("col")
+    for k in range(n_row):
+        at = pl.multiple_of((me_row ^ k) * pieces, pieces)
+        source[pl.ds(at, pieces), :] = sources[k][...]
+    whole = source[...]
+    for k in range(n_col):
+        at = pl.multiple_of((me_col ^ k) * pieces, pieces)
+        outs[k][...] = jnp.dot(
+            block_ref[pl.ds(at, pieces), :], whole, preferred_element_type=jnp.float32
+        ).astype(jnp.bfloat16)
+
+
+def forward_parts(block, sources, n_col):
+    pieces, feat = sources[0].shape
+    n_row = len(sources)
+    vmem = pl.BlockSpec(memory_space=pltpu.VMEM)
+    return pl.pallas_call(
+        functools.partial(forward_kernel, n_row, n_col),
+        out_shape=[jax.ShapeDtypeStruct((pieces, feat), jnp.bfloat16)] * n_col,
+        in_specs=[vmem] * (1 + n_row),
+        out_specs=[vmem] * n_col,
+        scratch_shapes=[pltpu.VMEM((pieces * n_row, feat), jnp.bfloat16)],
+        compiler_params=pltpu.CompilerParams(vmem_limit_bytes=LIMIT),
+        name="forward_parts",
+    )(block, *sources)
+
+
+def dense_kernel(
+    n_col, degree_ref, weight_ref, bias_ref, cot_ref, *refs
+):
+    parts = refs[:n_col]
+    hidden_ref, grad_ref, terms_ref = refs[n_col:]
+    total = parts[0][...].astype(jnp.float32)
+    for k in range(1, n_col):
+        total += parts[k][...].astype(jnp.float32)
+    inv_row = lax.rsqrt(degree_ref[...].astype(jnp.float32))
+    aggregate = (column_of(inv_row) * total).astype(jnp.bfloat16)
+    weight = weight_ref[...]
+    preact = jnp.dot(aggregate, weight, preferred_element_type=jnp.float32) + bias_ref[...]
+    decay = jnp.exp(jnp.minimum(preact, 0.0))
+    positive = preact > 0
+    hidden_ref[...] = jnp.where(positive, preact, decay - 1.0).astype(jnp.bfloat16)
+    grad_pre = cot_ref[...].astype(jnp.float32) * jnp.where(positive, 1.0, decay)
+    grad_pre_b = grad_pre.astype(jnp.bfloat16)
+    back = lax.dot_general(
+        weight, grad_pre_b, (((1,), (1,)), ((), ())), preferred_element_type=jnp.float32
+    )
+    grad_ref[...] = (inv_row * back).astype(jnp.bfloat16)
+    feat = weight.shape[0]
+    terms_ref[:feat, :] = lax.dot_general(
+        aggregate, grad_pre_b, (((0,), (0,)), ((), ())), preferred_element_type=jnp.float32
+    ).astype(jnp.bfloat16)
+    bias_terms = jnp.sum(grad_pre, axis=0, keepdims=True)
+    terms_ref[feat:, :] = jnp.broadcast_to(bias_terms, (16, feat)).astype(jnp.bfloat16)
+
+
+def dense_step(degree, weight, bias, cotangent, parts):
+    pieces, feat = cotangent.shape
+    vmem = pl.BlockSpec(memory_space=pltpu.VMEM)
+    return pl.pallas_call(
+        functools.partial(dense_kernel, len(parts)),
+        out_shape=[
+            jax.ShapeDtypeStruct((pieces, feat), jnp.bfloat16),
+            jax.ShapeDtypeStruct((feat, pieces), jnp.bfloat16),
+            jax.ShapeDtypeStruct((feat + 16, feat), jnp.bfloat16),
+        ],
+        in_specs=[vmem] * (4 + len(parts)),
+        out_specs=[vmem] * 3,
+        compiler_params=pltpu.CompilerParams(vmem_limit_bytes=LIMIT),
+        name="dense_step",
+    )(degree.reshape(1, pieces), weight, bias.reshape(1, feat), cotangent, *parts)
+
+
+def backward_kernel(n_row, n_col, first, block_ref, *refs):
+    sources = refs[:n_col]
+    out_ref = refs[n_col]
+    pieces = sources[0].shape[1]
+    feat = sources[0].shape[0]
+    me_row = lax.axis_index("row")
+    me_col = lax.axis_index("col")
+    for m in range(n_row // 2):
+        across = pl.ds(pl.multiple_of((me_row ^ (2 * m + first)) * pieces, pieces), pieces)
+        total = jnp.zeros((feat, pieces), jnp.float32)
+        for k in range(n_col):
+            down = pl.ds(pl.multiple_of((me_col ^ k) * pieces, pieces), pieces)
+            total += jnp.dot(
+                sources[k][...], block_ref[down, across], preferred_element_type=jnp.float32
+            )
+        out_ref[m * feat : (m + 1) * feat, :] = total.astype(jnp.bfloat16)
+
+
+def backward_parts(block, sources, n_row, first):
+    feat, pieces = sources[0].shape
+    n_col = len(sources)
+    vmem = pl.BlockSpec(memory_space=pltpu.VMEM)
+    return pl.pallas_call(
+        functools.partial(backward_kernel, n_row, n_col, first),
+        out_shape=jax.ShapeDtypeStruct((n_row // 2 * feat, pieces), jnp.bfloat16),
+        in_specs=[vmem] * (1 + n_col),
+        out_specs=vmem,
+        compiler_params=pltpu.CompilerParams(vmem_limit_bytes=LIMIT),
+        name="backward_other" if first else "backward_own",
+    )(block, *sources)
+
+
+def pair_kernel(n, mine_ref, theirs_ref, *refs):
+    terms, outs = refs[:-n], refs[-n:]
+    feat = outs[0].shape[0]
+    for m in range(n):
+        span = slice(m * feat, (m + 1) * feat)
+        outs[m][...] = (
+            mine_ref[span, :].astype(jnp.float32) + theirs_ref[span, :].astype(jnp.float32)
+        ).astype(jnp.bfloat16)
+
+
+def pair_sum(mine, theirs, n):
+    rows, width = mine.shape
+    vmem = pl.BlockSpec(memory_space=pltpu.VMEM)
+    return pl.pallas_call(
+        functools.partial(pair_kernel, n),
+        out_shape=[jax.ShapeDtypeStruct((rows // n, width), jnp.bfloat16)] * n,
+        in_specs=[vmem] * 2,
+        out_specs=[vmem] * n,
+        compiler_params=pltpu.CompilerParams(vmem_limit_bytes=LIMIT),
+        name="pair_sum",
+    )(mine, theirs)
+
+
+def finish_kernel(n, degree_ref, *refs):
+    parts, out_ref = refs[:n], refs[n]
+    total = parts[0][...].astype(jnp.float32)
+    for k in range(1, n):
+        total += parts[k][...].astype(jnp.float32)
+    inv_row = lax.rsqrt(degree_ref[...].astype(jnp.float32))
+    out_ref[...] = (inv_row * total).T.astype(jnp.bfloat16)
+
+
+def finish(degree, parts):
+    feat, pieces = parts[0].shape
+    vmem = pl.BlockSpec(memory_space=pltpu.VMEM)
+    return pl.pallas_call(
+        functools.partial(finish_kernel, len(parts)),
+        out_shape=jax.ShapeDtypeStruct((pieces, feat), jnp.bfloat16),
+        in_specs=[vmem] * (1 + len(parts)),
+        out_specs=vmem,
+        compiler_params=pltpu.CompilerParams(vmem_limit_bytes=LIMIT),
+        name="finish",
+    )(degree.reshape(1, pieces), *parts)
+
+
+def terms_kernel(n, scale, *refs):
+    parts, out_ref = refs[:n], refs[n]
+    total = parts[0][...].astype(jnp.float32)
+    for k in range(1, n):
+        total += parts[k][...].astype(jnp.float32)
+    out_ref[...] = (total * scale).astype(out_ref.dtype)
+
+
+def terms_sum(parts, scale, dtype):
+    vmem = pl.BlockSpec(memory_space=pltpu.VMEM)
+    return pl.pallas_call(
+        functools.partial(terms_kernel, len(parts), scale),
+        out_shape=jax.ShapeDtypeStruct(parts[0].shape, dtype),
+        in_specs=[vmem] * len(parts),
+        out_specs=vmem,
+        compiler_params=pltpu.CompilerParams(vmem_limit_bytes=LIMIT),
+        name="terms_sum",
+    )(*parts)
+
+
+def dense_local(
+    features, degree, weight, bias, cotangent, tile_rows, tile_cols, tile_count, tile_codes
+):
+    pieces, feat = features.shape
+    n_row = lax.axis_size("row")
+    n_col = lax.axis_size("col")
+    grad_scale = 1.0 / math.sqrt(pieces * n_row * n_col)
+    inv_root = lax.rsqrt(degree.astype(jnp.float32))[:, None]
+    scaled = (inv_root * features.astype(jnp.float32)).astype(jnp.bfloat16)
+    block = build_block(
+        tile_rows[0, 0],
+        tile_cols[0, 0],
+        tile_count[0, 0],
+        tile_codes[0, 0],
+        pieces * n_col,
+        pieces * n_row,
+    )
+    sources = [None] * n_row
+    sources[0] = scaled
+    for m in range(2, n_row, 2):
+        sources[m] = swap(scaled, "row", m)
+    for m in range(0, n_row, 2):
+        sources[m + 1] = swap(sources[m], "row", 1)
+    parts = forward_parts(block, sources, n_col)
+    landed = [parts[0]] + [swap(parts[k], "col", k) for k in range(1, n_col)]
+    hidden, grad_own, terms = dense_step(degree, weight, bias, cotangent, landed)
+    grads = [grad_own] + [swap(grad_own, "col", k) for k in range(1, n_col)]
+    for_other = backward_parts(block, grads, n_row, 1)
+    from_other = swap(for_other, "row", 1)
+    for_own = backward_parts(block, grads, n_row, 0)
+    chunks = pair_sum(for_own, from_other, n_row // 2)
+    landed = [chunks[0]] + [swap(chunks[m], "row", 2 * m) for m in range(1, n_row // 2)]
+    grad_features = finish(degree, landed)
+    by_chip = terms_sum(
+        [terms] + [swap(terms, "row", k) for k in range(1, n_row)], 1.0, jnp.bfloat16
+    )
+    all_terms = terms_sum(
+        [by_chip] + [swap(by_chip, "col", k) for k in range(1, n_col)], grad_scale, jnp.float32
+    )
+    return (hidden, grad_features, all_terms[:feat], all_terms[feat])
+
+
+def power_of_two(n):
+    return n & (n - 1) == 0
 
 
 def solution(mesh):
@@ -114,6 +419,15 @@
         P("row", "col", None),
         P("row", "col", None, None),
     )
+    n_row, n_col = mesh.shape["row"], mesh.shape["col"]
+
+    def local(features, *rest):
+        block_bytes = 2 * features.shape[0] ** 2 * n_row * n_col
+        paired = power_of_two(n_row) and power_of_two(n_col) and n_row > 1
+        if paired and block_bytes <= DENSE_BYTES:
+            return dense_local(features, *rest)
+        return sparse_local(features, *rest)
+
     return jax.shard_map(
         local,
         mesh=mesh,

time: 199 us -> 68.5 us (0.34)
  blocking collectives: 61.5 us -> 0 us
  other arithmetic: 56.4 us -> 1.63 us
  matrix products: 34.2 us -> 0 us
  starting transfers between devices: 0.08 us -> 27 us
  between operations: 14.1 us -> 1.44 us
  local copies, waits for them, and re-layouts: 14.8 us -> 3.37 us
  waiting for transfers between devices: 16.3 us -> 26.6 us
  Pallas kernels: 0 us -> 8.22 us
    all_gather x3 -> x0, blocking collectives: 38.4 us -> none  [the longest x1 16 us: local(): lax.all_gather(cotangent, 'col', axis=0, tiled=True)]
    dot_general x19 -> x0, matrix products: 34.2 us -> none  [the longest x8 19.3 us: block_step(): jnp.einsum('tij,tif->tjf', keep, picked, preferred_element_type=jnp.float32)]
    ppermute x0 -> x27, starting transfers between devices: none -> 27 us  [swap(): return lax.ppermute(value, axis, [(i, i ^ bits) for i in range(size)])]
    ppermute x0 -> x27, waiting for transfers between devices: none -> 26.6 us  [swap(): return lax.ppermute(value, axis, [(i, i ^ bits) for i in range(size)])]
    scatter-add x16 -> x0, other arithmetic: 25.6 us -> none  [block_step(): return summed.at[target].add(product)]
    psum x1 -> x0, blocking collectives: 23.1 us -> none  [local(): lax.psum((grad_weight * grad_scale).astype(jnp.bfloat16), 'row')]
    mul x16 -> x0, other arithmetic: 11.6 us -> none  [tile_mask(): hashed = (row_code * col_code + row_code + 3 * col_code) % 4093]
    and x16 -> x0, other arithmetic: 11.6 us -> none  [block_step(): picked = jnp.take(source, anchor, axis=0)]
  transfers between devices with their start and end apart: 2 -> 27, of which waited for: 2 -> 16; matrix products, arithmetic and copies ran while one was open for 1% -> 2% of each run, Pallas kernels for 0% -> 7%
where the time goes in v1:
time: 68.5 us; the launch traced here: 68.2 us
  starting transfers between devices  27 us (39%)
  waiting for transfers between devices  26.6 us (39%)
  Pallas kernels  8.22 us (12%)
  local copies, waits for them, and re-layouts  3.37 us (5%)
  other arithmetic  1.63 us (2%)
  between operations  1.44 us (2%)
    ppermute x27, starting transfers between devices, swap(): return lax.ppermute(value, axis, [(i, i ^ bits) for i in range(size)])  27 us
    ppermute x27, waiting for transfers between devices, swap(): return lax.ppermute(value, axis, [(i, i ^ bits) for i in range(size)])  26.6 us
    pallas_call x1, Pallas kernels, build_block(): pl.pallas_call(build_kernel, out_shape=jax.ShapeDtypeStruct((row_nodes, c...  4.21 us
    unnamed x14, local copies, waits for them, and re-layouts  2.22 us
  transfers between devices with their start and end apart: 27, of which 16 were waited for; matrix products, arithmetic and copies ran while one was open for 2% of the time, Pallas kernels for 7%

profile of v1, /device:TPU:0, one launch (start us, length us, event | category | flops | bytes accessed | tf_op | source)
XLA Modules:
  0.0 68.2 jit_solution(15716511595339398007)
XLA Ops:
  2.3 3.0 %collective-permute-start.1 = (bf16[256,128]{1,0:T(8,128)(2,1)S(1)}, bf16[256,128]{1,0:T(8,128)(2,1)S(1)}, u32[]{:S(2)}, u32[]{:S(2)}) collective-permute-start(bf16[256,128]{1,0:T(8,128)(2,1)S(1)} %multiply_convert_fusion.refs_0_), channel_id=1, source_target_pairs={{0,8},{4,12},{8,0},{12,4},{16,24},{20,28},{24,16},{28,20},{1,9},{5... | collective-permute-start | bytes 196616 | tf_op jit(solution)/shard_map/ppermute | solution.py:119
  5.3 1.5 %collective-permute-start.3 = (bf16[256,128]{1,0:T(8,128)(2,1)S(1)}, bf16[256,128]{1,0:T(8,128)(2,1)S(1)}, u32[]{:S(2)}, u32[]{:S(2)}) collective-permute-start(bf16[256,128]{1,0:T(8,128)(2,1)S(1)} %multiply_convert_fusion.refs_0_), channel_id=1, source_target_pairs={{0,16},{4,20},{8,24},{12,28},{16,0},{20,4},{24,8},{28,12},{1,17},{... | collective-permute-start | bytes 196616 | tf_op jit(solution)/shard_map/ppermute | solution.py:119
  7.6 1.9 %collective-permute-done.3.refs_4_ = bf16[256,128]{1,0:T(8,128)(2,1)S(1)} collective-permute-done((bf16[256,128]{1,0:T(8,128)(2,1)S(1)}, bf16[256,128]{1,0:T(8,128)(2,1)S(1)}, u32[]{:S(2)}, u32[]{:S(2)}) %collective-permute-start.3) | collective-permute-done | bytes 65568 | tf_op jit(solution)/shard_map/ppermute | solution.py:119
  9.5 2.4 %collective-permute-done.5.refs_6_ = bf16[256,128]{1,0:T(8,128)(2,1)S(1)} collective-permute-done((bf16[256,128]{1,0:T(8,128)(2,1)S(1)}, bf16[256,128]{1,0:T(8,128)(2,1)S(1)}, u32[]{:S(2)}, u32[]{:S(2)}) %collective-permute-start.5) | collective-permute-done | bytes 65568 | tf_op jit(solution)/shard_map/ppermute | solution.py:119
  14.8 4.2 %build_block.1.block_ref = bf16[1024,2048]{1,0:T(8,128)(2,1)S(1)} custom-call(s32[128]{0:T(128)S(1)} %bitcast.12, s32[128]{0:T(128)S(1)} %bitcast.13, s32[1]{0:T(128)} %bitcast.8.count_ref, s32[128,256]{1,0:T(8,128)S(1)} %bitcast.9), custom_call_target="tpu_custom_call" | custom-call | flops 41943040 | bytes 16777216 | tf_op jit(solution)/shard_map/build_block/pallas_call | solution.py:171
  19.1 1.3 %forward_parts.1 = (bf16[256,128]{1,0:T(8,128)(2,1)S(1)}, bf16[256,128]{1,0:T(8,128)(2,1)S(1)}, bf16[256,128]{1,0:T(8,128)(2,1)S(1)}, bf16[256,128]{1,0:T(8,128)(2,1)S(1)}) custom-call(bf16[1024,2048]{1,0:T(8,128)(2,1)S(1)} %build_block.1.block_ref, bf16[256,128]{1,0:T(8,128)(2,1)S(1)} %multiply_convert_fusion.refs_0_, ...), custom_call_target="tpu_custom_call" | custom-call | tf_op jit(solution)/shard_map/forward_parts/pallas_call | solution.py:210
  20.4 1.6 %collective-permute-start.7 = (bf16[256,128]{1,0:T(8,128)(2,1)S(1)}, bf16[256,128]{1,0:T(8,128)(2,1)S(1)}, u32[]{:S(2)}, u32[]{:S(2)}) collective-permute-start(bf16[256,128]{1,0:T(8,128)(2,1)S(1)} %get-tuple-element.16), channel_id=1, source_target_pairs={{0,1},{1,0},{2,3},{3,2},{4,5},{5,4},{6,7},{7,6},{8,9},{9,8},{10,11... | collective-permute-start | bytes 196616 | tf_op jit(solution)/shard_map/ppermute | solution.py:119
  22.0 2.6 %collective-permute-start.8 = (bf16[256,128]{1,0:T(8,128)(2,1)S(1)}, bf16[256,128]{1,0:T(8,128)(2,1)S(1)}, u32[]{:S(2)}, u32[]{:S(2)}) collective-permute-start(bf16[256,128]{1,0:T(8,128)(2,1)S(1)} %get-tuple-element.17), channel_id=1, source_target_pairs={{0,2},{1,3},{2,0},{3,1},{4,6},{5,7},{6,4},{7,5},{8,10},{9,11},{10,... | collective-permute-start | bytes 196616 | tf_op jit(solution)/shard_map/ppermute | solution.py:119
  25.0 4.0 %collective-permute-done.8.refs_2_ = bf16[256,128]{1,0:T(8,128)(2,1)S(1)} collective-permute-done((bf16[256,128]{1,0:T(8,128)(2,1)S(1)}, bf16[256,128]{1,0:T(8,128)(2,1)S(1)}, u32[]{:S(2)}, u32[]{:S(2)}) %collective-permute-start.8) | collective-permute-done | bytes 65568 | tf_op jit(solution)/shard_map/ppermute | solution.py:119
  29.0 1.8 %collective-permute-done.9.refs_3_ = bf16[256,128]{1,0:T(8,128)(2,1)S(1)} collective-permute-done((bf16[256,128]{1,0:T(8,128)(2,1)S(1)}, bf16[256,128]{1,0:T(8,128)(2,1)S(1)}, u32[]{:S(2)}, u32[]{:S(2)}) %collective-permute-start.9) | collective-permute-done | bytes 65568 | tf_op jit(solution)/shard_map/ppermute | solution.py:119
  31.7 1.2 %collective-permute-start.10 = (bf16[128,256]{1,0:T(8,128)(2,1)S(1)}, bf16[128,256]{1,0:T(8,128)(2,1)S(1)}, u32[]{:S(2)}, u32[]{:S(2)}) collective-permute-start(bf16[128,256]{1,0:T(8,128)(2,1)S(1)} %get-tuple-element.20.refs_0_), channel_id=1, source_target_pairs={{0,1},{1,0},{2,3},{3,2},{4,5},{5,4},{6,7},{7,6},{8,9},{9,8},{10,11... | collective-permute-start | bytes 196616 | tf_op jit(solution)/shard_map/ppermute | solution.py:119
  32.9 1.7 %collective-permute-start.11 = (bf16[128,256]{1,0:T(8,128)(2,1)S(1)}, bf16[128,256]{1,0:T(8,128)(2,1)S(1)}, u32[]{:S(2)}, u32[]{:S(2)}) collective-permute-start(bf16[128,256]{1,0:T(8,128)(2,1)S(1)} %get-tuple-element.20.refs_0_), channel_id=1, source_target_pairs={{0,2},{1,3},{2,0},{3,1},{4,6},{5,7},{6,4},{7,5},{8,10},{9,11},{10,... | collective-permute-start | bytes 196616 | tf_op jit(solution)/shard_map/ppermute | solution.py:119
  34.6 1.4 %collective-permute-start.12 = (bf16[128,256]{1,0:T(8,128)(2,1)S(1)}, bf16[128,256]{1,0:T(8,128)(2,1)S(1)}, u32[]{:S(2)}, u32[]{:S(2)}) collective-permute-start(bf16[128,256]{1,0:T(8,128)(2,1)S(1)} %get-tuple-element.20.refs_0_), channel_id=1, source_target_pairs={{0,3},{1,2},{2,1},{3,0},{4,7},{5,6},{6,5},{7,4},{8,11},{9,10},{10,... | collective-permute-start | bytes 196616 | tf_op jit(solution)/shard_map/ppermute | solution.py:119
  36.0 3.9 %collective-permute-done.11.refs_2_ = bf16[128,256]{1,0:T(8,128)(2,1)S(1)} collective-permute-done((bf16[128,256]{1,0:T(8,128)(2,1)S(1)}, bf16[128,256]{1,0:T(8,128)(2,1)S(1)}, u32[]{:S(2)}, u32[]{:S(2)}) %collective-permute-start.11) | collective-permute-done | bytes 65568 | tf_op jit(solution)/shard_map/ppermute | solution.py:119
  43.8 1.6 %collective-permute-start.21 = (bf16[144,128]{1,0:T(8,128)(2,1)S(1)}, bf16[144,128]{1,0:T(8,128)(2,1)S(1)}, u32[]{:S(2)}, u32[]{:S(2)}) collective-permute-start(bf16[144,128]{1,0:T(8,128)(2,1)S(1)} %get-tuple-element.25.refs_0_), channel_id=1, source_target_pairs={{0,20},{4,16},{8,28},{12,24},{16,4},{20,0},{24,12},{28,8},{1,21},{... | collective-permute-start | bytes 110600 | tf_op jit(solution)/shard_map/ppermute | solution.py:119
  46.3 1.4 %collective-permute-start.23 = (bf16[144,128]{1,0:T(8,128)(2,1)S(1)}, bf16[144,128]{1,0:T(8,128)(2,1)S(1)}, u32[]{:S(2)}, u32[]{:S(2)}) collective-permute-start(bf16[144,128]{1,0:T(8,128)(2,1)S(1)} %get-tuple-element.25.refs_0_), channel_id=1, source_target_pairs={{0,28},{4,24},{8,20},{12,16},{16,12},{20,8},{24,4},{28,0},{1,29},{... | collective-permute-start | bytes 110600 | tf_op jit(solution)/shard_map/ppermute | solution.py:119
  47.9 3.1 %collective-permute-done.22.refs_6_ = bf16[144,128]{1,0:T(8,128)(2,1)S(1)} collective-permute-done((bf16[144,128]{1,0:T(8,128)(2,1)S(1)}, bf16[144,128]{1,0:T(8,128)(2,1)S(1)}, u32[]{:S(2)}, u32[]{:S(2)}) %collective-permute-start.22) | collective-permute-done | bytes 36896 | tf_op jit(solution)/shard_map/ppermute | solution.py:119
  51.1 1.2 %collective-permute-start.24 = (bf16[144,128]{1,0:T(8,128)(2,1)S(1)}, bf16[144,128]{1,0:T(8,128)(2,1)S(1)}, u32[]{:S(2)}, u32[]{:S(2)}) collective-permute-start(bf16[144,128]{1,0:T(8,128)(2,1)S(1)} %terms_sum.2.refs_0_), channel_id=1, source_target_pairs={{0,1},{1,0},{2,3},{3,2},{4,5},{5,4},{6,7},{7,6},{8,9},{9,8},{10,11... | collective-permute-start | bytes 110600 | tf_op jit(solution)/shard_map/ppermute | solution.py:119
  52.3 1.2 %collective-permute-start.25 = (bf16[144,128]{1,0:T(8,128)(2,1)S(1)}, bf16[144,128]{1,0:T(8,128)(2,1)S(1)}, u32[]{:S(2)}, u32[]{:S(2)}) collective-permute-start(bf16[144,128]{1,0:T(8,128)(2,1)S(1)} %terms_sum.2.refs_0_), channel_id=1, source_target_pairs={{0,2},{1,3},{2,0},{3,1},{4,6},{5,7},{6,4},{7,5},{8,10},{9,11},{10,... | collective-permute-start | bytes 110600 | tf_op jit(solution)/shard_map/ppermute | solution.py:119
  53.5 2.1 %collective-permute-start.26 = (bf16[144,128]{1,0:T(8,128)(2,1)S(1)}, bf16[144,128]{1,0:T(8,128)(2,1)S(1)}, u32[]{:S(2)}, u32[]{:S(2)}) collective-permute-start(bf16[144,128]{1,0:T(8,128)(2,1)S(1)} %terms_sum.2.refs_0_), channel_id=1, source_target_pairs={{0,3},{1,2},{2,1},{3,0},{4,7},{5,6},{6,5},{7,4},{8,11},{9,10},{10,... | collective-permute-start | bytes 110600 | tf_op jit(solution)/shard_map/ppermute | solution.py:119
  56.0 2.1 %collective-permute-done.25.refs_2_ = bf16[144,128]{1,0:T(8,128)(2,1)S(1)} collective-permute-done((bf16[144,128]{1,0:T(8,128)(2,1)S(1)}, bf16[144,128]{1,0:T(8,128)(2,1)S(1)}, u32[]{:S(2)}, u32[]{:S(2)}) %collective-permute-start.25) | collective-permute-done | bytes 36896 | tf_op jit(solution)/shard_map/ppermute | solution.py:119
  59.3 1.6 %collective-permute-start.14 = (bf16[128,256]{1,0:T(8,128)(2,1)S(1)}, bf16[128,256]{1,0:T(8,128)(2,1)S(1)}, u32[]{:S(2)}, u32[]{:S(2)}) collective-permute-start(bf16[128,256]{1,0:T(8,128)(2,1)S(1)} %get-tuple-element.22), channel_id=1, source_target_pairs={{0,8},{4,12},{8,0},{12,4},{16,24},{20,28},{24,16},{28,20},{1,9},{5... | collective-permute-start | bytes 196616 | tf_op jit(solution)/shard_map/ppermute | solution.py:119
  61.0 1.4 %collective-permute-start.15 = (bf16[128,256]{1,0:T(8,128)(2,1)S(1)}, bf16[128,256]{1,0:T(8,128)(2,1)S(1)}, u32[]{:S(2)}, u32[]{:S(2)}) collective-permute-start(bf16[128,256]{1,0:T(8,128)(2,1)S(1)} %get-tuple-element.23), channel_id=1, source_target_pairs={{0,16},{4,20},{8,24},{12,28},{16,0},{20,4},{24,8},{28,12},{1,17},{... | collective-permute-start | bytes 196616 | tf_op jit(solution)/shard_map/ppermute | solution.py:119
  65.2 2.3 %collective-permute-done.16.refs_3_ = bf16[128,256]{1,0:T(8,128)(2,1)S(1)} collective-permute-done((bf16[128,256]{1,0:T(8,128)(2,1)S(1)}, bf16[128,256]{1,0:T(8,128)(2,1)S(1)}, u32[]{:S(2)}, u32[]{:S(2)}) %collective-permute-start.16) | collective-permute-done | bytes 65568 | tf_op jit(solution)/shard_map/ppermute | solution.py:119
  (57 shorter events, 16.4 us)
Async XLA Ops:
  2.3 5.4 %collective-permute-start.1 = (bf16[256,128]{1,0:T(8,128)(2,1)S(1)}, bf16[256,128]{1,0:T(8,128)(2,1)S(1)}, u32[]{:S(2)}, u32[]{:S(2)}) collective-permute-start(bf16[256,128]{1,0:T(8,128)(2,1)S(1)} %multiply_convert_fusion.refs_0_), channel_id=1, source_target_pairs={{0,8},{4,12},{8,0},{12,4},{16,24},{20,28},{24,16},{28,20},{1,9},{5... | collective-permute-start | bytes 196616 | tf_op jit(solution)/shard_map/ppermute | solution.py:119
  5.3 4.3 %collective-permute-start.3 = (bf16[256,128]{1,0:T(8,128)(2,1)S(1)}, bf16[256,128]{1,0:T(8,128)(2,1)S(1)}, u32[]{:S(2)}, u32[]{:S(2)}) collective-permute-start(bf16[256,128]{1,0:T(8,128)(2,1)S(1)} %multiply_convert_fusion.refs_0_), channel_id=1, source_target_pairs={{0,16},{4,20},{8,24},{12,28},{16,0},{20,4},{24,8},{28,12},{1,17},{... | collective-permute-start | bytes 196616 | tf_op jit(solution)/shard_map/ppermute | solution.py:119
  6.8 5.2 %collective-permute-start.5 = (bf16[256,128]{1,0:T(8,128)(2,1)S(1)}, bf16[256,128]{1,0:T(8,128)(2,1)S(1)}, u32[]{:S(2)}, u32[]{:S(2)}) collective-permute-start(bf16[256,128]{1,0:T(8,128)(2,1)S(1)} %multiply_convert_fusion.refs_0_), channel_id=1, source_target_pairs={{0,24},{4,28},{8,16},{12,20},{16,8},{20,12},{24,0},{28,4},{1,25},{... | collective-permute-start | bytes 196616 | tf_op jit(solution)/shard_map/ppermute | solution.py:119
  6.8 12.2 %collective-permute-start = (bf16[256,128]{1,0:T(8,128)(2,1)S(1)}, bf16[256,128]{1,0:T(8,128)(2,1)S(1)}, u32[]{:S(2)}, u32[]{:S(2)}) collective-permute-start(bf16[256,128]{1,0:T(8,128)(2,1)S(1)} %multiply_convert_fusion.refs_0_), channel_id=1, source_target_pairs={{0,4},{4,0},{8,12},{12,8},{16,20},{20,16},{24,28},{28,24},{1,5},{5... | collective-permute-start | bytes 196616 | tf_op jit(solution)/shard_map/ppermute | solution.py:119
  7.6 11.4 %collective-permute-start.2 = (bf16[256,128]{1,0:T(8,128)(2,1)S(1)}, bf16[256,128]{1,0:T(8,128)(2,1)S(1)}, u32[]{:S(2)}, u32[]{:S(2)}) collective-permute-start(bf16[256,128]{1,0:T(8,128)(2,1)S(1)} %collective-permute-done.1.refs_2_), channel_id=1, source_target_pairs={{0,4},{4,0},{8,12},{12,8},{16,20},{20,16},{24,28},{28,24},{1,5},{5... | collective-permute-start | bytes 196616 | tf_op jit(solution)/shard_map/ppermute | solution.py:119
  9.5 9.5 %collective-permute-start.4 = (bf16[256,128]{1,0:T(8,128)(2,1)S(1)}, bf16[256,128]{1,0:T(8,128)(2,1)S(1)}, u32[]{:S(2)}, u32[]{:S(2)}) collective-permute-start(bf16[256,128]{1,0:T(8,128)(2,1)S(1)} %collective-permute-done.3.refs_4_), channel_id=1, source_target_pairs={{0,4},{4,0},{8,12},{12,8},{16,20},{20,16},{24,28},{28,24},{1,5},{5... | collective-permute-start | bytes 196616 | tf_op jit(solution)/shard_map/ppermute | solution.py:119
  11.9 7.1 %collective-permute-start.6 = (bf16[256,128]{1,0:T(8,128)(2,1)S(1)}, bf16[256,128]{1,0:T(8,128)(2,1)S(1)}, u32[]{:S(2)}, u32[]{:S(2)}) collective-permute-start(bf16[256,128]{1,0:T(8,128)(2,1)S(1)} %collective-permute-done.5.refs_6_), channel_id=1, source_target_pairs={{0,4},{4,0},{8,12},{12,8},{16,20},{20,16},{24,28},{28,24},{1,5},{5... | collective-permute-start | bytes 196616 | tf_op jit(solution)/shard_map/ppermute | solution.py:119
  20.4 4.6 %collective-permute-start.7 = (bf16[256,128]{1,0:T(8,128)(2,1)S(1)}, bf16[256,128]{1,0:T(8,128)(2,1)S(1)}, u32[]{:S(2)}, u32[]{:S(2)}) collective-permute-start(bf16[256,128]{1,0:T(8,128)(2,1)S(1)} %get-tuple-element.16), channel_id=1, source_target_pairs={{0,1},{1,0},{2,3},{3,2},{4,5},{5,4},{6,7},{7,6},{8,9},{9,8},{10,11... | collective-permute-start | bytes 196616 | tf_op jit(solution)/shard_map/ppermute | solution.py:119
  22.0 7.0 %collective-permute-start.8 = (bf16[256,128]{1,0:T(8,128)(2,1)S(1)}, bf16[256,128]{1,0:T(8,128)(2,1)S(1)}, u32[]{:S(2)}, u32[]{:S(2)}) collective-permute-start(bf16[256,128]{1,0:T(8,128)(2,1)S(1)} %get-tuple-element.17), channel_id=1, source_target_pairs={{0,2},{1,3},{2,0},{3,1},{4,6},{5,7},{6,4},{7,5},{8,10},{9,11},{10,... | collective-permute-start | bytes 196616 | tf_op jit(solution)/shard_map/ppermute | solution.py:119
  24.6 6.1 %collective-permute-start.9 = (bf16[256,128]{1,0:T(8,128)(2,1)S(1)}, bf16[256,128]{1,0:T(8,128)(2,1)S(1)}, u32[]{:S(2)}, u32[]{:S(2)}) collective-permute-start(bf16[256,128]{1,0:T(8,128)(2,1)S(1)} %get-tuple-element.18), channel_id=1, source_target_pairs={{0,3},{1,2},{2,1},{3,0},{4,7},{5,6},{6,5},{7,4},{8,11},{9,10},{10,... | collective-permute-start | bytes 196616 | tf_op jit(solution)/shard_map/ppermute | solution.py:119
  31.7 4.4 %collective-permute-start.10 = (bf16[128,256]{1,0:T(8,128)(2,1)S(1)}, bf16[128,256]{1,0:T(8,128)(2,1)S(1)}, u32[]{:S(2)}, u32[]{:S(2)}) collective-permute-start(bf16[128,256]{1,0:T(8,128)(2,1)S(1)} %get-tuple-element.20.refs_0_), channel_id=1, source_target_pairs={{0,1},{1,0},{2,3},{3,2},{4,5},{5,4},{6,7},{7,6},{8,9},{9,8},{10,11... | collective-permute-start | bytes 196616 | tf_op jit(solution)/shard_map/ppermute | solution.py:119
  32.9 7.0 %collective-permute-start.11 = (bf16[128,256]{1,0:T(8,128)(2,1)S(1)}, bf16[128,256]{1,0:T(8,128)(2,1)S(1)}, u32[]{:S(2)}, u32[]{:S(2)}) collective-permute-start(bf16[128,256]{1,0:T(8,128)(2,1)S(1)} %get-tuple-element.20.refs_0_), channel_id=1, source_target_pairs={{0,2},{1,3},{2,0},{3,1},{4,6},{5,7},{6,4},{7,5},{8,10},{9,11},{10,... | collective-permute-start | bytes 196616 | tf_op jit(solution)/shard_map/ppermute | solution.py:119
  34.6 6.2 %collective-permute-start.12 = (bf16[128,256]{1,0:T(8,128)(2,1)S(1)}, bf16[128,256]{1,0:T(8,128)(2,1)S(1)}, u32[]{:S(2)}, u32[]{:S(2)}) collective-permute-start(bf16[128,256]{1,0:T(8,128)(2,1)S(1)} %get-tuple-element.20.refs_0_), channel_id=1, source_target_pairs={{0,3},{1,2},{2,1},{3,0},{4,7},{5,6},{6,5},{7,4},{8,11},{9,10},{10,... | collective-permute-start | bytes 196616 | tf_op jit(solution)/shard_map/ppermute | solution.py:119
  41.3 18.0 %collective-permute-start.13 = (bf16[512,256]{1,0:T(8,128)(2,1)S(1)}, bf16[512,256]{1,0:T(8,128)(2,1)S(1)}, u32[]{:S(2)}, u32[]{:S(2)}) collective-permute-start(bf16[512,256]{1,0:T(8,128)(2,1)S(1)} %backward_other.1), channel_id=1, source_target_pairs={{0,4},{4,0},{8,12},{12,8},{16,20},{20,16},{24,28},{28,24},{1,5},{5... | collective-permute-start | bytes 786440 | tf_op jit(solution)/shard_map/ppermute | solution.py:119
  41.9 4.3 %collective-permute-start.18 = (bf16[144,128]{1,0:T(8,128)(2,1)S(1)}, bf16[144,128]{1,0:T(8,128)(2,1)S(1)}, u32[]{:S(2)}, u32[]{:S(2)}) collective-permute-start(bf16[144,128]{1,0:T(8,128)(2,1)S(1)} %get-tuple-element.25.refs_0_), channel_id=1, source_target_pairs={{0,8},{4,12},{8,0},{12,4},{16,24},{20,28},{24,16},{28,20},{1,9},{5... | collective-permute-start | bytes 110600 | tf_op jit(solution)/shard_map/ppermute | solution.py:119
  43.3 4.4 %collective-permute-start.20 = (bf16[144,128]{1,0:T(8,128)(2,1)S(1)}, bf16[144,128]{1,0:T(8,128)(2,1)S(1)}, u32[]{:S(2)}, u32[]{:S(2)}) collective-permute-start(bf16[144,128]{1,0:T(8,128)(2,1)S(1)} %get-tuple-element.25.refs_0_), channel_id=1, source_target_pairs={{0,16},{4,20},{8,24},{12,28},{16,0},{20,4},{24,8},{28,12},{1,17},{... | collective-permute-start | bytes 110600 | tf_op jit(solution)/shard_map/ppermute | solution.py:119
  46.2 4.9 %collective-permute-start.22 = (bf16[144,128]{1,0:T(8,128)(2,1)S(1)}, bf16[144,128]{1,0:T(8,128)(2,1)S(1)}, u32[]{:S(2)}, u32[]{:S(2)}) collective-permute-start(bf16[144,128]{1,0:T(8,128)(2,1)S(1)} %get-tuple-element.25.refs_0_), channel_id=1, source_target_pairs={{0,24},{4,28},{8,16},{12,20},{16,8},{20,12},{24,0},{28,4},{1,25},{... | collective-permute-start | bytes 110600 | tf_op jit(solution)/shard_map/ppermute | solution.py:119
  46.3 4.7 %collective-permute-start.23 = (bf16[144,128]{1,0:T(8,128)(2,1)S(1)}, bf16[144,128]{1,0:T(8,128)(2,1)S(1)}, u32[]{:S(2)}, u32[]{:S(2)}) collective-permute-start(bf16[144,128]{1,0:T(8,128)(2,1)S(1)} %get-tuple-element.25.refs_0_), channel_id=1, source_target_pairs={{0,28},{4,24},{8,20},{12,16},{16,12},{20,8},{24,4},{28,0},{1,29},{... | collective-permute-start | bytes 110600 | tf_op jit(solution)/shard_map/ppermute | solution.py:119
  51.1 4.9 %collective-permute-start.24 = (bf16[144,128]{1,0:T(8,128)(2,1)S(1)}, bf16[144,128]{1,0:T(8,128)(2,1)S(1)}, u32[]{:S(2)}, u32[]{:S(2)}) collective-permute-start(bf16[144,128]{1,0:T(8,128)(2,1)S(1)} %terms_sum.2.refs_0_), channel_id=1, source_target_pairs={{0,1},{1,0},{2,3},{3,2},{4,5},{5,4},{6,7},{7,6},{8,9},{9,8},{10,11... | collective-permute-start | bytes 110600 | tf_op jit(solution)/shard_map/ppermute | solution.py:119
  52.3 5.8 %collective-permute-start.25 = (bf16[144,128]{1,0:T(8,128)(2,1)S(1)}, bf16[144,128]{1,0:T(8,128)(2,1)S(1)}, u32[]{:S(2)}, u32[]{:S(2)}) collective-permute-start(bf16[144,128]{1,0:T(8,128)(2,1)S(1)} %terms_sum.2.refs_0_), channel_id=1, source_target_pairs={{0,2},{1,3},{2,0},{3,1},{4,6},{5,7},{6,4},{7,5},{8,10},{9,11},{10,... | collective-permute-start | bytes 110600 | tf_op jit(solution)/shard_map/ppermute | solution.py:119
  53.5 5.8 %collective-permute-start.26 = (bf16[144,128]{1,0:T(8,128)(2,1)S(1)}, bf16[144,128]{1,0:T(8,128)(2,1)S(1)}, u32[]{:S(2)}, u32[]{:S(2)}) collective-permute-start(bf16[144,128]{1,0:T(8,128)(2,1)S(1)} %terms_sum.2.refs_0_), channel_id=1, source_target_pairs={{0,3},{1,2},{2,1},{3,0},{4,7},{5,6},{6,5},{7,4},{8,11},{9,10},{10,... | collective-permute-start | bytes 110600 | tf_op jit(solution)/shard_map/ppermute | solution.py:119
  59.3 5.0 %collective-permute-start.14 = (bf16[128,256]{1,0:T(8,128)(2,1)S(1)}, bf16[128,256]{1,0:T(8,128)(2,1)S(1)}, u32[]{:S(2)}, u32[]{:S(2)}) collective-permute-start(bf16[128,256]{1,0:T(8,128)(2,1)S(1)} %get-tuple-element.22), channel_id=1, source_target_pairs={{0,8},{4,12},{8,0},{12,4},{16,24},{20,28},{24,16},{28,20},{1,9},{5... | collective-permute-start | bytes 196616 | tf_op jit(solution)/shard_map/ppermute | solution.py:119
  61.0 4.3 %collective-permute-start.15 = (bf16[128,256]{1,0:T(8,128)(2,1)S(1)}, bf16[128,256]{1,0:T(8,128)(2,1)S(1)}, u32[]{:S(2)}, u32[]{:S(2)}) collective-permute-start(bf16[128,256]{1,0:T(8,128)(2,1)S(1)} %get-tuple-element.23), channel_id=1, source_target_pairs={{0,16},{4,20},{8,24},{12,28},{16,0},{20,4},{24,8},{28,12},{1,17},{... | collective-permute-start | bytes 196616 | tf_op jit(solution)/shard_map/ppermute | solution.py:119
  62.3 5.2 %collective-permute-start.16 = (bf16[128,256]{1,0:T(8,128)(2,1)S(1)}, bf16[128,256]{1,0:T(8,128)(2,1)S(1)}, u32[]{:S(2)}, u32[]{:S(2)}) collective-permute-start(bf16[128,256]{1,0:T(8,128)(2,1)S(1)} %get-tuple-element.24), channel_id=1, source_target_pairs={{0,24},{4,28},{8,16},{12,20},{16,8},{20,12},{24,0},{28,4},{1,25},{... | collective-permute-start | bytes 196616 | tf_op jit(solution)/shard_map/ppermute | solution.py:119
  (10 other events, 76.4 us)

commit v2 on v1

--- a/solution.py
+++ b/solution.py
@@ -127,14 +127,30 @@
     return jnp.concatenate(blocks, axis=0)
 
 
-def build_kernel(rows_ref, cols_ref, count_ref, codes_ref, block_ref, row_scr, col_scr):
+def fetch(sources, targets, sems):
+    copies = [
+        pltpu.make_async_copy(src, dst, sems.at[k])
+        for k, (src, dst) in enumerate(zip(sources, targets))
+    ]
+    for copy in copies:
+        copy.start()
+    return copies
+
+
+def build_kernel(
+    rows_vmem, cols_vmem, count_vmem, codes_ref, block_ref, row_scr, col_scr, rows_ref, cols_ref,
+    count_ref, sems
+):
     slots = codes_ref.shape[0]
     side = codes_ref.shape[1] // 2
+    copies = fetch((rows_vmem, cols_vmem, count_vmem), (rows_ref, cols_ref, count_ref), sems)
     block_ref[...] = jnp.zeros_like(block_ref)
+    for copy in copies:
+        copy.wait()
     row_code = codes_ref[:, :side].astype(jnp.float32) + 3.0
     row_code = jnp.where(row_code > MOD // 2, row_code - MOD, row_code)
     slot = lax.broadcasted_iota(jnp.int32, (slots, side), 0)
-    row_code = jnp.where(slot < count_ref[0], row_code, 0.0)
+    row_code = jnp.where(slot < count_ref[0, 0], row_code, 0.0)
     col_code = codes_ref[:, side:].astype(jnp.float32) + 1.0
     col_code = jnp.where(col_code > MOD // 2, col_code - MOD, col_code)
     coarse = 2.0**-12
@@ -155,8 +171,8 @@
             part = turns - jnp.round(turns)
             middle = 3.0 + (HIT - 1) / 2.0
             keep = jnp.abs(part - middle / MOD) < (HIT / 2.0) / MOD
-            down = pl.ds(pl.multiple_of(rows_ref[s] * side, side), side)
-            across = pl.ds(pl.multiple_of(cols_ref[s] * side, side), side)
+            down = pl.ds(pl.multiple_of(rows_ref[0, s] * side, side), side)
+            across = pl.ds(pl.multiple_of(cols_ref[0, s] * side, side), side)
             block_ref[down, across] += keep.astype(jnp.float32).astype(jnp.bfloat16)
         return carry
 
@@ -166,16 +182,19 @@
 def build_block(tile_rows, tile_cols, tile_count, codes, row_nodes, col_nodes):
     slots, width = codes.shape
     side = width // 2
-    smem = pl.BlockSpec(memory_space=pltpu.SMEM)
     vmem = pl.BlockSpec(memory_space=pltpu.VMEM)
     return pl.pallas_call(
         build_kernel,
         out_shape=jax.ShapeDtypeStruct((row_nodes, col_nodes), jnp.bfloat16),
-        in_specs=[smem, smem, smem, vmem],
+        in_specs=[vmem] * 4,
         out_specs=vmem,
         scratch_shapes=[
             pltpu.VMEM((slots // GROUP, side, slots), jnp.float32),
             pltpu.VMEM((slots, side), jnp.float32),
+            pltpu.SMEM((1, slots), jnp.int32),
+            pltpu.SMEM((1, slots), jnp.int32),
+            pltpu.SMEM((1, 1), jnp.int32),
+            pltpu.SemaphoreType.DMA((3,)),
         ],
         compiler_params=pltpu.CompilerParams(vmem_limit_bytes=LIMIT),
         cost_estimate=pl.CostEstimate(
@@ -185,10 +204,10 @@
     )(tile_rows, tile_cols, tile_count, codes)
 
 
-def forward_kernel(n_row, n_col, block_ref, *refs):
+def forward_kernel(n_row, far, block_ref, *refs):
     sources = refs[:n_row]
-    outs = refs[n_row : n_row + n_col]
-    source = refs[n_row + n_col]
+    outs = refs[n_row : n_row + len(far)]
+    source = refs[-1]
     pieces = sources[0].shape[0]
     me_row = lax.axis_index("row")
     me_col = lax.axis_index("col")
@@ -196,79 +215,106 @@
         at = pl.multiple_of((me_row ^ k) * pieces, pieces)
         source[pl.ds(at, pieces), :] = sources[k][...]
     whole = source[...]
-    for k in range(n_col):
+    for out, k in zip(outs, far):
         at = pl.multiple_of((me_col ^ k) * pieces, pieces)
-        outs[k][...] = jnp.dot(
+        out[...] = jnp.dot(
             block_ref[pl.ds(at, pieces), :], whole, preferred_element_type=jnp.float32
         ).astype(jnp.bfloat16)
 
 
-def forward_parts(block, sources, n_col):
+def forward_parts(block, sources, far, name):
     pieces, feat = sources[0].shape
     n_row = len(sources)
     vmem = pl.BlockSpec(memory_space=pltpu.VMEM)
     return pl.pallas_call(
-        functools.partial(forward_kernel, n_row, n_col),
-        out_shape=[jax.ShapeDtypeStruct((pieces, feat), jnp.bfloat16)] * n_col,
+        functools.partial(forward_kernel, n_row, far),
+        out_shape=[jax.ShapeDtypeStruct((pieces, feat), jnp.bfloat16)] * len(far),
         in_specs=[vmem] * (1 + n_row),
-        out_specs=[vmem] * n_col,
+        out_specs=[vmem] * len(far),
         scratch_shapes=[pltpu.VMEM((pieces * n_row, feat), jnp.bfloat16)],
         compiler_params=pltpu.CompilerParams(vmem_limit_bytes=LIMIT),
-        name="forward_parts",
+        name=name,
     )(block, *sources)
 
 
-def dense_kernel(
-    n_col, degree_ref, weight_ref, bias_ref, cot_ref, *refs
-):
+def slope_of(aggregate, weight, bias, cotangent):
+    preact = jnp.dot(aggregate, weight, preferred_element_type=jnp.float32) + bias
+    decay = jnp.exp(jnp.minimum(preact, 0.0))
+    positive = preact > 0
+    grad_pre = cotangent.astype(jnp.float32) * jnp.where(positive, 1.0, decay)
+    return jnp.where(positive, preact, decay - 1.0), grad_pre
+
+
+def gradient_kernel(n_col, degree_ref, weight_ref, bias_ref, cot_ref, *refs):
     parts = refs[:n_col]
-    hidden_ref, grad_ref, terms_ref = refs[n_col:]
+    grad_ref, both_ref, aggregate_ref = refs[n_col:]
     total = parts[0][...].astype(jnp.float32)
     for k in range(1, n_col):
         total += parts[k][...].astype(jnp.float32)
     inv_row = lax.rsqrt(degree_ref[...].astype(jnp.float32))
     aggregate = (column_of(inv_row) * total).astype(jnp.bfloat16)
+    aggregate_ref[...] = aggregate
     weight = weight_ref[...]
-    preact = jnp.dot(aggregate, weight, preferred_element_type=jnp.float32) + bias_ref[...]
-    decay = jnp.exp(jnp.minimum(preact, 0.0))
-    positive = preact > 0
-    hidden_ref[...] = jnp.where(positive, preact, decay - 1.0).astype(jnp.bfloat16)
-    grad_pre = cot_ref[...].astype(jnp.float32) * jnp.where(positive, 1.0, decay)
+    feat = weight.shape[0]
+    half = feat // 2
+    _, grad_pre = slope_of(aggregate, weight, bias_ref[...], cot_ref[...])
     grad_pre_b = grad_pre.astype(jnp.bfloat16)
     back = lax.dot_general(
         weight, grad_pre_b, (((1,), (1,)), ((), ())), preferred_element_type=jnp.float32
     )
-    grad_ref[...] = (inv_row * back).astype(jnp.bfloat16)
-    feat = weight.shape[0]
-    terms_ref[:feat, :] = lax.dot_general(
+    grad = (inv_row * back).astype(jnp.bfloat16)
+    grad_ref[...] = grad
+    both_ref[:feat, :] = grad
+    weight_terms = lax.dot_general(
         aggregate, grad_pre_b, (((0,), (0,)), ((), ())), preferred_element_type=jnp.float32
     ).astype(jnp.bfloat16)
+    both_ref[feat : feat + half, :feat] = weight_terms[:half]
+    both_ref[feat : feat + half, feat:] = weight_terms[half:]
     bias_terms = jnp.sum(grad_pre, axis=0, keepdims=True)
-    terms_ref[feat:, :] = jnp.broadcast_to(bias_terms, (16, feat)).astype(jnp.bfloat16)
-
-
-def dense_step(degree, weight, bias, cotangent, parts):
+    bias_terms = jnp.broadcast_to(bias_terms, (16, feat)).astype(jnp.bfloat16)
+    both_ref[feat + half :, :feat] = bias_terms
+    both_ref[feat + half :, feat:] = bias_terms
+
+
+def gradient_step(degree, weight, bias, cotangent, parts):
     pieces, feat = cotangent.shape
     vmem = pl.BlockSpec(memory_space=pltpu.VMEM)
     return pl.pallas_call(
-        functools.partial(dense_kernel, len(parts)),
+        functools.partial(gradient_kernel, len(parts)),
         out_shape=[
+            jax.ShapeDtypeStruct((feat, pieces), jnp.bfloat16),
+            jax.ShapeDtypeStruct((feat + feat // 2 + 16, pieces), jnp.bfloat16),
             jax.ShapeDtypeStruct((pieces, feat), jnp.bfloat16),
-            jax.ShapeDtypeStruct((feat, pieces), jnp.bfloat16),
-            jax.ShapeDtypeStruct((feat + 16, feat), jnp.bfloat16),
         ],
         in_specs=[vmem] * (4 + len(parts)),
         out_specs=[vmem] * 3,
         compiler_params=pltpu.CompilerParams(vmem_limit_bytes=LIMIT),
-        name="dense_step",
+        name="gradient_step",
     )(degree.reshape(1, pieces), weight, bias.reshape(1, feat), cotangent, *parts)
 
 
+def hidden_kernel(weight_ref, bias_ref, cot_ref, aggregate_ref, hidden_ref):
+    hidden, _ = slope_of(aggregate_ref[...], weight_ref[...], bias_ref[...], cot_ref[...])
+    hidden_ref[...] = hidden.astype(jnp.bfloat16)
+
+
+def hidden_step(weight, bias, cotangent, aggregate):
+    pieces, feat = cotangent.shape
+    vmem = pl.BlockSpec(memory_space=pltpu.VMEM)
+    return pl.pallas_call(
+        hidden_kernel,
+        out_shape=jax.ShapeDtypeStruct((pieces, feat), jnp.bfloat16),
+        in_specs=[vmem] * 4,
+        out_specs=vmem,
+        compiler_params=pltpu.CompilerParams(vmem_limit_bytes=LIMIT),
+        name="hidden_step",
+    )(weight, bias.reshape(1, feat), cotangent, aggregate)
+
+
 def backward_kernel(n_row, n_col, first, block_ref, *refs):
-    sources = refs[:n_col]
-    out_ref = refs[n_col]
-    pieces = sources[0].shape[1]
-    feat = sources[0].shape[0]
+    sources, terms = refs[:n_col], refs[n_col:-1]
+    out_ref = refs[-1]
+    feat, pieces = sources[0].shape
     me_row = lax.axis_index("row")
     me_col = lax.axis_index("col")
     for m in range(n_row // 2):
@@ -277,88 +323,147 @@
         for k in range(n_col):
             down = pl.ds(pl.multiple_of((me_col ^ k) * pieces, pieces), pieces)
             total += jnp.dot(
-                sources[k][...], block_ref[down, across], preferred_element_type=jnp.float32
+                sources[k][:feat, :], block_ref[down, across], preferred_element_type=jnp.float32
             )
         out_ref[m * feat : (m + 1) * feat, :] = total.astype(jnp.bfloat16)
-
-
-def backward_parts(block, sources, n_row, first):
+    if terms:
+        out_ref[n_row // 2 * feat :, :] = sum_of(terms).astype(jnp.bfloat16)
+
+
+def sum_of(refs):
+    total = refs[0][...].astype(jnp.float32)
+    for ref in refs[1:]:
+        total += ref[...].astype(jnp.float32)
+    return total
+
+
+def backward_parts(block, sources, terms, n_row, first):
     feat, pieces = sources[0].shape
     n_col = len(sources)
+    extra = terms[0].shape[0] if terms else 0
     vmem = pl.BlockSpec(memory_space=pltpu.VMEM)
     return pl.pallas_call(
         functools.partial(backward_kernel, n_row, n_col, first),
-        out_shape=jax.ShapeDtypeStruct((n_row // 2 * feat, pieces), jnp.bfloat16),
-        in_specs=[vmem] * (1 + n_col),
+        out_shape=jax.ShapeDtypeStruct((n_row // 2 * feat + extra, pieces), jnp.bfloat16),
+        in_specs=[vmem] * (1 + n_col + len(terms)),
         out_specs=vmem,
         compiler_params=pltpu.CompilerParams(vmem_limit_bytes=LIMIT),
         name="backward_other" if first else "backward_own",
-    )(block, *sources)
-
-
-def pair_kernel(n, mine_ref, theirs_ref, *refs):
-    terms, outs = refs[:-n], refs[-n:]
+    )(block, *sources, *terms)
+
+
+def pair_kernel(n, mine_ref, sent_ref, theirs_ref, *outs):
     feat = outs[0].shape[0]
     for m in range(n):
         span = slice(m * feat, (m + 1) * feat)
         outs[m][...] = (
             mine_ref[span, :].astype(jnp.float32) + theirs_ref[span, :].astype(jnp.float32)
         ).astype(jnp.bfloat16)
-
-
-def pair_sum(mine, theirs, n):
+    outs[n][...] = (
+        sent_ref[n * feat :, :].astype(jnp.float32) + theirs_ref[n * feat :, :].astype(jnp.float32)
+    ).astype(jnp.bfloat16)
+
+
+def pair_sum(mine, sent, theirs, n):
     rows, width = mine.shape
     vmem = pl.BlockSpec(memory_space=pltpu.VMEM)
-    return pl.pallas_call(
+    *chunks, terms = pl.pallas_call(
         functools.partial(pair_kernel, n),
-        out_shape=[jax.ShapeDtypeStruct((rows // n, width), jnp.bfloat16)] * n,
+        out_shape=[jax.ShapeDtypeStruct((rows // n, width), jnp.bfloat16)] * n
+        + [jax.ShapeDtypeStruct((sent.shape[0] - rows, width), jnp.bfloat16)],
+        in_specs=[vmem] * 3,
+        out_specs=[vmem] * (n + 1),
+        compiler_params=pltpu.CompilerParams(vmem_limit_bytes=LIMIT),
+        name="pair_sum",
+    )(mine, sent, theirs)
+    return chunks, terms
+
+
+def finish_kernel(n, scale, degree_ref, *refs):
+    parts, terms = refs[:n], refs[n:-3]
+    out_ref, weight_ref, bias_ref = refs[-3:]
+    inv_row = lax.rsqrt(degree_ref[...].astype(jnp.float32))
+    out_ref[...] = (inv_row * sum_of(parts)).T.astype(jnp.bfloat16)
+    total = sum_of(terms) * scale
+    feat = weight_ref.shape[0]
+    half = feat // 2
+    weight_ref[:half, :] = total[:half, :feat]
+    weight_ref[half:, :] = total[:half, feat:]
+    bias_ref[...] = total[half : half + 1, :feat]
+
+
+def finish(degree, parts, terms, scale):
+    feat, pieces = parts[0].shape
+    vmem = pl.BlockSpec(memory_space=pltpu.VMEM)
+    grad_features, grad_weight, grad_bias = pl.pallas_call(
+        functools.partial(finish_kernel, len(parts), scale),
+        out_shape=[
+            jax.ShapeDtypeStruct((pieces, feat), jnp.bfloat16),
+            jax.ShapeDtypeStruct((feat, feat), jnp.float32),
+            jax.ShapeDtypeStruct((1, feat), jnp.float32),
+        ],
+        in_specs=[vmem] * (1 + len(parts) + len(terms)),
+        out_specs=[vmem] * 3,
+        compiler_params=pltpu.CompilerParams(vmem_limit_bytes=LIMIT),
+        name="finish",
+    )(degree.reshape(1, pieces), *parts, *terms)
+    return grad_features, grad_weight, grad_bias.reshape(feat)
+
+
+def scale_kernel(n, degree_hbm, features_hbm, *refs):
+    degree_ref, features_ref, sems = refs[-3:]
+    out_ref = refs[n]
+    first, second, *others = fetch(
+        (degree_hbm, features_hbm) + refs[:n],
+        (degree_ref, features_ref) + refs[n + 1 : 2 * n + 1],
+        sems,
+    )
+    first.wait()
+    inv_root = column_of(lax.rsqrt(degree_ref[...].astype(jnp.float32)))
+    second.wait()
+    out_ref[...] = (inv_root * features_ref[...].astype(jnp.float32)).astype(jnp.bfloat16)
+    for copy in others:
+        copy.wait()
+
+
+def scale_rows(degree, features, *others):
+    pieces, feat = features.shape
+    n = len(others)
+    operands = (degree.reshape(1, pieces), features, *others)
+    return pl.pallas_call(
+        functools.partial(scale_kernel, n),
+        out_shape=[
+            pltpu.VMEM(features.shape, jnp.bfloat16),
+            *(pltpu.VMEM(x.shape, x.dtype) for x in others),
+        ],
+        in_specs=[pl.BlockSpec(memory_space=pl.ANY)] * (2 + n),
+        out_specs=[pl.BlockSpec(memory_space=pltpu.VMEM)] * (1 + n),
+        scratch_shapes=[
+            pltpu.VMEM((1, pieces), jnp.int32),
+            pltpu.VMEM((pieces, feat), jnp.bfloat16),
+            pltpu.SemaphoreType.DMA((2 + n,)),
+        ],
+        compiler_params=pltpu.CompilerParams(vmem_limit_bytes=60*2**20),
+        name="scale_rows",
+    )(*operands)
+
+
+def terms_kernel(feat, mine_ref, theirs_ref, out_ref):
+    out_ref[...] = (
+        mine_ref[feat:, :].astype(jnp.float32) + theirs_ref[feat:, :].astype(jnp.float32)
+    ).astype(jnp.bfloat16)
+
+
+def terms_sum(mine, theirs, feat):
+    vmem = pl.BlockSpec(memory_space=pltpu.VMEM)
+    return pl.pallas_call(
+        functools.partial(terms_kernel, feat),
+        out_shape=jax.ShapeDtypeStruct((mine.shape[0] - feat, mine.shape[1]), jnp.bfloat16),
         in_specs=[vmem] * 2,
-        out_specs=[vmem] * n,
-        compiler_params=pltpu.CompilerParams(vmem_limit_bytes=LIMIT),
-        name="pair_sum",
+        out_specs=vmem,
+        compiler_params=pltpu.CompilerParams(vmem_limit_bytes=LIMIT),
+        name="terms_sum",
     )(mine, theirs)
-
-
-def finish_kernel(n, degree_ref, *refs):
-    parts, out_ref = refs[:n], refs[n]
-    total = parts[0][...].astype(jnp.float32)
-    for k in range(1, n):
-        total += parts[k][...].astype(jnp.float32)
-    inv_row = lax.rsqrt(degree_ref[...].astype(jnp.float32))
-    out_ref[...] = (inv_row * total).T.astype(jnp.bfloat16)
-
-
-def finish(degree, parts):
-    feat, pieces = parts[0].shape
-    vmem = pl.BlockSpec(memory_space=pltpu.VMEM)
-    return pl.pallas_call(
-        functools.partial(finish_kernel, len(parts)),
-        out_shape=jax.ShapeDtypeStruct((pieces, feat), jnp.bfloat16),
-        in_specs=[vmem] * (1 + len(parts)),
-        out_specs=vmem,
-        compiler_params=pltpu.CompilerParams(vmem_limit_bytes=LIMIT),
-        name="finish",
-    )(degree.reshape(1, pieces), *parts)
-
-
-def terms_kernel(n, scale, *refs):
-    parts, out_ref = refs[:n], refs[n]
-    total = parts[0][...].astype(jnp.float32)
-    for k in range(1, n):
-        total += parts[k][...].astype(jnp.float32)
-    out_ref[...] = (total * scale).astype(out_ref.dtype)
-
-
-def terms_sum(parts, scale, dtype):
-    vmem = pl.BlockSpec(memory_space=pltpu.VMEM)
-    return pl.pallas_call(
-        functools.partial(terms_kernel, len(parts), scale),
-        out_shape=jax.ShapeDtypeStruct(parts[0].shape, dtype),
-        in_specs=[vmem] * len(parts),
-        out_specs=vmem,
-        compiler_params=pltpu.CompilerParams(vmem_limit_bytes=LIMIT),
-        name="terms_sum",
-    )(*parts)
 
 
 def dense_local(
@@ -368,39 +473,42 @@
     n_row = lax.axis_size("row")
     n_col = lax.axis_size("col")
     grad_scale = 1.0 / math.sqrt(pieces * n_row * n_col)
-    inv_root = lax.rsqrt(degree.astype(jnp.float32))[:, None]
-    scaled = (inv_root * features.astype(jnp.float32)).astype(jnp.bfloat16)
-    block = build_block(
-        tile_rows[0, 0],
-        tile_cols[0, 0],
-        tile_count[0, 0],
-        tile_codes[0, 0],
-        pieces * n_col,
-        pieces * n_row,
-    )
+    scaled, *lists = scale_rows(
+        degree, features, tile_rows[0], tile_cols[0], tile_count[0], tile_codes[0, 0]
+    )
+    block = build_block(*lists, pieces * n_col, pieces * n_row)
+    chips = list(range(n_row - 2, 0, -2))
+    lines = list(range(n_col - 1, 0, -1))
     sources = [None] * n_row
     sources[0] = scaled
-    for m in range(2, n_row, 2):
+    for m in chips:
         sources[m] = swap(scaled, "row", m)
-    for m in range(0, n_row, 2):
-        sources[m + 1] = swap(sources[m], "row", 1)
-    parts = forward_parts(block, sources, n_col)
-    landed = [parts[0]] + [swap(parts[k], "col", k) for k in range(1, n_col)]
-    hidden, grad_own, terms = dense_step(degree, weight, bias, cotangent, landed)
-    grads = [grad_own] + [swap(grad_own, "col", k) for k in range(1, n_col)]
-    for_other = backward_parts(block, grads, n_row, 1)
+    sources[1] = swap(scaled, "row", 1)
+    block, *landed = lax.optimization_barrier((block, *(sources[m] for m in chips)))
+    for m, value in zip(chips, landed):
+        sources[m] = value
+        sources[m + 1] = swap(value, "row", 1)
+    half = max(1, n_col // 2)
+    far = forward_parts(block, sources, lines[:half], "forward_far")
+    near = forward_parts(block, sources, lines[half:] + [0], "forward_near")
+    parts = dict(zip(lines + [0], far + near))
+    landed = [parts[0]] + [swap(parts[k], "col", k) for k in lines]
+    grad_own, both, aggregate = gradient_step(degree, weight, bias, cotangent, landed)
+    grads = [grad_own, swap(both, "col", 1)] + [swap(grad_own, "col", k) for k in range(2, n_col)]
+    grads[1], aggregate = lax.optimization_barrier((grads[1], aggregate))
+    hidden = hidden_step(weight, bias, cotangent, aggregate)
+    terms = terms_sum(both, grads[1], feat)
+    from_chips = [swap(terms, "row", m) for m in chips]
+    grads[2:], from_chips = lax.optimization_barrier((grads[2:], from_chips))
+    for_other = backward_parts(block, grads, [terms] + from_chips, n_row, 1)
     from_other = swap(for_other, "row", 1)
-    for_own = backward_parts(block, grads, n_row, 0)
-    chunks = pair_sum(for_own, from_other, n_row // 2)
-    landed = [chunks[0]] + [swap(chunks[m], "row", 2 * m) for m in range(1, n_row // 2)]
-    grad_features = finish(degree, landed)
-    by_chip = terms_sum(
-        [terms] + [swap(terms, "row", k) for k in range(1, n_row)], 1.0, jnp.bfloat16
-    )
-    all_terms = terms_sum(
-        [by_chip] + [swap(by_chip, "col", k) for k in range(1, n_col)], grad_scale, jnp.float32
-    )
-    return (hidden, grad_features, all_terms[:feat], all_terms[feat])
+    for_own = backward_parts(block, grads, [], n_row, 0)
+    chunks, terms = pair_sum(for_own, for_other, from_other, n_row // 2)
+    landed = [chunks[0]] + [swap(chunks[m // 2], "row", m) for m in chips]
+    for k in range(1, n_col.bit_length() - 1):
+        terms = [terms, swap(terms, "col", 2**k)]
+    grad_features, grad_weight, grad_bias = finish(degree, landed, terms, grad_scale)
+    return (hidden, grad_features, grad_weight, grad_bias)
 
 
 def power_of_two(n):

time: 68.5 us -> 51 us (0.74)
  waiting for transfers between devices: 26.6 us -> 15 us
  starting transfers between devices: 27 us -> 23.3 us
  local copies, waits for them, and re-layouts: 3.37 us -> 0.03 us
  Pallas kernels: 8.22 us -> 11 us
  other arithmetic: 1.63 us -> 0 us
    ppermute x27 -> x21, waiting for transfers between devices: 26.6 us -> 15 us  [swap(): return lax.ppermute(value, axis, [(i, i ^ bits) for i in range(size)])]
    ppermute x27 -> x21, starting transfers between devices: 27 us -> 23.3 us  [swap(): return lax.ppermute(value, axis, [(i, i ^ bits) for i in range(size)])]
    unnamed x14 -> x8, local copies, waits for them, and re-layouts: 2.22 us -> 0.03 us
    pallas_call x5 -> x7, Pallas kernels: 3 us -> 5.03 us  [the longest x1 1.55 us: scale_rows(): pl.pallas_call(functools.partial(scale_kernel, n), out_shape=[pltpu.VMEM(...]
    convert_element_type x1 -> x0, other arithmetic: 0.94 us -> none  [dense_local(): scaled = (inv_root * features.astype(jnp.float32)).astype(jnp.bfloat16)]
    pallas_call x1, Pallas kernels: 4.21 us -> 4.91 us  [build_block(): pl.pallas_call(build_kernel, out_shape=jax.ShapeDtypeStruct((row_nodes, c...]
  transfers between devices with their start and end apart: 27 -> 21, of which waited for: 16 -> 13; matrix products, arithmetic and copies ran while one was open for 2% -> 0% of each run, Pallas kernels for 7% -> 14%
where the time goes in v2:
time: 51 us; the launch traced here: 50.8 us
  starting transfers between devices  23.3 us (46%)
  waiting for transfers between devices  15 us (29%)
  Pallas kernels  11 us (22%)
  between operations  1.43 us (3%)
    ppermute x21, starting transfers between devices, swap(): return lax.ppermute(value, axis, [(i, i ^ bits) for i in range(size)])  23.3 us
    ppermute x21, waiting for transfers between devices, swap(): return lax.ppermute(value, axis, [(i, i ^ bits) for i in range(size)])  15 us
    pallas_call x1, Pallas kernels, build_block(): pl.pallas_call(build_kernel, out_shape=jax.ShapeDtypeStruct((row_nodes, c...  4.91 us
    pallas_call x1, Pallas kernels, scale_rows(): pl.pallas_call(functools.partial(scale_kernel, n), out_shape=[pltpu.VMEM(...  1.55 us
    pallas_call x2, Pallas kernels, forward_parts(): pl.pallas_call(functools.partial(forward_kernel, n_row, far), out_shape=[...  1.48 us
  transfers between devices with their start and end apart: 21, of which 13 were waited for; matrix products, arithmetic and copies ran while one was open for 0% of the time, Pallas kernels for 14%

profile of v2, /device:TPU:0, one launch (start us, length us, event | category | flops | bytes accessed | tf_op | source)
XLA Modules:
  0.0 50.8 jit_solution(16491344165216324313)
XLA Ops:
  1.3 1.6 %scale_rows.1 = (bf16[256,128]{1,0:T(8,128)(2,1)S(1)}, s32[1,128]{1,0:T(1,128)S(1)}, s32[1,128]{1,0:T(1,128)S(1)}, s32[1,1]{1,0:T(1,128)}, s32[128,256]{1,0:T(8,128)S(1)}) custom-call(s32[1,256]{1,0:T(1,128)} %bitcast.8, bf16[256,128]{1,0:T(8,128)(2,1)} %features_hbm.1, s32[1,128]{1,0:T(1,128)} %bitcast.14, s32[1,128]{1,0:T(1,128)} %bitcast.15, ...), custom_call_target="tpu_custom_call" | custom-call | tf_op jit(solution)/shard_map/scale_rows/pallas_call | solution.py:433
  2.8 3.0 %collective-permute-start.2 = (bf16[256,128]{1,0:T(8,128)(2,1)S(1)}, bf16[256,128]{1,0:T(8,128)(2,1)S(1)}, u32[]{:S(2)}, u32[]{:S(2)}) collective-permute-start(bf16[256,128]{1,0:T(8,128)(2,1)S(1)} %get-tuple-element.39.refs_0_), channel_id=1, source_target_pairs={{0,8},{4,12},{8,0},{12,4},{16,24},{20,28},{24,16},{28,20},{1,9},{5... | collective-permute-start | bytes 196616 | tf_op jit(solution)/shard_map/ppermute | solution.py:119
  5.8 1.5 %collective-permute-start.1 = (bf16[256,128]{1,0:T(8,128)(2,1)S(1)}, bf16[256,128]{1,0:T(8,128)(2,1)S(1)}, u32[]{:S(2)}, u32[]{:S(2)}) collective-permute-start(bf16[256,128]{1,0:T(8,128)(2,1)S(1)} %get-tuple-element.39.refs_0_), channel_id=1, source_target_pairs={{0,16},{4,20},{8,24},{12,28},{16,0},{20,4},{24,8},{28,12},{1,17},{... | collective-permute-start | bytes 196616 | tf_op jit(solution)/shard_map/ppermute | solution.py:119
  7.4 4.9 %build_block.1.block_ref = bf16[1024,2048]{1,0:T(8,128)(2,1)S(1)} custom-call(s32[1,128]{1,0:T(1,128)S(1)} %get-tuple-element.35.rows_vmem, s32[1,128]{1,0:T(1,128)S(1)} %get-tuple-element.36.cols_vmem, s32[1,1]{1,0:T(1,128)} %get-tuple-element.37.count_vmem, s32[128,256]{1,0:T(8,128)S(1)} %get-tuple-element.38.codes_ref), custom_call_target="tpu_custom_call" | custom-call | flops 41943040 | bytes 16777216 | tf_op jit(solution)/shard_map/build_block/pallas_call | solution.py:186
  14.4 0.7 %forward_far.1 = (bf16[256,128]{1,0:T(8,128)(2,1)S(1)}, bf16[256,128]{1,0:T(8,128)(2,1)S(1)}) custom-call(bf16[1024,2048]{1,0:T(8,128)(2,1)S(1)} %build_block.1.block_ref, bf16[256,128]{1,0:T(8,128)(2,1)S(1)} %get-tuple-element.39.refs_0_, bf16[256,128]{1,0:T(8,128)(2,1)S(1)} %collective-permute-done.3.refs_1_, ...), custom_call_target="tpu_custom_call" | custom-call | tf_op jit(solution)/shard_map/forward_far/pallas_call | solution.py:229
  15.1 4.1 %collective-permute-start.7 = (bf16[256,128]{1,0:T(8,128)(2,1)S(1)}, bf16[256,128]{1,0:T(8,128)(2,1)S(1)}, u32[]{:S(2)}, u32[]{:S(2)}) collective-permute-start(bf16[256,128]{1,0:T(8,128)(2,1)S(1)} %get-tuple-element.45), channel_id=1, source_target_pairs={{0,3},{1,2},{2,1},{3,0},{4,7},{5,6},{6,5},{7,4},{8,11},{9,10},{10,... | collective-permute-start | bytes 196616 | tf_op jit(solution)/shard_map/ppermute | solution.py:119
  19.2 0.7 %forward_near.1 = (bf16[256,128]{1,0:T(8,128)(2,1)S(1)}, bf16[256,128]{1,0:T(8,128)(2,1)S(1)}) custom-call(bf16[1024,2048]{1,0:T(8,128)(2,1)S(1)} %build_block.1.block_ref, bf16[256,128]{1,0:T(8,128)(2,1)S(1)} %get-tuple-element.39.refs_0_, bf16[256,128]{1,0:T(8,128)(2,1)S(1)} %collective-permute-done.3.refs_1_, ...), custom_call_target="tpu_custom_call" | custom-call | tf_op jit(solution)/shard_map/forward_near/pallas_call | solution.py:229
  20.7 1.4 %collective-permute-done.7.refs_1_ = bf16[256,128]{1,0:T(8,128)(2,1)S(1)} collective-permute-done((bf16[256,128]{1,0:T(8,128)(2,1)S(1)}, bf16[256,128]{1,0:T(8,128)(2,1)S(1)}, u32[]{:S(2)}, u32[]{:S(2)}) %collective-permute-start.7) | collective-permute-done | bytes 65568 | tf_op jit(solution)/shard_map/ppermute | solution.py:119
  22.1 3.3 %collective-permute-done.8.refs_2_ = bf16[256,128]{1,0:T(8,128)(2,1)S(1)} collective-permute-done((bf16[256,128]{1,0:T(8,128)(2,1)S(1)}, bf16[256,128]{1,0:T(8,128)(2,1)S(1)}, u32[]{:S(2)}, u32[]{:S(2)}) %collective-permute-start.8) | collective-permute-done | bytes 65568 | tf_op jit(solution)/shard_map/ppermute | solution.py:119
  26.1 0.9 %collective-permute-start.10 = (bf16[208,256]{1,0:T(8,128)(2,1)S(1)}, bf16[208,256]{1,0:T(8,128)(2,1)S(1)}, u32[]{:S(2)}, u32[]{:S(2)}) collective-permute-start(bf16[208,256]{1,0:T(8,128)(2,1)S(1)} %get-tuple-element.48.mine_ref), channel_id=1, source_target_pairs={{0,1},{1,0},{2,3},{3,2},{4,5},{5,4},{6,7},{7,6},{8,9},{9,8},{10,11... | collective-permute-start | bytes 319496 | tf_op jit(solution)/shard_map/ppermute | solution.py:119
  27.0 2.3 %collective-permute-start.12 = (bf16[128,256]{1,0:T(8,128)(2,1)S(1)}, bf16[128,256]{1,0:T(8,128)(2,1)S(1)}, u32[]{:S(2)}, u32[]{:S(2)}) collective-permute-start(bf16[128,256]{1,0:T(8,128)(2,1)S(1)} %get-tuple-element.51.refs_0_), channel_id=1, source_target_pairs={{0,3},{1,2},{2,1},{3,0},{4,7},{5,6},{6,5},{7,4},{8,11},{9,10},{10,... | collective-permute-start | bytes 196616 | tf_op jit(solution)/shard_map/ppermute | solution.py:119
  29.6 1.6 %collective-permute-done.10.theirs_ref.refs_1_ = bf16[208,256]{1,0:T(8,128)(2,1)S(1)} collective-permute-done((bf16[208,256]{1,0:T(8,128)(2,1)S(1)}, bf16[208,256]{1,0:T(8,128)(2,1)S(1)}, u32[]{:S(2)}, u32[]{:S(2)}) %collective-permute-start.10) | collective-permute-done | bytes 106528 | tf_op jit(solution)/shard_map/ppermute | solution.py:119
  31.3 1.7 %collective-permute-start.15 = (bf16[80,256]{1,0:T(8,128)(2,1)S(1)}, bf16[80,256]{1,0:T(8,128)(2,1)S(1)}, u32[]{:S(2)}, u32[]{:S(2)}) collective-permute-start(bf16[80,256]{1,0:T(8,128)(2,1)S(1)} %terms_sum.1.refs_4_), channel_id=1, source_target_pairs={{0,8},{4,12},{8,0},{12,4},{16,24},{20,28},{24,16},{28,20},{1,9},{5... | collective-permute-start | bytes 122888 | tf_op jit(solution)/shard_map/ppermute | solution.py:119
  32.9 1.5 %collective-permute-start.14 = (bf16[80,256]{1,0:T(8,128)(2,1)S(1)}, bf16[80,256]{1,0:T(8,128)(2,1)S(1)}, u32[]{:S(2)}, u32[]{:S(2)}) collective-permute-start(bf16[80,256]{1,0:T(8,128)(2,1)S(1)} %terms_sum.1.refs_4_), channel_id=1, source_target_pairs={{0,16},{4,20},{8,24},{12,28},{16,0},{20,4},{24,8},{28,12},{1,17},{... | collective-permute-start | bytes 122888 | tf_op jit(solution)/shard_map/ppermute | solution.py:119
  34.8 0.9 %collective-permute-done.11.refs_2_ = bf16[128,256]{1,0:T(8,128)(2,1)S(1)} collective-permute-done((bf16[128,256]{1,0:T(8,128)(2,1)S(1)}, bf16[128,256]{1,0:T(8,128)(2,1)S(1)}, u32[]{:S(2)}, u32[]{:S(2)}) %collective-permute-start.11) | collective-permute-done | bytes 65568 | tf_op jit(solution)/shard_map/ppermute | solution.py:119
  35.7 1.2 %collective-permute-done.14.refs_6_ = bf16[80,256]{1,0:T(8,128)(2,1)S(1)} collective-permute-done((bf16[80,256]{1,0:T(8,128)(2,1)S(1)}, bf16[80,256]{1,0:T(8,128)(2,1)S(1)}, u32[]{:S(2)}, u32[]{:S(2)}) %collective-permute-start.14) | collective-permute-done | bytes 40992 | tf_op jit(solution)/shard_map/ppermute | solution.py:119
  36.9 2.4 %collective-permute-done.13.refs_5_ = bf16[80,256]{1,0:T(8,128)(2,1)S(1)} collective-permute-done((bf16[80,256]{1,0:T(8,128)(2,1)S(1)}, bf16[80,256]{1,0:T(8,128)(2,1)S(1)}, u32[]{:S(2)}, u32[]{:S(2)}) %collective-permute-start.13) | collective-permute-done | bytes 40992 | tf_op jit(solution)/shard_map/ppermute | solution.py:119
  40.4 1.1 %collective-permute-done.16.theirs_ref = bf16[592,256]{1,0:T(8,128)(2,1)S(1)} collective-permute-done((bf16[592,256]{1,0:T(8,128)(2,1)S(1)}, bf16[592,256]{1,0:T(8,128)(2,1)S(1)}, u32[]{:S(2)}, u32[]{:S(2)}) %collective-permute-start.16) | collective-permute-done | bytes 303136 | tf_op jit(solution)/shard_map/ppermute | solution.py:119
  42.0 1.6 %collective-permute-start.18 = (bf16[128,256]{1,0:T(8,128)(2,1)S(1)}, bf16[128,256]{1,0:T(8,128)(2,1)S(1)}, u32[]{:S(2)}, u32[]{:S(2)}) collective-permute-start(bf16[128,256]{1,0:T(8,128)(2,1)S(1)} %get-tuple-element.60), channel_id=1, source_target_pairs={{0,16},{4,20},{8,24},{12,28},{16,0},{20,4},{24,8},{28,12},{1,17},{... | collective-permute-start | bytes 196616 | tf_op jit(solution)/shard_map/ppermute | solution.py:119
  43.6 1.5 %collective-permute-start.19 = (bf16[128,256]{1,0:T(8,128)(2,1)S(1)}, bf16[128,256]{1,0:T(8,128)(2,1)S(1)}, u32[]{:S(2)}, u32[]{:S(2)}) collective-permute-start(bf16[128,256]{1,0:T(8,128)(2,1)S(1)} %get-tuple-element.61), channel_id=1, source_target_pairs={{0,8},{4,12},{8,0},{12,4},{16,24},{20,28},{24,16},{28,20},{1,9},{5... | collective-permute-start | bytes 196616 | tf_op jit(solution)/shard_map/ppermute | solution.py:119
  45.1 2.3 %collective-permute-start.20 = (bf16[80,256]{1,0:T(8,128)(2,1)S(1)}, bf16[80,256]{1,0:T(8,128)(2,1)S(1)}, u32[]{:S(2)}, u32[]{:S(2)}) collective-permute-start(bf16[80,256]{1,0:T(8,128)(2,1)S(1)} %get-tuple-element.62.refs_4_), channel_id=1, source_target_pairs={{0,2},{1,3},{2,0},{3,1},{4,6},{5,7},{6,4},{7,5},{8,10},{9,11},{10,... | collective-permute-start | bytes 122888 | tf_op jit(solution)/shard_map/ppermute | solution.py:119
  47.4 0.8 %hidden_step.1 = bf16[256,128]{1,0:T(8,128)(2,1)} custom-call(bf16[128,128]{1,0:T(8,128)(2,1)S(1)} %copy-done.1, f32[1,128]{1,0:T(1,128)S(1)} %bitcast.12, bf16[256,128]{1,0:T(8,128)(2,1)S(1)} %copy-done, bf16[256,128]{1,0:T(8,128)(2,1)S(1)} %get-tuple-element.50.aggregate_ref), custom_call_target="tpu_custom_call" | custom-call | tf_op jit(solution)/shard_map/hidden_step/pallas_call | solution.py:304
  48.2 1.8 %collective-permute-done.20.refs_5_ = bf16[80,256]{1,0:T(8,128)(2,1)S(1)} collective-permute-done((bf16[80,256]{1,0:T(8,128)(2,1)S(1)}, bf16[80,256]{1,0:T(8,128)(2,1)S(1)}, u32[]{:S(2)}, u32[]{:S(2)}) %collective-permute-start.20) | collective-permute-done | bytes 40992 | tf_op jit(solution)/shard_map/ppermute | solution.py:119
  50.0 0.8 %finish.1 = (bf16[256,128]{1,0:T(8,128)(2,1)}, f32[128,128]{1,0:T(8,128)}, f32[1,128]{1,0:T(1,128)}) custom-call(s32[1,256]{1,0:T(1,128)S(1)} %bitcast.10, bf16[128,256]{1,0:T(8,128)(2,1)S(1)} %get-tuple-element.58.refs_0_, bf16[128,256]{1,0:T(8,128)(2,1)S(1)} %collective-permute-done.17.refs_1_, bf16[128,256]{1,0:T(8,128)(2,1)S(1)} %collective-permute-done.18.refs_2_, ...), custom_call_target="tpu_custom_call" | custom-call | tf_op jit(solution)/shard_map/finish/pallas_call | solution.py:398
  (37 shorter events, 5.9 us)
Async XLA Ops:
  2.8 9.5 %collective-permute-start.2 = (bf16[256,128]{1,0:T(8,128)(2,1)S(1)}, bf16[256,128]{1,0:T(8,128)(2,1)S(1)}, u32[]{:S(2)}, u32[]{:S(2)}) collective-permute-start(bf16[256,128]{1,0:T(8,128)(2,1)S(1)} %get-tuple-element.39.refs_0_), channel_id=1, source_target_pairs={{0,8},{4,12},{8,0},{12,4},{16,24},{20,28},{24,16},{28,20},{1,9},{5... | collective-permute-start | bytes 196616 | tf_op jit(solution)/shard_map/ppermute | solution.py:119
  5.8 6.5 %collective-permute-start.1 = (bf16[256,128]{1,0:T(8,128)(2,1)S(1)}, bf16[256,128]{1,0:T(8,128)(2,1)S(1)}, u32[]{:S(2)}, u32[]{:S(2)}) collective-permute-start(bf16[256,128]{1,0:T(8,128)(2,1)S(1)} %get-tuple-element.39.refs_0_), channel_id=1, source_target_pairs={{0,16},{4,20},{8,24},{12,28},{16,0},{20,4},{24,8},{28,12},{1,17},{... | collective-permute-start | bytes 196616 | tf_op jit(solution)/shard_map/ppermute | solution.py:119
  7.4 5.2 %collective-permute-start = (bf16[256,128]{1,0:T(8,128)(2,1)S(1)}, bf16[256,128]{1,0:T(8,128)(2,1)S(1)}, u32[]{:S(2)}, u32[]{:S(2)}) collective-permute-start(bf16[256,128]{1,0:T(8,128)(2,1)S(1)} %get-tuple-element.39.refs_0_), channel_id=1, source_target_pairs={{0,24},{4,28},{8,16},{12,20},{16,8},{20,12},{24,0},{28,4},{1,25},{... | collective-permute-start | bytes 196616 | tf_op jit(solution)/shard_map/ppermute | solution.py:119
  7.4 6.1 %collective-permute-start.3 = (bf16[256,128]{1,0:T(8,128)(2,1)S(1)}, bf16[256,128]{1,0:T(8,128)(2,1)S(1)}, u32[]{:S(2)}, u32[]{:S(2)}) collective-permute-start(bf16[256,128]{1,0:T(8,128)(2,1)S(1)} %get-tuple-element.39.refs_0_), channel_id=1, source_target_pairs={{0,4},{4,0},{8,12},{12,8},{16,20},{20,16},{24,28},{28,24},{1,5},{5... | collective-permute-start | bytes 196616 | tf_op jit(solution)/shard_map/ppermute | solution.py:119
  12.3 13.3 %copy-start = (bf16[256,128]{1,0:T(8,128)(2,1)S(1)}, bf16[256,128]{1,0:T(8,128)(2,1)}, u32[]{:S(2)}) copy-start(bf16[256,128]{1,0:T(8,128)(2,1)} %cot_ref.3) | copy-start | bytes 196612
  12.3 13.3 %copy-start.1 = (bf16[128,128]{1,0:T(8,128)(2,1)S(1)}, bf16[128,128]{1,0:T(8,128)(2,1)}, u32[]{:S(2)}) copy-start(bf16[128,128]{1,0:T(8,128)(2,1)} %weight_ref.3) | copy-start | bytes 98308
  12.3 13.3 %copy-start.2 = (s32[256]{0:T(256)S(1)}, s32[256]{0:T(256)}, u32[]{:S(2)}) copy-start(s32[256]{0:T(256)} %param.10) | copy-start | bytes 3076
  12.5 1.3 %collective-permute-start.4 = (bf16[256,128]{1,0:T(8,128)(2,1)S(1)}, bf16[256,128]{1,0:T(8,128)(2,1)S(1)}, u32[]{:S(2)}, u32[]{:S(2)}) collective-permute-start(bf16[256,128]{1,0:T(8,128)(2,1)S(1)} %collective-permute-done.2.refs_2_), channel_id=1, source_target_pairs={{0,4},{4,0},{8,12},{12,8},{16,20},{20,16},{24,28},{28,24},{1,5},{5... | collective-permute-start | bytes 196616 | tf_op jit(solution)/shard_map/ppermute | solution.py:119
  13.0 1.3 %collective-permute-start.5 = (bf16[256,128]{1,0:T(8,128)(2,1)S(1)}, bf16[256,128]{1,0:T(8,128)(2,1)S(1)}, u32[]{:S(2)}, u32[]{:S(2)}) collective-permute-start(bf16[256,128]{1,0:T(8,128)(2,1)S(1)} %collective-permute-done.1.refs_4_), channel_id=1, source_target_pairs={{0,4},{4,0},{8,12},{12,8},{16,20},{20,16},{24,28},{28,24},{1,5},{5... | collective-permute-start | bytes 196616 | tf_op jit(solution)/shard_map/ppermute | solution.py:119
  13.0 1.3 %collective-permute-start.6 = (bf16[256,128]{1,0:T(8,128)(2,1)S(1)}, bf16[256,128]{1,0:T(8,128)(2,1)S(1)}, u32[]{:S(2)}, u32[]{:S(2)}) collective-permute-start(bf16[256,128]{1,0:T(8,128)(2,1)S(1)} %collective-permute-done.refs_6_), channel_id=1, source_target_pairs={{0,4},{4,0},{8,12},{12,8},{16,20},{20,16},{24,28},{28,24},{1,5},{5... | collective-permute-start | bytes 196616 | tf_op jit(solution)/shard_map/ppermute | solution.py:119
  15.1 6.9 %collective-permute-start.7 = (bf16[256,128]{1,0:T(8,128)(2,1)S(1)}, bf16[256,128]{1,0:T(8,128)(2,1)S(1)}, u32[]{:S(2)}, u32[]{:S(2)}) collective-permute-start(bf16[256,128]{1,0:T(8,128)(2,1)S(1)} %get-tuple-element.45), channel_id=1, source_target_pairs={{0,3},{1,2},{2,1},{3,0},{4,7},{5,6},{6,5},{7,4},{8,11},{9,10},{10,... | collective-permute-start | bytes 196616 | tf_op jit(solution)/shard_map/ppermute | solution.py:119
  19.2 6.1 %collective-permute-start.8 = (bf16[256,128]{1,0:T(8,128)(2,1)S(1)}, bf16[256,128]{1,0:T(8,128)(2,1)S(1)}, u32[]{:S(2)}, u32[]{:S(2)}) collective-permute-start(bf16[256,128]{1,0:T(8,128)(2,1)S(1)} %get-tuple-element.46), channel_id=1, source_target_pairs={{0,2},{1,3},{2,0},{3,1},{4,6},{5,7},{6,4},{7,5},{8,10},{9,11},{10,... | collective-permute-start | bytes 196616 | tf_op jit(solution)/shard_map/ppermute | solution.py:119
  20.0 5.6 %collective-permute-start.9 = (bf16[256,128]{1,0:T(8,128)(2,1)S(1)}, bf16[256,128]{1,0:T(8,128)(2,1)S(1)}, u32[]{:S(2)}, u32[]{:S(2)}) collective-permute-start(bf16[256,128]{1,0:T(8,128)(2,1)S(1)} %get-tuple-element.47), channel_id=1, source_target_pairs={{0,1},{1,0},{2,3},{3,2},{4,5},{5,4},{6,7},{7,6},{8,9},{9,8},{10,11... | collective-permute-start | bytes 196616 | tf_op jit(solution)/shard_map/ppermute | solution.py:119
  26.1 5.2 %collective-permute-start.10 = (bf16[208,256]{1,0:T(8,128)(2,1)S(1)}, bf16[208,256]{1,0:T(8,128)(2,1)S(1)}, u32[]{:S(2)}, u32[]{:S(2)}) collective-permute-start(bf16[208,256]{1,0:T(8,128)(2,1)S(1)} %get-tuple-element.48.mine_ref), channel_id=1, source_target_pairs={{0,1},{1,0},{2,3},{3,2},{4,5},{5,4},{6,7},{7,6},{8,9},{9,8},{10,11... | collective-permute-start | bytes 319496 | tf_op jit(solution)/shard_map/ppermute | solution.py:119
  27.0 7.9 %collective-permute-start.12 = (bf16[128,256]{1,0:T(8,128)(2,1)S(1)}, bf16[128,256]{1,0:T(8,128)(2,1)S(1)}, u32[]{:S(2)}, u32[]{:S(2)}) collective-permute-start(bf16[128,256]{1,0:T(8,128)(2,1)S(1)} %get-tuple-element.51.refs_0_), channel_id=1, source_target_pairs={{0,3},{1,2},{2,1},{3,0},{4,7},{5,6},{6,5},{7,4},{8,11},{9,10},{10,... | collective-permute-start | bytes 196616 | tf_op jit(solution)/shard_map/ppermute | solution.py:119
  29.2 6.5 %collective-permute-start.11 = (bf16[128,256]{1,0:T(8,128)(2,1)S(1)}, bf16[128,256]{1,0:T(8,128)(2,1)S(1)}, u32[]{:S(2)}, u32[]{:S(2)}) collective-permute-start(bf16[128,256]{1,0:T(8,128)(2,1)S(1)} %get-tuple-element.51.refs_0_), channel_id=1, source_target_pairs={{0,2},{1,3},{2,0},{3,1},{4,6},{5,7},{6,4},{7,5},{8,10},{9,11},{10,... | collective-permute-start | bytes 196616 | tf_op jit(solution)/shard_map/ppermute | solution.py:119
  31.3 4.5 %collective-permute-start.15 = (bf16[80,256]{1,0:T(8,128)(2,1)S(1)}, bf16[80,256]{1,0:T(8,128)(2,1)S(1)}, u32[]{:S(2)}, u32[]{:S(2)}) collective-permute-start(bf16[80,256]{1,0:T(8,128)(2,1)S(1)} %terms_sum.1.refs_4_), channel_id=1, source_target_pairs={{0,8},{4,12},{8,0},{12,4},{16,24},{20,28},{24,16},{28,20},{1,9},{5... | collective-permute-start | bytes 122888 | tf_op jit(solution)/shard_map/ppermute | solution.py:119
  32.9 4.0 %collective-permute-start.14 = (bf16[80,256]{1,0:T(8,128)(2,1)S(1)}, bf16[80,256]{1,0:T(8,128)(2,1)S(1)}, u32[]{:S(2)}, u32[]{:S(2)}) collective-permute-start(bf16[80,256]{1,0:T(8,128)(2,1)S(1)} %terms_sum.1.refs_4_), channel_id=1, source_target_pairs={{0,16},{4,20},{8,24},{12,28},{16,0},{20,4},{24,8},{28,12},{1,17},{... | collective-permute-start | bytes 122888 | tf_op jit(solution)/shard_map/ppermute | solution.py:119
  34.4 4.9 %collective-permute-start.13 = (bf16[80,256]{1,0:T(8,128)(2,1)S(1)}, bf16[80,256]{1,0:T(8,128)(2,1)S(1)}, u32[]{:S(2)}, u32[]{:S(2)}) collective-permute-start(bf16[80,256]{1,0:T(8,128)(2,1)S(1)} %terms_sum.1.refs_4_), channel_id=1, source_target_pairs={{0,24},{4,28},{8,16},{12,20},{16,8},{20,12},{24,0},{28,4},{1,25},{... | collective-permute-start | bytes 122888 | tf_op jit(solution)/shard_map/ppermute | solution.py:119
  39.8 1.7 %collective-permute-start.16 = (bf16[592,256]{1,0:T(8,128)(2,1)S(1)}, bf16[592,256]{1,0:T(8,128)(2,1)S(1)}, u32[]{:S(2)}, u32[]{:S(2)}) collective-permute-start(bf16[592,256]{1,0:T(8,128)(2,1)S(1)} %backward_other.1.sent_ref), channel_id=1, source_target_pairs={{0,4},{4,0},{8,12},{12,8},{16,20},{20,16},{24,28},{28,24},{1,5},{5... | collective-permute-start | bytes 909320 | tf_op jit(solution)/shard_map/ppermute | solution.py:119
  41.6 8.5 %collective-permute-start.17 = (bf16[128,256]{1,0:T(8,128)(2,1)S(1)}, bf16[128,256]{1,0:T(8,128)(2,1)S(1)}, u32[]{:S(2)}, u32[]{:S(2)}) collective-permute-start(bf16[128,256]{1,0:T(8,128)(2,1)S(1)} %get-tuple-element.59), channel_id=1, source_target_pairs={{0,24},{4,28},{8,16},{12,20},{16,8},{20,12},{24,0},{28,4},{1,25},{... | collective-permute-start | bytes 196616 | tf_op jit(solution)/shard_map/ppermute | solution.py:119
  42.0 8.0 %collective-permute-start.18 = (bf16[128,256]{1,0:T(8,128)(2,1)S(1)}, bf16[128,256]{1,0:T(8,128)(2,1)S(1)}, u32[]{:S(2)}, u32[]{:S(2)}) collective-permute-start(bf16[128,256]{1,0:T(8,128)(2,1)S(1)} %get-tuple-element.60), channel_id=1, source_target_pairs={{0,16},{4,20},{8,24},{12,28},{16,0},{20,4},{24,8},{28,12},{1,17},{... | collective-permute-start | bytes 196616 | tf_op jit(solution)/shard_map/ppermute | solution.py:119
  43.6 6.4 %collective-permute-start.19 = (bf16[128,256]{1,0:T(8,128)(2,1)S(1)}, bf16[128,256]{1,0:T(8,128)(2,1)S(1)}, u32[]{:S(2)}, u32[]{:S(2)}) collective-permute-start(bf16[128,256]{1,0:T(8,128)(2,1)S(1)} %get-tuple-element.61), channel_id=1, source_target_pairs={{0,8},{4,12},{8,0},{12,4},{16,24},{20,28},{24,16},{28,20},{1,9},{5... | collective-permute-start | bytes 196616 | tf_op jit(solution)/shard_map/ppermute | solution.py:119
  45.1 4.9 %collective-permute-start.20 = (bf16[80,256]{1,0:T(8,128)(2,1)S(1)}, bf16[80,256]{1,0:T(8,128)(2,1)S(1)}, u32[]{:S(2)}, u32[]{:S(2)}) collective-permute-start(bf16[80,256]{1,0:T(8,128)(2,1)S(1)} %get-tuple-element.62.refs_4_), channel_id=1, source_target_pairs={{0,2},{1,3},{2,0},{3,1},{4,6},{5,7},{6,4},{7,5},{8,10},{9,11},{10,... | collective-permute-start | bytes 122888 | tf_op jit(solution)/shard_map/ppermute | solution.py:119
  (1 other events, 13.3 us)

commit v3 on v2

--- a/solution.py
+++ b/solution.py
@@ -137,20 +137,16 @@
     return copies
 
 
-def build_kernel(
-    rows_vmem, cols_vmem, count_vmem, codes_ref, block_ref, row_scr, col_scr, rows_ref, cols_ref,
-    count_ref, sems
-):
+def build_kernel(lists_vmem, codes_ref, block_ref, row_scr, col_scr, lists_ref, sems):
     slots = codes_ref.shape[0]
     side = codes_ref.shape[1] // 2
-    copies = fetch((rows_vmem, cols_vmem, count_vmem), (rows_ref, cols_ref, count_ref), sems)
+    (copy,) = fetch((lists_vmem,), (lists_ref,), sems)
     block_ref[...] = jnp.zeros_like(block_ref)
-    for copy in copies:
-        copy.wait()
+    copy.wait()
     row_code = codes_ref[:, :side].astype(jnp.float32) + 3.0
     row_code = jnp.where(row_code > MOD // 2, row_code - MOD, row_code)
     slot = lax.broadcasted_iota(jnp.int32, (slots, side), 0)
-    row_code = jnp.where(slot < count_ref[0, 0], row_code, 0.0)
+    row_code = jnp.where(slot < lists_ref[2, 0], row_code, 0.0)
     col_code = codes_ref[:, side:].astype(jnp.float32) + 1.0
     col_code = jnp.where(col_code > MOD // 2, col_code - MOD, col_code)
     coarse = 2.0**-12
@@ -171,37 +167,35 @@
             part = turns - jnp.round(turns)
             middle = 3.0 + (HIT - 1) / 2.0
             keep = jnp.abs(part - middle / MOD) < (HIT / 2.0) / MOD
-            down = pl.ds(pl.multiple_of(rows_ref[0, s] * side, side), side)
-            across = pl.ds(pl.multiple_of(cols_ref[0, s] * side, side), side)
+            down = pl.ds(pl.multiple_of(lists_ref[0, s] * side, side), side)
+            across = pl.ds(pl.multiple_of(lists_ref[1, s] * side, side), side)
             block_ref[down, across] += keep.astype(jnp.float32).astype(jnp.bfloat16)
         return carry
 
     lax.fori_loop(0, groups, step, 0)
 
 
-def build_block(tile_rows, tile_cols, tile_count, codes, row_nodes, col_nodes):
+def build_block(lists, codes, row_nodes, col_nodes):
     slots, width = codes.shape
     side = width // 2
     vmem = pl.BlockSpec(memory_space=pltpu.VMEM)
     return pl.pallas_call(
         build_kernel,
         out_shape=jax.ShapeDtypeStruct((row_nodes, col_nodes), jnp.bfloat16),
-        in_specs=[vmem] * 4,
+        in_specs=[vmem] * 2,
         out_specs=vmem,
         scratch_shapes=[
             pltpu.VMEM((slots // GROUP, side, slots), jnp.float32),
             pltpu.VMEM((slots, side), jnp.float32),
-            pltpu.SMEM((1, slots), jnp.int32),
-            pltpu.SMEM((1, slots), jnp.int32),
-            pltpu.SMEM((1, 1), jnp.int32),
-            pltpu.SemaphoreType.DMA((3,)),
+            pltpu.SMEM(lists.shape, jnp.int32),
+            pltpu.SemaphoreType.DMA((1,)),
         ],
         compiler_params=pltpu.CompilerParams(vmem_limit_bytes=LIMIT),
         cost_estimate=pl.CostEstimate(
             flops=20 * slots * side * side, bytes_accessed=2**24, transcendentals=0
         ),
         name="build_block",
-    )(tile_rows, tile_cols, tile_count, codes)
+    )(lists, codes)
 
 
 def forward_kernel(n_row, far, block_ref, *refs):
@@ -353,69 +347,78 @@
 
 
 def pair_kernel(n, mine_ref, sent_ref, theirs_ref, *outs):
-    feat = outs[0].shape[0]
+    feat = mine_ref.shape[0] // n
+    terms = (
+        sent_ref[n * feat :, :].astype(jnp.float32) + theirs_ref[n * feat :, :].astype(jnp.float32)
+    ).astype(jnp.bfloat16)
     for m in range(n):
         span = slice(m * feat, (m + 1) * feat)
-        outs[m][...] = (
+        outs[m][:feat, :] = (
             mine_ref[span, :].astype(jnp.float32) + theirs_ref[span, :].astype(jnp.float32)
         ).astype(jnp.bfloat16)
-    outs[n][...] = (
-        sent_ref[n * feat :, :].astype(jnp.float32) + theirs_ref[n * feat :, :].astype(jnp.float32)
-    ).astype(jnp.bfloat16)
+        outs[m][feat:, :] = terms
 
 
 def pair_sum(mine, sent, theirs, n):
     rows, width = mine.shape
     vmem = pl.BlockSpec(memory_space=pltpu.VMEM)
-    *chunks, terms = pl.pallas_call(
+    chunk = rows // n + sent.shape[0] - rows
+    return pl.pallas_call(
         functools.partial(pair_kernel, n),
-        out_shape=[jax.ShapeDtypeStruct((rows // n, width), jnp.bfloat16)] * n
-        + [jax.ShapeDtypeStruct((sent.shape[0] - rows, width), jnp.bfloat16)],
+        out_shape=[jax.ShapeDtypeStruct((chunk, width), jnp.bfloat16)] * n,
         in_specs=[vmem] * 3,
-        out_specs=[vmem] * (n + 1),
+        out_specs=[vmem] * n,
         compiler_params=pltpu.CompilerParams(vmem_limit_bytes=LIMIT),
         name="pair_sum",
     )(mine, sent, theirs)
-    return chunks, terms
-
-
-def finish_kernel(n, scale, degree_ref, *refs):
-    parts, terms = refs[:n], refs[n:-3]
+
+
+def finish_kernel(scale, degree_ref, *refs):
+    parts = refs[:-3]
     out_ref, weight_ref, bias_ref = refs[-3:]
     inv_row = lax.rsqrt(degree_ref[...].astype(jnp.float32))
-    out_ref[...] = (inv_row * sum_of(parts)).T.astype(jnp.bfloat16)
-    total = sum_of(terms) * scale
+    total = sum_of(parts)
     feat = weight_ref.shape[0]
     half = feat // 2
-    weight_ref[:half, :] = total[:half, :feat]
-    weight_ref[half:, :] = total[:half, feat:]
-    bias_ref[...] = total[half : half + 1, :feat]
-
-
-def finish(degree, parts, terms, scale):
-    feat, pieces = parts[0].shape
+    out_ref[...] = (inv_row * total[:feat]).T.astype(jnp.bfloat16)
+    weight_ref[:half, :] = total[feat : feat + half, :feat] * scale
+    weight_ref[half:, :] = total[feat : feat + half, feat:] * scale
+    bias_ref[...] = total[feat + half : feat + half + 1, :feat] * scale
+
+
+def finish(degree, parts, feat, scale):
+    pieces = parts[0].shape[1]
     vmem = pl.BlockSpec(memory_space=pltpu.VMEM)
     grad_features, grad_weight, grad_bias = pl.pallas_call(
-        functools.partial(finish_kernel, len(parts), scale),
+        functools.partial(finish_kernel, scale),
         out_shape=[
             jax.ShapeDtypeStruct((pieces, feat), jnp.bfloat16),
             jax.ShapeDtypeStruct((feat, feat), jnp.float32),
             jax.ShapeDtypeStruct((1, feat), jnp.float32),
         ],
-        in_specs=[vmem] * (1 + len(parts) + len(terms)),
+        in_specs=[vmem] * (1 + len(parts)),
         out_specs=[vmem] * 3,
         compiler_params=pltpu.CompilerParams(vmem_limit_bytes=LIMIT),
         name="finish",
-    )(degree.reshape(1, pieces), *parts, *terms)
+    )(degree.reshape(1, pieces), *parts)
     return grad_features, grad_weight, grad_bias.reshape(feat)
 
 
-def scale_kernel(n, degree_hbm, features_hbm, *refs):
-    degree_ref, features_ref, sems = refs[-3:]
-    out_ref = refs[n]
+def scale_kernel(
+    degree_hbm, features_hbm, rows_hbm, cols_hbm, count_hbm, codes_hbm, out_ref, lists_ref,
+    codes_ref, degree_ref, features_ref, count_ref, sems
+):
+    slots = codes_ref.shape[0]
     first, second, *others = fetch(
-        (degree_hbm, features_hbm) + refs[:n],
-        (degree_ref, features_ref) + refs[n + 1 : 2 * n + 1],
+        (degree_hbm, features_hbm, rows_hbm.at[0], cols_hbm.at[0], count_hbm, codes_hbm),
+        (
+            degree_ref,
+            features_ref,
+            lists_ref.at[0:1, 0:slots],
+            lists_ref.at[1:2, 0:slots],
+            count_ref,
+            codes_ref,
+        ),
         sems,
     )
     first.wait()
@@ -424,28 +427,29 @@
     out_ref[...] = (inv_root * features_ref[...].astype(jnp.float32)).astype(jnp.bfloat16)
     for copy in others:
         copy.wait()
-
-
-def scale_rows(degree, features, *others):
+    lists_ref[2:3, :] = jnp.broadcast_to(count_ref[0], (1, slots))
+
+
+def scale_rows(degree, features, tile_rows, tile_cols, tile_count, codes):
     pieces, feat = features.shape
-    n = len(others)
-    operands = (degree.reshape(1, pieces), features, *others)
-    return pl.pallas_call(
-        functools.partial(scale_kernel, n),
+    return pl.pallas_call(
+        scale_kernel,
         out_shape=[
             pltpu.VMEM(features.shape, jnp.bfloat16),
-            *(pltpu.VMEM(x.shape, x.dtype) for x in others),
+            pltpu.VMEM((8, codes.shape[0]), jnp.int32),
+            pltpu.VMEM(codes.shape, codes.dtype),
         ],
-        in_specs=[pl.BlockSpec(memory_space=pl.ANY)] * (2 + n),
-        out_specs=[pl.BlockSpec(memory_space=pltpu.VMEM)] * (1 + n),
+        in_specs=[pl.BlockSpec(memory_space=pl.ANY)] * 6,
+        out_specs=[pl.BlockSpec(memory_space=pltpu.VMEM)] * 3,
         scratch_shapes=[
             pltpu.VMEM((1, pieces), jnp.int32),
             pltpu.VMEM((pieces, feat), jnp.bfloat16),
-            pltpu.SemaphoreType.DMA((2 + n,)),
+            pltpu.VMEM((1, 1, 1), jnp.int32),
+            pltpu.SemaphoreType.DMA((6,)),
         ],
-        compiler_params=pltpu.CompilerParams(vmem_limit_bytes=60*2**20),
+        compiler_params=pltpu.CompilerParams(vmem_limit_bytes=60 * 2**20),
         name="scale_rows",
-    )(*operands)
+    )(degree.reshape(1, pieces), features, tile_rows, tile_cols, tile_count, codes)
 
 
 def terms_kernel(feat, mine_ref, theirs_ref, out_ref):
@@ -473,10 +477,10 @@
     n_row = lax.axis_size("row")
     n_col = lax.axis_size("col")
     grad_scale = 1.0 / math.sqrt(pieces * n_row * n_col)
-    scaled, *lists = scale_rows(
-        degree, features, tile_rows[0], tile_cols[0], tile_count[0], tile_codes[0, 0]
-    )
-    block = build_block(*lists, pieces * n_col, pieces * n_row)
+    scaled, lists, codes = scale_rows(
+        degree, features, tile_rows, tile_cols, tile_count, tile_codes[0, 0]
+    )
+    block = build_block(lists, codes, pieces * n_col, pieces * n_row)
     chips = list(range(n_row - 2, 0, -2))
     lines = list(range(n_col - 1, 0, -1))
     sources = [None] * n_row
@@ -497,17 +501,15 @@
     grads = [grad_own, swap(both, "col", 1)] + [swap(grad_own, "col", k) for k in range(2, n_col)]
     grads[1], aggregate = lax.optimization_barrier((grads[1], aggregate))
     hidden = hidden_step(weight, bias, cotangent, aggregate)
-    terms = terms_sum(both, grads[1], feat)
-    from_chips = [swap(terms, "row", m) for m in chips]
-    grads[2:], from_chips = lax.optimization_barrier((grads[2:], from_chips))
-    for_other = backward_parts(block, grads, [terms] + from_chips, n_row, 1)
+    terms = [terms_sum(both, grads[1], feat)]
+    terms += [swap(terms[0], "col", k) for k in range(2, n_col, 2)]
+    grads[2:], terms = lax.optimization_barrier((grads[2:], terms))
+    for_other = backward_parts(block, grads, terms, n_row, 1)
     from_other = swap(for_other, "row", 1)
     for_own = backward_parts(block, grads, [], n_row, 0)
-    chunks, terms = pair_sum(for_own, for_other, from_other, n_row // 2)
+    chunks = pair_sum(for_own, for_other, from_other, n_row // 2)
     landed = [chunks[0]] + [swap(chunks[m // 2], "row", m) for m in chips]
-    for k in range(1, n_col.bit_length() - 1):
-        terms = [terms, swap(terms, "col", 2**k)]
-    grad_features, grad_weight, grad_bias = finish(degree, landed, terms, grad_scale)
+    grad_features, grad_weight, grad_bias = finish(degree, landed, feat, grad_scale)
     return (hidden, grad_features, grad_weight, grad_bias)
 
 

time: 51 us -> 47.7 us (0.935)
  starting transfers between devices: 23.3 us -> 18.4 us
  waiting for transfers between devices: 15 us -> 18 us
  Pallas kernels: 11 us -> 9.69 us
    ppermute x21 -> x18, starting transfers between devices: 23.3 us -> 18.4 us  [swap(): return lax.ppermute(value, axis, [(i, i ^ bits) for i in range(size)])]
    ppermute x21 -> x18, waiting for transfers between devices: 15 us -> 18 us  [swap(): return lax.ppermute(value, axis, [(i, i ^ bits) for i in range(size)])]
    pallas_call x1, Pallas kernels: 4.91 us -> 4.05 us  [build_block(): pl.pallas_call(build_kernel, out_shape=jax.ShapeDtypeStruct((row_nodes, c...]
  transfers between devices with their start and end apart: 21 -> 18, of which waited for: 13 -> 14; matrix products, arithmetic and copies ran while one was open for 0% -> 0% of each run, Pallas kernels for 14% -> 13%
where the time goes in v3:
time: 47.7 us; the launch traced here: 47.5 us
  starting transfers between devices  18.4 us (39%)
  waiting for transfers between devices  18 us (38%)
  Pallas kernels  9.69 us (20%)
  between operations  1.42 us (3%)
    ppermute x18, starting transfers between devices, swap(): return lax.ppermute(value, axis, [(i, i ^ bits) for i in range(size)])  18.4 us
    ppermute x18, waiting for transfers between devices, swap(): return lax.ppermute(value, axis, [(i, i ^ bits) for i in range(size)])  18 us
    pallas_call x1, Pallas kernels, build_block(): pl.pallas_call(build_kernel, out_shape=jax.ShapeDtypeStruct((row_nodes, c...  4.05 us
    pallas_call x2, Pallas kernels, forward_parts(): pl.pallas_call(functools.partial(forward_kernel, n_row, far), out_shape=[...  1.48 us
    pallas_call x1, Pallas kernels, scale_rows(): pl.pallas_call(scale_kernel, out_shape=[pltpu.VMEM(features.shape, jnp.bf...  1.11 us
    pallas_call x2, Pallas kernels, backward_parts(): pl.pallas_call(functools.partial(backward_kernel, n_row, n_col, first), o...  0.98 us
  transfers between devices with their start and end apart: 18, of which 14 were waited for; matrix products, arithmetic and copies ran while one was open for 0% of the time, Pallas kernels for 13%

profile of v3, /device:TPU:0, one launch (start us, length us, event | category | flops | bytes accessed | tf_op | source)
XLA Modules:
  0.0 47.5 jit_solution(2769484877609972140)
XLA Ops:
  1.3 1.1 %scale_rows.1 = (bf16[256,128]{1,0:T(8,128)(2,1)S(1)}, s32[8,128]{1,0:T(8,128)S(1)}, s32[128,256]{1,0:T(8,128)S(1)}) custom-call(s32[1,256]{1,0:T(1,128)} %bitcast.4, bf16[256,128]{1,0:T(8,128)(2,1)} %features_hbm.1, s32[1,1,128]{2,1,0:T(1,128)} %rows_hbm.1, s32[1,1,128]{2,1,0:T(1,128)} %cols_hbm.1, s32[1,1,1]{2,1,0:T(1,128)S(6)} %copy.13.count_hbm, ...), custom_call_target="tpu_custom_call" | custom-call | tf_op jit(solution)/shard_map/scale_rows/pallas_call | solution.py:435
  2.4 3.0 %collective-permute-start.2 = (bf16[256,128]{1,0:T(8,128)(2,1)S(1)}, bf16[256,128]{1,0:T(8,128)(2,1)S(1)}, u32[]{:S(2)}, u32[]{:S(2)}) collective-permute-start(bf16[256,128]{1,0:T(8,128)(2,1)S(1)} %get-tuple-element.33.refs_0_), channel_id=1, source_target_pairs={{0,8},{4,12},{8,0},{12,4},{16,24},{20,28},{24,16},{28,20},{1,9},{5... | collective-permute-start | bytes 196616 | tf_op jit(solution)/shard_map/ppermute | solution.py:119
  5.4 1.5 %collective-permute-start.1 = (bf16[256,128]{1,0:T(8,128)(2,1)S(1)}, bf16[256,128]{1,0:T(8,128)(2,1)S(1)}, u32[]{:S(2)}, u32[]{:S(2)}) collective-permute-start(bf16[256,128]{1,0:T(8,128)(2,1)S(1)} %get-tuple-element.33.refs_0_), channel_id=1, source_target_pairs={{0,16},{4,20},{8,24},{12,28},{16,0},{20,4},{24,8},{28,12},{1,17},{... | collective-permute-start | bytes 196616 | tf_op jit(solution)/shard_map/ppermute | solution.py:119
  6.9 4.1 %build_block.1.block_ref = bf16[1024,2048]{1,0:T(8,128)(2,1)S(1)} custom-call(s32[8,128]{1,0:T(8,128)S(1)} %get-tuple-element.31.lists_vmem, s32[128,256]{1,0:T(8,128)S(1)} %get-tuple-element.32.codes_ref), custom_call_target="tpu_custom_call" | custom-call | flops 41943040 | bytes 16777216 | tf_op jit(solution)/shard_map/build_block/pallas_call | solution.py:182
  11.1 1.0 %collective-permute-done.refs_6_ = bf16[256,128]{1,0:T(8,128)(2,1)S(1)} collective-permute-done((bf16[256,128]{1,0:T(8,128)(2,1)S(1)}, bf16[256,128]{1,0:T(8,128)(2,1)S(1)}, u32[]{:S(2)}, u32[]{:S(2)}) %collective-permute-start) | collective-permute-done | bytes 65568 | tf_op jit(solution)/shard_map/ppermute | solution.py:119
  12.6 0.7 %collective-permute-done.4.refs_3_ = bf16[256,128]{1,0:T(8,128)(2,1)S(1)} collective-permute-done((bf16[256,128]{1,0:T(8,128)(2,1)S(1)}, bf16[256,128]{1,0:T(8,128)(2,1)S(1)}, u32[]{:S(2)}, u32[]{:S(2)}) %collective-permute-start.4) | collective-permute-done | bytes 65568 | tf_op jit(solution)/shard_map/ppermute | solution.py:119
  13.9 0.7 %forward_far.1 = (bf16[256,128]{1,0:T(8,128)(2,1)S(1)}, bf16[256,128]{1,0:T(8,128)(2,1)S(1)}) custom-call(bf16[1024,2048]{1,0:T(8,128)(2,1)S(1)} %build_block.1.block_ref, bf16[256,128]{1,0:T(8,128)(2,1)S(1)} %get-tuple-element.33.refs_0_, bf16[256,128]{1,0:T(8,128)(2,1)S(1)} %collective-permute-done.3.refs_1_, ...), custom_call_target="tpu_custom_call" | custom-call | tf_op jit(solution)/shard_map/forward_far/pallas_call | solution.py:223
  14.6 3.7 %collective-permute-start.7 = (bf16[256,128]{1,0:T(8,128)(2,1)S(1)}, bf16[256,128]{1,0:T(8,128)(2,1)S(1)}, u32[]{:S(2)}, u32[]{:S(2)}) collective-permute-start(bf16[256,128]{1,0:T(8,128)(2,1)S(1)} %get-tuple-element.39), channel_id=1, source_target_pairs={{0,3},{1,2},{2,1},{3,0},{4,7},{5,6},{6,5},{7,4},{8,11},{9,10},{10,... | collective-permute-start | bytes 196616 | tf_op jit(solution)/shard_map/ppermute | solution.py:119
  18.3 0.7 %forward_near.1 = (bf16[256,128]{1,0:T(8,128)(2,1)S(1)}, bf16[256,128]{1,0:T(8,128)(2,1)S(1)}) custom-call(bf16[1024,2048]{1,0:T(8,128)(2,1)S(1)} %build_block.1.block_ref, bf16[256,128]{1,0:T(8,128)(2,1)S(1)} %get-tuple-element.33.refs_0_, bf16[256,128]{1,0:T(8,128)(2,1)S(1)} %collective-permute-done.3.refs_1_, ...), custom_call_target="tpu_custom_call" | custom-call | tf_op jit(solution)/shard_map/forward_near/pallas_call | solution.py:223
  19.0 0.8 %collective-permute-start.9 = (bf16[256,128]{1,0:T(8,128)(2,1)S(1)}, bf16[256,128]{1,0:T(8,128)(2,1)S(1)}, u32[]{:S(2)}, u32[]{:S(2)}) collective-permute-start(bf16[256,128]{1,0:T(8,128)(2,1)S(1)} %get-tuple-element.41), channel_id=1, source_target_pairs={{0,1},{1,0},{2,3},{3,2},{4,5},{5,4},{6,7},{7,6},{8,9},{9,8},{10,11... | collective-permute-start | bytes 196616 | tf_op jit(solution)/shard_map/ppermute | solution.py:119
  19.9 1.1 %collective-permute-done.7.refs_1_ = bf16[256,128]{1,0:T(8,128)(2,1)S(1)} collective-permute-done((bf16[256,128]{1,0:T(8,128)(2,1)S(1)}, bf16[256,128]{1,0:T(8,128)(2,1)S(1)}, u32[]{:S(2)}, u32[]{:S(2)}) %collective-permute-start.7) | collective-permute-done | bytes 65568 | tf_op jit(solution)/shard_map/ppermute | solution.py:119
  20.9 3.3 %collective-permute-done.8.refs_2_ = bf16[256,128]{1,0:T(8,128)(2,1)S(1)} collective-permute-done((bf16[256,128]{1,0:T(8,128)(2,1)S(1)}, bf16[256,128]{1,0:T(8,128)(2,1)S(1)}, u32[]{:S(2)}, u32[]{:S(2)}) %collective-permute-start.8) | collective-permute-done | bytes 65568 | tf_op jit(solution)/shard_map/ppermute | solution.py:119
  25.1 0.7 %collective-permute-start.10 = (bf16[208,256]{1,0:T(8,128)(2,1)S(1)}, bf16[208,256]{1,0:T(8,128)(2,1)S(1)}, u32[]{:S(2)}, u32[]{:S(2)}) collective-permute-start(bf16[208,256]{1,0:T(8,128)(2,1)S(1)} %get-tuple-element.42.mine_ref), channel_id=1, source_target_pairs={{0,1},{1,0},{2,3},{3,2},{4,5},{5,4},{6,7},{7,6},{8,9},{9,8},{10,11... | collective-permute-start | bytes 319496 | tf_op jit(solution)/shard_map/ppermute | solution.py:119
  25.8 2.5 %collective-permute-start.12 = (bf16[128,256]{1,0:T(8,128)(2,1)S(1)}, bf16[128,256]{1,0:T(8,128)(2,1)S(1)}, u32[]{:S(2)}, u32[]{:S(2)}) collective-permute-start(bf16[128,256]{1,0:T(8,128)(2,1)S(1)} %get-tuple-element.45.refs_0_), channel_id=1, source_target_pairs={{0,3},{1,2},{2,1},{3,0},{4,7},{5,6},{6,5},{7,4},{8,11},{9,10},{10,... | collective-permute-start | bytes 196616 | tf_op jit(solution)/shard_map/ppermute | solution.py:119
  28.6 2.2 %collective-permute-done.10.theirs_ref.refs_1_ = bf16[208,256]{1,0:T(8,128)(2,1)S(1)} collective-permute-done((bf16[208,256]{1,0:T(8,128)(2,1)S(1)}, bf16[208,256]{1,0:T(8,128)(2,1)S(1)}, u32[]{:S(2)}, u32[]{:S(2)}) %collective-permute-start.10) | collective-permute-done | bytes 106528 | tf_op jit(solution)/shard_map/ppermute | solution.py:119
  30.8 1.6 %collective-permute-start.13 = (bf16[80,256]{1,0:T(8,128)(2,1)S(1)}, bf16[80,256]{1,0:T(8,128)(2,1)S(1)}, u32[]{:S(2)}, u32[]{:S(2)}) collective-permute-start(bf16[80,256]{1,0:T(8,128)(2,1)S(1)} %terms_sum.1.refs_4_), channel_id=1, source_target_pairs={{0,2},{1,3},{2,0},{3,1},{4,6},{5,7},{6,4},{7,5},{8,10},{9,11},{10,... | collective-permute-start | bytes 122888 | tf_op jit(solution)/shard_map/ppermute | solution.py:119
  32.9 2.1 %collective-permute-done.11.refs_2_ = bf16[128,256]{1,0:T(8,128)(2,1)S(1)} collective-permute-done((bf16[128,256]{1,0:T(8,128)(2,1)S(1)}, bf16[128,256]{1,0:T(8,128)(2,1)S(1)}, u32[]{:S(2)}, u32[]{:S(2)}) %collective-permute-start.11) | collective-permute-done | bytes 65568 | tf_op jit(solution)/shard_map/ppermute | solution.py:119
  35.0 1.2 %collective-permute-done.13.refs_5_ = bf16[80,256]{1,0:T(8,128)(2,1)S(1)} collective-permute-done((bf16[80,256]{1,0:T(8,128)(2,1)S(1)}, bf16[80,256]{1,0:T(8,128)(2,1)S(1)}, u32[]{:S(2)}, u32[]{:S(2)}) %collective-permute-start.13) | collective-permute-done | bytes 40992 | tf_op jit(solution)/shard_map/ppermute | solution.py:119
  37.3 1.1 %collective-permute-done.14.theirs_ref = bf16[592,256]{1,0:T(8,128)(2,1)S(1)} collective-permute-done((bf16[592,256]{1,0:T(8,128)(2,1)S(1)}, bf16[592,256]{1,0:T(8,128)(2,1)S(1)}, u32[]{:S(2)}, u32[]{:S(2)}) %collective-permute-start.14) | collective-permute-done | bytes 303136 | tf_op jit(solution)/shard_map/ppermute | solution.py:119
  38.5 2.4 %collective-permute-start.15 = (bf16[208,256]{1,0:T(8,128)(2,1)S(1)}, bf16[208,256]{1,0:T(8,128)(2,1)S(1)}, u32[]{:S(2)}, u32[]{:S(2)}) collective-permute-start(bf16[208,256]{1,0:T(8,128)(2,1)S(1)} %get-tuple-element.52), channel_id=1, source_target_pairs={{0,24},{4,28},{8,16},{12,20},{16,8},{20,12},{24,0},{28,4},{1,25},{... | collective-permute-start | bytes 319496 | tf_op jit(solution)/shard_map/ppermute | solution.py:119
  42.0 0.8 %hidden_step.1 = bf16[256,128]{1,0:T(8,128)(2,1)} custom-call(bf16[128,128]{1,0:T(8,128)(2,1)S(1)} %copy-done.1, f32[1,128]{1,0:T(1,128)S(1)} %bitcast.8, bf16[256,128]{1,0:T(8,128)(2,1)S(1)} %copy-done, bf16[256,128]{1,0:T(8,128)(2,1)S(1)} %get-tuple-element.44.aggregate_ref), custom_call_target="tpu_custom_call" | custom-call | tf_op jit(solution)/shard_map/hidden_step/pallas_call | solution.py:298
  42.8 1.7 %collective-permute-done.15.refs_1_ = bf16[208,256]{1,0:T(8,128)(2,1)S(1)} collective-permute-done((bf16[208,256]{1,0:T(8,128)(2,1)S(1)}, bf16[208,256]{1,0:T(8,128)(2,1)S(1)}, u32[]{:S(2)}, u32[]{:S(2)}) %collective-permute-start.15) | collective-permute-done | bytes 106528 | tf_op jit(solution)/shard_map/ppermute | solution.py:119
  44.6 2.2 %collective-permute-done.16.refs_2_ = bf16[208,256]{1,0:T(8,128)(2,1)S(1)} collective-permute-done((bf16[208,256]{1,0:T(8,128)(2,1)S(1)}, bf16[208,256]{1,0:T(8,128)(2,1)S(1)}, u32[]{:S(2)}, u32[]{:S(2)}) %collective-permute-start.16) | collective-permute-done | bytes 106528 | tf_op jit(solution)/shard_map/ppermute | solution.py:119
  46.7 0.7 %finish.1 = (bf16[256,128]{1,0:T(8,128)(2,1)}, f32[128,128]{1,0:T(8,128)}, f32[1,128]{1,0:T(1,128)}) custom-call(s32[1,256]{1,0:T(1,128)S(1)} %bitcast.6, bf16[208,256]{1,0:T(8,128)(2,1)S(1)} %get-tuple-element.51.refs_0_, bf16[208,256]{1,0:T(8,128)(2,1)S(1)} %collective-permute-done.15.refs_1_, bf16[208,256]{1,0:T(8,128)(2,1)S(1)} %collective-permute-done.16.refs_2_, ...), custom_call_target="tpu_custom_call" | custom-call | tf_op jit(solution)/shard_map/finish/pallas_call | solution.py:392
  (31 shorter events, 4.9 us)
Async XLA Ops:
  2.4 8.7 %collective-permute-start.2 = (bf16[256,128]{1,0:T(8,128)(2,1)S(1)}, bf16[256,128]{1,0:T(8,128)(2,1)S(1)}, u32[]{:S(2)}, u32[]{:S(2)}) collective-permute-start(bf16[256,128]{1,0:T(8,128)(2,1)S(1)} %get-tuple-element.33.refs_0_), channel_id=1, source_target_pairs={{0,8},{4,12},{8,0},{12,4},{16,24},{20,28},{24,16},{28,20},{1,9},{5... | collective-permute-start | bytes 196616 | tf_op jit(solution)/shard_map/ppermute | solution.py:119
  5.4 5.7 %collective-permute-start.1 = (bf16[256,128]{1,0:T(8,128)(2,1)S(1)}, bf16[256,128]{1,0:T(8,128)(2,1)S(1)}, u32[]{:S(2)}, u32[]{:S(2)}) collective-permute-start(bf16[256,128]{1,0:T(8,128)(2,1)S(1)} %get-tuple-element.33.refs_0_), channel_id=1, source_target_pairs={{0,16},{4,20},{8,24},{12,28},{16,0},{20,4},{24,8},{28,12},{1,17},{... | collective-permute-start | bytes 196616 | tf_op jit(solution)/shard_map/ppermute | solution.py:119
  6.9 5.2 %collective-permute-start = (bf16[256,128]{1,0:T(8,128)(2,1)S(1)}, bf16[256,128]{1,0:T(8,128)(2,1)S(1)}, u32[]{:S(2)}, u32[]{:S(2)}) collective-permute-start(bf16[256,128]{1,0:T(8,128)(2,1)S(1)} %get-tuple-element.33.refs_0_), channel_id=1, source_target_pairs={{0,24},{4,28},{8,16},{12,20},{16,8},{20,12},{24,0},{28,4},{1,25},{... | collective-permute-start | bytes 196616 | tf_op jit(solution)/shard_map/ppermute | solution.py:119
  6.9 5.7 %collective-permute-start.3 = (bf16[256,128]{1,0:T(8,128)(2,1)S(1)}, bf16[256,128]{1,0:T(8,128)(2,1)S(1)}, u32[]{:S(2)}, u32[]{:S(2)}) collective-permute-start(bf16[256,128]{1,0:T(8,128)(2,1)S(1)} %get-tuple-element.33.refs_0_), channel_id=1, source_target_pairs={{0,4},{4,0},{8,12},{12,8},{16,20},{20,16},{24,28},{28,24},{1,5},{5... | collective-permute-start | bytes 196616 | tf_op jit(solution)/shard_map/ppermute | solution.py:119
  11.0 13.6 %copy-start = (bf16[256,128]{1,0:T(8,128)(2,1)S(1)}, bf16[256,128]{1,0:T(8,128)(2,1)}, u32[]{:S(2)}) copy-start(bf16[256,128]{1,0:T(8,128)(2,1)} %cot_ref.3) | copy-start | bytes 196612
  11.0 13.6 %copy-start.1 = (bf16[128,128]{1,0:T(8,128)(2,1)S(1)}, bf16[128,128]{1,0:T(8,128)(2,1)}, u32[]{:S(2)}) copy-start(bf16[128,128]{1,0:T(8,128)(2,1)} %weight_ref.3) | copy-start | bytes 98308
  11.0 13.6 %copy-start.2 = (s32[256]{0:T(256)S(1)}, s32[256]{0:T(256)}, u32[]{:S(2)}) copy-start(s32[256]{0:T(256)} %param.10) | copy-start | bytes 3076
  11.0 13.6 %copy-start.3 = (f32[128]{0:T(128)S(1)}, f32[128]{0:T(128)}, u32[]{:S(2)}) copy-start(f32[128]{0:T(128)} %param.12) | copy-start | bytes 1540
  12.1 1.3 %collective-permute-start.4 = (bf16[256,128]{1,0:T(8,128)(2,1)S(1)}, bf16[256,128]{1,0:T(8,128)(2,1)S(1)}, u32[]{:S(2)}, u32[]{:S(2)}) collective-permute-start(bf16[256,128]{1,0:T(8,128)(2,1)S(1)} %collective-permute-done.2.refs_2_), channel_id=1, source_target_pairs={{0,4},{4,0},{8,12},{12,8},{16,20},{20,16},{24,28},{28,24},{1,5},{5... | collective-permute-start | bytes 196616 | tf_op jit(solution)/shard_map/ppermute | solution.py:119
  12.1 1.4 %collective-permute-start.5 = (bf16[256,128]{1,0:T(8,128)(2,1)S(1)}, bf16[256,128]{1,0:T(8,128)(2,1)S(1)}, u32[]{:S(2)}, u32[]{:S(2)}) collective-permute-start(bf16[256,128]{1,0:T(8,128)(2,1)S(1)} %collective-permute-done.1.refs_4_), channel_id=1, source_target_pairs={{0,4},{4,0},{8,12},{12,8},{16,20},{20,16},{24,28},{28,24},{1,5},{5... | collective-permute-start | bytes 196616 | tf_op jit(solution)/shard_map/ppermute | solution.py:119
  12.6 1.3 %collective-permute-start.6 = (bf16[256,128]{1,0:T(8,128)(2,1)S(1)}, bf16[256,128]{1,0:T(8,128)(2,1)S(1)}, u32[]{:S(2)}, u32[]{:S(2)}) collective-permute-start(bf16[256,128]{1,0:T(8,128)(2,1)S(1)} %collective-permute-done.refs_6_), channel_id=1, source_target_pairs={{0,4},{4,0},{8,12},{12,8},{16,20},{20,16},{24,28},{28,24},{1,5},{5... | collective-permute-start | bytes 196616 | tf_op jit(solution)/shard_map/ppermute | solution.py:119
  14.6 6.3 %collective-permute-start.7 = (bf16[256,128]{1,0:T(8,128)(2,1)S(1)}, bf16[256,128]{1,0:T(8,128)(2,1)S(1)}, u32[]{:S(2)}, u32[]{:S(2)}) collective-permute-start(bf16[256,128]{1,0:T(8,128)(2,1)S(1)} %get-tuple-element.39), channel_id=1, source_target_pairs={{0,3},{1,2},{2,1},{3,0},{4,7},{5,6},{6,5},{7,4},{8,11},{9,10},{10,... | collective-permute-start | bytes 196616 | tf_op jit(solution)/shard_map/ppermute | solution.py:119
  18.3 6.0 %collective-permute-start.8 = (bf16[256,128]{1,0:T(8,128)(2,1)S(1)}, bf16[256,128]{1,0:T(8,128)(2,1)S(1)}, u32[]{:S(2)}, u32[]{:S(2)}) collective-permute-start(bf16[256,128]{1,0:T(8,128)(2,1)S(1)} %get-tuple-element.40), channel_id=1, source_target_pairs={{0,2},{1,3},{2,0},{3,1},{4,6},{5,7},{6,4},{7,5},{8,10},{9,11},{10,... | collective-permute-start | bytes 196616 | tf_op jit(solution)/shard_map/ppermute | solution.py:119
  19.0 5.6 %collective-permute-start.9 = (bf16[256,128]{1,0:T(8,128)(2,1)S(1)}, bf16[256,128]{1,0:T(8,128)(2,1)S(1)}, u32[]{:S(2)}, u32[]{:S(2)}) collective-permute-start(bf16[256,128]{1,0:T(8,128)(2,1)S(1)} %get-tuple-element.41), channel_id=1, source_target_pairs={{0,1},{1,0},{2,3},{3,2},{4,5},{5,4},{6,7},{7,6},{8,9},{9,8},{10,11... | collective-permute-start | bytes 196616 | tf_op jit(solution)/shard_map/ppermute | solution.py:119
  25.1 5.8 %collective-permute-start.10 = (bf16[208,256]{1,0:T(8,128)(2,1)S(1)}, bf16[208,256]{1,0:T(8,128)(2,1)S(1)}, u32[]{:S(2)}, u32[]{:S(2)}) collective-permute-start(bf16[208,256]{1,0:T(8,128)(2,1)S(1)} %get-tuple-element.42.mine_ref), channel_id=1, source_target_pairs={{0,1},{1,0},{2,3},{3,2},{4,5},{5,4},{6,7},{7,6},{8,9},{9,8},{10,11... | collective-permute-start | bytes 319496 | tf_op jit(solution)/shard_map/ppermute | solution.py:119
  25.8 7.1 %collective-permute-start.12 = (bf16[128,256]{1,0:T(8,128)(2,1)S(1)}, bf16[128,256]{1,0:T(8,128)(2,1)S(1)}, u32[]{:S(2)}, u32[]{:S(2)}) collective-permute-start(bf16[128,256]{1,0:T(8,128)(2,1)S(1)} %get-tuple-element.45.refs_0_), channel_id=1, source_target_pairs={{0,3},{1,2},{2,1},{3,0},{4,7},{5,6},{6,5},{7,4},{8,11},{9,10},{10,... | collective-permute-start | bytes 196616 | tf_op jit(solution)/shard_map/ppermute | solution.py:119
  28.3 6.8 %collective-permute-start.11 = (bf16[128,256]{1,0:T(8,128)(2,1)S(1)}, bf16[128,256]{1,0:T(8,128)(2,1)S(1)}, u32[]{:S(2)}, u32[]{:S(2)}) collective-permute-start(bf16[128,256]{1,0:T(8,128)(2,1)S(1)} %get-tuple-element.45.refs_0_), channel_id=1, source_target_pairs={{0,2},{1,3},{2,0},{3,1},{4,6},{5,7},{6,4},{7,5},{8,10},{9,11},{10,... | collective-permute-start | bytes 196616 | tf_op jit(solution)/shard_map/ppermute | solution.py:119
  30.8 5.4 %collective-permute-start.13 = (bf16[80,256]{1,0:T(8,128)(2,1)S(1)}, bf16[80,256]{1,0:T(8,128)(2,1)S(1)}, u32[]{:S(2)}, u32[]{:S(2)}) collective-permute-start(bf16[80,256]{1,0:T(8,128)(2,1)S(1)} %terms_sum.1.refs_4_), channel_id=1, source_target_pairs={{0,2},{1,3},{2,0},{3,1},{4,6},{5,7},{6,4},{7,5},{8,10},{9,11},{10,... | collective-permute-start | bytes 122888 | tf_op jit(solution)/shard_map/ppermute | solution.py:119
  36.7 1.7 %collective-permute-start.14 = (bf16[592,256]{1,0:T(8,128)(2,1)S(1)}, bf16[592,256]{1,0:T(8,128)(2,1)S(1)}, u32[]{:S(2)}, u32[]{:S(2)}) collective-permute-start(bf16[592,256]{1,0:T(8,128)(2,1)S(1)} %backward_other.1.sent_ref), channel_id=1, source_target_pairs={{0,4},{4,0},{8,12},{12,8},{16,20},{20,16},{24,28},{28,24},{1,5},{5... | collective-permute-start | bytes 909320 | tf_op jit(solution)/shard_map/ppermute | solution.py:119
  38.5 6.1 %collective-permute-start.15 = (bf16[208,256]{1,0:T(8,128)(2,1)S(1)}, bf16[208,256]{1,0:T(8,128)(2,1)S(1)}, u32[]{:S(2)}, u32[]{:S(2)}) collective-permute-start(bf16[208,256]{1,0:T(8,128)(2,1)S(1)} %get-tuple-element.52), channel_id=1, source_target_pairs={{0,24},{4,28},{8,16},{12,20},{16,8},{20,12},{24,0},{28,4},{1,25},{... | collective-permute-start | bytes 319496 | tf_op jit(solution)/shard_map/ppermute | solution.py:119
  40.9 5.8 %collective-permute-start.16 = (bf16[208,256]{1,0:T(8,128)(2,1)S(1)}, bf16[208,256]{1,0:T(8,128)(2,1)S(1)}, u32[]{:S(2)}, u32[]{:S(2)}) collective-permute-start(bf16[208,256]{1,0:T(8,128)(2,1)S(1)} %get-tuple-element.53), channel_id=1, source_target_pairs={{0,16},{4,20},{8,24},{12,28},{16,0},{20,4},{24,8},{28,12},{1,17},{... | collective-permute-start | bytes 319496 | tf_op jit(solution)/shard_map/ppermute | solution.py:119
  41.4 5.3 %collective-permute-start.17 = (bf16[208,256]{1,0:T(8,128)(2,1)S(1)}, bf16[208,256]{1,0:T(8,128)(2,1)S(1)}, u32[]{:S(2)}, u32[]{:S(2)}) collective-permute-start(bf16[208,256]{1,0:T(8,128)(2,1)S(1)} %get-tuple-element.54), channel_id=1, source_target_pairs={{0,8},{4,12},{8,0},{12,4},{16,24},{20,28},{24,16},{28,20},{1,9},{5... | collective-permute-start | bytes 319496 | tf_op jit(solution)/shard_map/ppermute | solution.py:119

commit v4 on v3

--- a/solution.py
+++ b/solution.py
@@ -9,7 +9,7 @@
 from jax.sharding import PartitionSpec as P
 
 BLOCK = 16
-GROUP = 16
+GROUP = 32
 MOD = 4093
 HIT = 64
 DENSE_BYTES = 8 * 2**20
@@ -137,24 +137,29 @@
     return copies
 
 
-def build_kernel(lists_vmem, codes_ref, block_ref, row_scr, col_scr, lists_ref, sems):
+def build_kernel(first, last, lists_vmem, count_ref, codes_ref, *refs):
+    block_ref, row_scr, col_scr, lists_ref, sems = refs[-5:]
     slots = codes_ref.shape[0]
     side = codes_ref.shape[1] // 2
     (copy,) = fetch((lists_vmem,), (lists_ref,), sems)
-    block_ref[...] = jnp.zeros_like(block_ref)
-    copy.wait()
+    if first == 0:
+        block_ref[...] = jnp.zeros_like(block_ref)
     row_code = codes_ref[:, :side].astype(jnp.float32) + 3.0
     row_code = jnp.where(row_code > MOD // 2, row_code - MOD, row_code)
     slot = lax.broadcasted_iota(jnp.int32, (slots, side), 0)
-    row_code = jnp.where(slot < lists_ref[2, 0], row_code, 0.0)
+    row_code = jnp.where(slot < count_ref[0, 0, 0], row_code, 0.0)
     col_code = codes_ref[:, side:].astype(jnp.float32) + 1.0
     col_code = jnp.where(col_code > MOD // 2, col_code - MOD, col_code)
     coarse = 2.0**-12
     col_scr[...] = col_code * coarse + col_code * (1.0 / MOD - coarse)
     by_side = row_code.T
-    groups = slots // GROUP
-    for g in range(groups):
+    groups = range(first // GROUP, last // GROUP)
+    for g in groups:
         row_scr[g] = by_side if g == 0 else pltpu.roll(by_side, slots - g * GROUP, axis=1)
+    copy.wait()
+    middle = (3.0 + (HIT - 1) / 2.0) / MOD
+    reach = jnp.bfloat16(2.0**-7)
+    one, zero = jnp.bfloat16(1.0), jnp.bfloat16(0.0)
 
     def step(g, carry):
         row_vals = row_scr[g]
@@ -165,25 +170,26 @@
                 col_vals[t : t + 1, :], (side, side)
             )
             part = turns - jnp.round(turns)
-            middle = 3.0 + (HIT - 1) / 2.0
-            keep = jnp.abs(part - middle / MOD) < (HIT / 2.0) / MOD
+            keep = jnp.abs((part - middle).astype(jnp.bfloat16)) < reach
             down = pl.ds(pl.multiple_of(lists_ref[0, s] * side, side), side)
             across = pl.ds(pl.multiple_of(lists_ref[1, s] * side, side), side)
-            block_ref[down, across] += keep.astype(jnp.float32).astype(jnp.bfloat16)
+            block_ref[down, across] += jnp.where(keep, one, zero)
         return carry
 
-    lax.fori_loop(0, groups, step, 0)
-
-
-def build_block(lists, codes, row_nodes, col_nodes):
+    lax.fori_loop(groups.start, groups.stop, step, 0)
+
+
+def build_block(lists, tile_count, codes, row_nodes, col_nodes, first, last, block=None):
     slots, width = codes.shape
     side = width // 2
     vmem = pl.BlockSpec(memory_space=pltpu.VMEM)
-    return pl.pallas_call(
-        build_kernel,
-        out_shape=jax.ShapeDtypeStruct((row_nodes, col_nodes), jnp.bfloat16),
-        in_specs=[vmem] * 2,
+    begun = [] if block is None else [block]
+    return pl.pallas_call(
+        functools.partial(build_kernel, first, last),
+        out_shape=pltpu.VMEM((row_nodes, col_nodes), jnp.bfloat16),
+        in_specs=[vmem, pl.BlockSpec(memory_space=pltpu.SMEM), vmem] + [vmem] * len(begun),
         out_specs=vmem,
+        input_output_aliases={3: 0} if begun else {},
         scratch_shapes=[
             pltpu.VMEM((slots // GROUP, side, slots), jnp.float32),
             pltpu.VMEM((slots, side), jnp.float32),
@@ -192,22 +198,48 @@
         ],
         compiler_params=pltpu.CompilerParams(vmem_limit_bytes=LIMIT),
         cost_estimate=pl.CostEstimate(
-            flops=20 * slots * side * side, bytes_accessed=2**24, transcendentals=0
+            flops=20 * (last - first) * side * side, bytes_accessed=2**23, transcendentals=0
         ),
-        name="build_block",
-    )(lists, codes)
-
-
-def forward_kernel(n_row, far, block_ref, *refs):
-    sources = refs[:n_row]
-    outs = refs[n_row : n_row + len(far)]
+        name="build_rest" if begun else "build_block",
+    )(lists, tile_count, codes, *begun)
+
+
+def stack_kernel(*refs):
+    *parts, out_ref = refs
+    rows = parts[0].shape[0]
+    for m, part in enumerate(parts):
+        out_ref[m * rows : (m + 1) * rows, :] = part[...]
+
+
+def stack(parts):
+    rows, width = parts[0].shape
+    vmem = pl.BlockSpec(memory_space=pltpu.VMEM)
+    return pl.pallas_call(
+        stack_kernel,
+        out_shape=jax.ShapeDtypeStruct((len(parts) * rows, width), parts[0].dtype),
+        in_specs=[vmem] * len(parts),
+        out_specs=vmem,
+        compiler_params=pltpu.CompilerParams(vmem_limit_bytes=LIMIT),
+        name="stack",
+    )(*parts)
+
+
+def forward_kernel(n_own, n_row, far, block_ref, *refs):
+    own, other = refs[:n_own], refs[n_own : -1 - len(far)]
+    outs = refs[-1 - len(far) : -1]
     source = refs[-1]
-    pieces = sources[0].shape[0]
+    pieces = own[0].shape[0]
     me_row = lax.axis_index("row")
     me_col = lax.axis_index("col")
-    for k in range(n_row):
-        at = pl.multiple_of((me_row ^ k) * pieces, pieces)
-        source[pl.ds(at, pieces), :] = sources[k][...]
+    for m, part in enumerate(own):
+        at = pl.multiple_of((me_row ^ (2 * m)) * pieces, pieces)
+        source[pl.ds(at, pieces), :] = part[...]
+    bits = 1
+    for part in other:
+        for k in range(part.shape[0] // pieces):
+            at = pl.multiple_of((me_row ^ bits) * pieces, pieces)
+            source[pl.ds(at, pieces), :] = part[k * pieces : (k + 1) * pieces, :]
+            bits += 2
     whole = source[...]
     for out, k in zip(outs, far):
         at = pl.multiple_of((me_col ^ k) * pieces, pieces)
@@ -216,19 +248,18 @@
         ).astype(jnp.bfloat16)
 
 
-def forward_parts(block, sources, far, name):
-    pieces, feat = sources[0].shape
-    n_row = len(sources)
-    vmem = pl.BlockSpec(memory_space=pltpu.VMEM)
-    return pl.pallas_call(
-        functools.partial(forward_kernel, n_row, far),
+def forward_parts(block, own, other, n_row, far, name):
+    pieces, feat = own[0].shape
+    vmem = pl.BlockSpec(memory_space=pltpu.VMEM)
+    return pl.pallas_call(
+        functools.partial(forward_kernel, len(own), n_row, far),
         out_shape=[jax.ShapeDtypeStruct((pieces, feat), jnp.bfloat16)] * len(far),
-        in_specs=[vmem] * (1 + n_row),
+        in_specs=[vmem] * (1 + len(own) + len(other)),
         out_specs=[vmem] * len(far),
         scratch_shapes=[pltpu.VMEM((pieces * n_row, feat), jnp.bfloat16)],
         compiler_params=pltpu.CompilerParams(vmem_limit_bytes=LIMIT),
         name=name,
-    )(block, *sources)
+    )(block, *own, *other)
 
 
 def slope_of(aggregate, weight, bias, cotangent):
@@ -305,25 +336,6 @@
     )(weight, bias.reshape(1, feat), cotangent, aggregate)
 
 
-def backward_kernel(n_row, n_col, first, block_ref, *refs):
-    sources, terms = refs[:n_col], refs[n_col:-1]
-    out_ref = refs[-1]
-    feat, pieces = sources[0].shape
-    me_row = lax.axis_index("row")
-    me_col = lax.axis_index("col")
-    for m in range(n_row // 2):
-        across = pl.ds(pl.multiple_of((me_row ^ (2 * m + first)) * pieces, pieces), pieces)
-        total = jnp.zeros((feat, pieces), jnp.float32)
-        for k in range(n_col):
-            down = pl.ds(pl.multiple_of((me_col ^ k) * pieces, pieces), pieces)
-            total += jnp.dot(
-                sources[k][:feat, :], block_ref[down, across], preferred_element_type=jnp.float32
-            )
-        out_ref[m * feat : (m + 1) * feat, :] = total.astype(jnp.bfloat16)
-    if terms:
-        out_ref[n_row // 2 * feat :, :] = sum_of(terms).astype(jnp.bfloat16)
-
-
 def sum_of(refs):
     total = refs[0][...].astype(jnp.float32)
     for ref in refs[1:]:
@@ -331,19 +343,42 @@
     return total
 
 
-def backward_parts(block, sources, terms, n_row, first):
+def backward_kernel(feat, kinds, chunks, begun, block_ref, *refs):
+    sources, out_ref = refs[: len(kinds)], refs[-1]
+    terms = refs[len(kinds) + begun : -1]
+    pieces = out_ref.shape[1]
+    me_row = lax.axis_index("row")
+    me_col = lax.axis_index("col")
+    for m, chunk in enumerate(chunks):
+        across = pl.ds(pl.multiple_of((me_row ^ chunk) * pieces, pieces), pieces)
+        if begun:
+            total = refs[len(kinds)][chunk * feat : (chunk + 1) * feat, :]
+        else:
+            total = jnp.zeros((feat, pieces), jnp.float32)
+        for k, source in zip(kinds, sources):
+            down = pl.ds(pl.multiple_of((me_col ^ k) * pieces, pieces), pieces)
+            total += jnp.dot(
+                source[:feat, :], block_ref[down, across], preferred_element_type=jnp.float32
+            )
+        out_ref[m * feat : (m + 1) * feat, :] = total.astype(out_ref.dtype)
+    if terms:
+        out_ref[len(chunks) * feat :, :] = sum_of(terms).astype(out_ref.dtype)
+
+
+def backward_parts(block, sources, kinds, chunks, begun, terms, name):
     feat, pieces = sources[0].shape
-    n_col = len(sources)
+    begun = [] if begun is None else [begun]
     extra = terms[0].shape[0] if terms else 0
     vmem = pl.BlockSpec(memory_space=pltpu.VMEM)
-    return pl.pallas_call(
-        functools.partial(backward_kernel, n_row, n_col, first),
-        out_shape=jax.ShapeDtypeStruct((n_row // 2 * feat + extra, pieces), jnp.bfloat16),
-        in_specs=[vmem] * (1 + n_col + len(terms)),
+    dtype = jnp.bfloat16 if begun else jnp.float32
+    return pl.pallas_call(
+        functools.partial(backward_kernel, feat, kinds, chunks, len(begun)),
+        out_shape=jax.ShapeDtypeStruct((len(chunks) * feat + extra, pieces), dtype),
+        in_specs=[vmem] * (1 + len(kinds) + len(begun) + len(terms)),
         out_specs=vmem,
         compiler_params=pltpu.CompilerParams(vmem_limit_bytes=LIMIT),
-        name="backward_other" if first else "backward_own",
-    )(block, *sources, *terms)
+        name=name,
+    )(block, *(sources[k] for k in kinds), *begun, *terms)
 
 
 def pair_kernel(n, mine_ref, sent_ref, theirs_ref, *outs):
@@ -405,18 +440,17 @@
 
 
 def scale_kernel(
-    degree_hbm, features_hbm, rows_hbm, cols_hbm, count_hbm, codes_hbm, out_ref, lists_ref,
-    codes_ref, degree_ref, features_ref, count_ref, sems
+    degree_hbm, features_hbm, rows_hbm, cols_hbm, codes_hbm, out_ref, lists_ref, codes_ref,
+    degree_ref, features_ref, sems
 ):
     slots = codes_ref.shape[0]
     first, second, *others = fetch(
-        (degree_hbm, features_hbm, rows_hbm.at[0], cols_hbm.at[0], count_hbm, codes_hbm),
+        (degree_hbm, features_hbm, rows_hbm.at[0], cols_hbm.at[0], codes_hbm),
         (
             degree_ref,
             features_ref,
             lists_ref.at[0:1, 0:slots],
             lists_ref.at[1:2, 0:slots],
-            count_ref,
             codes_ref,
         ),
         sems,
@@ -427,10 +461,9 @@
     out_ref[...] = (inv_root * features_ref[...].astype(jnp.float32)).astype(jnp.bfloat16)
     for copy in others:
         copy.wait()
-    lists_ref[2:3, :] = jnp.broadcast_to(count_ref[0], (1, slots))
-
-
-def scale_rows(degree, features, tile_rows, tile_cols, tile_count, codes):
+
+
+def scale_rows(degree, features, tile_rows, tile_cols, codes):
     pieces, feat = features.shape
     return pl.pallas_call(
         scale_kernel,
@@ -439,35 +472,37 @@
             pltpu.VMEM((8, codes.shape[0]), jnp.int32),
             pltpu.VMEM(codes.shape, codes.dtype),
         ],
-        in_specs=[pl.BlockSpec(memory_space=pl.ANY)] * 6,
+        in_specs=[pl.BlockSpec(memory_space=pl.ANY)] * 5,
         out_specs=[pl.BlockSpec(memory_space=pltpu.VMEM)] * 3,
         scratch_shapes=[
             pltpu.VMEM((1, pieces), jnp.int32),
             pltpu.VMEM((pieces, feat), jnp.bfloat16),
-            pltpu.VMEM((1, 1, 1), jnp.int32),
-            pltpu.SemaphoreType.DMA((6,)),
+            pltpu.SemaphoreType.DMA((5,)),
         ],
         compiler_params=pltpu.CompilerParams(vmem_limit_bytes=60 * 2**20),
         name="scale_rows",
-    )(degree.reshape(1, pieces), features, tile_rows, tile_cols, tile_count, codes)
-
-
-def terms_kernel(feat, mine_ref, theirs_ref, out_ref):
-    out_ref[...] = (
-        mine_ref[feat:, :].astype(jnp.float32) + theirs_ref[feat:, :].astype(jnp.float32)
-    ).astype(jnp.bfloat16)
-
-
-def terms_sum(mine, theirs, feat):
-    vmem = pl.BlockSpec(memory_space=pltpu.VMEM)
-    return pl.pallas_call(
-        functools.partial(terms_kernel, feat),
-        out_shape=jax.ShapeDtypeStruct((mine.shape[0] - feat, mine.shape[1]), jnp.bfloat16),
-        in_specs=[vmem] * 2,
+    )(degree.reshape(1, pieces), features, tile_rows, tile_cols, codes)
+
+
+def terms_kernel(skip, *refs):
+    *parts, out_ref = refs
+    total = parts[0][skip:, :].astype(jnp.float32)
+    for part in parts[1:]:
+        total += part[skip:, :].astype(jnp.float32)
+    out_ref[...] = total.astype(jnp.bfloat16)
+
+
+def terms_sum(parts, skip, name):
+    rows, width = parts[0].shape
+    vmem = pl.BlockSpec(memory_space=pltpu.VMEM)
+    return pl.pallas_call(
+        functools.partial(terms_kernel, skip),
+        out_shape=jax.ShapeDtypeStruct((rows - skip, width), jnp.bfloat16),
+        in_specs=[vmem] * len(parts),
         out_specs=vmem,
         compiler_params=pltpu.CompilerParams(vmem_limit_bytes=LIMIT),
-        name="terms_sum",
-    )(mine, theirs)
+        name=name,
+    )(*parts)
 
 
 def dense_local(
@@ -478,37 +513,41 @@
     n_col = lax.axis_size("col")
     grad_scale = 1.0 / math.sqrt(pieces * n_row * n_col)
     scaled, lists, codes = scale_rows(
-        degree, features, tile_rows, tile_cols, tile_count, tile_codes[0, 0]
-    )
-    block = build_block(lists, codes, pieces * n_col, pieces * n_row)
-    chips = list(range(n_row - 2, 0, -2))
+        degree, features, tile_rows, tile_cols, tile_codes[0, 0]
+    )
+    chips = list(range(2, n_row, 2))
     lines = list(range(n_col - 1, 0, -1))
-    sources = [None] * n_row
-    sources[0] = scaled
-    for m in chips:
-        sources[m] = swap(scaled, "row", m)
-    sources[1] = swap(scaled, "row", 1)
-    block, *landed = lax.optimization_barrier((block, *(sources[m] for m in chips)))
-    for m, value in zip(chips, landed):
-        sources[m] = value
-        sources[m + 1] = swap(value, "row", 1)
+    own = [scaled] + [swap(scaled, "row", m) for m in chips]
+    other = [swap(scaled, "row", 1)]
+    slots = codes.shape[0]
+    middle = slots * 3 // 4 // GROUP * GROUP
+    size = (pieces * n_col, pieces * n_row)
+    block = build_block(lists, tile_count, codes, *size, 0, middle)
+    block, own = lax.optimization_barrier((block, own))
+    if chips:
+        other.append(swap(stack(own[1:]), "row", 1))
+    block = build_block(lists, tile_count, codes, *size, middle, slots, block)
     half = max(1, n_col // 2)
-    far = forward_parts(block, sources, lines[:half], "forward_far")
-    near = forward_parts(block, sources, lines[half:] + [0], "forward_near")
+    far = forward_parts(block, own, other, n_row, lines[:half], "forward_far")
+    near = forward_parts(block, own, other, n_row, lines[half:] + [0], "forward_near")
     parts = dict(zip(lines + [0], far + near))
     landed = [parts[0]] + [swap(parts[k], "col", k) for k in lines]
     grad_own, both, aggregate = gradient_step(degree, weight, bias, cotangent, landed)
     grads = [grad_own, swap(both, "col", 1)] + [swap(grad_own, "col", k) for k in range(2, n_col)]
     grads[1], aggregate = lax.optimization_barrier((grads[1], aggregate))
     hidden = hidden_step(weight, bias, cotangent, aggregate)
-    terms = [terms_sum(both, grads[1], feat)]
+    terms = [terms_sum([both, grads[1]], feat, "terms_col")]
     terms += [swap(terms[0], "col", k) for k in range(2, n_col, 2)]
-    grads[2:], terms = lax.optimization_barrier((grads[2:], terms))
-    for_other = backward_parts(block, grads, terms, n_row, 1)
+    begun = backward_parts(block, grads, [0, 1], range(n_row), None, [], "backward_near")
+    grads[2:], begun, terms = lax.optimization_barrier((grads[2:], begun, terms))
+    far = range(2, n_col)
+    for_other = backward_parts(
+        block, grads, far, range(1, n_row, 2), begun, terms, "backward_other"
+    )
     from_other = swap(for_other, "row", 1)
-    for_own = backward_parts(block, grads, [], n_row, 0)
+    for_own = backward_parts(block, grads, far, range(0, n_row, 2), begun, [], "backward_own")
     chunks = pair_sum(for_own, for_other, from_other, n_row // 2)
-    landed = [chunks[0]] + [swap(chunks[m // 2], "row", m) for m in chips]
+    landed = [chunks[0]] + [swap(chunks[m // 2], "row", m) for m in chips[::-1]]
     grad_features, grad_weight, grad_bias = finish(degree, landed, feat, grad_scale)
     return (hidden, grad_features, grad_weight, grad_bias)
 
@@ -533,7 +572,7 @@
 
     def local(features, *rest):
         block_bytes = 2 * features.shape[0] ** 2 * n_row * n_col
-        paired = power_of_two(n_row) and power_of_two(n_col) and n_row > 1
+        paired = power_of_two(n_row) and power_of_two(n_col) and n_row > 1 and n_col > 2
         if paired and block_bytes <= DENSE_BYTES:
             return dense_local(features, *rest)
         return sparse_local(features, *rest)

time: 47.7 us -> 45.8 us (0.960)
  waiting for transfers between devices: 18 us -> 15 us
  starting transfers between devices: 18.4 us -> 19.5 us
    ppermute x18 -> x16, waiting for transfers between devices: 18 us -> 15 us  [swap(): return lax.ppermute(value, axis, [(i, i ^ bits) for i in range(size)])]
    ppermute x18 -> x16, starting transfers between devices: 18.4 us -> 19.5 us  [swap(): return lax.ppermute(value, axis, [(i, i ^ bits) for i in range(size)])]
    pallas_call x6 -> x9, Pallas kernels: 6.53 us -> 6.54 us  [the longest x2 3.9 us: build_block(): pl.pallas_call(functools.partial(build_kernel, first, last), out_shape=pl...]
  transfers between devices with their start and end apart: 18 -> 16, of which waited for: 14 -> 11; matrix products, arithmetic and copies ran while one was open for 0% -> 0% of each run, Pallas kernels for 13% -> 14%
where the time goes in v4:
time: 45.8 us; the launch traced here: 45.7 us
  starting transfers between devices  19.5 us (43%)
  waiting for transfers between devices  15 us (33%)
  Pallas kernels  9.63 us (21%)
  between operations  1.46 us (3%)
    ppermute x16, starting transfers between devices, swap(): return lax.ppermute(value, axis, [(i, i ^ bits) for i in range(size)])  19.5 us
    ppermute x16, waiting for transfers between devices, swap(): return lax.ppermute(value, axis, [(i, i ^ bits) for i in range(size)])  15 us
    pallas_call x2, Pallas kernels, build_block(): pl.pallas_call(functools.partial(build_kernel, first, last), out_shape=pl...  3.9 us
    pallas_call x2, Pallas kernels, forward_parts(): pl.pallas_call(functools.partial(forward_kernel, len(own), n_row, far), o...  1.5 us
    pallas_call x3, Pallas kernels, backward_parts(): pl.pallas_call(functools.partial(backward_kernel, feat, kinds, chunks, le...  1.12 us
    pallas_call x1, Pallas kernels, scale_rows(): pl.pallas_call(scale_kernel, out_shape=[pltpu.VMEM(features.shape, jnp.bf...  1.03 us
  transfers between devices with their start and end apart: 16, of which 11 were waited for; matrix products, arithmetic and copies ran while one was open for 0% of the time, Pallas kernels for 14%

profile of v4, /device:TPU:0, one launch (start us, length us, event | category | flops | bytes accessed | tf_op | source)
XLA Modules:
  0.0 45.7 jit_solution(15374593611162181220)
XLA Ops:
  0.6 1.0 %scale_rows.1 = (bf16[256,128]{1,0:T(8,128)(2,1)S(1)}, s32[8,128]{1,0:T(8,128)S(1)}, s32[128,256]{1,0:T(8,128)S(1)}) custom-call(s32[1,256]{1,0:T(1,128)} %bitcast.4, bf16[256,128]{1,0:T(8,128)(2,1)} %features_hbm.1, s32[1,1,128]{2,1,0:T(1,128)} %rows_hbm.1, s32[1,1,128]{2,1,0:T(1,128)} %cols_hbm.1, s32[128,256]{1,0:T(8,128)} %bitcast.9), custom_call_target="tpu_custom_call" | custom-call | tf_op jit(solution)/shard_map/scale_rows/pallas_call | solution.py:468
  1.7 3.0 %collective-permute-start = (bf16[256,128]{1,0:T(8,128)(2,1)S(1)}, bf16[256,128]{1,0:T(8,128)(2,1)S(1)}, u32[]{:S(2)}, u32[]{:S(2)}) collective-permute-start(bf16[256,128]{1,0:T(8,128)(2,1)S(1)} %get-tuple-element.37.refs_0_), channel_id=1, source_target_pairs={{0,8},{4,12},{8,0},{12,4},{16,24},{20,28},{24,16},{28,20},{1,9},{5... | collective-permute-start | bytes 196616 | tf_op jit(solution)/shard_map/ppermute | solution.py:119
  4.7 1.5 %collective-permute-start.1 = (bf16[256,128]{1,0:T(8,128)(2,1)S(1)}, bf16[256,128]{1,0:T(8,128)(2,1)S(1)}, u32[]{:S(2)}, u32[]{:S(2)}) collective-permute-start(bf16[256,128]{1,0:T(8,128)(2,1)S(1)} %get-tuple-element.37.refs_0_), channel_id=1, source_target_pairs={{0,16},{4,20},{8,24},{12,28},{16,0},{20,4},{24,8},{28,12},{1,17},{... | collective-permute-start | bytes 196616 | tf_op jit(solution)/shard_map/ppermute | solution.py:119
  6.9 2.6 %build_block.1.refs_0_ = bf16[1024,2048]{1,0:T(8,128)(2,1)S(1)} custom-call(s32[8,128]{1,0:T(8,128)S(1)} %get-tuple-element.33.lists_vmem, s32[1,1,1]{2,1,0:T(1,128)S(6)} %copy.15.count_ref, s32[128,256]{1,0:T(8,128)S(1)} %get-tuple-element.34.codes_ref), custom_call_target="tpu_custom_call" | custom-call | flops 31457280 | bytes 8388608 | tf_op jit(solution)/shard_map/build_block/pallas_call | solution.py:187
  9.5 1.8 %collective-permute-done.2.refs_2_.refs_3_ = bf16[256,128]{1,0:T(8,128)(2,1)S(1)} collective-permute-done((bf16[256,128]{1,0:T(8,128)(2,1)S(1)}, bf16[256,128]{1,0:T(8,128)(2,1)S(1)}, u32[]{:S(2)}, u32[]{:S(2)}) %collective-permute-start.2) | collective-permute-done | bytes 65568 | tf_op jit(solution)/shard_map/ppermute | solution.py:119
  12.0 1.3 %build_rest.1.block_ref = bf16[1024,2048]{1,0:T(8,128)(2,1)S(1)} custom-call(s32[8,128]{1,0:T(8,128)S(1)} %get-tuple-element.33.lists_vmem, s32[1,1,1]{2,1,0:T(1,128)S(6)} %copy.15.count_ref, s32[128,256]{1,0:T(8,128)S(1)} %get-tuple-element.34.codes_ref, bf16[1024,2048]{1,0:T(8,128)(2,1)S(1)} %build_block.1.refs_0_), custom_call_target="tpu_custom_call", output_to_operand_aliasing={{}: (3, {})} | custom-call | flops 10485760 | bytes 8388608 | tf_op jit(solution)/shard_map/build_rest/pallas_call | solution.py:187
  13.3 0.7 %forward_far.1 = (bf16[256,128]{1,0:T(8,128)(2,1)S(1)}, bf16[256,128]{1,0:T(8,128)(2,1)S(1)}) custom-call(bf16[1024,2048]{1,0:T(8,128)(2,1)S(1)} %build_rest.1.block_ref, bf16[256,128]{1,0:T(8,128)(2,1)S(1)} %get-tuple-element.37.refs_0_, bf16[256,128]{1,0:T(8,128)(2,1)S(1)} %collective-permute-done.refs_0_.refs_1_, ...), custom_call_target="tpu_custom_call" | custom-call | tf_op jit(solution)/shard_map/forward_far/pallas_call | solution.py:254
  14.1 3.7 %collective-permute-start.5 = (bf16[256,128]{1,0:T(8,128)(2,1)S(1)}, bf16[256,128]{1,0:T(8,128)(2,1)S(1)}, u32[]{:S(2)}, u32[]{:S(2)}) collective-permute-start(bf16[256,128]{1,0:T(8,128)(2,1)S(1)} %get-tuple-element.42), channel_id=1, source_target_pairs={{0,3},{1,2},{2,1},{3,0},{4,7},{5,6},{6,5},{7,4},{8,11},{9,10},{10,... | collective-permute-start | bytes 196616 | tf_op jit(solution)/shard_map/ppermute | solution.py:119
  18.5 0.8 %collective-permute-start.7 = (bf16[256,128]{1,0:T(8,128)(2,1)S(1)}, bf16[256,128]{1,0:T(8,128)(2,1)S(1)}, u32[]{:S(2)}, u32[]{:S(2)}) collective-permute-start(bf16[256,128]{1,0:T(8,128)(2,1)S(1)} %get-tuple-element.44), channel_id=1, source_target_pairs={{0,1},{1,0},{2,3},{3,2},{4,5},{5,4},{6,7},{7,6},{8,9},{9,8},{10,11... | collective-permute-start | bytes 196616 | tf_op jit(solution)/shard_map/ppermute | solution.py:119
  19.3 1.2 %collective-permute-done.5.refs_1_ = bf16[256,128]{1,0:T(8,128)(2,1)S(1)} collective-permute-done((bf16[256,128]{1,0:T(8,128)(2,1)S(1)}, bf16[256,128]{1,0:T(8,128)(2,1)S(1)}, u32[]{:S(2)}, u32[]{:S(2)}) %collective-permute-start.5) | collective-permute-done | bytes 65568 | tf_op jit(solution)/shard_map/ppermute | solution.py:119
  20.5 3.2 %collective-permute-done.6.refs_2_ = bf16[256,128]{1,0:T(8,128)(2,1)S(1)} collective-permute-done((bf16[256,128]{1,0:T(8,128)(2,1)S(1)}, bf16[256,128]{1,0:T(8,128)(2,1)S(1)}, u32[]{:S(2)}, u32[]{:S(2)}) %collective-permute-start.6) | collective-permute-done | bytes 65568 | tf_op jit(solution)/shard_map/ppermute | solution.py:119
  25.2 2.2 %collective-permute-start.9 = (bf16[128,256]{1,0:T(8,128)(2,1)S(1)}, bf16[128,256]{1,0:T(8,128)(2,1)S(1)}, u32[]{:S(2)}, u32[]{:S(2)}) collective-permute-start(bf16[128,256]{1,0:T(8,128)(2,1)S(1)} %get-tuple-element.48.refs_0_), channel_id=1, source_target_pairs={{0,2},{1,3},{2,0},{3,1},{4,6},{5,7},{6,4},{7,5},{8,10},{9,11},{10,... | collective-permute-start | bytes 196616 | tf_op jit(solution)/shard_map/ppermute | solution.py:119
  27.4 1.6 %collective-permute-start.10 = (bf16[128,256]{1,0:T(8,128)(2,1)S(1)}, bf16[128,256]{1,0:T(8,128)(2,1)S(1)}, u32[]{:S(2)}, u32[]{:S(2)}) collective-permute-start(bf16[128,256]{1,0:T(8,128)(2,1)S(1)} %get-tuple-element.48.refs_0_), channel_id=1, source_target_pairs={{0,3},{1,2},{2,1},{3,0},{4,7},{5,6},{6,5},{7,4},{8,11},{9,10},{10,... | collective-permute-start | bytes 196616 | tf_op jit(solution)/shard_map/ppermute | solution.py:119
  29.4 1.8 %collective-permute-start.11 = (bf16[80,256]{1,0:T(8,128)(2,1)S(1)}, bf16[80,256]{1,0:T(8,128)(2,1)S(1)}, u32[]{:S(2)}, u32[]{:S(2)}) collective-permute-start(bf16[80,256]{1,0:T(8,128)(2,1)S(1)} %terms_col.1.refs_3_), channel_id=1, source_target_pairs={{0,2},{1,3},{2,0},{3,1},{4,6},{5,7},{6,4},{7,5},{8,10},{9,11},{10,... | collective-permute-start | bytes 122888 | tf_op jit(solution)/shard_map/ppermute | solution.py:119
  32.4 1.1 %collective-permute-done.10.refs_1_ = bf16[128,256]{1,0:T(8,128)(2,1)S(1)} collective-permute-done((bf16[128,256]{1,0:T(8,128)(2,1)S(1)}, bf16[128,256]{1,0:T(8,128)(2,1)S(1)}, u32[]{:S(2)}, u32[]{:S(2)}) %collective-permute-start.10) | collective-permute-done | bytes 65568 | tf_op jit(solution)/shard_map/ppermute | solution.py:119
  33.5 1.2 %collective-permute-done.11.refs_4_ = bf16[80,256]{1,0:T(8,128)(2,1)S(1)} collective-permute-done((bf16[80,256]{1,0:T(8,128)(2,1)S(1)}, bf16[80,256]{1,0:T(8,128)(2,1)S(1)}, u32[]{:S(2)}, u32[]{:S(2)}) %collective-permute-start.11) | collective-permute-done | bytes 40992 | tf_op jit(solution)/shard_map/ppermute | solution.py:119
  35.4 1.2 %collective-permute-done.12.theirs_ref = bf16[592,256]{1,0:T(8,128)(2,1)S(1)} collective-permute-done((bf16[592,256]{1,0:T(8,128)(2,1)S(1)}, bf16[592,256]{1,0:T(8,128)(2,1)S(1)}, u32[]{:S(2)}, u32[]{:S(2)}) %collective-permute-start.12) | collective-permute-done | bytes 303136 | tf_op jit(solution)/shard_map/ppermute | solution.py:119
  36.7 1.2 %collective-permute-start.13 = (bf16[208,256]{1,0:T(8,128)(2,1)S(1)}, bf16[208,256]{1,0:T(8,128)(2,1)S(1)}, u32[]{:S(2)}, u32[]{:S(2)}) collective-permute-start(bf16[208,256]{1,0:T(8,128)(2,1)S(1)} %get-tuple-element.56), channel_id=1, source_target_pairs={{0,24},{4,28},{8,16},{12,20},{16,8},{20,12},{24,0},{28,4},{1,25},{... | collective-permute-start | bytes 319496 | tf_op jit(solution)/shard_map/ppermute | solution.py:119
  37.9 0.9 %collective-permute-start.14 = (bf16[208,256]{1,0:T(8,128)(2,1)S(1)}, bf16[208,256]{1,0:T(8,128)(2,1)S(1)}, u32[]{:S(2)}, u32[]{:S(2)}) collective-permute-start(bf16[208,256]{1,0:T(8,128)(2,1)S(1)} %get-tuple-element.57), channel_id=1, source_target_pairs={{0,16},{4,20},{8,24},{12,28},{16,0},{20,4},{24,8},{28,12},{1,17},{... | collective-permute-start | bytes 319496 | tf_op jit(solution)/shard_map/ppermute | solution.py:119
  38.8 1.5 %collective-permute-start.15 = (bf16[208,256]{1,0:T(8,128)(2,1)S(1)}, bf16[208,256]{1,0:T(8,128)(2,1)S(1)}, u32[]{:S(2)}, u32[]{:S(2)}) collective-permute-start(bf16[208,256]{1,0:T(8,128)(2,1)S(1)} %get-tuple-element.58), channel_id=1, source_target_pairs={{0,8},{4,12},{8,0},{12,4},{16,24},{20,28},{24,16},{28,20},{1,9},{5... | collective-permute-start | bytes 319496 | tf_op jit(solution)/shard_map/ppermute | solution.py:119
  40.3 0.8 %hidden_step.1 = bf16[256,128]{1,0:T(8,128)(2,1)} custom-call(bf16[128,128]{1,0:T(8,128)(2,1)S(1)} %copy-done.1, f32[1,128]{1,0:T(1,128)S(1)} %bitcast.8, bf16[256,128]{1,0:T(8,128)(2,1)S(1)} %copy-done, bf16[256,128]{1,0:T(8,128)(2,1)S(1)} %get-tuple-element.47.aggregate_ref), custom_call_target="tpu_custom_call" | custom-call | tf_op jit(solution)/shard_map/hidden_step/pallas_call | solution.py:329
  41.1 2.5 %collective-permute-done.13.refs_1_ = bf16[208,256]{1,0:T(8,128)(2,1)S(1)} collective-permute-done((bf16[208,256]{1,0:T(8,128)(2,1)S(1)}, bf16[208,256]{1,0:T(8,128)(2,1)S(1)}, u32[]{:S(2)}, u32[]{:S(2)}) %collective-permute-start.13) | collective-permute-done | bytes 106528 | tf_op jit(solution)/shard_map/ppermute | solution.py:119
  43.5 1.4 %collective-permute-done.14.refs_2_ = bf16[208,256]{1,0:T(8,128)(2,1)S(1)} collective-permute-done((bf16[208,256]{1,0:T(8,128)(2,1)S(1)}, bf16[208,256]{1,0:T(8,128)(2,1)S(1)}, u32[]{:S(2)}, u32[]{:S(2)}) %collective-permute-start.14) | collective-permute-done | bytes 106528 | tf_op jit(solution)/shard_map/ppermute | solution.py:119
  44.9 0.7 %finish.1 = (bf16[256,128]{1,0:T(8,128)(2,1)}, f32[128,128]{1,0:T(8,128)}, f32[1,128]{1,0:T(1,128)}) custom-call(s32[1,256]{1,0:T(1,128)S(1)} %bitcast.6, bf16[208,256]{1,0:T(8,128)(2,1)S(1)} %get-tuple-element.55.refs_0_, bf16[208,256]{1,0:T(8,128)(2,1)S(1)} %collective-permute-done.13.refs_1_, bf16[208,256]{1,0:T(8,128)(2,1)S(1)} %collective-permute-done.14.refs_2_, ...), custom_call_target="tpu_custom_call" | custom-call | tf_op jit(solution)/shard_map/finish/pallas_call | solution.py:427
  (30 shorter events, 5.3 us)
Async XLA Ops:
  1.7 7.8 %collective-permute-start = (bf16[256,128]{1,0:T(8,128)(2,1)S(1)}, bf16[256,128]{1,0:T(8,128)(2,1)S(1)}, u32[]{:S(2)}, u32[]{:S(2)}) collective-permute-start(bf16[256,128]{1,0:T(8,128)(2,1)S(1)} %get-tuple-element.37.refs_0_), channel_id=1, source_target_pairs={{0,8},{4,12},{8,0},{12,4},{16,24},{20,28},{24,16},{28,20},{1,9},{5... | collective-permute-start | bytes 196616 | tf_op jit(solution)/shard_map/ppermute | solution.py:119
  4.7 4.8 %collective-permute-start.1 = (bf16[256,128]{1,0:T(8,128)(2,1)S(1)}, bf16[256,128]{1,0:T(8,128)(2,1)S(1)}, u32[]{:S(2)}, u32[]{:S(2)}) collective-permute-start(bf16[256,128]{1,0:T(8,128)(2,1)S(1)} %get-tuple-element.37.refs_0_), channel_id=1, source_target_pairs={{0,16},{4,20},{8,24},{12,28},{16,0},{20,4},{24,8},{28,12},{1,17},{... | collective-permute-start | bytes 196616 | tf_op jit(solution)/shard_map/ppermute | solution.py:119
  6.2 5.2 %collective-permute-start.2 = (bf16[256,128]{1,0:T(8,128)(2,1)S(1)}, bf16[256,128]{1,0:T(8,128)(2,1)S(1)}, u32[]{:S(2)}, u32[]{:S(2)}) collective-permute-start(bf16[256,128]{1,0:T(8,128)(2,1)S(1)} %get-tuple-element.37.refs_0_), channel_id=1, source_target_pairs={{0,24},{4,28},{8,16},{12,20},{16,8},{20,12},{24,0},{28,4},{1,25},{... | collective-permute-start | bytes 196616 | tf_op jit(solution)/shard_map/ppermute | solution.py:119
  11.4 1.9 %collective-permute-start.4 = (bf16[768,128]{1,0:T(8,128)(2,1)S(1)}, bf16[768,128]{1,0:T(8,128)(2,1)S(1)}, u32[]{:S(2)}, u32[]{:S(2)}) collective-permute-start(bf16[768,128]{1,0:T(8,128)(2,1)S(1)} %stack.1), channel_id=1, source_target_pairs={{0,4},{4,0},{8,12},{12,8},{16,20},{20,16},{24,28},{28,24},{1,5},{5... | collective-permute-start | bytes 589832 | tf_op jit(solution)/shard_map/ppermute | solution.py:119
  11.5 1.8 %collective-permute-start.3 = (bf16[256,128]{1,0:T(8,128)(2,1)S(1)}, bf16[256,128]{1,0:T(8,128)(2,1)S(1)}, u32[]{:S(2)}, u32[]{:S(2)}) collective-permute-start(bf16[256,128]{1,0:T(8,128)(2,1)S(1)} %get-tuple-element.37.refs_0_), channel_id=1, source_target_pairs={{0,4},{4,0},{8,12},{12,8},{16,20},{20,16},{24,28},{28,24},{1,5},{5... | collective-permute-start | bytes 196616 | tf_op jit(solution)/shard_map/ppermute | solution.py:119
  13.2 10.8 %copy-start = (bf16[256,128]{1,0:T(8,128)(2,1)S(1)}, bf16[256,128]{1,0:T(8,128)(2,1)}, u32[]{:S(2)}) copy-start(bf16[256,128]{1,0:T(8,128)(2,1)} %cot_ref.3) | copy-start | bytes 196612
  13.3 10.8 %copy-start.1 = (bf16[128,128]{1,0:T(8,128)(2,1)S(1)}, bf16[128,128]{1,0:T(8,128)(2,1)}, u32[]{:S(2)}) copy-start(bf16[128,128]{1,0:T(8,128)(2,1)} %weight_ref.3) | copy-start | bytes 98308
  13.3 10.8 %copy-start.2 = (s32[256]{0:T(256)S(1)}, s32[256]{0:T(256)}, u32[]{:S(2)}) copy-start(s32[256]{0:T(256)} %param.10) | copy-start | bytes 3076
  13.3 10.8 %copy-start.3 = (f32[128]{0:T(128)S(1)}, f32[128]{0:T(128)}, u32[]{:S(2)}) copy-start(f32[128]{0:T(128)} %param.12) | copy-start | bytes 1540
  14.1 6.4 %collective-permute-start.5 = (bf16[256,128]{1,0:T(8,128)(2,1)S(1)}, bf16[256,128]{1,0:T(8,128)(2,1)S(1)}, u32[]{:S(2)}, u32[]{:S(2)}) collective-permute-start(bf16[256,128]{1,0:T(8,128)(2,1)S(1)} %get-tuple-element.42), channel_id=1, source_target_pairs={{0,3},{1,2},{2,1},{3,0},{4,7},{5,6},{6,5},{7,4},{8,11},{9,10},{10,... | collective-permute-start | bytes 196616 | tf_op jit(solution)/shard_map/ppermute | solution.py:119
  17.7 6.0 %collective-permute-start.6 = (bf16[256,128]{1,0:T(8,128)(2,1)S(1)}, bf16[256,128]{1,0:T(8,128)(2,1)S(1)}, u32[]{:S(2)}, u32[]{:S(2)}) collective-permute-start(bf16[256,128]{1,0:T(8,128)(2,1)S(1)} %get-tuple-element.43), channel_id=1, source_target_pairs={{0,2},{1,3},{2,0},{3,1},{4,6},{5,7},{6,4},{7,5},{8,10},{9,11},{10,... | collective-permute-start | bytes 196616 | tf_op jit(solution)/shard_map/ppermute | solution.py:119
  18.5 5.5 %collective-permute-start.7 = (bf16[256,128]{1,0:T(8,128)(2,1)S(1)}, bf16[256,128]{1,0:T(8,128)(2,1)S(1)}, u32[]{:S(2)}, u32[]{:S(2)}) collective-permute-start(bf16[256,128]{1,0:T(8,128)(2,1)S(1)} %get-tuple-element.44), channel_id=1, source_target_pairs={{0,1},{1,0},{2,3},{3,2},{4,5},{5,4},{6,7},{7,6},{8,9},{9,8},{10,11... | collective-permute-start | bytes 196616 | tf_op jit(solution)/shard_map/ppermute | solution.py:119
  24.5 4.9 %collective-permute-start.8 = (bf16[208,256]{1,0:T(8,128)(2,1)S(1)}, bf16[208,256]{1,0:T(8,128)(2,1)S(1)}, u32[]{:S(2)}, u32[]{:S(2)}) collective-permute-start(bf16[208,256]{1,0:T(8,128)(2,1)S(1)} %get-tuple-element.45.refs_0_), channel_id=1, source_target_pairs={{0,1},{1,0},{2,3},{3,2},{4,5},{5,4},{6,7},{7,6},{8,9},{9,8},{10,11... | collective-permute-start | bytes 319496 | tf_op jit(solution)/shard_map/ppermute | solution.py:119
  25.2 7.2 %collective-permute-start.9 = (bf16[128,256]{1,0:T(8,128)(2,1)S(1)}, bf16[128,256]{1,0:T(8,128)(2,1)S(1)}, u32[]{:S(2)}, u32[]{:S(2)}) collective-permute-start(bf16[128,256]{1,0:T(8,128)(2,1)S(1)} %get-tuple-element.48.refs_0_), channel_id=1, source_target_pairs={{0,2},{1,3},{2,0},{3,1},{4,6},{5,7},{6,4},{7,5},{8,10},{9,11},{10,... | collective-permute-start | bytes 196616 | tf_op jit(solution)/shard_map/ppermute | solution.py:119
  27.4 6.1 %collective-permute-start.10 = (bf16[128,256]{1,0:T(8,128)(2,1)S(1)}, bf16[128,256]{1,0:T(8,128)(2,1)S(1)}, u32[]{:S(2)}, u32[]{:S(2)}) collective-permute-start(bf16[128,256]{1,0:T(8,128)(2,1)S(1)} %get-tuple-element.48.refs_0_), channel_id=1, source_target_pairs={{0,3},{1,2},{2,1},{3,0},{4,7},{5,6},{6,5},{7,4},{8,11},{9,10},{10,... | collective-permute-start | bytes 196616 | tf_op jit(solution)/shard_map/ppermute | solution.py:119
  29.4 5.3 %collective-permute-start.11 = (bf16[80,256]{1,0:T(8,128)(2,1)S(1)}, bf16[80,256]{1,0:T(8,128)(2,1)S(1)}, u32[]{:S(2)}, u32[]{:S(2)}) collective-permute-start(bf16[80,256]{1,0:T(8,128)(2,1)S(1)} %terms_col.1.refs_3_), channel_id=1, source_target_pairs={{0,2},{1,3},{2,0},{3,1},{4,6},{5,7},{6,4},{7,5},{8,10},{9,11},{10,... | collective-permute-start | bytes 122888 | tf_op jit(solution)/shard_map/ppermute | solution.py:119
  35.0 1.7 %collective-permute-start.12 = (bf16[592,256]{1,0:T(8,128)(2,1)S(1)}, bf16[592,256]{1,0:T(8,128)(2,1)S(1)}, u32[]{:S(2)}, u32[]{:S(2)}) collective-permute-start(bf16[592,256]{1,0:T(8,128)(2,1)S(1)} %backward_other.1.sent_ref), channel_id=1, source_target_pairs={{0,4},{4,0},{8,12},{12,8},{16,20},{20,16},{24,28},{28,24},{1,5},{5... | collective-permute-start | bytes 909320 | tf_op jit(solution)/shard_map/ppermute | solution.py:119
  36.7 6.8 %collective-permute-start.13 = (bf16[208,256]{1,0:T(8,128)(2,1)S(1)}, bf16[208,256]{1,0:T(8,128)(2,1)S(1)}, u32[]{:S(2)}, u32[]{:S(2)}) collective-permute-start(bf16[208,256]{1,0:T(8,128)(2,1)S(1)} %get-tuple-element.56), channel_id=1, source_target_pairs={{0,24},{4,28},{8,16},{12,20},{16,8},{20,12},{24,0},{28,4},{1,25},{... | collective-permute-start | bytes 319496 | tf_op jit(solution)/shard_map/ppermute | solution.py:119
  37.9 7.0 %collective-permute-start.14 = (bf16[208,256]{1,0:T(8,128)(2,1)S(1)}, bf16[208,256]{1,0:T(8,128)(2,1)S(1)}, u32[]{:S(2)}, u32[]{:S(2)}) collective-permute-start(bf16[208,256]{1,0:T(8,128)(2,1)S(1)} %get-tuple-element.57), channel_id=1, source_target_pairs={{0,16},{4,20},{8,24},{12,28},{16,0},{20,4},{24,8},{28,12},{1,17},{... | collective-permute-start | bytes 319496 | tf_op jit(solution)/shard_map/ppermute | solution.py:119
  38.8 6.1 %collective-permute-start.15 = (bf16[208,256]{1,0:T(8,128)(2,1)S(1)}, bf16[208,256]{1,0:T(8,128)(2,1)S(1)}, u32[]{:S(2)}, u32[]{:S(2)}) collective-permute-start(bf16[208,256]{1,0:T(8,128)(2,1)S(1)} %get-tuple-element.58), channel_id=1, source_target_pairs={{0,8},{4,12},{8,0},{12,4},{16,24},{20,28},{24,16},{28,20},{1,9},{5... | collective-permute-start | bytes 319496 | tf_op jit(solution)/shard_map/ppermute | solution.py:119

commit v5 on v4

--- a/solution.py
+++ b/solution.py
@@ -224,42 +224,37 @@
     )(*parts)
 
 
-def forward_kernel(n_own, n_row, far, block_ref, *refs):
-    own, other = refs[:n_own], refs[n_own : -1 - len(far)]
-    outs = refs[-1 - len(far) : -1]
-    source = refs[-1]
-    pieces = own[0].shape[0]
+def forward_kernel(bits, high, block_ref, *refs):
+    *parts, even_ref, odd_ref, source = refs
+    pieces = parts[0].shape[0]
     me_row = lax.axis_index("row")
     me_col = lax.axis_index("col")
-    for m, part in enumerate(own):
-        at = pl.multiple_of((me_row ^ (2 * m)) * pieces, pieces)
-        source[pl.ds(at, pieces), :] = part[...]
-    bits = 1
-    for part in other:
-        for k in range(part.shape[0] // pieces):
-            at = pl.multiple_of((me_row ^ bits) * pieces, pieces)
-            source[pl.ds(at, pieces), :] = part[k * pieces : (k + 1) * pieces, :]
-            bits += 2
-    whole = source[...]
-    for out, k in zip(outs, far):
-        at = pl.multiple_of((me_col ^ k) * pieces, pieces)
-        out[...] = jnp.dot(
-            block_ref[pl.ds(at, pieces), :], whole, preferred_element_type=jnp.float32
-        ).astype(jnp.bfloat16)
-
-
-def forward_parts(block, own, other, n_row, far, name):
-    pieces, feat = own[0].shape
-    vmem = pl.BlockSpec(memory_space=pltpu.VMEM)
-    return pl.pallas_call(
-        functools.partial(forward_kernel, len(own), n_row, far),
-        out_shape=[jax.ShapeDtypeStruct((pieces, feat), jnp.bfloat16)] * len(far),
-        in_specs=[vmem] * (1 + len(own) + len(other)),
-        out_specs=[vmem] * len(far),
-        scratch_shapes=[pltpu.VMEM((pieces * n_row, feat), jnp.bfloat16)],
+    place = iter(bits)
+    for part in parts:
+        for m in range(part.shape[0] // pieces):
+            at = pl.multiple_of((me_row ^ next(place)) * pieces, pieces)
+            source[pl.ds(at, pieces), :] = part[m * pieces : (m + 1) * pieces, :]
+    down = pl.multiple_of((me_col ^ high) // 2 * (2 * pieces), 2 * pieces)
+    both = jnp.dot(
+        block_ref[pl.ds(down, 2 * pieces), :], source[...], preferred_element_type=jnp.float32
+    ).astype(jnp.bfloat16)
+    first = me_col % 2 == 0
+    even_ref[...] = jnp.where(first, both[:pieces], both[pieces:])
+    odd_ref[...] = jnp.where(first, both[pieces:], both[:pieces])
+
+
+def forward_parts(block, parts, bits, high, name):
+    pieces, feat = parts[0].shape
+    vmem = pl.BlockSpec(memory_space=pltpu.VMEM)
+    return pl.pallas_call(
+        functools.partial(forward_kernel, bits, high),
+        out_shape=[jax.ShapeDtypeStruct((pieces, feat), jnp.bfloat16)] * 2,
+        in_specs=[vmem] * (1 + len(parts)),
+        out_specs=[vmem] * 2,
+        scratch_shapes=[pltpu.VMEM((pieces * len(bits), feat), jnp.bfloat16)],
         compiler_params=pltpu.CompilerParams(vmem_limit_bytes=LIMIT),
         name=name,
-    )(block, *own, *other)
+    )(block, *parts)
 
 
 def slope_of(aggregate, weight, bias, cotangent):
@@ -381,31 +376,27 @@
     )(block, *(sources[k] for k in kinds), *begun, *terms)
 
 
-def pair_kernel(n, mine_ref, sent_ref, theirs_ref, *outs):
-    feat = mine_ref.shape[0] // n
-    terms = (
-        sent_ref[n * feat :, :].astype(jnp.float32) + theirs_ref[n * feat :, :].astype(jnp.float32)
-    ).astype(jnp.bfloat16)
-    for m in range(n):
-        span = slice(m * feat, (m + 1) * feat)
-        outs[m][:feat, :] = (
-            mine_ref[span, :].astype(jnp.float32) + theirs_ref[span, :].astype(jnp.float32)
-        ).astype(jnp.bfloat16)
-        outs[m][feat:, :] = terms
-
-
-def pair_sum(mine, sent, theirs, n):
-    rows, width = mine.shape
-    vmem = pl.BlockSpec(memory_space=pltpu.VMEM)
-    chunk = rows // n + sent.shape[0] - rows
-    return pl.pallas_call(
-        functools.partial(pair_kernel, n),
-        out_shape=[jax.ShapeDtypeStruct((chunk, width), jnp.bfloat16)] * n,
-        in_specs=[vmem] * 3,
-        out_specs=[vmem] * n,
-        compiler_params=pltpu.CompilerParams(vmem_limit_bytes=LIMIT),
-        name="pair_sum",
-    )(mine, sent, theirs)
+def pair_kernel(first, mine_ref, theirs_ref, sent_ref, got_ref, *outs):
+    feat = mine_ref.shape[0] // 4
+    terms = sum_of((sent_ref.at[2 * feat :], got_ref.at[2 * feat :])).astype(jnp.bfloat16)
+    for m, out in enumerate(outs):
+        mine = mine_ref[(first + m) * feat : (first + m + 1) * feat, :].astype(jnp.float32)
+        theirs = theirs_ref[m * feat : (m + 1) * feat, :].astype(jnp.float32)
+        out[:feat, :] = (mine + theirs).astype(jnp.bfloat16)
+        out[feat:, :] = terms
+
+
+def pair_sum(first, mine, theirs, sent, got):
+    vmem = pl.BlockSpec(memory_space=pltpu.VMEM)
+    rows = sent.shape[0] - mine.shape[0] // 4
+    return pl.pallas_call(
+        functools.partial(pair_kernel, first),
+        out_shape=[jax.ShapeDtypeStruct((rows, mine.shape[1]), jnp.bfloat16)] * 2,
+        in_specs=[vmem] * 4,
+        out_specs=[vmem] * 2,
+        compiler_params=pltpu.CompilerParams(vmem_limit_bytes=LIMIT),
+        name="pair_near" if first else "pair_far",
+    )(mine, theirs, sent, got)
 
 
 def finish_kernel(scale, degree_ref, *refs):
@@ -515,22 +506,21 @@
     scaled, lists, codes = scale_rows(
         degree, features, tile_rows, tile_cols, tile_codes[0, 0]
     )
-    chips = list(range(2, n_row, 2))
+    chips = [6, 4, 2]
     lines = list(range(n_col - 1, 0, -1))
-    own = [scaled] + [swap(scaled, "row", m) for m in chips]
-    other = [swap(scaled, "row", 1)]
+    landed = [swap(scaled, "row", m) for m in chips]
+    sibling = swap(scaled, "row", 1)
     slots = codes.shape[0]
     middle = slots * 3 // 4 // GROUP * GROUP
     size = (pieces * n_col, pieces * n_row)
     block = build_block(lists, tile_count, codes, *size, 0, middle)
-    block, own = lax.optimization_barrier((block, own))
-    if chips:
-        other.append(swap(stack(own[1:]), "row", 1))
+    block, landed = lax.optimization_barrier((block, landed))
+    parts = [scaled, sibling, *landed, swap(stack(landed), "row", 1)]
+    bits = [0, 1, *chips, *(m + 1 for m in chips)]
     block = build_block(lists, tile_count, codes, *size, middle, slots, block)
-    half = max(1, n_col // 2)
-    far = forward_parts(block, own, other, n_row, lines[:half], "forward_far")
-    near = forward_parts(block, own, other, n_row, lines[half:] + [0], "forward_near")
-    parts = dict(zip(lines + [0], far + near))
+    far = forward_parts(block, parts, bits, 2, "forward_far")
+    near = forward_parts(block, parts, bits, 0, "forward_near")
+    parts = [*near, *far]
     landed = [parts[0]] + [swap(parts[k], "col", k) for k in lines]
     grad_own, both, aggregate = gradient_step(degree, weight, bias, cotangent, landed)
     grads = [grad_own, swap(both, "col", 1)] + [swap(grad_own, "col", k) for k in range(2, n_col)]
@@ -541,19 +531,16 @@
     begun = backward_parts(block, grads, [0, 1], range(n_row), None, [], "backward_near")
     grads[2:], begun, terms = lax.optimization_barrier((grads[2:], begun, terms))
     far = range(2, n_col)
-    for_other = backward_parts(
-        block, grads, far, range(1, n_row, 2), begun, terms, "backward_other"
-    )
-    from_other = swap(for_other, "row", 1)
-    for_own = backward_parts(block, grads, far, range(0, n_row, 2), begun, [], "backward_own")
-    chunks = pair_sum(for_own, for_other, from_other, n_row // 2)
-    landed = [chunks[0]] + [swap(chunks[m // 2], "row", m) for m in chips[::-1]]
+    sent = backward_parts(block, grads, far, [7, 5], begun, terms, "backward_other")
+    got = swap(sent, "row", 1)
+    rest = swap(backward_parts(block, grads, far, [3, 1], begun, [], "backward_rest"), "row", 1)
+    mine = backward_parts(block, grads, far, [6, 4, 2, 0], begun, [], "backward_own")
+    chunks = pair_sum(0, mine, got, sent, got)
+    landed = [swap(chunk, "row", m) for chunk, m in zip(chunks, chips)]
+    chunks = pair_sum(2, mine, rest, sent, got)
+    landed = [chunks[1], *landed, swap(chunks[0], "row", chips[2])]
     grad_features, grad_weight, grad_bias = finish(degree, landed, feat, grad_scale)
     return (hidden, grad_features, grad_weight, grad_bias)
-
-
-def power_of_two(n):
-    return n & (n - 1) == 0
 
 
 def solution(mesh):
@@ -572,7 +559,7 @@
 
     def local(features, *rest):
         block_bytes = 2 * features.shape[0] ** 2 * n_row * n_col
-        paired = power_of_two(n_row) and power_of_two(n_col) and n_row > 1 and n_col > 2
+        paired = n_row == 8 and n_col == 4
         if paired and block_bytes <= DENSE_BYTES:
             return dense_local(features, *rest)
         return sparse_local(features, *rest)

time: 45.8 us -> 44.8 us (0.978)
  waiting for transfers between devices: 15 us -> 13.1 us
  starting transfers between devices: 19.5 us -> 20.2 us
    ppermute x16 -> x17, waiting for transfers between devices: 15 us -> 13.1 us  [swap(): return lax.ppermute(value, axis, [(i, i ^ bits) for i in range(size)])]
    ppermute x16 -> x17, starting transfers between devices: 19.5 us -> 20.2 us  [swap(): return lax.ppermute(value, axis, [(i, i ^ bits) for i in range(size)])]
    pallas_call x3 -> x4, Pallas kernels: 1.12 us -> 1.28 us  [backward_parts(): pl.pallas_call(functools.partial(backward_kernel, feat, kinds, chunks, le...]
    pallas_call x3 -> x4, Pallas kernels: 1.57 us -> 1.6 us  [the longest x2 1.52 us: forward_parts(): pl.pallas_call(functools.partial(forward_kernel, bits, high), out_shape=[...]
  transfers between devices with their start and end apart: 16 -> 17, of which waited for: 11 -> 13; matrix products, arithmetic and copies ran while one was open for 0% -> 0% of each run, Pallas kernels for 14% -> 15%
where the time goes in v5:
time: 44.8 us; the launch traced here: 44.6 us
  starting transfers between devices  20.2 us (45%)
  waiting for transfers between devices  13.1 us (29%)
  Pallas kernels  9.84 us (22%)
  between operations  1.47 us (3%)
    ppermute x17, starting transfers between devices, swap(): return lax.ppermute(value, axis, [(i, i ^ bits) for i in range(size)])  20.2 us
    ppermute x17, waiting for transfers between devices, swap(): return lax.ppermute(value, axis, [(i, i ^ bits) for i in range(size)])  13.1 us
    pallas_call x2, Pallas kernels, build_block(): pl.pallas_call(functools.partial(build_kernel, first, last), out_shape=pl...  3.91 us
    pallas_call x2, Pallas kernels, forward_parts(): pl.pallas_call(functools.partial(forward_kernel, bits, high), out_shape=[...  1.52 us
    pallas_call x4, Pallas kernels, backward_parts(): pl.pallas_call(functools.partial(backward_kernel, feat, kinds, chunks, le...  1.28 us
    pallas_call x1, Pallas kernels, scale_rows(): pl.pallas_call(scale_kernel, out_shape=[pltpu.VMEM(features.shape, jnp.bf...  1.03 us
  transfers between devices with their start and end apart: 17, of which 13 were waited for; matrix products, arithmetic and copies ran while one was open for 0% of the time, Pallas kernels for 15%

profile of v5, /device:TPU:0, one launch (start us, length us, event | category | flops | bytes accessed | tf_op | source)
XLA Modules:
  0.0 44.6 jit_solution(18337062356683891685)
XLA Ops:
  0.6 1.0 %scale_rows.1 = (bf16[256,128]{1,0:T(8,128)(2,1)S(1)}, s32[8,128]{1,0:T(8,128)S(1)}, s32[128,256]{1,0:T(8,128)S(1)}) custom-call(s32[1,256]{1,0:T(1,128)} %bitcast.4, bf16[256,128]{1,0:T(8,128)(2,1)} %features_hbm.1, s32[1,1,128]{2,1,0:T(1,128)} %rows_hbm.1, s32[1,1,128]{2,1,0:T(1,128)} %cols_hbm.1, s32[128,256]{1,0:T(8,128)} %bitcast.9), custom_call_target="tpu_custom_call" | custom-call | tf_op jit(solution)/shard_map/scale_rows/pallas_call | solution.py:459
  1.7 4.0 %collective-permute-start = (bf16[256,128]{1,0:T(8,128)(2,1)S(1)}, bf16[256,128]{1,0:T(8,128)(2,1)S(1)}, u32[]{:S(2)}, u32[]{:S(2)}) collective-permute-start(bf16[256,128]{1,0:T(8,128)(2,1)S(1)} %get-tuple-element.34.refs_0_), channel_id=1, source_target_pairs={{0,24},{4,28},{8,16},{12,20},{16,8},{20,12},{24,0},{28,4},{1,25},{... | collective-permute-start | bytes 196616 | tf_op jit(solution)/shard_map/ppermute | solution.py:119
  6.9 2.6 %build_block.1.refs_0_ = bf16[1024,2048]{1,0:T(8,128)(2,1)S(1)} custom-call(s32[8,128]{1,0:T(8,128)S(1)} %get-tuple-element.32.lists_vmem, s32[1,1,1]{2,1,0:T(1,128)S(6)} %copy.15.count_ref, s32[128,256]{1,0:T(8,128)S(1)} %get-tuple-element.33.codes_ref), custom_call_target="tpu_custom_call" | custom-call | flops 31457280 | bytes 8388608 | tf_op jit(solution)/shard_map/build_block/pallas_call | solution.py:187
  11.0 1.3 %build_rest.1.block_ref = bf16[1024,2048]{1,0:T(8,128)(2,1)S(1)} custom-call(s32[8,128]{1,0:T(8,128)S(1)} %get-tuple-element.32.lists_vmem, s32[1,1,1]{2,1,0:T(1,128)S(6)} %copy.15.count_ref, s32[128,256]{1,0:T(8,128)S(1)} %get-tuple-element.33.codes_ref, bf16[1024,2048]{1,0:T(8,128)(2,1)S(1)} %build_block.1.refs_0_), custom_call_target="tpu_custom_call", output_to_operand_aliasing={{}: (3, {})} | custom-call | flops 10485760 | bytes 8388608 | tf_op jit(solution)/shard_map/build_rest/pallas_call | solution.py:187
  12.4 0.8 %forward_far.1 = (bf16[256,128]{1,0:T(8,128)(2,1)S(1)}, bf16[256,128]{1,0:T(8,128)(2,1)S(1)}) custom-call(bf16[1024,2048]{1,0:T(8,128)(2,1)S(1)} %build_rest.1.block_ref, bf16[256,128]{1,0:T(8,128)(2,1)S(1)} %get-tuple-element.34.refs_0_, bf16[256,128]{1,0:T(8,128)(2,1)S(1)} %collective-permute-done.3.refs_1_, ...), custom_call_target="tpu_custom_call" | custom-call | tf_op jit(solution)/shard_map/forward_far/pallas_call | solution.py:249
  13.1 3.7 %collective-permute-start.5 = (bf16[256,128]{1,0:T(8,128)(2,1)S(1)}, bf16[256,128]{1,0:T(8,128)(2,1)S(1)}, u32[]{:S(2)}, u32[]{:S(2)}) collective-permute-start(bf16[256,128]{1,0:T(8,128)(2,1)S(1)} %get-tuple-element.40), channel_id=1, source_target_pairs={{0,3},{1,2},{2,1},{3,0},{4,7},{5,6},{6,5},{7,4},{8,11},{9,10},{10,... | collective-permute-start | bytes 196616 | tf_op jit(solution)/shard_map/ppermute | solution.py:119
  16.8 0.8 %forward_near.1 = (bf16[256,128]{1,0:T(8,128)(2,1)S(1)}, bf16[256,128]{1,0:T(8,128)(2,1)S(1)}) custom-call(bf16[1024,2048]{1,0:T(8,128)(2,1)S(1)} %build_rest.1.block_ref, bf16[256,128]{1,0:T(8,128)(2,1)S(1)} %get-tuple-element.34.refs_0_, bf16[256,128]{1,0:T(8,128)(2,1)S(1)} %collective-permute-done.3.refs_1_, ...), custom_call_target="tpu_custom_call" | custom-call | tf_op jit(solution)/shard_map/forward_near/pallas_call | solution.py:249
  17.6 0.8 %collective-permute-start.7 = (bf16[256,128]{1,0:T(8,128)(2,1)S(1)}, bf16[256,128]{1,0:T(8,128)(2,1)S(1)}, u32[]{:S(2)}, u32[]{:S(2)}) collective-permute-start(bf16[256,128]{1,0:T(8,128)(2,1)S(1)} %get-tuple-element.42), channel_id=1, source_target_pairs={{0,1},{1,0},{2,3},{3,2},{4,5},{5,4},{6,7},{7,6},{8,9},{9,8},{10,11... | collective-permute-start | bytes 196616 | tf_op jit(solution)/shard_map/ppermute | solution.py:119
  18.4 1.1 %collective-permute-done.5.refs_1_ = bf16[256,128]{1,0:T(8,128)(2,1)S(1)} collective-permute-done((bf16[256,128]{1,0:T(8,128)(2,1)S(1)}, bf16[256,128]{1,0:T(8,128)(2,1)S(1)}, u32[]{:S(2)}, u32[]{:S(2)}) %collective-permute-start.5) | collective-permute-done | bytes 65568 | tf_op jit(solution)/shard_map/ppermute | solution.py:119
  19.6 3.2 %collective-permute-done.6.refs_2_ = bf16[256,128]{1,0:T(8,128)(2,1)S(1)} collective-permute-done((bf16[256,128]{1,0:T(8,128)(2,1)S(1)}, bf16[256,128]{1,0:T(8,128)(2,1)S(1)}, u32[]{:S(2)}, u32[]{:S(2)}) %collective-permute-start.6) | collective-permute-done | bytes 65568 | tf_op jit(solution)/shard_map/ppermute | solution.py:119
  23.6 0.7 %collective-permute-start.8 = (bf16[208,256]{1,0:T(8,128)(2,1)S(1)}, bf16[208,256]{1,0:T(8,128)(2,1)S(1)}, u32[]{:S(2)}, u32[]{:S(2)}) collective-permute-start(bf16[208,256]{1,0:T(8,128)(2,1)S(1)} %get-tuple-element.43.refs_0_), channel_id=1, source_target_pairs={{0,1},{1,0},{2,3},{3,2},{4,5},{5,4},{6,7},{7,6},{8,9},{9,8},{10,11... | collective-permute-start | bytes 319496 | tf_op jit(solution)/shard_map/ppermute | solution.py:119
  24.2 2.2 %collective-permute-start.9 = (bf16[128,256]{1,0:T(8,128)(2,1)S(1)}, bf16[128,256]{1,0:T(8,128)(2,1)S(1)}, u32[]{:S(2)}, u32[]{:S(2)}) collective-permute-start(bf16[128,256]{1,0:T(8,128)(2,1)S(1)} %get-tuple-element.46.refs_0_), channel_id=1, source_target_pairs={{0,2},{1,3},{2,0},{3,1},{4,6},{5,7},{6,4},{7,5},{8,10},{9,11},{10,... | collective-permute-start | bytes 196616 | tf_op jit(solution)/shard_map/ppermute | solution.py:119
  26.4 1.6 %collective-permute-start.10 = (bf16[128,256]{1,0:T(8,128)(2,1)S(1)}, bf16[128,256]{1,0:T(8,128)(2,1)S(1)}, u32[]{:S(2)}, u32[]{:S(2)}) collective-permute-start(bf16[128,256]{1,0:T(8,128)(2,1)S(1)} %get-tuple-element.46.refs_0_), channel_id=1, source_target_pairs={{0,3},{1,2},{2,1},{3,0},{4,7},{5,6},{6,5},{7,4},{8,11},{9,10},{10,... | collective-permute-start | bytes 196616 | tf_op jit(solution)/shard_map/ppermute | solution.py:119
  28.4 1.8 %collective-permute-start.11 = (bf16[80,256]{1,0:T(8,128)(2,1)S(1)}, bf16[80,256]{1,0:T(8,128)(2,1)S(1)}, u32[]{:S(2)}, u32[]{:S(2)}) collective-permute-start(bf16[80,256]{1,0:T(8,128)(2,1)S(1)} %terms_col.1.refs_3_), channel_id=1, source_target_pairs={{0,2},{1,3},{2,0},{3,1},{4,6},{5,7},{6,4},{7,5},{8,10},{9,11},{10,... | collective-permute-start | bytes 122888 | tf_op jit(solution)/shard_map/ppermute | solution.py:119
  30.7 0.7 %collective-permute-done.9.refs_0_ = bf16[128,256]{1,0:T(8,128)(2,1)S(1)} collective-permute-done((bf16[128,256]{1,0:T(8,128)(2,1)S(1)}, bf16[128,256]{1,0:T(8,128)(2,1)S(1)}, u32[]{:S(2)}, u32[]{:S(2)}) %collective-permute-start.9) | collective-permute-done | bytes 65568 | tf_op jit(solution)/shard_map/ppermute | solution.py:119
  31.4 1.1 %collective-permute-done.10.refs_1_ = bf16[128,256]{1,0:T(8,128)(2,1)S(1)} collective-permute-done((bf16[128,256]{1,0:T(8,128)(2,1)S(1)}, bf16[128,256]{1,0:T(8,128)(2,1)S(1)}, u32[]{:S(2)}, u32[]{:S(2)}) %collective-permute-start.10) | collective-permute-done | bytes 65568 | tf_op jit(solution)/shard_map/ppermute | solution.py:119
  32.5 1.2 %collective-permute-done.11.refs_4_ = bf16[80,256]{1,0:T(8,128)(2,1)S(1)} collective-permute-done((bf16[80,256]{1,0:T(8,128)(2,1)S(1)}, bf16[80,256]{1,0:T(8,128)(2,1)S(1)}, u32[]{:S(2)}, u32[]{:S(2)}) %collective-permute-start.11) | collective-permute-done | bytes 40992 | tf_op jit(solution)/shard_map/ppermute | solution.py:119
  34.3 0.5 %collective-permute-start.12 = (bf16[256,256]{1,0:T(8,128)(2,1)S(1)}, bf16[256,256]{1,0:T(8,128)(2,1)S(1)}, u32[]{:S(2)}, u32[]{:S(2)}) collective-permute-start(bf16[256,256]{1,0:T(8,128)(2,1)S(1)} %backward_rest.1), channel_id=1, source_target_pairs={{0,4},{4,0},{8,12},{12,8},{16,20},{20,16},{24,28},{28,24},{1,5},{5... | collective-permute-start | bytes 393224 | tf_op jit(solution)/shard_map/ppermute | solution.py:119
  35.5 2.1 %collective-permute-start.14 = (bf16[208,256]{1,0:T(8,128)(2,1)S(1)}, bf16[208,256]{1,0:T(8,128)(2,1)S(1)}, u32[]{:S(2)}, u32[]{:S(2)}) collective-permute-start(bf16[208,256]{1,0:T(8,128)(2,1)S(1)} %get-tuple-element.54), channel_id=1, source_target_pairs={{0,24},{4,28},{8,16},{12,20},{16,8},{20,12},{24,0},{28,4},{1,25},{... | collective-permute-start | bytes 319496 | tf_op jit(solution)/shard_map/ppermute | solution.py:119
  38.2 1.0 %collective-permute-start.16 = (bf16[208,256]{1,0:T(8,128)(2,1)S(1)}, bf16[208,256]{1,0:T(8,128)(2,1)S(1)}, u32[]{:S(2)}, u32[]{:S(2)}) collective-permute-start(bf16[208,256]{1,0:T(8,128)(2,1)S(1)} %get-tuple-element.56), channel_id=1, source_target_pairs={{0,8},{4,12},{8,0},{12,4},{16,24},{20,28},{24,16},{28,20},{1,9},{5... | collective-permute-start | bytes 319496 | tf_op jit(solution)/shard_map/ppermute | solution.py:119
  39.2 0.8 %hidden_step.1 = bf16[256,128]{1,0:T(8,128)(2,1)} custom-call(bf16[128,128]{1,0:T(8,128)(2,1)S(1)} %copy-done.1, f32[1,128]{1,0:T(1,128)S(1)} %bitcast.8, bf16[256,128]{1,0:T(8,128)(2,1)S(1)} %copy-done, bf16[256,128]{1,0:T(8,128)(2,1)S(1)} %get-tuple-element.45.aggregate_ref), custom_call_target="tpu_custom_call" | custom-call | tf_op jit(solution)/shard_map/hidden_step/pallas_call | solution.py:324
  40.0 1.6 %collective-permute-done.14.refs_1_ = bf16[208,256]{1,0:T(8,128)(2,1)S(1)} collective-permute-done((bf16[208,256]{1,0:T(8,128)(2,1)S(1)}, bf16[208,256]{1,0:T(8,128)(2,1)S(1)}, u32[]{:S(2)}, u32[]{:S(2)}) %collective-permute-start.14) | collective-permute-done | bytes 106528 | tf_op jit(solution)/shard_map/ppermute | solution.py:119
  41.6 2.2 %collective-permute-done.15.refs_2_ = bf16[208,256]{1,0:T(8,128)(2,1)S(1)} collective-permute-done((bf16[208,256]{1,0:T(8,128)(2,1)S(1)}, bf16[208,256]{1,0:T(8,128)(2,1)S(1)}, u32[]{:S(2)}, u32[]{:S(2)}) %collective-permute-start.15) | collective-permute-done | bytes 106528 | tf_op jit(solution)/shard_map/ppermute | solution.py:119
  43.9 0.7 %finish.1 = (bf16[256,128]{1,0:T(8,128)(2,1)}, f32[128,128]{1,0:T(8,128)}, f32[1,128]{1,0:T(1,128)}) custom-call(s32[1,256]{1,0:T(1,128)S(1)} %bitcast.6, bf16[208,256]{1,0:T(8,128)(2,1)S(1)} %get-tuple-element.53.refs_0_, bf16[208,256]{1,0:T(8,128)(2,1)S(1)} %collective-permute-done.14.refs_1_, bf16[208,256]{1,0:T(8,128)(2,1)S(1)} %collective-permute-done.15.refs_2_, ...), custom_call_target="tpu_custom_call" | custom-call | tf_op jit(solution)/shard_map/finish/pallas_call | solution.py:418
  (34 shorter events, 5.6 us)
Async XLA Ops:
  1.7 7.9 %collective-permute-start = (bf16[256,128]{1,0:T(8,128)(2,1)S(1)}, bf16[256,128]{1,0:T(8,128)(2,1)S(1)}, u32[]{:S(2)}, u32[]{:S(2)}) collective-permute-start(bf16[256,128]{1,0:T(8,128)(2,1)S(1)} %get-tuple-element.34.refs_0_), channel_id=1, source_target_pairs={{0,24},{4,28},{8,16},{12,20},{16,8},{20,12},{24,0},{28,4},{1,25},{... | collective-permute-start | bytes 196616 | tf_op jit(solution)/shard_map/ppermute | solution.py:119
  5.6 4.3 %collective-permute-start.1 = (bf16[256,128]{1,0:T(8,128)(2,1)S(1)}, bf16[256,128]{1,0:T(8,128)(2,1)S(1)}, u32[]{:S(2)}, u32[]{:S(2)}) collective-permute-start(bf16[256,128]{1,0:T(8,128)(2,1)S(1)} %get-tuple-element.34.refs_0_), channel_id=1, source_target_pairs={{0,16},{4,20},{8,24},{12,28},{16,0},{20,4},{24,8},{28,12},{1,17},{... | collective-permute-start | bytes 196616 | tf_op jit(solution)/shard_map/ppermute | solution.py:119
  6.1 4.3 %collective-permute-start.2 = (bf16[256,128]{1,0:T(8,128)(2,1)S(1)}, bf16[256,128]{1,0:T(8,128)(2,1)S(1)}, u32[]{:S(2)}, u32[]{:S(2)}) collective-permute-start(bf16[256,128]{1,0:T(8,128)(2,1)S(1)} %get-tuple-element.34.refs_0_), channel_id=1, source_target_pairs={{0,8},{4,12},{8,0},{12,4},{16,24},{20,28},{24,16},{28,20},{1,9},{5... | collective-permute-start | bytes 196616 | tf_op jit(solution)/shard_map/ppermute | solution.py:119
  10.4 1.9 %collective-permute-start.4 = (bf16[768,128]{1,0:T(8,128)(2,1)S(1)}, bf16[768,128]{1,0:T(8,128)(2,1)S(1)}, u32[]{:S(2)}, u32[]{:S(2)}) collective-permute-start(bf16[768,128]{1,0:T(8,128)(2,1)S(1)} %stack.1), channel_id=1, source_target_pairs={{0,4},{4,0},{8,12},{12,8},{16,20},{20,16},{24,28},{28,24},{1,5},{5... | collective-permute-start | bytes 589832 | tf_op jit(solution)/shard_map/ppermute | solution.py:119
  10.5 1.8 %collective-permute-start.3 = (bf16[256,128]{1,0:T(8,128)(2,1)S(1)}, bf16[256,128]{1,0:T(8,128)(2,1)S(1)}, u32[]{:S(2)}, u32[]{:S(2)}) collective-permute-start(bf16[256,128]{1,0:T(8,128)(2,1)S(1)} %get-tuple-element.34.refs_0_), channel_id=1, source_target_pairs={{0,4},{4,0},{8,12},{12,8},{16,20},{20,16},{24,28},{28,24},{1,5},{5... | collective-permute-start | bytes 196616 | tf_op jit(solution)/shard_map/ppermute | solution.py:119
  12.3 10.8 %copy-start = (bf16[256,128]{1,0:T(8,128)(2,1)S(1)}, bf16[256,128]{1,0:T(8,128)(2,1)}, u32[]{:S(2)}) copy-start(bf16[256,128]{1,0:T(8,128)(2,1)} %cot_ref.3) | copy-start | bytes 196612
  12.3 10.8 %copy-start.1 = (bf16[128,128]{1,0:T(8,128)(2,1)S(1)}, bf16[128,128]{1,0:T(8,128)(2,1)}, u32[]{:S(2)}) copy-start(bf16[128,128]{1,0:T(8,128)(2,1)} %weight_ref.3) | copy-start | bytes 98308
  12.3 10.8 %copy-start.2 = (s32[256]{0:T(256)S(1)}, s32[256]{0:T(256)}, u32[]{:S(2)}) copy-start(s32[256]{0:T(256)} %param.10) | copy-start | bytes 3076
  12.3 10.8 %copy-start.3 = (f32[128]{0:T(128)S(1)}, f32[128]{0:T(128)}, u32[]{:S(2)}) copy-start(f32[128]{0:T(128)} %param.12) | copy-start | bytes 1540
  13.1 6.4 %collective-permute-start.5 = (bf16[256,128]{1,0:T(8,128)(2,1)S(1)}, bf16[256,128]{1,0:T(8,128)(2,1)S(1)}, u32[]{:S(2)}, u32[]{:S(2)}) collective-permute-start(bf16[256,128]{1,0:T(8,128)(2,1)S(1)} %get-tuple-element.40), channel_id=1, source_target_pairs={{0,3},{1,2},{2,1},{3,0},{4,7},{5,6},{6,5},{7,4},{8,11},{9,10},{10,... | collective-permute-start | bytes 196616 | tf_op jit(solution)/shard_map/ppermute | solution.py:119
  16.8 6.0 %collective-permute-start.6 = (bf16[256,128]{1,0:T(8,128)(2,1)S(1)}, bf16[256,128]{1,0:T(8,128)(2,1)S(1)}, u32[]{:S(2)}, u32[]{:S(2)}) collective-permute-start(bf16[256,128]{1,0:T(8,128)(2,1)S(1)} %get-tuple-element.41), channel_id=1, source_target_pairs={{0,2},{1,3},{2,0},{3,1},{4,6},{5,7},{6,4},{7,5},{8,10},{9,11},{10,... | collective-permute-start | bytes 196616 | tf_op jit(solution)/shard_map/ppermute | solution.py:119
  17.6 5.5 %collective-permute-start.7 = (bf16[256,128]{1,0:T(8,128)(2,1)S(1)}, bf16[256,128]{1,0:T(8,128)(2,1)S(1)}, u32[]{:S(2)}, u32[]{:S(2)}) collective-permute-start(bf16[256,128]{1,0:T(8,128)(2,1)S(1)} %get-tuple-element.42), channel_id=1, source_target_pairs={{0,1},{1,0},{2,3},{3,2},{4,5},{5,4},{6,7},{7,6},{8,9},{9,8},{10,11... | collective-permute-start | bytes 196616 | tf_op jit(solution)/shard_map/ppermute | solution.py:119
  23.6 4.9 %collective-permute-start.8 = (bf16[208,256]{1,0:T(8,128)(2,1)S(1)}, bf16[208,256]{1,0:T(8,128)(2,1)S(1)}, u32[]{:S(2)}, u32[]{:S(2)}) collective-permute-start(bf16[208,256]{1,0:T(8,128)(2,1)S(1)} %get-tuple-element.43.refs_0_), channel_id=1, source_target_pairs={{0,1},{1,0},{2,3},{3,2},{4,5},{5,4},{6,7},{7,6},{8,9},{9,8},{10,11... | collective-permute-start | bytes 319496 | tf_op jit(solution)/shard_map/ppermute | solution.py:119
  24.2 7.2 %collective-permute-start.9 = (bf16[128,256]{1,0:T(8,128)(2,1)S(1)}, bf16[128,256]{1,0:T(8,128)(2,1)S(1)}, u32[]{:S(2)}, u32[]{:S(2)}) collective-permute-start(bf16[128,256]{1,0:T(8,128)(2,1)S(1)} %get-tuple-element.46.refs_0_), channel_id=1, source_target_pairs={{0,2},{1,3},{2,0},{3,1},{4,6},{5,7},{6,4},{7,5},{8,10},{9,11},{10,... | collective-permute-start | bytes 196616 | tf_op jit(solution)/shard_map/ppermute | solution.py:119
  26.4 6.1 %collective-permute-start.10 = (bf16[128,256]{1,0:T(8,128)(2,1)S(1)}, bf16[128,256]{1,0:T(8,128)(2,1)S(1)}, u32[]{:S(2)}, u32[]{:S(2)}) collective-permute-start(bf16[128,256]{1,0:T(8,128)(2,1)S(1)} %get-tuple-element.46.refs_0_), channel_id=1, source_target_pairs={{0,3},{1,2},{2,1},{3,0},{4,7},{5,6},{6,5},{7,4},{8,11},{9,10},{10,... | collective-permute-start | bytes 196616 | tf_op jit(solution)/shard_map/ppermute | solution.py:119
  28.4 5.3 %collective-permute-start.11 = (bf16[80,256]{1,0:T(8,128)(2,1)S(1)}, bf16[80,256]{1,0:T(8,128)(2,1)S(1)}, u32[]{:S(2)}, u32[]{:S(2)}) collective-permute-start(bf16[80,256]{1,0:T(8,128)(2,1)S(1)} %terms_col.1.refs_3_), channel_id=1, source_target_pairs={{0,2},{1,3},{2,0},{3,1},{4,6},{5,7},{6,4},{7,5},{8,10},{9,11},{10,... | collective-permute-start | bytes 122888 | tf_op jit(solution)/shard_map/ppermute | solution.py:119
  34.0 1.5 %collective-permute-start.13 = (bf16[336,256]{1,0:T(8,128)(2,1)S(1)}, bf16[336,256]{1,0:T(8,128)(2,1)S(1)}, u32[]{:S(2)}, u32[]{:S(2)}) collective-permute-start(bf16[336,256]{1,0:T(8,128)(2,1)S(1)} %backward_other.1.sent_ref), channel_id=1, source_target_pairs={{0,4},{4,0},{8,12},{12,8},{16,20},{20,16},{24,28},{28,24},{1,5},{5... | collective-permute-start | bytes 516104 | tf_op jit(solution)/shard_map/ppermute | solution.py:119
  34.3 3.8 %collective-permute-start.12 = (bf16[256,256]{1,0:T(8,128)(2,1)S(1)}, bf16[256,256]{1,0:T(8,128)(2,1)S(1)}, u32[]{:S(2)}, u32[]{:S(2)}) collective-permute-start(bf16[256,256]{1,0:T(8,128)(2,1)S(1)} %backward_rest.1), channel_id=1, source_target_pairs={{0,4},{4,0},{8,12},{12,8},{16,20},{20,16},{24,28},{28,24},{1,5},{5... | collective-permute-start | bytes 393224 | tf_op jit(solution)/shard_map/ppermute | solution.py:119
  35.5 6.1 %collective-permute-start.14 = (bf16[208,256]{1,0:T(8,128)(2,1)S(1)}, bf16[208,256]{1,0:T(8,128)(2,1)S(1)}, u32[]{:S(2)}, u32[]{:S(2)}) collective-permute-start(bf16[208,256]{1,0:T(8,128)(2,1)S(1)} %get-tuple-element.54), channel_id=1, source_target_pairs={{0,24},{4,28},{8,16},{12,20},{16,8},{20,12},{24,0},{28,4},{1,25},{... | collective-permute-start | bytes 319496 | tf_op jit(solution)/shard_map/ppermute | solution.py:119
  37.6 6.1 %collective-permute-start.15 = (bf16[208,256]{1,0:T(8,128)(2,1)S(1)}, bf16[208,256]{1,0:T(8,128)(2,1)S(1)}, u32[]{:S(2)}, u32[]{:S(2)}) collective-permute-start(bf16[208,256]{1,0:T(8,128)(2,1)S(1)} %get-tuple-element.55), channel_id=1, source_target_pairs={{0,16},{4,20},{8,24},{12,28},{16,0},{20,4},{24,8},{28,12},{1,17},{... | collective-permute-start | bytes 319496 | tf_op jit(solution)/shard_map/ppermute | solution.py:119
  38.2 5.7 %collective-permute-start.16 = (bf16[208,256]{1,0:T(8,128)(2,1)S(1)}, bf16[208,256]{1,0:T(8,128)(2,1)S(1)}, u32[]{:S(2)}, u32[]{:S(2)}) collective-permute-start(bf16[208,256]{1,0:T(8,128)(2,1)S(1)} %get-tuple-element.56), channel_id=1, source_target_pairs={{0,8},{4,12},{8,0},{12,4},{16,24},{20,28},{24,16},{28,20},{1,9},{5... | collective-permute-start | bytes 319496 | tf_op jit(solution)/shard_map/ppermute | solution.py:119

commit v6 on v5

--- a/solution.py
+++ b/solution.py
@@ -119,12 +119,8 @@
     return lax.ppermute(value, axis, [(i, i ^ bits) for i in range(size)])
 
 
-def column_of(row):
-    n = row.shape[1]
-    blocks = [
-        jnp.broadcast_to(row[:, k : k + 128], (128, 128)).T for k in range(0, n, 128)
-    ]
-    return jnp.concatenate(blocks, axis=0)
+def turned(lhs, rhs):
+    return lax.dot_general(lhs, rhs, (((1,), (1,)), ((), ())), preferred_element_type=jnp.float32)
 
 
 def fetch(sources, targets, sems):
@@ -138,7 +134,7 @@
 
 
 def build_kernel(first, last, lists_vmem, count_ref, codes_ref, *refs):
-    block_ref, row_scr, col_scr, lists_ref, sems = refs[-5:]
+    block_ref, col_scr, row_scr, lists_ref, sems = refs[-5:]
     slots = codes_ref.shape[0]
     side = codes_ref.shape[1] // 2
     (copy,) = fetch((lists_vmem,), (lists_ref,), sems)
@@ -146,33 +142,33 @@
         block_ref[...] = jnp.zeros_like(block_ref)
     row_code = codes_ref[:, :side].astype(jnp.float32) + 3.0
     row_code = jnp.where(row_code > MOD // 2, row_code - MOD, row_code)
-    slot = lax.broadcasted_iota(jnp.int32, (slots, side), 0)
-    row_code = jnp.where(slot < count_ref[0, 0, 0], row_code, 0.0)
     col_code = codes_ref[:, side:].astype(jnp.float32) + 1.0
     col_code = jnp.where(col_code > MOD // 2, col_code - MOD, col_code)
+    slot = lax.broadcasted_iota(jnp.int32, (slots, side), 0)
+    col_code = jnp.where(slot < count_ref[0, 0, 0], col_code, 0.0)
     coarse = 2.0**-12
-    col_scr[...] = col_code * coarse + col_code * (1.0 / MOD - coarse)
-    by_side = row_code.T
+    row_scr[...] = row_code * coarse + row_code * (1.0 / MOD - coarse)
+    by_side = col_code.T
     groups = range(first // GROUP, last // GROUP)
     for g in groups:
-        row_scr[g] = by_side if g == 0 else pltpu.roll(by_side, slots - g * GROUP, axis=1)
+        col_scr[g] = by_side if g == 0 else pltpu.roll(by_side, slots - g * GROUP, axis=1)
     copy.wait()
     middle = (3.0 + (HIT - 1) / 2.0) / MOD
     reach = jnp.bfloat16(2.0**-7)
     one, zero = jnp.bfloat16(1.0), jnp.bfloat16(0.0)
 
     def step(g, carry):
-        row_vals = row_scr[g]
-        col_vals = col_scr[pl.ds(pl.multiple_of(g * GROUP, GROUP), GROUP), :]
+        col_vals = col_scr[g]
+        row_vals = row_scr[pl.ds(pl.multiple_of(g * GROUP, GROUP), GROUP), :]
         for t in range(GROUP):
             s = g * GROUP + t
-            turns = jnp.broadcast_to(row_vals[:, t : t + 1], (side, side)) * jnp.broadcast_to(
-                col_vals[t : t + 1, :], (side, side)
+            turns = jnp.broadcast_to(col_vals[:, t : t + 1], (side, side)) * jnp.broadcast_to(
+                row_vals[t : t + 1, :], (side, side)
             )
             part = turns - jnp.round(turns)
             keep = jnp.abs((part - middle).astype(jnp.bfloat16)) < reach
-            down = pl.ds(pl.multiple_of(lists_ref[0, s] * side, side), side)
-            across = pl.ds(pl.multiple_of(lists_ref[1, s] * side, side), side)
+            down = pl.ds(pl.multiple_of(lists_ref[1, s] * side, side), side)
+            across = pl.ds(pl.multiple_of(lists_ref[0, s] * side, side), side)
             block_ref[down, across] += jnp.where(keep, one, zero)
         return carry
 
@@ -186,7 +182,7 @@
     begun = [] if block is None else [block]
     return pl.pallas_call(
         functools.partial(build_kernel, first, last),
-        out_shape=pltpu.VMEM((row_nodes, col_nodes), jnp.bfloat16),
+        out_shape=pltpu.VMEM((col_nodes, row_nodes), jnp.bfloat16),
         in_specs=[vmem, pl.BlockSpec(memory_space=pltpu.SMEM), vmem] + [vmem] * len(begun),
         out_specs=vmem,
         input_output_aliases={3: 0} if begun else {},
@@ -224,111 +220,136 @@
     )(*parts)
 
 
-def forward_kernel(bits, high, block_ref, *refs):
-    *parts, even_ref, odd_ref, source = refs
-    pieces = parts[0].shape[0]
+def forward_kernel(bits, far, block_ref, *refs):
+    outs = refs[len(refs) - len(far) :]
+    parts = refs[: len(refs) - len(far)]
+    feat, pieces = parts[0].shape
     me_row = lax.axis_index("row")
     me_col = lax.axis_index("col")
-    place = iter(bits)
-    for part in parts:
-        for m in range(part.shape[0] // pieces):
-            at = pl.multiple_of((me_row ^ next(place)) * pieces, pieces)
-            source[pl.ds(at, pieces), :] = part[m * pieces : (m + 1) * pieces, :]
-    down = pl.multiple_of((me_col ^ high) // 2 * (2 * pieces), 2 * pieces)
-    both = jnp.dot(
-        block_ref[pl.ds(down, 2 * pieces), :], source[...], preferred_element_type=jnp.float32
-    ).astype(jnp.bfloat16)
-    first = me_col % 2 == 0
-    even_ref[...] = jnp.where(first, both[:pieces], both[pieces:])
-    odd_ref[...] = jnp.where(first, both[pieces:], both[:pieces])
-
-
-def forward_parts(block, parts, bits, high, name):
-    pieces, feat = parts[0].shape
-    vmem = pl.BlockSpec(memory_space=pltpu.VMEM)
-    return pl.pallas_call(
-        functools.partial(forward_kernel, bits, high),
-        out_shape=[jax.ShapeDtypeStruct((pieces, feat), jnp.bfloat16)] * 2,
+    for out, k in zip(outs, far):
+        across = pl.ds(pl.multiple_of((me_col ^ k) * pieces, pieces), pieces)
+        total = jnp.zeros((feat, pieces), jnp.float32)
+        place = iter(bits)
+        for part in parts:
+            for m in range(part.shape[0] // feat):
+                down = pl.ds(pl.multiple_of((me_row ^ next(place)) * pieces, pieces), pieces)
+                total += jnp.dot(
+                    part[m * feat : (m + 1) * feat, :],
+                    block_ref[down, across],
+                    preferred_element_type=jnp.float32,
+                )
+        out[...] = total.astype(jnp.bfloat16)
+
+
+def forward_parts(block, parts, bits, far, name):
+    feat, pieces = parts[0].shape
+    vmem = pl.BlockSpec(memory_space=pltpu.VMEM)
+    return pl.pallas_call(
+        functools.partial(forward_kernel, bits, far),
+        out_shape=[jax.ShapeDtypeStruct((feat, pieces), jnp.bfloat16)] * len(far),
         in_specs=[vmem] * (1 + len(parts)),
-        out_specs=[vmem] * 2,
-        scratch_shapes=[pltpu.VMEM((pieces * len(bits), feat), jnp.bfloat16)],
+        out_specs=[vmem] * len(far),
         compiler_params=pltpu.CompilerParams(vmem_limit_bytes=LIMIT),
         name=name,
     )(block, *parts)
 
 
-def slope_of(aggregate, weight, bias, cotangent):
-    preact = jnp.dot(aggregate, weight, preferred_element_type=jnp.float32) + bias
-    decay = jnp.exp(jnp.minimum(preact, 0.0))
-    positive = preact > 0
-    grad_pre = cotangent.astype(jnp.float32) * jnp.where(positive, 1.0, decay)
-    return jnp.where(positive, preact, decay - 1.0), grad_pre
-
-
-def gradient_kernel(n_col, degree_ref, weight_ref, bias_ref, cot_ref, *refs):
-    parts = refs[:n_col]
+def turn_kernel(
+    weight_ref, bias_ref, cot_ref, degree_ref, weight_out, bias_out, cot_out, root_out
+):
+    feat, pieces = cot_out.shape
+    weight_out[...] = weight_ref[...].T
+    bias_out[...] = jnp.broadcast_to(bias_ref[...], (feat, feat)).T
+    cot_out[...] = cot_ref[...].T
+    inv_row = lax.rsqrt(degree_ref[...].astype(jnp.float32))
+    root_out[...] = jnp.broadcast_to(inv_row, (feat, pieces)).T
+
+
+def turn(weight, bias, cotangent, degree):
+    pieces, feat = cotangent.shape
+    vmem = pl.BlockSpec(memory_space=pltpu.VMEM)
+    return pl.pallas_call(
+        turn_kernel,
+        out_shape=[
+            jax.ShapeDtypeStruct((feat, feat), jnp.bfloat16),
+            jax.ShapeDtypeStruct((feat, feat), jnp.float32),
+            jax.ShapeDtypeStruct((feat, pieces), jnp.bfloat16),
+            jax.ShapeDtypeStruct((pieces, feat), jnp.float32),
+        ],
+        in_specs=[vmem] * 4,
+        out_specs=[vmem] * 4,
+        compiler_params=pltpu.CompilerParams(vmem_limit_bytes=LIMIT),
+        name="turn",
+    )(weight, bias.reshape(1, feat), cotangent, degree.reshape(1, pieces))
+
+
+def preact_of(aggregate, weight_turned, bias_turned):
+    repeats = aggregate.shape[1] // bias_turned.shape[1]
+    bias = jnp.concatenate([bias_turned] * repeats, axis=1)
+    return jnp.dot(weight_turned, aggregate, preferred_element_type=jnp.float32) + bias
+
+
+def gradient_kernel(n_col, degree_ref, weight_ref, turned_ref, bias_ref, cot_ref, *refs):
     grad_ref, both_ref, aggregate_ref = refs[n_col:]
-    total = parts[0][...].astype(jnp.float32)
-    for k in range(1, n_col):
-        total += parts[k][...].astype(jnp.float32)
     inv_row = lax.rsqrt(degree_ref[...].astype(jnp.float32))
-    aggregate = (column_of(inv_row) * total).astype(jnp.bfloat16)
+    aggregate = (inv_row * sum_of(refs[:n_col])).astype(jnp.bfloat16)
     aggregate_ref[...] = aggregate
-    weight = weight_ref[...]
-    feat = weight.shape[0]
-    half = feat // 2
-    _, grad_pre = slope_of(aggregate, weight, bias_ref[...], cot_ref[...])
+    feat = weight_ref.shape[0]
+    preact = preact_of(aggregate, turned_ref[...], bias_ref[...])
+    slope = jnp.where(preact > 0, 1.0, jnp.exp(jnp.minimum(preact, 0.0)))
+    grad_pre = cot_ref[...].astype(jnp.float32) * slope
+    grad = lax.dot_general(
+        (inv_row * grad_pre).astype(jnp.bfloat16),
+        weight_ref[...],
+        (((0,), (1,)), ((), ())),
+        preferred_element_type=jnp.float32,
+    ).astype(jnp.bfloat16)
+    pieces = grad.shape[0]
+    grad_ref[...] = grad
+    both_ref[:pieces, :] = grad
     grad_pre_b = grad_pre.astype(jnp.bfloat16)
-    back = lax.dot_general(
-        weight, grad_pre_b, (((1,), (1,)), ((), ())), preferred_element_type=jnp.float32
-    )
-    grad = (inv_row * back).astype(jnp.bfloat16)
-    grad_ref[...] = grad
-    both_ref[:feat, :] = grad
-    weight_terms = lax.dot_general(
-        aggregate, grad_pre_b, (((0,), (0,)), ((), ())), preferred_element_type=jnp.float32
-    ).astype(jnp.bfloat16)
-    both_ref[feat : feat + half, :feat] = weight_terms[:half]
-    both_ref[feat : feat + half, feat:] = weight_terms[half:]
-    bias_terms = jnp.sum(grad_pre, axis=0, keepdims=True)
-    bias_terms = jnp.broadcast_to(bias_terms, (16, feat)).astype(jnp.bfloat16)
-    both_ref[feat + half :, :feat] = bias_terms
-    both_ref[feat + half :, feat:] = bias_terms
-
-
-def gradient_step(degree, weight, bias, cotangent, parts):
-    pieces, feat = cotangent.shape
+    both_ref[pieces : pieces + feat, :] = turned(aggregate, grad_pre_b).astype(jnp.bfloat16)
+    ones = jnp.ones((16, pieces), jnp.bfloat16)
+    rest = (grad_pre - grad_pre_b.astype(jnp.float32)).astype(jnp.bfloat16)
+    both_ref[pieces + feat :, :] = (turned(ones, grad_pre_b) + turned(ones, rest)).astype(
+        jnp.bfloat16
+    )
+
+
+def gradient_step(degree, weight, turned_operands, parts):
+    feat, pieces = parts[0].shape
     vmem = pl.BlockSpec(memory_space=pltpu.VMEM)
     return pl.pallas_call(
         functools.partial(gradient_kernel, len(parts)),
         out_shape=[
+            jax.ShapeDtypeStruct((pieces, feat), jnp.bfloat16),
+            jax.ShapeDtypeStruct((pieces + feat + 16, feat), jnp.bfloat16),
             jax.ShapeDtypeStruct((feat, pieces), jnp.bfloat16),
-            jax.ShapeDtypeStruct((feat + feat // 2 + 16, pieces), jnp.bfloat16),
-            jax.ShapeDtypeStruct((pieces, feat), jnp.bfloat16),
         ],
-        in_specs=[vmem] * (4 + len(parts)),
+        in_specs=[vmem] * (5 + len(parts)),
         out_specs=[vmem] * 3,
         compiler_params=pltpu.CompilerParams(vmem_limit_bytes=LIMIT),
         name="gradient_step",
-    )(degree.reshape(1, pieces), weight, bias.reshape(1, feat), cotangent, *parts)
-
-
-def hidden_kernel(weight_ref, bias_ref, cot_ref, aggregate_ref, hidden_ref):
-    hidden, _ = slope_of(aggregate_ref[...], weight_ref[...], bias_ref[...], cot_ref[...])
-    hidden_ref[...] = hidden.astype(jnp.bfloat16)
-
-
-def hidden_step(weight, bias, cotangent, aggregate):
-    pieces, feat = cotangent.shape
+    )(degree.reshape(1, pieces), weight, *turned_operands, *parts)
+
+
+def hidden_kernel(turned_ref, bias_ref, aggregate_ref, hidden_ref):
+    preact = preact_of(aggregate_ref[...], turned_ref[...], bias_ref[...])
+    hidden = jnp.where(preact > 0, preact, jnp.exp(jnp.minimum(preact, 0.0)) - 1.0)
+    hidden_ref[...] = hidden.astype(jnp.bfloat16).T
+
+
+def hidden_step(weight_turned, bias_turned, aggregate):
+    feat, pieces = aggregate.shape
     vmem = pl.BlockSpec(memory_space=pltpu.VMEM)
     return pl.pallas_call(
         hidden_kernel,
         out_shape=jax.ShapeDtypeStruct((pieces, feat), jnp.bfloat16),
-        in_specs=[vmem] * 4,
+        in_specs=[vmem] * 3,
         out_specs=vmem,
         compiler_params=pltpu.CompilerParams(vmem_limit_bytes=LIMIT),
         name="hidden_step",
-    )(weight, bias.reshape(1, feat), cotangent, aggregate)
+    )(weight_turned, bias_turned, aggregate)
 
 
 def sum_of(refs):
@@ -338,37 +359,37 @@
     return total
 
 
-def backward_kernel(feat, kinds, chunks, begun, block_ref, *refs):
+def backward_kernel(pieces, kinds, chunks, begun, block_ref, *refs):
     sources, out_ref = refs[: len(kinds)], refs[-1]
     terms = refs[len(kinds) + begun : -1]
-    pieces = out_ref.shape[1]
+    feat = out_ref.shape[1]
     me_row = lax.axis_index("row")
     me_col = lax.axis_index("col")
     for m, chunk in enumerate(chunks):
-        across = pl.ds(pl.multiple_of((me_row ^ chunk) * pieces, pieces), pieces)
+        down = pl.ds(pl.multiple_of((me_row ^ chunk) * pieces, pieces), pieces)
         if begun:
-            total = refs[len(kinds)][chunk * feat : (chunk + 1) * feat, :]
+            total = refs[len(kinds)][chunk * pieces : (chunk + 1) * pieces, :]
         else:
-            total = jnp.zeros((feat, pieces), jnp.float32)
+            total = jnp.zeros((pieces, feat), jnp.float32)
         for k, source in zip(kinds, sources):
-            down = pl.ds(pl.multiple_of((me_col ^ k) * pieces, pieces), pieces)
+            across = pl.ds(pl.multiple_of((me_col ^ k) * pieces, pieces), pieces)
             total += jnp.dot(
-                source[:feat, :], block_ref[down, across], preferred_element_type=jnp.float32
+                block_ref[down, across], source[:pieces, :], preferred_element_type=jnp.float32
             )
-        out_ref[m * feat : (m + 1) * feat, :] = total.astype(out_ref.dtype)
+        out_ref[m * pieces : (m + 1) * pieces, :] = total.astype(out_ref.dtype)
     if terms:
-        out_ref[len(chunks) * feat :, :] = sum_of(terms).astype(out_ref.dtype)
+        out_ref[len(chunks) * pieces :, :] = sum_of(terms).astype(out_ref.dtype)
 
 
 def backward_parts(block, sources, kinds, chunks, begun, terms, name):
-    feat, pieces = sources[0].shape
+    pieces, feat = sources[0].shape
     begun = [] if begun is None else [begun]
     extra = terms[0].shape[0] if terms else 0
     vmem = pl.BlockSpec(memory_space=pltpu.VMEM)
     dtype = jnp.bfloat16 if begun else jnp.float32
     return pl.pallas_call(
-        functools.partial(backward_kernel, feat, kinds, chunks, len(begun)),
-        out_shape=jax.ShapeDtypeStruct((len(chunks) * feat + extra, pieces), dtype),
+        functools.partial(backward_kernel, pieces, kinds, chunks, len(begun)),
+        out_shape=jax.ShapeDtypeStruct((len(chunks) * pieces + extra, feat), dtype),
         in_specs=[vmem] * (1 + len(kinds) + len(begun) + len(terms)),
         out_specs=vmem,
         compiler_params=pltpu.CompilerParams(vmem_limit_bytes=LIMIT),
@@ -399,21 +420,17 @@
     )(mine, theirs, sent, got)
 
 
-def finish_kernel(scale, degree_ref, *refs):
-    parts = refs[:-3]
-    out_ref, weight_ref, bias_ref = refs[-3:]
-    inv_row = lax.rsqrt(degree_ref[...].astype(jnp.float32))
+def finish_kernel(scale, root_ref, *refs):
+    *parts, out_ref, weight_ref, bias_ref = refs
     total = sum_of(parts)
-    feat = weight_ref.shape[0]
-    half = feat // 2
-    out_ref[...] = (inv_row * total[:feat]).T.astype(jnp.bfloat16)
-    weight_ref[:half, :] = total[feat : feat + half, :feat] * scale
-    weight_ref[half:, :] = total[feat : feat + half, feat:] * scale
-    bias_ref[...] = total[feat + half : feat + half + 1, :feat] * scale
-
-
-def finish(degree, parts, feat, scale):
-    pieces = parts[0].shape[1]
+    pieces, feat = out_ref.shape
+    out_ref[...] = (root_ref[...] * total[:pieces]).astype(jnp.bfloat16)
+    weight_ref[...] = total[pieces : pieces + feat] * scale
+    bias_ref[...] = total[pieces + feat : pieces + feat + 1] * scale
+
+
+def finish(root, parts, scale):
+    pieces, feat = root.shape
     vmem = pl.BlockSpec(memory_space=pltpu.VMEM)
     grad_features, grad_weight, grad_bias = pl.pallas_call(
         functools.partial(finish_kernel, scale),
@@ -426,7 +443,7 @@
         out_specs=[vmem] * 3,
         compiler_params=pltpu.CompilerParams(vmem_limit_bytes=LIMIT),
         name="finish",
-    )(degree.reshape(1, pieces), *parts)
+    )(root, *parts)
     return grad_features, grad_weight, grad_bias.reshape(feat)
 
 
@@ -447,9 +464,9 @@
         sems,
     )
     first.wait()
-    inv_root = column_of(lax.rsqrt(degree_ref[...].astype(jnp.float32)))
+    inv_row = lax.rsqrt(degree_ref[...].astype(jnp.float32))
     second.wait()
-    out_ref[...] = (inv_root * features_ref[...].astype(jnp.float32)).astype(jnp.bfloat16)
+    out_ref[...] = (inv_row * features_ref[...].astype(jnp.float32).T).astype(jnp.bfloat16)
     for copy in others:
         copy.wait()
 
@@ -459,7 +476,7 @@
     return pl.pallas_call(
         scale_kernel,
         out_shape=[
-            pltpu.VMEM(features.shape, jnp.bfloat16),
+            pltpu.VMEM((feat, pieces), jnp.bfloat16),
             pltpu.VMEM((8, codes.shape[0]), jnp.int32),
             pltpu.VMEM(codes.shape, codes.dtype),
         ],
@@ -518,15 +535,18 @@
     parts = [scaled, sibling, *landed, swap(stack(landed), "row", 1)]
     bits = [0, 1, *chips, *(m + 1 for m in chips)]
     block = build_block(lists, tile_count, codes, *size, middle, slots, block)
-    far = forward_parts(block, parts, bits, 2, "forward_far")
-    near = forward_parts(block, parts, bits, 0, "forward_near")
-    parts = [*near, *far]
+    half = max(1, n_col // 2)
+    far = forward_parts(block, parts, bits, lines[:half], "forward_far")
+    near = forward_parts(block, parts, bits, lines[half:] + [0], "forward_near")
+    parts = dict(zip(lines + [0], [*far, *near]))
+    *dense, parts[0] = lax.optimization_barrier((weight, bias, cotangent, degree, parts[0]))
+    *dense, root = turn(*dense)
     landed = [parts[0]] + [swap(parts[k], "col", k) for k in lines]
-    grad_own, both, aggregate = gradient_step(degree, weight, bias, cotangent, landed)
+    grad_own, both, aggregate = gradient_step(degree, weight, dense, landed)
     grads = [grad_own, swap(both, "col", 1)] + [swap(grad_own, "col", k) for k in range(2, n_col)]
     grads[1], aggregate = lax.optimization_barrier((grads[1], aggregate))
-    hidden = hidden_step(weight, bias, cotangent, aggregate)
-    terms = [terms_sum([both, grads[1]], feat, "terms_col")]
+    hidden = hidden_step(dense[0], dense[1], aggregate)
+    terms = [terms_sum([both, grads[1]], pieces, "terms_col")]
     terms += [swap(terms[0], "col", k) for k in range(2, n_col, 2)]
     begun = backward_parts(block, grads, [0, 1], range(n_row), None, [], "backward_near")
     grads[2:], begun, terms = lax.optimization_barrier((grads[2:], begun, terms))
@@ -539,7 +559,7 @@
     landed = [swap(chunk, "row", m) for chunk, m in zip(chunks, chips)]
     chunks = pair_sum(2, mine, rest, sent, got)
     landed = [chunks[1], *landed, swap(chunks[0], "row", chips[2])]
-    grad_features, grad_weight, grad_bias = finish(degree, landed, feat, grad_scale)
+    grad_features, grad_weight, grad_bias = finish(root, landed, grad_scale)
     return (hidden, grad_features, grad_weight, grad_bias)
 
 

time: 44.8 us -> 44 us (0.982)
  waiting for transfers between devices: 13.1 us -> 12.5 us
    ppermute x17, waiting for transfers between devices: 13.1 us -> 12.5 us  [swap(): return lax.ppermute(value, axis, [(i, i ^ bits) for i in range(size)])]
    pallas_call x7 -> x8, Pallas kernels: 3.83 us -> 3.87 us  [the longest x4 1.72 us: backward_parts(): pl.pallas_call(functools.partial(backward_kernel, pieces, kinds, chunks,...]
  transfers between devices with their start and end apart: 17 -> 17, of which waited for: 13 -> 12; matrix products, arithmetic and copies ran while one was open for 0% -> 0% of each run, Pallas kernels for 15% -> 16%
where the time goes in v6:
time: 44 us; the launch traced here: 43.8 us
  starting transfers between devices  20 us (45%)
  waiting for transfers between devices  12.5 us (28%)
  Pallas kernels  9.84 us (22%)
  between operations  1.46 us (3%)
    ppermute x17, starting transfers between devices, swap(): return lax.ppermute(value, axis, [(i, i ^ bits) for i in range(size)])  20 us
    ppermute x17, waiting for transfers between devices, swap(): return lax.ppermute(value, axis, [(i, i ^ bits) for i in range(size)])  12.5 us
    pallas_call x2, Pallas kernels, build_block(): pl.pallas_call(functools.partial(build_kernel, first, last), out_shape=pl...  3.91 us
    pallas_call x4, Pallas kernels, backward_parts(): pl.pallas_call(functools.partial(backward_kernel, pieces, kinds, chunks,...  1.72 us
    pallas_call x1, Pallas kernels, scale_rows(): pl.pallas_call(scale_kernel, out_shape=[pltpu.VMEM((feat, pieces), jnp.bf...  1.03 us
    pallas_call x2, Pallas kernels, forward_parts(): pl.pallas_call(functools.partial(forward_kernel, bits, far), out_shape=[j...  0.97 us
  transfers between devices with their start and end apart: 17, of which 12 were waited for; matrix products, arithmetic and copies ran while one was open for 0% of the time, Pallas kernels for 16%

profile of v6, /device:TPU:0, one launch (start us, length us, event | category | flops | bytes accessed | tf_op | source)
XLA Modules:
  0.0 43.8 jit_solution(6439670754595924939)
XLA Ops:
  0.6 1.0 %scale_rows.1 = (bf16[128,256]{1,0:T(8,128)(2,1)S(1)}, s32[8,128]{1,0:T(8,128)S(1)}, s32[128,256]{1,0:T(8,128)S(1)}) custom-call(s32[1,256]{1,0:T(1,128)} %bitcast.5, bf16[256,128]{1,0:T(8,128)(2,1)} %features_hbm.1, s32[1,1,128]{2,1,0:T(1,128)} %rows_hbm.1, s32[1,1,128]{2,1,0:T(1,128)} %cols_hbm.1, s32[128,256]{1,0:T(8,128)} %bitcast.9), custom_call_target="tpu_custom_call" | custom-call | tf_op jit(solution)/shard_map/scale_rows/pallas_call | solution.py:476
  1.7 4.0 %collective-permute-start = (bf16[128,256]{1,0:T(8,128)(2,1)S(1)}, bf16[128,256]{1,0:T(8,128)(2,1)S(1)}, u32[]{:S(2)}, u32[]{:S(2)}) collective-permute-start(bf16[128,256]{1,0:T(8,128)(2,1)S(1)} %get-tuple-element.43.refs_0_), channel_id=1, source_target_pairs={{0,24},{4,28},{8,16},{12,20},{16,8},{20,12},{24,0},{28,4},{1,25},{... | collective-permute-start | bytes 196616 | tf_op jit(solution)/shard_map/ppermute | solution.py:119
  5.6 0.5 %collective-permute-start.1 = (bf16[128,256]{1,0:T(8,128)(2,1)S(1)}, bf16[128,256]{1,0:T(8,128)(2,1)S(1)}, u32[]{:S(2)}, u32[]{:S(2)}) collective-permute-start(bf16[128,256]{1,0:T(8,128)(2,1)S(1)} %get-tuple-element.43.refs_0_), channel_id=1, source_target_pairs={{0,16},{4,20},{8,24},{12,28},{16,0},{20,4},{24,8},{28,12},{1,17},{... | collective-permute-start | bytes 196616 | tf_op jit(solution)/shard_map/ppermute | solution.py:119
  6.9 2.6 %build_block.1.refs_0_ = bf16[2048,1024]{1,0:T(8,128)(2,1)S(1)} custom-call(s32[8,128]{1,0:T(8,128)S(1)} %get-tuple-element.41.lists_vmem, s32[1,1,1]{2,1,0:T(1,128)S(6)} %copy.15.count_ref, s32[128,256]{1,0:T(8,128)S(1)} %get-tuple-element.42.codes_ref), custom_call_target="tpu_custom_call" | custom-call | flops 31457280 | bytes 8388608 | tf_op jit(solution)/shard_map/build_block/pallas_call | solution.py:183
  9.9 0.5 %collective-permute-done.2.refs_2_.refs_4_ = bf16[128,256]{1,0:T(8,128)(2,1)S(1)} collective-permute-done((bf16[128,256]{1,0:T(8,128)(2,1)S(1)}, bf16[128,256]{1,0:T(8,128)(2,1)S(1)}, u32[]{:S(2)}, u32[]{:S(2)}) %collective-permute-start.2) | collective-permute-done | bytes 65568 | tf_op jit(solution)/shard_map/ppermute | solution.py:119
  11.0 1.3 %build_rest.1.block_ref = bf16[2048,1024]{1,0:T(8,128)(2,1)S(1)} custom-call(s32[8,128]{1,0:T(8,128)S(1)} %get-tuple-element.41.lists_vmem, s32[1,1,1]{2,1,0:T(1,128)S(6)} %copy.15.count_ref, s32[128,256]{1,0:T(8,128)S(1)} %get-tuple-element.42.codes_ref, bf16[2048,1024]{1,0:T(8,128)(2,1)S(1)} %build_block.1.refs_0_), custom_call_target="tpu_custom_call", output_to_operand_aliasing={{}: (3, {})} | custom-call | flops 10485760 | bytes 8388608 | tf_op jit(solution)/shard_map/build_rest/pallas_call | solution.py:183
  12.9 3.6 %collective-permute-start.5 = (bf16[128,256]{1,0:T(8,128)(2,1)S(1)}, bf16[128,256]{1,0:T(8,128)(2,1)S(1)}, u32[]{:S(2)}, u32[]{:S(2)}) collective-permute-start(bf16[128,256]{1,0:T(8,128)(2,1)S(1)} %get-tuple-element.57), channel_id=1, source_target_pairs={{0,3},{1,2},{2,1},{3,0},{4,7},{5,6},{6,5},{7,4},{8,11},{9,10},{10,... | collective-permute-start | bytes 196616 | tf_op jit(solution)/shard_map/ppermute | solution.py:119
  17.0 0.9 %collective-permute-start.7 = (bf16[128,256]{1,0:T(8,128)(2,1)S(1)}, bf16[128,256]{1,0:T(8,128)(2,1)S(1)}, u32[]{:S(2)}, u32[]{:S(2)}) collective-permute-start(bf16[128,256]{1,0:T(8,128)(2,1)S(1)} %get-tuple-element.59), channel_id=1, source_target_pairs={{0,1},{1,0},{2,3},{3,2},{4,5},{5,4},{6,7},{7,6},{8,9},{9,8},{10,11... | collective-permute-start | bytes 196616 | tf_op jit(solution)/shard_map/ppermute | solution.py:119
  18.0 1.3 %collective-permute-done.5.refs_1_ = bf16[128,256]{1,0:T(8,128)(2,1)S(1)} collective-permute-done((bf16[128,256]{1,0:T(8,128)(2,1)S(1)}, bf16[128,256]{1,0:T(8,128)(2,1)S(1)}, u32[]{:S(2)}, u32[]{:S(2)}) %collective-permute-start.5) | collective-permute-done | bytes 65568 | tf_op jit(solution)/shard_map/ppermute | solution.py:119
  19.3 3.1 %collective-permute-done.6.refs_2_ = bf16[128,256]{1,0:T(8,128)(2,1)S(1)} collective-permute-done((bf16[128,256]{1,0:T(8,128)(2,1)S(1)}, bf16[128,256]{1,0:T(8,128)(2,1)S(1)}, u32[]{:S(2)}, u32[]{:S(2)}) %collective-permute-start.6) | collective-permute-done | bytes 65568 | tf_op jit(solution)/shard_map/ppermute | solution.py:119
  23.0 0.9 %collective-permute-start.8 = (bf16[400,128]{1,0:T(8,128)(2,1)S(1)}, bf16[400,128]{1,0:T(8,128)(2,1)S(1)}, u32[]{:S(2)}, u32[]{:S(2)}) collective-permute-start(bf16[400,128]{1,0:T(8,128)(2,1)S(1)} %get-tuple-element.60.refs_0_), channel_id=1, source_target_pairs={{0,1},{1,0},{2,3},{3,2},{4,5},{5,4},{6,7},{7,6},{8,9},{9,8},{10,11... | collective-permute-start | bytes 307208 | tf_op jit(solution)/shard_map/ppermute | solution.py:119
  23.9 2.0 %collective-permute-start.9 = (bf16[256,128]{1,0:T(8,128)(2,1)S(1)}, bf16[256,128]{1,0:T(8,128)(2,1)S(1)}, u32[]{:S(2)}, u32[]{:S(2)}) collective-permute-start(bf16[256,128]{1,0:T(8,128)(2,1)S(1)} %get-tuple-element.64.refs_0_), channel_id=1, source_target_pairs={{0,2},{1,3},{2,0},{3,1},{4,6},{5,7},{6,4},{7,5},{8,10},{9,11},{10,... | collective-permute-start | bytes 196616 | tf_op jit(solution)/shard_map/ppermute | solution.py:119
  25.9 1.6 %collective-permute-start.10 = (bf16[256,128]{1,0:T(8,128)(2,1)S(1)}, bf16[256,128]{1,0:T(8,128)(2,1)S(1)}, u32[]{:S(2)}, u32[]{:S(2)}) collective-permute-start(bf16[256,128]{1,0:T(8,128)(2,1)S(1)} %get-tuple-element.64.refs_0_), channel_id=1, source_target_pairs={{0,3},{1,2},{2,1},{3,0},{4,7},{5,6},{6,5},{7,4},{8,11},{9,10},{10,... | collective-permute-start | bytes 196616 | tf_op jit(solution)/shard_map/ppermute | solution.py:119
  28.0 1.6 %collective-permute-start.11 = (bf16[144,128]{1,0:T(8,128)(2,1)S(1)}, bf16[144,128]{1,0:T(8,128)(2,1)S(1)}, u32[]{:S(2)}, u32[]{:S(2)}) collective-permute-start(bf16[144,128]{1,0:T(8,128)(2,1)S(1)} %terms_col.1.refs_3_), channel_id=1, source_target_pairs={{0,2},{1,3},{2,0},{3,1},{4,6},{5,7},{6,4},{7,5},{8,10},{9,11},{10,... | collective-permute-start | bytes 110600 | tf_op jit(solution)/shard_map/ppermute | solution.py:119
  29.6 0.7 %backward_near.1.refs_2_ = f32[2048,128]{1,0:T(8,128)S(1)} custom-call(bf16[2048,1024]{1,0:T(8,128)(2,1)S(1)} %build_rest.1.block_ref, bf16[256,128]{1,0:T(8,128)(2,1)S(1)} %get-tuple-element.64.refs_0_, bf16[400,128]{1,0:T(8,128)(2,1)S(1)} %collective-permute-done.8.refs_1_), custom_call_target="tpu_custom_call" | custom-call | tf_op jit(solution)/shard_map/backward_near/pallas_call | solution.py:390
  30.3 1.7 %collective-permute-done.10.refs_1_ = bf16[256,128]{1,0:T(8,128)(2,1)S(1)} collective-permute-done((bf16[256,128]{1,0:T(8,128)(2,1)S(1)}, bf16[256,128]{1,0:T(8,128)(2,1)S(1)}, u32[]{:S(2)}, u32[]{:S(2)}) %collective-permute-start.10) | collective-permute-done | bytes 65568 | tf_op jit(solution)/shard_map/ppermute | solution.py:119
  32.0 1.1 %collective-permute-done.11.refs_4_ = bf16[144,128]{1,0:T(8,128)(2,1)S(1)} collective-permute-done((bf16[144,128]{1,0:T(8,128)(2,1)S(1)}, bf16[144,128]{1,0:T(8,128)(2,1)S(1)}, u32[]{:S(2)}, u32[]{:S(2)}) %collective-permute-start.11) | collective-permute-done | bytes 36896 | tf_op jit(solution)/shard_map/ppermute | solution.py:119
  33.8 0.6 %collective-permute-start.12 = (bf16[512,128]{1,0:T(8,128)(2,1)S(1)}, bf16[512,128]{1,0:T(8,128)(2,1)S(1)}, u32[]{:S(2)}, u32[]{:S(2)}) collective-permute-start(bf16[512,128]{1,0:T(8,128)(2,1)S(1)} %backward_rest.1), channel_id=1, source_target_pairs={{0,4},{4,0},{8,12},{12,8},{16,20},{20,16},{24,28},{28,24},{1,5},{5... | collective-permute-start | bytes 393224 | tf_op jit(solution)/shard_map/ppermute | solution.py:119
  34.9 2.1 %collective-permute-start.14 = (bf16[400,128]{1,0:T(8,128)(2,1)S(1)}, bf16[400,128]{1,0:T(8,128)(2,1)S(1)}, u32[]{:S(2)}, u32[]{:S(2)}) collective-permute-start(bf16[400,128]{1,0:T(8,128)(2,1)S(1)} %get-tuple-element.72), channel_id=1, source_target_pairs={{0,24},{4,28},{8,16},{12,20},{16,8},{20,12},{24,0},{28,4},{1,25},{... | collective-permute-start | bytes 307208 | tf_op jit(solution)/shard_map/ppermute | solution.py:119
  37.6 1.0 %collective-permute-start.16 = (bf16[400,128]{1,0:T(8,128)(2,1)S(1)}, bf16[400,128]{1,0:T(8,128)(2,1)S(1)}, u32[]{:S(2)}, u32[]{:S(2)}) collective-permute-start(bf16[400,128]{1,0:T(8,128)(2,1)S(1)} %get-tuple-element.74), channel_id=1, source_target_pairs={{0,8},{4,12},{8,0},{12,4},{16,24},{20,28},{24,16},{28,20},{1,9},{5... | collective-permute-start | bytes 307208 | tf_op jit(solution)/shard_map/ppermute | solution.py:119
  38.6 0.9 %hidden_step.1 = bf16[256,128]{1,0:T(8,128)(2,1)} custom-call(bf16[128,128]{1,0:T(8,128)(2,1)S(1)} %get-tuple-element.53.turned_ref, f32[128,128]{1,0:T(8,128)S(1)} %get-tuple-element.54.bias_ref, bf16[128,256]{1,0:T(8,128)(2,1)S(1)} %get-tuple-element.62.aggregate_ref), custom_call_target="tpu_custom_call" | custom-call | tf_op jit(solution)/shard_map/hidden_step/pallas_call | solution.py:345
  39.4 1.5 %collective-permute-done.14.refs_1_ = bf16[400,128]{1,0:T(8,128)(2,1)S(1)} collective-permute-done((bf16[400,128]{1,0:T(8,128)(2,1)S(1)}, bf16[400,128]{1,0:T(8,128)(2,1)S(1)}, u32[]{:S(2)}, u32[]{:S(2)}) %collective-permute-start.14) | collective-permute-done | bytes 102432 | tf_op jit(solution)/shard_map/ppermute | solution.py:119
  40.9 2.1 %collective-permute-done.15.refs_2_ = bf16[400,128]{1,0:T(8,128)(2,1)S(1)} collective-permute-done((bf16[400,128]{1,0:T(8,128)(2,1)S(1)}, bf16[400,128]{1,0:T(8,128)(2,1)S(1)}, u32[]{:S(2)}, u32[]{:S(2)}) %collective-permute-start.15) | collective-permute-done | bytes 102432 | tf_op jit(solution)/shard_map/ppermute | solution.py:119
  43.1 0.7 %finish.1 = (bf16[256,128]{1,0:T(8,128)(2,1)}, f32[128,128]{1,0:T(8,128)}, f32[1,128]{1,0:T(1,128)}) custom-call(f32[256,128]{1,0:T(8,128)S(1)} %get-tuple-element.63.root_ref, bf16[400,128]{1,0:T(8,128)(2,1)S(1)} %get-tuple-element.71.refs_0_, bf16[400,128]{1,0:T(8,128)(2,1)S(1)} %collective-permute-done.14.refs_1_, ...), custom_call_target="tpu_custom_call" | custom-call | tf_op jit(solution)/shard_map/finish/pallas_call | solution.py:435
  (35 shorter events, 5.1 us)
Async XLA Ops:
  1.7 7.9 %collective-permute-start = (bf16[128,256]{1,0:T(8,128)(2,1)S(1)}, bf16[128,256]{1,0:T(8,128)(2,1)S(1)}, u32[]{:S(2)}, u32[]{:S(2)}) collective-permute-start(bf16[128,256]{1,0:T(8,128)(2,1)S(1)} %get-tuple-element.43.refs_0_), channel_id=1, source_target_pairs={{0,24},{4,28},{8,16},{12,20},{16,8},{20,12},{24,0},{28,4},{1,25},{... | collective-permute-start | bytes 196616 | tf_op jit(solution)/shard_map/ppermute | solution.py:119
  5.6 4.3 %collective-permute-start.1 = (bf16[128,256]{1,0:T(8,128)(2,1)S(1)}, bf16[128,256]{1,0:T(8,128)(2,1)S(1)}, u32[]{:S(2)}, u32[]{:S(2)}) collective-permute-start(bf16[128,256]{1,0:T(8,128)(2,1)S(1)} %get-tuple-element.43.refs_0_), channel_id=1, source_target_pairs={{0,16},{4,20},{8,24},{12,28},{16,0},{20,4},{24,8},{28,12},{1,17},{... | collective-permute-start | bytes 196616 | tf_op jit(solution)/shard_map/ppermute | solution.py:119
  6.1 4.3 %collective-permute-start.2 = (bf16[128,256]{1,0:T(8,128)(2,1)S(1)}, bf16[128,256]{1,0:T(8,128)(2,1)S(1)}, u32[]{:S(2)}, u32[]{:S(2)}) collective-permute-start(bf16[128,256]{1,0:T(8,128)(2,1)S(1)} %get-tuple-element.43.refs_0_), channel_id=1, source_target_pairs={{0,8},{4,12},{8,0},{12,4},{16,24},{20,28},{24,16},{28,20},{1,9},{5... | collective-permute-start | bytes 196616 | tf_op jit(solution)/shard_map/ppermute | solution.py:119
  10.4 1.9 %collective-permute-start.4 = (bf16[384,256]{1,0:T(8,128)(2,1)S(1)}, bf16[384,256]{1,0:T(8,128)(2,1)S(1)}, u32[]{:S(2)}, u32[]{:S(2)}) collective-permute-start(bf16[384,256]{1,0:T(8,128)(2,1)S(1)} %stack.1), channel_id=1, source_target_pairs={{0,4},{4,0},{8,12},{12,8},{16,20},{20,16},{24,28},{28,24},{1,5},{5... | collective-permute-start | bytes 589832 | tf_op jit(solution)/shard_map/ppermute | solution.py:119
  10.5 1.8 %collective-permute-start.3 = (bf16[128,256]{1,0:T(8,128)(2,1)S(1)}, bf16[128,256]{1,0:T(8,128)(2,1)S(1)}, u32[]{:S(2)}, u32[]{:S(2)}) collective-permute-start(bf16[128,256]{1,0:T(8,128)(2,1)S(1)} %get-tuple-element.43.refs_0_), channel_id=1, source_target_pairs={{0,4},{4,0},{8,12},{12,8},{16,20},{20,16},{24,28},{28,24},{1,5},{5... | collective-permute-start | bytes 196616 | tf_op jit(solution)/shard_map/ppermute | solution.py:119
  12.3 5.6 %copy-start = (bf16[128,128]{1,0:T(8,128)(2,1)S(1)}, bf16[128,128]{1,0:T(8,128)(2,1)}, u32[]{:S(2)}) copy-start(bf16[128,128]{1,0:T(8,128)(2,1)} %weight_ref.2) | copy-start | bytes 98308
  12.3 5.6 %copy-start.1 = (bf16[256,128]{1,0:T(8,128)(2,1)S(1)}, bf16[256,128]{1,0:T(8,128)(2,1)}, u32[]{:S(2)}) copy-start(bf16[256,128]{1,0:T(8,128)(2,1)} %cot_ref) | copy-start | bytes 196612
  12.3 5.6 %copy-start.2 = (s32[256]{0:T(256)S(1)}, s32[256]{0:T(256)}, u32[]{:S(2)}) copy-start(s32[256]{0:T(256)} %param.10) | copy-start | bytes 3076
  12.3 5.6 %copy-start.3 = (f32[128]{0:T(128)S(1)}, f32[128]{0:T(128)}, u32[]{:S(2)}) copy-start(f32[128]{0:T(128)} %param.12) | copy-start | bytes 1540
  12.9 6.5 %collective-permute-start.5 = (bf16[128,256]{1,0:T(8,128)(2,1)S(1)}, bf16[128,256]{1,0:T(8,128)(2,1)S(1)}, u32[]{:S(2)}, u32[]{:S(2)}) collective-permute-start(bf16[128,256]{1,0:T(8,128)(2,1)S(1)} %get-tuple-element.57), channel_id=1, source_target_pairs={{0,3},{1,2},{2,1},{3,0},{4,7},{5,6},{6,5},{7,4},{8,11},{9,10},{10,... | collective-permute-start | bytes 196616 | tf_op jit(solution)/shard_map/ppermute | solution.py:119
  16.5 5.9 %collective-permute-start.6 = (bf16[128,256]{1,0:T(8,128)(2,1)S(1)}, bf16[128,256]{1,0:T(8,128)(2,1)S(1)}, u32[]{:S(2)}, u32[]{:S(2)}) collective-permute-start(bf16[128,256]{1,0:T(8,128)(2,1)S(1)} %get-tuple-element.58), channel_id=1, source_target_pairs={{0,2},{1,3},{2,0},{3,1},{4,6},{5,7},{6,4},{7,5},{8,10},{9,11},{10,... | collective-permute-start | bytes 196616 | tf_op jit(solution)/shard_map/ppermute | solution.py:119
  17.0 5.7 %collective-permute-start.7 = (bf16[128,256]{1,0:T(8,128)(2,1)S(1)}, bf16[128,256]{1,0:T(8,128)(2,1)S(1)}, u32[]{:S(2)}, u32[]{:S(2)}) collective-permute-start(bf16[128,256]{1,0:T(8,128)(2,1)S(1)} %get-tuple-element.59), channel_id=1, source_target_pairs={{0,1},{1,0},{2,3},{3,2},{4,5},{5,4},{6,7},{7,6},{8,9},{9,8},{10,11... | collective-permute-start | bytes 196616 | tf_op jit(solution)/shard_map/ppermute | solution.py:119
  23.0 4.9 %collective-permute-start.8 = (bf16[400,128]{1,0:T(8,128)(2,1)S(1)}, bf16[400,128]{1,0:T(8,128)(2,1)S(1)}, u32[]{:S(2)}, u32[]{:S(2)}) collective-permute-start(bf16[400,128]{1,0:T(8,128)(2,1)S(1)} %get-tuple-element.60.refs_0_), channel_id=1, source_target_pairs={{0,1},{1,0},{2,3},{3,2},{4,5},{5,4},{6,7},{7,6},{8,9},{9,8},{10,11... | collective-permute-start | bytes 307208 | tf_op jit(solution)/shard_map/ppermute | solution.py:119
  23.9 6.4 %collective-permute-start.9 = (bf16[256,128]{1,0:T(8,128)(2,1)S(1)}, bf16[256,128]{1,0:T(8,128)(2,1)S(1)}, u32[]{:S(2)}, u32[]{:S(2)}) collective-permute-start(bf16[256,128]{1,0:T(8,128)(2,1)S(1)} %get-tuple-element.64.refs_0_), channel_id=1, source_target_pairs={{0,2},{1,3},{2,0},{3,1},{4,6},{5,7},{6,4},{7,5},{8,10},{9,11},{10,... | collective-permute-start | bytes 196616 | tf_op jit(solution)/shard_map/ppermute | solution.py:119
  25.9 6.1 %collective-permute-start.10 = (bf16[256,128]{1,0:T(8,128)(2,1)S(1)}, bf16[256,128]{1,0:T(8,128)(2,1)S(1)}, u32[]{:S(2)}, u32[]{:S(2)}) collective-permute-start(bf16[256,128]{1,0:T(8,128)(2,1)S(1)} %get-tuple-element.64.refs_0_), channel_id=1, source_target_pairs={{0,3},{1,2},{2,1},{3,0},{4,7},{5,6},{6,5},{7,4},{8,11},{9,10},{10,... | collective-permute-start | bytes 196616 | tf_op jit(solution)/shard_map/ppermute | solution.py:119
  28.0 5.1 %collective-permute-start.11 = (bf16[144,128]{1,0:T(8,128)(2,1)S(1)}, bf16[144,128]{1,0:T(8,128)(2,1)S(1)}, u32[]{:S(2)}, u32[]{:S(2)}) collective-permute-start(bf16[144,128]{1,0:T(8,128)(2,1)S(1)} %terms_col.1.refs_3_), channel_id=1, source_target_pairs={{0,2},{1,3},{2,0},{3,1},{4,6},{5,7},{6,4},{7,5},{8,10},{9,11},{10,... | collective-permute-start | bytes 110600 | tf_op jit(solution)/shard_map/ppermute | solution.py:119
  33.4 1.5 %collective-permute-start.13 = (bf16[656,128]{1,0:T(8,128)(2,1)S(1)}, bf16[656,128]{1,0:T(8,128)(2,1)S(1)}, u32[]{:S(2)}, u32[]{:S(2)}) collective-permute-start(bf16[656,128]{1,0:T(8,128)(2,1)S(1)} %backward_other.1.sent_ref), channel_id=1, source_target_pairs={{0,4},{4,0},{8,12},{12,8},{16,20},{20,16},{24,28},{28,24},{1,5},{5... | collective-permute-start | bytes 503816 | tf_op jit(solution)/shard_map/ppermute | solution.py:119
  33.8 3.8 %collective-permute-start.12 = (bf16[512,128]{1,0:T(8,128)(2,1)S(1)}, bf16[512,128]{1,0:T(8,128)(2,1)S(1)}, u32[]{:S(2)}, u32[]{:S(2)}) collective-permute-start(bf16[512,128]{1,0:T(8,128)(2,1)S(1)} %backward_rest.1), channel_id=1, source_target_pairs={{0,4},{4,0},{8,12},{12,8},{16,20},{20,16},{24,28},{28,24},{1,5},{5... | collective-permute-start | bytes 393224 | tf_op jit(solution)/shard_map/ppermute | solution.py:119
  34.9 6.0 %collective-permute-start.14 = (bf16[400,128]{1,0:T(8,128)(2,1)S(1)}, bf16[400,128]{1,0:T(8,128)(2,1)S(1)}, u32[]{:S(2)}, u32[]{:S(2)}) collective-permute-start(bf16[400,128]{1,0:T(8,128)(2,1)S(1)} %get-tuple-element.72), channel_id=1, source_target_pairs={{0,24},{4,28},{8,16},{12,20},{16,8},{20,12},{24,0},{28,4},{1,25},{... | collective-permute-start | bytes 307208 | tf_op jit(solution)/shard_map/ppermute | solution.py:119
  37.0 6.0 %collective-permute-start.15 = (bf16[400,128]{1,0:T(8,128)(2,1)S(1)}, bf16[400,128]{1,0:T(8,128)(2,1)S(1)}, u32[]{:S(2)}, u32[]{:S(2)}) collective-permute-start(bf16[400,128]{1,0:T(8,128)(2,1)S(1)} %get-tuple-element.73), channel_id=1, source_target_pairs={{0,16},{4,20},{8,24},{12,28},{16,0},{20,4},{24,8},{28,12},{1,17},{... | collective-permute-start | bytes 307208 | tf_op jit(solution)/shard_map/ppermute | solution.py:119
  37.6 5.5 %collective-permute-start.16 = (bf16[400,128]{1,0:T(8,128)(2,1)S(1)}, bf16[400,128]{1,0:T(8,128)(2,1)S(1)}, u32[]{:S(2)}, u32[]{:S(2)}) collective-permute-start(bf16[400,128]{1,0:T(8,128)(2,1)S(1)} %get-tuple-element.74), channel_id=1, source_target_pairs={{0,8},{4,12},{8,0},{12,4},{16,24},{20,28},{24,16},{28,20},{1,9},{5... | collective-permute-start | bytes 307208 | tf_op jit(solution)/shard_map/ppermute | solution.py:119

commit v7 on v6

--- a/solution.py
+++ b/solution.py
@@ -220,35 +220,34 @@
     )(*parts)
 
 
-def forward_kernel(bits, far, block_ref, *refs):
-    outs = refs[len(refs) - len(far) :]
-    parts = refs[: len(refs) - len(far)]
-    feat, pieces = parts[0].shape
+def forward_kernel(bits, high, block_ref, *refs):
+    *parts, even_ref, odd_ref, source = refs
+    feat, pieces = even_ref.shape
     me_row = lax.axis_index("row")
     me_col = lax.axis_index("col")
-    for out, k in zip(outs, far):
-        across = pl.ds(pl.multiple_of((me_col ^ k) * pieces, pieces), pieces)
-        total = jnp.zeros((feat, pieces), jnp.float32)
-        place = iter(bits)
-        for part in parts:
-            for m in range(part.shape[0] // feat):
-                down = pl.ds(pl.multiple_of((me_row ^ next(place)) * pieces, pieces), pieces)
-                total += jnp.dot(
-                    part[m * feat : (m + 1) * feat, :],
-                    block_ref[down, across],
-                    preferred_element_type=jnp.float32,
-                )
-        out[...] = total.astype(jnp.bfloat16)
-
-
-def forward_parts(block, parts, bits, far, name):
+    place = iter(bits)
+    for part in parts:
+        for m in range(part.shape[0] // feat):
+            at = pl.multiple_of((me_row ^ next(place)) * pieces, pieces)
+            source[:, pl.ds(at, pieces)] = part[m * feat : (m + 1) * feat, :]
+    across = pl.multiple_of((me_col ^ high) // 2 * (2 * pieces), 2 * pieces)
+    both = jnp.dot(
+        source[...], block_ref[:, pl.ds(across, 2 * pieces)], preferred_element_type=jnp.float32
+    ).astype(jnp.bfloat16)
+    first = me_col % 2 == 0
+    even_ref[...] = jnp.where(first, both[:, :pieces], both[:, pieces:])
+    odd_ref[...] = jnp.where(first, both[:, pieces:], both[:, :pieces])
+
+
+def forward_parts(block, parts, bits, high, name):
     feat, pieces = parts[0].shape
     vmem = pl.BlockSpec(memory_space=pltpu.VMEM)
     return pl.pallas_call(
-        functools.partial(forward_kernel, bits, far),
-        out_shape=[jax.ShapeDtypeStruct((feat, pieces), jnp.bfloat16)] * len(far),
+        functools.partial(forward_kernel, bits, high),
+        out_shape=[jax.ShapeDtypeStruct((feat, pieces), jnp.bfloat16)] * 2,
         in_specs=[vmem] * (1 + len(parts)),
-        out_specs=[vmem] * len(far),
+        out_specs=[vmem] * 2,
+        scratch_shapes=[pltpu.VMEM((feat, pieces * len(bits)), jnp.bfloat16)],
         compiler_params=pltpu.CompilerParams(vmem_limit_bytes=LIMIT),
         name=name,
     )(block, *parts)
@@ -535,10 +534,9 @@
     parts = [scaled, sibling, *landed, swap(stack(landed), "row", 1)]
     bits = [0, 1, *chips, *(m + 1 for m in chips)]
     block = build_block(lists, tile_count, codes, *size, middle, slots, block)
-    half = max(1, n_col // 2)
-    far = forward_parts(block, parts, bits, lines[:half], "forward_far")
-    near = forward_parts(block, parts, bits, lines[half:] + [0], "forward_near")
-    parts = dict(zip(lines + [0], [*far, *near]))
+    far = forward_parts(block, parts, bits, 2, "forward_far")
+    near = forward_parts(block, parts, bits, 0, "forward_near")
+    parts = [*near, *far]
     *dense, parts[0] = lax.optimization_barrier((weight, bias, cotangent, degree, parts[0]))
     *dense, root = turn(*dense)
     landed = [parts[0]] + [swap(parts[k], "col", k) for k in lines]

time: 44 us -> 44 us (level)
  no operation moved by 1% of the time
where the time goes in v7:
time: 44 us; the launch traced here: 43.8 us
  starting transfers between devices  20 us (45%)
  waiting for transfers between devices  12.5 us (28%)
  Pallas kernels  9.87 us (22%)
  between operations  1.46 us (3%)
    ppermute x17, starting transfers between devices, swap(): return lax.ppermute(value, axis, [(i, i ^ bits) for i in range(size)])  20 us
    ppermute x17, waiting for transfers between devices, swap(): return lax.ppermute(value, axis, [(i, i ^ bits) for i in range(size)])  12.5 us
    pallas_call x2, Pallas kernels, build_block(): pl.pallas_call(functools.partial(build_kernel, first, last), out_shape=pl...  3.9 us
    pallas_call x4, Pallas kernels, backward_parts(): pl.pallas_call(functools.partial(backward_kernel, pieces, kinds, chunks,...  1.72 us
    pallas_call x1, Pallas kernels, scale_rows(): pl.pallas_call(scale_kernel, out_shape=[pltpu.VMEM((feat, pieces), jnp.bf...  1.03 us
    pallas_call x2, Pallas kernels, forward_parts(): pl.pallas_call(functools.partial(forward_kernel, bits, high), out_shape=[...  1 us
  transfers between devices with their start and end apart: 17, of which 12 were waited for; matrix products, arithmetic and copies ran while one was open for 0% of the time, Pallas kernels for 16%

profile of v7, /device:TPU:0, one launch (start us, length us, event | category | flops | bytes accessed | tf_op | source)
XLA Modules:
  0.0 43.8 jit_solution(12814399971123618009)
XLA Ops:
  0.6 1.0 %scale_rows.1 = (bf16[128,256]{1,0:T(8,128)(2,1)S(1)}, s32[8,128]{1,0:T(8,128)S(1)}, s32[128,256]{1,0:T(8,128)S(1)}) custom-call(s32[1,256]{1,0:T(1,128)} %bitcast.5, bf16[256,128]{1,0:T(8,128)(2,1)} %features_hbm.1, s32[1,1,128]{2,1,0:T(1,128)} %rows_hbm.1, s32[1,1,128]{2,1,0:T(1,128)} %cols_hbm.1, s32[128,256]{1,0:T(8,128)} %bitcast.9), custom_call_target="tpu_custom_call" | custom-call | tf_op jit(solution)/shard_map/scale_rows/pallas_call | solution.py:475
  1.7 4.0 %collective-permute-start = (bf16[128,256]{1,0:T(8,128)(2,1)S(1)}, bf16[128,256]{1,0:T(8,128)(2,1)S(1)}, u32[]{:S(2)}, u32[]{:S(2)}) collective-permute-start(bf16[128,256]{1,0:T(8,128)(2,1)S(1)} %get-tuple-element.43.refs_0_), channel_id=1, source_target_pairs={{0,24},{4,28},{8,16},{12,20},{16,8},{20,12},{24,0},{28,4},{1,25},{... | collective-permute-start | bytes 196616 | tf_op jit(solution)/shard_map/ppermute | solution.py:119
  5.6 0.5 %collective-permute-start.1 = (bf16[128,256]{1,0:T(8,128)(2,1)S(1)}, bf16[128,256]{1,0:T(8,128)(2,1)S(1)}, u32[]{:S(2)}, u32[]{:S(2)}) collective-permute-start(bf16[128,256]{1,0:T(8,128)(2,1)S(1)} %get-tuple-element.43.refs_0_), channel_id=1, source_target_pairs={{0,16},{4,20},{8,24},{12,28},{16,0},{20,4},{24,8},{28,12},{1,17},{... | collective-permute-start | bytes 196616 | tf_op jit(solution)/shard_map/ppermute | solution.py:119
  6.9 2.6 %build_block.1.refs_0_ = bf16[2048,1024]{1,0:T(8,128)(2,1)S(1)} custom-call(s32[8,128]{1,0:T(8,128)S(1)} %get-tuple-element.41.lists_vmem, s32[1,1,1]{2,1,0:T(1,128)S(6)} %copy.15.count_ref, s32[128,256]{1,0:T(8,128)S(1)} %get-tuple-element.42.codes_ref), custom_call_target="tpu_custom_call" | custom-call | flops 31457280 | bytes 8388608 | tf_op jit(solution)/shard_map/build_block/pallas_call | solution.py:183
  11.0 1.3 %build_rest.1.block_ref = bf16[2048,1024]{1,0:T(8,128)(2,1)S(1)} custom-call(s32[8,128]{1,0:T(8,128)S(1)} %get-tuple-element.41.lists_vmem, s32[1,1,1]{2,1,0:T(1,128)S(6)} %copy.15.count_ref, s32[128,256]{1,0:T(8,128)S(1)} %get-tuple-element.42.codes_ref, bf16[2048,1024]{1,0:T(8,128)(2,1)S(1)} %build_block.1.refs_0_), custom_call_target="tpu_custom_call", output_to_operand_aliasing={{}: (3, {})} | custom-call | flops 10485760 | bytes 8388608 | tf_op jit(solution)/shard_map/build_rest/pallas_call | solution.py:183
  12.3 0.5 %forward_far.1 = (bf16[128,256]{1,0:T(8,128)(2,1)S(1)}, bf16[128,256]{1,0:T(8,128)(2,1)S(1)}) custom-call(bf16[2048,1024]{1,0:T(8,128)(2,1)S(1)} %build_rest.1.block_ref, bf16[128,256]{1,0:T(8,128)(2,1)S(1)} %get-tuple-element.43.refs_0_, bf16[128,256]{1,0:T(8,128)(2,1)S(1)} %collective-permute-done.3.refs_1_, ...), custom_call_target="tpu_custom_call" | custom-call | tf_op jit(solution)/shard_map/forward_far/pallas_call | solution.py:245
  12.9 3.7 %collective-permute-start.5 = (bf16[128,256]{1,0:T(8,128)(2,1)S(1)}, bf16[128,256]{1,0:T(8,128)(2,1)S(1)}, u32[]{:S(2)}, u32[]{:S(2)}) collective-permute-start(bf16[128,256]{1,0:T(8,128)(2,1)S(1)} %get-tuple-element.57), channel_id=1, source_target_pairs={{0,3},{1,2},{2,1},{3,0},{4,7},{5,6},{6,5},{7,4},{8,11},{9,10},{10,... | collective-permute-start | bytes 196616 | tf_op jit(solution)/shard_map/ppermute | solution.py:119
  17.0 0.9 %collective-permute-start.7 = (bf16[128,256]{1,0:T(8,128)(2,1)S(1)}, bf16[128,256]{1,0:T(8,128)(2,1)S(1)}, u32[]{:S(2)}, u32[]{:S(2)}) collective-permute-start(bf16[128,256]{1,0:T(8,128)(2,1)S(1)} %get-tuple-element.59), channel_id=1, source_target_pairs={{0,1},{1,0},{2,3},{3,2},{4,5},{5,4},{6,7},{7,6},{8,9},{9,8},{10,11... | collective-permute-start | bytes 196616 | tf_op jit(solution)/shard_map/ppermute | solution.py:119
  18.1 1.2 %collective-permute-done.5.refs_1_ = bf16[128,256]{1,0:T(8,128)(2,1)S(1)} collective-permute-done((bf16[128,256]{1,0:T(8,128)(2,1)S(1)}, bf16[128,256]{1,0:T(8,128)(2,1)S(1)}, u32[]{:S(2)}, u32[]{:S(2)}) %collective-permute-start.5) | collective-permute-done | bytes 65568 | tf_op jit(solution)/shard_map/ppermute | solution.py:119
  19.3 3.2 %collective-permute-done.6.refs_2_ = bf16[128,256]{1,0:T(8,128)(2,1)S(1)} collective-permute-done((bf16[128,256]{1,0:T(8,128)(2,1)S(1)}, bf16[128,256]{1,0:T(8,128)(2,1)S(1)}, u32[]{:S(2)}, u32[]{:S(2)}) %collective-permute-start.6) | collective-permute-done | bytes 65568 | tf_op jit(solution)/shard_map/ppermute | solution.py:119
  23.1 0.8 %collective-permute-start.8 = (bf16[400,128]{1,0:T(8,128)(2,1)S(1)}, bf16[400,128]{1,0:T(8,128)(2,1)S(1)}, u32[]{:S(2)}, u32[]{:S(2)}) collective-permute-start(bf16[400,128]{1,0:T(8,128)(2,1)S(1)} %get-tuple-element.60.refs_0_), channel_id=1, source_target_pairs={{0,1},{1,0},{2,3},{3,2},{4,5},{5,4},{6,7},{7,6},{8,9},{9,8},{10,11... | collective-permute-start | bytes 307208 | tf_op jit(solution)/shard_map/ppermute | solution.py:119
  23.9 2.0 %collective-permute-start.9 = (bf16[256,128]{1,0:T(8,128)(2,1)S(1)}, bf16[256,128]{1,0:T(8,128)(2,1)S(1)}, u32[]{:S(2)}, u32[]{:S(2)}) collective-permute-start(bf16[256,128]{1,0:T(8,128)(2,1)S(1)} %get-tuple-element.64.refs_0_), channel_id=1, source_target_pairs={{0,2},{1,3},{2,0},{3,1},{4,6},{5,7},{6,4},{7,5},{8,10},{9,11},{10,... | collective-permute-start | bytes 196616 | tf_op jit(solution)/shard_map/ppermute | solution.py:119
  26.0 1.6 %collective-permute-start.10 = (bf16[256,128]{1,0:T(8,128)(2,1)S(1)}, bf16[256,128]{1,0:T(8,128)(2,1)S(1)}, u32[]{:S(2)}, u32[]{:S(2)}) collective-permute-start(bf16[256,128]{1,0:T(8,128)(2,1)S(1)} %get-tuple-element.64.refs_0_), channel_id=1, source_target_pairs={{0,3},{1,2},{2,1},{3,0},{4,7},{5,6},{6,5},{7,4},{8,11},{9,10},{10,... | collective-permute-start | bytes 196616 | tf_op jit(solution)/shard_map/ppermute | solution.py:119
  28.0 1.6 %collective-permute-start.11 = (bf16[144,128]{1,0:T(8,128)(2,1)S(1)}, bf16[144,128]{1,0:T(8,128)(2,1)S(1)}, u32[]{:S(2)}, u32[]{:S(2)}) collective-permute-start(bf16[144,128]{1,0:T(8,128)(2,1)S(1)} %terms_col.1.refs_3_), channel_id=1, source_target_pairs={{0,2},{1,3},{2,0},{3,1},{4,6},{5,7},{6,4},{7,5},{8,10},{9,11},{10,... | collective-permute-start | bytes 110600 | tf_op jit(solution)/shard_map/ppermute | solution.py:119
  29.6 0.7 %backward_near.1.refs_2_ = f32[2048,128]{1,0:T(8,128)S(1)} custom-call(bf16[2048,1024]{1,0:T(8,128)(2,1)S(1)} %build_rest.1.block_ref, bf16[256,128]{1,0:T(8,128)(2,1)S(1)} %get-tuple-element.64.refs_0_, bf16[400,128]{1,0:T(8,128)(2,1)S(1)} %collective-permute-done.8.refs_1_), custom_call_target="tpu_custom_call" | custom-call | tf_op jit(solution)/shard_map/backward_near/pallas_call | solution.py:389
  30.4 1.7 %collective-permute-done.10.refs_1_ = bf16[256,128]{1,0:T(8,128)(2,1)S(1)} collective-permute-done((bf16[256,128]{1,0:T(8,128)(2,1)S(1)}, bf16[256,128]{1,0:T(8,128)(2,1)S(1)}, u32[]{:S(2)}, u32[]{:S(2)}) %collective-permute-start.10) | collective-permute-done | bytes 65568 | tf_op jit(solution)/shard_map/ppermute | solution.py:119
  32.0 1.1 %collective-permute-done.11.refs_4_ = bf16[144,128]{1,0:T(8,128)(2,1)S(1)} collective-permute-done((bf16[144,128]{1,0:T(8,128)(2,1)S(1)}, bf16[144,128]{1,0:T(8,128)(2,1)S(1)}, u32[]{:S(2)}, u32[]{:S(2)}) %collective-permute-start.11) | collective-permute-done | bytes 36896 | tf_op jit(solution)/shard_map/ppermute | solution.py:119
  33.8 0.6 %collective-permute-start.12 = (bf16[512,128]{1,0:T(8,128)(2,1)S(1)}, bf16[512,128]{1,0:T(8,128)(2,1)S(1)}, u32[]{:S(2)}, u32[]{:S(2)}) collective-permute-start(bf16[512,128]{1,0:T(8,128)(2,1)S(1)} %backward_rest.1), channel_id=1, source_target_pairs={{0,4},{4,0},{8,12},{12,8},{16,20},{20,16},{24,28},{28,24},{1,5},{5... | collective-permute-start | bytes 393224 | tf_op jit(solution)/shard_map/ppermute | solution.py:119
  34.9 2.1 %collective-permute-start.14 = (bf16[400,128]{1,0:T(8,128)(2,1)S(1)}, bf16[400,128]{1,0:T(8,128)(2,1)S(1)}, u32[]{:S(2)}, u32[]{:S(2)}) collective-permute-start(bf16[400,128]{1,0:T(8,128)(2,1)S(1)} %get-tuple-element.72), channel_id=1, source_target_pairs={{0,24},{4,28},{8,16},{12,20},{16,8},{20,12},{24,0},{28,4},{1,25},{... | collective-permute-start | bytes 307208 | tf_op jit(solution)/shard_map/ppermute | solution.py:119
  37.6 1.0 %collective-permute-start.16 = (bf16[400,128]{1,0:T(8,128)(2,1)S(1)}, bf16[400,128]{1,0:T(8,128)(2,1)S(1)}, u32[]{:S(2)}, u32[]{:S(2)}) collective-permute-start(bf16[400,128]{1,0:T(8,128)(2,1)S(1)} %get-tuple-element.74), channel_id=1, source_target_pairs={{0,8},{4,12},{8,0},{12,4},{16,24},{20,28},{24,16},{28,20},{1,9},{5... | collective-permute-start | bytes 307208 | tf_op jit(solution)/shard_map/ppermute | solution.py:119
  38.6 0.9 %hidden_step.1 = bf16[256,128]{1,0:T(8,128)(2,1)} custom-call(bf16[128,128]{1,0:T(8,128)(2,1)S(1)} %get-tuple-element.53.turned_ref, f32[128,128]{1,0:T(8,128)S(1)} %get-tuple-element.54.bias_ref, bf16[128,256]{1,0:T(8,128)(2,1)S(1)} %get-tuple-element.62.aggregate_ref), custom_call_target="tpu_custom_call" | custom-call | tf_op jit(solution)/shard_map/hidden_step/pallas_call | solution.py:344
  39.5 1.5 %collective-permute-done.14.refs_1_ = bf16[400,128]{1,0:T(8,128)(2,1)S(1)} collective-permute-done((bf16[400,128]{1,0:T(8,128)(2,1)S(1)}, bf16[400,128]{1,0:T(8,128)(2,1)S(1)}, u32[]{:S(2)}, u32[]{:S(2)}) %collective-permute-start.14) | collective-permute-done | bytes 102432 | tf_op jit(solution)/shard_map/ppermute | solution.py:119
  40.9 2.1 %collective-permute-done.15.refs_2_ = bf16[400,128]{1,0:T(8,128)(2,1)S(1)} collective-permute-done((bf16[400,128]{1,0:T(8,128)(2,1)S(1)}, bf16[400,128]{1,0:T(8,128)(2,1)S(1)}, u32[]{:S(2)}, u32[]{:S(2)}) %collective-permute-start.15) | collective-permute-done | bytes 102432 | tf_op jit(solution)/shard_map/ppermute | solution.py:119
  43.1 0.7 %finish.1 = (bf16[256,128]{1,0:T(8,128)(2,1)}, f32[128,128]{1,0:T(8,128)}, f32[1,128]{1,0:T(1,128)}) custom-call(f32[256,128]{1,0:T(8,128)S(1)} %get-tuple-element.63.root_ref, bf16[400,128]{1,0:T(8,128)(2,1)S(1)} %get-tuple-element.71.refs_0_, bf16[400,128]{1,0:T(8,128)(2,1)S(1)} %collective-permute-done.14.refs_1_, ...), custom_call_target="tpu_custom_call" | custom-call | tf_op jit(solution)/shard_map/finish/pallas_call | solution.py:434
  (35 shorter events, 5.2 us)
Async XLA Ops:
  1.7 7.9 %collective-permute-start = (bf16[128,256]{1,0:T(8,128)(2,1)S(1)}, bf16[128,256]{1,0:T(8,128)(2,1)S(1)}, u32[]{:S(2)}, u32[]{:S(2)}) collective-permute-start(bf16[128,256]{1,0:T(8,128)(2,1)S(1)} %get-tuple-element.43.refs_0_), channel_id=1, source_target_pairs={{0,24},{4,28},{8,16},{12,20},{16,8},{20,12},{24,0},{28,4},{1,25},{... | collective-permute-start | bytes 196616 | tf_op jit(solution)/shard_map/ppermute | solution.py:119
  5.6 4.3 %collective-permute-start.1 = (bf16[128,256]{1,0:T(8,128)(2,1)S(1)}, bf16[128,256]{1,0:T(8,128)(2,1)S(1)}, u32[]{:S(2)}, u32[]{:S(2)}) collective-permute-start(bf16[128,256]{1,0:T(8,128)(2,1)S(1)} %get-tuple-element.43.refs_0_), channel_id=1, source_target_pairs={{0,16},{4,20},{8,24},{12,28},{16,0},{20,4},{24,8},{28,12},{1,17},{... | collective-permute-start | bytes 196616 | tf_op jit(solution)/shard_map/ppermute | solution.py:119
  6.1 4.3 %collective-permute-start.2 = (bf16[128,256]{1,0:T(8,128)(2,1)S(1)}, bf16[128,256]{1,0:T(8,128)(2,1)S(1)}, u32[]{:S(2)}, u32[]{:S(2)}) collective-permute-start(bf16[128,256]{1,0:T(8,128)(2,1)S(1)} %get-tuple-element.43.refs_0_), channel_id=1, source_target_pairs={{0,8},{4,12},{8,0},{12,4},{16,24},{20,28},{24,16},{28,20},{1,9},{5... | collective-permute-start | bytes 196616 | tf_op jit(solution)/shard_map/ppermute | solution.py:119
  10.4 1.9 %collective-permute-start.4 = (bf16[384,256]{1,0:T(8,128)(2,1)S(1)}, bf16[384,256]{1,0:T(8,128)(2,1)S(1)}, u32[]{:S(2)}, u32[]{:S(2)}) collective-permute-start(bf16[384,256]{1,0:T(8,128)(2,1)S(1)} %stack.1), channel_id=1, source_target_pairs={{0,4},{4,0},{8,12},{12,8},{16,20},{20,16},{24,28},{28,24},{1,5},{5... | collective-permute-start | bytes 589832 | tf_op jit(solution)/shard_map/ppermute | solution.py:119
  10.5 1.8 %collective-permute-start.3 = (bf16[128,256]{1,0:T(8,128)(2,1)S(1)}, bf16[128,256]{1,0:T(8,128)(2,1)S(1)}, u32[]{:S(2)}, u32[]{:S(2)}) collective-permute-start(bf16[128,256]{1,0:T(8,128)(2,1)S(1)} %get-tuple-element.43.refs_0_), channel_id=1, source_target_pairs={{0,4},{4,0},{8,12},{12,8},{16,20},{20,16},{24,28},{28,24},{1,5},{5... | collective-permute-start | bytes 196616 | tf_op jit(solution)/shard_map/ppermute | solution.py:119
  12.3 5.6 %copy-start = (bf16[128,128]{1,0:T(8,128)(2,1)S(1)}, bf16[128,128]{1,0:T(8,128)(2,1)}, u32[]{:S(2)}) copy-start(bf16[128,128]{1,0:T(8,128)(2,1)} %weight_ref.2) | copy-start | bytes 98308
  12.3 5.6 %copy-start.1 = (bf16[256,128]{1,0:T(8,128)(2,1)S(1)}, bf16[256,128]{1,0:T(8,128)(2,1)}, u32[]{:S(2)}) copy-start(bf16[256,128]{1,0:T(8,128)(2,1)} %cot_ref) | copy-start | bytes 196612
  12.3 5.6 %copy-start.2 = (s32[256]{0:T(256)S(1)}, s32[256]{0:T(256)}, u32[]{:S(2)}) copy-start(s32[256]{0:T(256)} %param.10) | copy-start | bytes 3076
  12.3 5.6 %copy-start.3 = (f32[128]{0:T(128)S(1)}, f32[128]{0:T(128)}, u32[]{:S(2)}) copy-start(f32[128]{0:T(128)} %param.12) | copy-start | bytes 1540
  12.9 6.4 %collective-permute-start.5 = (bf16[128,256]{1,0:T(8,128)(2,1)S(1)}, bf16[128,256]{1,0:T(8,128)(2,1)S(1)}, u32[]{:S(2)}, u32[]{:S(2)}) collective-permute-start(bf16[128,256]{1,0:T(8,128)(2,1)S(1)} %get-tuple-element.57), channel_id=1, source_target_pairs={{0,3},{1,2},{2,1},{3,0},{4,7},{5,6},{6,5},{7,4},{8,11},{9,10},{10,... | collective-permute-start | bytes 196616 | tf_op jit(solution)/shard_map/ppermute | solution.py:119
  16.5 6.0 %collective-permute-start.6 = (bf16[128,256]{1,0:T(8,128)(2,1)S(1)}, bf16[128,256]{1,0:T(8,128)(2,1)S(1)}, u32[]{:S(2)}, u32[]{:S(2)}) collective-permute-start(bf16[128,256]{1,0:T(8,128)(2,1)S(1)} %get-tuple-element.58), channel_id=1, source_target_pairs={{0,2},{1,3},{2,0},{3,1},{4,6},{5,7},{6,4},{7,5},{8,10},{9,11},{10,... | collective-permute-start | bytes 196616 | tf_op jit(solution)/shard_map/ppermute | solution.py:119
  17.0 5.7 %collective-permute-start.7 = (bf16[128,256]{1,0:T(8,128)(2,1)S(1)}, bf16[128,256]{1,0:T(8,128)(2,1)S(1)}, u32[]{:S(2)}, u32[]{:S(2)}) collective-permute-start(bf16[128,256]{1,0:T(8,128)(2,1)S(1)} %get-tuple-element.59), channel_id=1, source_target_pairs={{0,1},{1,0},{2,3},{3,2},{4,5},{5,4},{6,7},{7,6},{8,9},{9,8},{10,11... | collective-permute-start | bytes 196616 | tf_op jit(solution)/shard_map/ppermute | solution.py:119
  23.1 4.9 %collective-permute-start.8 = (bf16[400,128]{1,0:T(8,128)(2,1)S(1)}, bf16[400,128]{1,0:T(8,128)(2,1)S(1)}, u32[]{:S(2)}, u32[]{:S(2)}) collective-permute-start(bf16[400,128]{1,0:T(8,128)(2,1)S(1)} %get-tuple-element.60.refs_0_), channel_id=1, source_target_pairs={{0,1},{1,0},{2,3},{3,2},{4,5},{5,4},{6,7},{7,6},{8,9},{9,8},{10,11... | collective-permute-start | bytes 307208 | tf_op jit(solution)/shard_map/ppermute | solution.py:119
  23.9 6.4 %collective-permute-start.9 = (bf16[256,128]{1,0:T(8,128)(2,1)S(1)}, bf16[256,128]{1,0:T(8,128)(2,1)S(1)}, u32[]{:S(2)}, u32[]{:S(2)}) collective-permute-start(bf16[256,128]{1,0:T(8,128)(2,1)S(1)} %get-tuple-element.64.refs_0_), channel_id=1, source_target_pairs={{0,2},{1,3},{2,0},{3,1},{4,6},{5,7},{6,4},{7,5},{8,10},{9,11},{10,... | collective-permute-start | bytes 196616 | tf_op jit(solution)/shard_map/ppermute | solution.py:119
  26.0 6.1 %collective-permute-start.10 = (bf16[256,128]{1,0:T(8,128)(2,1)S(1)}, bf16[256,128]{1,0:T(8,128)(2,1)S(1)}, u32[]{:S(2)}, u32[]{:S(2)}) collective-permute-start(bf16[256,128]{1,0:T(8,128)(2,1)S(1)} %get-tuple-element.64.refs_0_), channel_id=1, source_target_pairs={{0,3},{1,2},{2,1},{3,0},{4,7},{5,6},{6,5},{7,4},{8,11},{9,10},{10,... | collective-permute-start | bytes 196616 | tf_op jit(solution)/shard_map/ppermute | solution.py:119
  28.0 5.1 %collective-permute-start.11 = (bf16[144,128]{1,0:T(8,128)(2,1)S(1)}, bf16[144,128]{1,0:T(8,128)(2,1)S(1)}, u32[]{:S(2)}, u32[]{:S(2)}) collective-permute-start(bf16[144,128]{1,0:T(8,128)(2,1)S(1)} %terms_col.1.refs_3_), channel_id=1, source_target_pairs={{0,2},{1,3},{2,0},{3,1},{4,6},{5,7},{6,4},{7,5},{8,10},{9,11},{10,... | collective-permute-start | bytes 110600 | tf_op jit(solution)/shard_map/ppermute | solution.py:119
  33.4 1.5 %collective-permute-start.13 = (bf16[656,128]{1,0:T(8,128)(2,1)S(1)}, bf16[656,128]{1,0:T(8,128)(2,1)S(1)}, u32[]{:S(2)}, u32[]{:S(2)}) collective-permute-start(bf16[656,128]{1,0:T(8,128)(2,1)S(1)} %backward_other.1.sent_ref), channel_id=1, source_target_pairs={{0,4},{4,0},{8,12},{12,8},{16,20},{20,16},{24,28},{28,24},{1,5},{5... | collective-permute-start | bytes 503816 | tf_op jit(solution)/shard_map/ppermute | solution.py:119
  33.8 3.7 %collective-permute-start.12 = (bf16[512,128]{1,0:T(8,128)(2,1)S(1)}, bf16[512,128]{1,0:T(8,128)(2,1)S(1)}, u32[]{:S(2)}, u32[]{:S(2)}) collective-permute-start(bf16[512,128]{1,0:T(8,128)(2,1)S(1)} %backward_rest.1), channel_id=1, source_target_pairs={{0,4},{4,0},{8,12},{12,8},{16,20},{20,16},{24,28},{28,24},{1,5},{5... | collective-permute-start | bytes 393224 | tf_op jit(solution)/shard_map/ppermute | solution.py:119
  34.9 6.0 %collective-permute-start.14 = (bf16[400,128]{1,0:T(8,128)(2,1)S(1)}, bf16[400,128]{1,0:T(8,128)(2,1)S(1)}, u32[]{:S(2)}, u32[]{:S(2)}) collective-permute-start(bf16[400,128]{1,0:T(8,128)(2,1)S(1)} %get-tuple-element.72), channel_id=1, source_target_pairs={{0,24},{4,28},{8,16},{12,20},{16,8},{20,12},{24,0},{28,4},{1,25},{... | collective-permute-start | bytes 307208 | tf_op jit(solution)/shard_map/ppermute | solution.py:119
  37.1 6.0 %collective-permute-start.15 = (bf16[400,128]{1,0:T(8,128)(2,1)S(1)}, bf16[400,128]{1,0:T(8,128)(2,1)S(1)}, u32[]{:S(2)}, u32[]{:S(2)}) collective-permute-start(bf16[400,128]{1,0:T(8,128)(2,1)S(1)} %get-tuple-element.73), channel_id=1, source_target_pairs={{0,16},{4,20},{8,24},{12,28},{16,0},{20,4},{24,8},{28,12},{1,17},{... | collective-permute-start | bytes 307208 | tf_op jit(solution)/shard_map/ppermute | solution.py:119
  37.6 5.6 %collective-permute-start.16 = (bf16[400,128]{1,0:T(8,128)(2,1)S(1)}, bf16[400,128]{1,0:T(8,128)(2,1)S(1)}, u32[]{:S(2)}, u32[]{:S(2)}) collective-permute-start(bf16[400,128]{1,0:T(8,128)(2,1)S(1)} %get-tuple-element.74), channel_id=1, source_target_pairs={{0,8},{4,12},{8,0},{12,4},{16,24},{20,28},{24,16},{28,20},{1,9},{5... | collective-permute-start | bytes 307208 | tf_op jit(solution)/shard_map/ppermute | solution.py:119

commit v8 on v6

--- a/solution.py
+++ b/solution.py
@@ -398,7 +398,7 @@
 
 
 def pair_kernel(first, mine_ref, theirs_ref, sent_ref, got_ref, *outs):
-    feat = mine_ref.shape[0] // 4
+    feat = mine_ref.shape[0] // 2
     terms = sum_of((sent_ref.at[2 * feat :], got_ref.at[2 * feat :])).astype(jnp.bfloat16)
     for m, out in enumerate(outs):
         mine = mine_ref[(first + m) * feat : (first + m + 1) * feat, :].astype(jnp.float32)
@@ -409,7 +409,7 @@
 
 def pair_sum(first, mine, theirs, sent, got):
     vmem = pl.BlockSpec(memory_space=pltpu.VMEM)
-    rows = sent.shape[0] - mine.shape[0] // 4
+    rows = sent.shape[0] - mine.shape[0] // 2
     return pl.pallas_call(
         functools.partial(pair_kernel, first),
         out_shape=[jax.ShapeDtypeStruct((rows, mine.shape[1]), jnp.bfloat16)] * 2,
@@ -554,10 +554,11 @@
     sent = backward_parts(block, grads, far, [7, 5], begun, terms, "backward_other")
     got = swap(sent, "row", 1)
     rest = swap(backward_parts(block, grads, far, [3, 1], begun, [], "backward_rest"), "row", 1)
-    mine = backward_parts(block, grads, far, [6, 4, 2, 0], begun, [], "backward_own")
+    mine = backward_parts(block, grads, far, [6, 4], begun, [], "backward_own")
     chunks = pair_sum(0, mine, got, sent, got)
     landed = [swap(chunk, "row", m) for chunk, m in zip(chunks, chips)]
-    chunks = pair_sum(2, mine, rest, sent, got)
+    mine = backward_parts(block, grads, far, [2, 0], begun, [], "backward_last")
+    chunks = pair_sum(0, mine, rest, sent, got)
     landed = [chunks[1], *landed, swap(chunks[0], "row", chips[2])]
     grad_features, grad_weight, grad_bias = finish(root, landed, grad_scale)
     return (hidden, grad_features, grad_weight, grad_bias)

time: 44 us -> 44 us (level)
    pallas_call x4 -> x5, Pallas kernels: 1.72 us -> 1.87 us  [backward_parts(): pl.pallas_call(functools.partial(backward_kernel, pieces, kinds, chunks,...]
  transfers between devices with their start and end apart: 17 -> 17, of which waited for: 12 -> 11; matrix products, arithmetic and copies ran while one was open for 0% -> 0% of each run, Pallas kernels for 16% -> 16%
where the time goes in v8:
time: 44 us; the launch traced here: 43.8 us
  starting transfers between devices  20 us (45%)
  waiting for transfers between devices  12.3 us (28%)
  Pallas kernels  9.99 us (23%)
  between operations  1.48 us (3%)
    ppermute x17, starting transfers between devices, swap(): return lax.ppermute(value, axis, [(i, i ^ bits) for i in range(size)])  20 us
    ppermute x17, waiting for transfers between devices, swap(): return lax.ppermute(value, axis, [(i, i ^ bits) for i in range(size)])  12.3 us
    pallas_call x2, Pallas kernels, build_block(): pl.pallas_call(functools.partial(build_kernel, first, last), out_shape=pl...  3.91 us
    pallas_call x5, Pallas kernels, backward_parts(): pl.pallas_call(functools.partial(backward_kernel, pieces, kinds, chunks,...  1.87 us
    pallas_call x1, Pallas kernels, scale_rows(): pl.pallas_call(scale_kernel, out_shape=[pltpu.VMEM((feat, pieces), jnp.bf...  1.03 us
    pallas_call x2, Pallas kernels, forward_parts(): pl.pallas_call(functools.partial(forward_kernel, bits, far), out_shape=[j...  0.96 us
  transfers between devices with their start and end apart: 17, of which 11 were waited for; matrix products, arithmetic and copies ran while one was open for 0% of the time, Pallas kernels for 16%

profile of v8, /device:TPU:0, one launch (start us, length us, event | category | flops | bytes accessed | tf_op | source)
XLA Modules:
  0.0 43.8 jit_solution(10877971058574712072)
XLA Ops:
  0.6 1.0 %scale_rows.1 = (bf16[128,256]{1,0:T(8,128)(2,1)S(1)}, s32[8,128]{1,0:T(8,128)S(1)}, s32[128,256]{1,0:T(8,128)S(1)}) custom-call(s32[1,256]{1,0:T(1,128)} %bitcast.5, bf16[256,128]{1,0:T(8,128)(2,1)} %features_hbm.1, s32[1,1,128]{2,1,0:T(1,128)} %rows_hbm.1, s32[1,1,128]{2,1,0:T(1,128)} %cols_hbm.1, s32[128,256]{1,0:T(8,128)} %bitcast.9), custom_call_target="tpu_custom_call" | custom-call | tf_op jit(solution)/shard_map/scale_rows/pallas_call | solution.py:476
  1.7 4.0 %collective-permute-start = (bf16[128,256]{1,0:T(8,128)(2,1)S(1)}, bf16[128,256]{1,0:T(8,128)(2,1)S(1)}, u32[]{:S(2)}, u32[]{:S(2)}) collective-permute-start(bf16[128,256]{1,0:T(8,128)(2,1)S(1)} %get-tuple-element.43.refs_0_), channel_id=1, source_target_pairs={{0,24},{4,28},{8,16},{12,20},{16,8},{20,12},{24,0},{28,4},{1,25},{... | collective-permute-start | bytes 196616 | tf_op jit(solution)/shard_map/ppermute | solution.py:119
  5.6 0.5 %collective-permute-start.1 = (bf16[128,256]{1,0:T(8,128)(2,1)S(1)}, bf16[128,256]{1,0:T(8,128)(2,1)S(1)}, u32[]{:S(2)}, u32[]{:S(2)}) collective-permute-start(bf16[128,256]{1,0:T(8,128)(2,1)S(1)} %get-tuple-element.43.refs_0_), channel_id=1, source_target_pairs={{0,16},{4,20},{8,24},{12,28},{16,0},{20,4},{24,8},{28,12},{1,17},{... | collective-permute-start | bytes 196616 | tf_op jit(solution)/shard_map/ppermute | solution.py:119
  6.9 2.6 %build_block.1.refs_0_ = bf16[2048,1024]{1,0:T(8,128)(2,1)S(1)} custom-call(s32[8,128]{1,0:T(8,128)S(1)} %get-tuple-element.41.lists_vmem, s32[1,1,1]{2,1,0:T(1,128)S(6)} %copy.15.count_ref, s32[128,256]{1,0:T(8,128)S(1)} %get-tuple-element.42.codes_ref), custom_call_target="tpu_custom_call" | custom-call | flops 31457280 | bytes 8388608 | tf_op jit(solution)/shard_map/build_block/pallas_call | solution.py:183
  9.9 0.5 %collective-permute-done.2.refs_2_.refs_4_ = bf16[128,256]{1,0:T(8,128)(2,1)S(1)} collective-permute-done((bf16[128,256]{1,0:T(8,128)(2,1)S(1)}, bf16[128,256]{1,0:T(8,128)(2,1)S(1)}, u32[]{:S(2)}, u32[]{:S(2)}) %collective-permute-start.2) | collective-permute-done | bytes 65568 | tf_op jit(solution)/shard_map/ppermute | solution.py:119
  11.0 1.3 %build_rest.1.block_ref = bf16[2048,1024]{1,0:T(8,128)(2,1)S(1)} custom-call(s32[8,128]{1,0:T(8,128)S(1)} %get-tuple-element.41.lists_vmem, s32[1,1,1]{2,1,0:T(1,128)S(6)} %copy.15.count_ref, s32[128,256]{1,0:T(8,128)S(1)} %get-tuple-element.42.codes_ref, bf16[2048,1024]{1,0:T(8,128)(2,1)S(1)} %build_block.1.refs_0_), custom_call_target="tpu_custom_call", output_to_operand_aliasing={{}: (3, {})} | custom-call | flops 10485760 | bytes 8388608 | tf_op jit(solution)/shard_map/build_rest/pallas_call | solution.py:183
  12.8 3.7 %collective-permute-start.5 = (bf16[128,256]{1,0:T(8,128)(2,1)S(1)}, bf16[128,256]{1,0:T(8,128)(2,1)S(1)}, u32[]{:S(2)}, u32[]{:S(2)}) collective-permute-start(bf16[128,256]{1,0:T(8,128)(2,1)S(1)} %get-tuple-element.57), channel_id=1, source_target_pairs={{0,3},{1,2},{2,1},{3,0},{4,7},{5,6},{6,5},{7,4},{8,11},{9,10},{10,... | collective-permute-start | bytes 196616 | tf_op jit(solution)/shard_map/ppermute | solution.py:119
  17.0 0.8 %collective-permute-start.7 = (bf16[128,256]{1,0:T(8,128)(2,1)S(1)}, bf16[128,256]{1,0:T(8,128)(2,1)S(1)}, u32[]{:S(2)}, u32[]{:S(2)}) collective-permute-start(bf16[128,256]{1,0:T(8,128)(2,1)S(1)} %get-tuple-element.59), channel_id=1, source_target_pairs={{0,1},{1,0},{2,3},{3,2},{4,5},{5,4},{6,7},{7,6},{8,9},{9,8},{10,11... | collective-permute-start | bytes 196616 | tf_op jit(solution)/shard_map/ppermute | solution.py:119
  18.0 1.3 %collective-permute-done.5.refs_1_ = bf16[128,256]{1,0:T(8,128)(2,1)S(1)} collective-permute-done((bf16[128,256]{1,0:T(8,128)(2,1)S(1)}, bf16[128,256]{1,0:T(8,128)(2,1)S(1)}, u32[]{:S(2)}, u32[]{:S(2)}) %collective-permute-start.5) | collective-permute-done | bytes 65568 | tf_op jit(solution)/shard_map/ppermute | solution.py:119
  19.3 3.2 %collective-permute-done.6.refs_2_ = bf16[128,256]{1,0:T(8,128)(2,1)S(1)} collective-permute-done((bf16[128,256]{1,0:T(8,128)(2,1)S(1)}, bf16[128,256]{1,0:T(8,128)(2,1)S(1)}, u32[]{:S(2)}, u32[]{:S(2)}) %collective-permute-start.6) | collective-permute-done | bytes 65568 | tf_op jit(solution)/shard_map/ppermute | solution.py:119
  23.1 0.9 %collective-permute-start.8 = (bf16[400,128]{1,0:T(8,128)(2,1)S(1)}, bf16[400,128]{1,0:T(8,128)(2,1)S(1)}, u32[]{:S(2)}, u32[]{:S(2)}) collective-permute-start(bf16[400,128]{1,0:T(8,128)(2,1)S(1)} %get-tuple-element.60.refs_0_), channel_id=1, source_target_pairs={{0,1},{1,0},{2,3},{3,2},{4,5},{5,4},{6,7},{7,6},{8,9},{9,8},{10,11... | collective-permute-start | bytes 307208 | tf_op jit(solution)/shard_map/ppermute | solution.py:119
  23.9 2.0 %collective-permute-start.9 = (bf16[256,128]{1,0:T(8,128)(2,1)S(1)}, bf16[256,128]{1,0:T(8,128)(2,1)S(1)}, u32[]{:S(2)}, u32[]{:S(2)}) collective-permute-start(bf16[256,128]{1,0:T(8,128)(2,1)S(1)} %get-tuple-element.64.refs_0_), channel_id=1, source_target_pairs={{0,2},{1,3},{2,0},{3,1},{4,6},{5,7},{6,4},{7,5},{8,10},{9,11},{10,... | collective-permute-start | bytes 196616 | tf_op jit(solution)/shard_map/ppermute | solution.py:119
  25.9 1.6 %collective-permute-start.10 = (bf16[256,128]{1,0:T(8,128)(2,1)S(1)}, bf16[256,128]{1,0:T(8,128)(2,1)S(1)}, u32[]{:S(2)}, u32[]{:S(2)}) collective-permute-start(bf16[256,128]{1,0:T(8,128)(2,1)S(1)} %get-tuple-element.64.refs_0_), channel_id=1, source_target_pairs={{0,3},{1,2},{2,1},{3,0},{4,7},{5,6},{6,5},{7,4},{8,11},{9,10},{10,... | collective-permute-start | bytes 196616 | tf_op jit(solution)/shard_map/ppermute | solution.py:119
  28.0 1.6 %collective-permute-start.11 = (bf16[144,128]{1,0:T(8,128)(2,1)S(1)}, bf16[144,128]{1,0:T(8,128)(2,1)S(1)}, u32[]{:S(2)}, u32[]{:S(2)}) collective-permute-start(bf16[144,128]{1,0:T(8,128)(2,1)S(1)} %terms_col.1.refs_3_), channel_id=1, source_target_pairs={{0,2},{1,3},{2,0},{3,1},{4,6},{5,7},{6,4},{7,5},{8,10},{9,11},{10,... | collective-permute-start | bytes 110600 | tf_op jit(solution)/shard_map/ppermute | solution.py:119
  29.6 0.7 %backward_near.1.refs_2_ = f32[2048,128]{1,0:T(8,128)S(1)} custom-call(bf16[2048,1024]{1,0:T(8,128)(2,1)S(1)} %build_rest.1.block_ref, bf16[256,128]{1,0:T(8,128)(2,1)S(1)} %get-tuple-element.64.refs_0_, bf16[400,128]{1,0:T(8,128)(2,1)S(1)} %collective-permute-done.8.refs_1_), custom_call_target="tpu_custom_call" | custom-call | tf_op jit(solution)/shard_map/backward_near/pallas_call | solution.py:390
  30.3 1.6 %collective-permute-done.10.refs_1_ = bf16[256,128]{1,0:T(8,128)(2,1)S(1)} collective-permute-done((bf16[256,128]{1,0:T(8,128)(2,1)S(1)}, bf16[256,128]{1,0:T(8,128)(2,1)S(1)}, u32[]{:S(2)}, u32[]{:S(2)}) %collective-permute-start.10) | collective-permute-done | bytes 65568 | tf_op jit(solution)/shard_map/ppermute | solution.py:119
  32.0 1.1 %collective-permute-done.11.refs_4_ = bf16[144,128]{1,0:T(8,128)(2,1)S(1)} collective-permute-done((bf16[144,128]{1,0:T(8,128)(2,1)S(1)}, bf16[144,128]{1,0:T(8,128)(2,1)S(1)}, u32[]{:S(2)}, u32[]{:S(2)}) %collective-permute-start.11) | collective-permute-done | bytes 36896 | tf_op jit(solution)/shard_map/ppermute | solution.py:119
  33.8 0.6 %collective-permute-start.12 = (bf16[512,128]{1,0:T(8,128)(2,1)S(1)}, bf16[512,128]{1,0:T(8,128)(2,1)S(1)}, u32[]{:S(2)}, u32[]{:S(2)}) collective-permute-start(bf16[512,128]{1,0:T(8,128)(2,1)S(1)} %backward_rest.1), channel_id=1, source_target_pairs={{0,4},{4,0},{8,12},{12,8},{16,20},{20,16},{24,28},{28,24},{1,5},{5... | collective-permute-start | bytes 393224 | tf_op jit(solution)/shard_map/ppermute | solution.py:119
  35.0 2.1 %collective-permute-start.14 = (bf16[400,128]{1,0:T(8,128)(2,1)S(1)}, bf16[400,128]{1,0:T(8,128)(2,1)S(1)}, u32[]{:S(2)}, u32[]{:S(2)}) collective-permute-start(bf16[400,128]{1,0:T(8,128)(2,1)S(1)} %get-tuple-element.72), channel_id=1, source_target_pairs={{0,24},{4,28},{8,16},{12,20},{16,8},{20,12},{24,0},{28,4},{1,25},{... | collective-permute-start | bytes 307208 | tf_op jit(solution)/shard_map/ppermute | solution.py:119
  37.6 1.0 %collective-permute-start.16 = (bf16[400,128]{1,0:T(8,128)(2,1)S(1)}, bf16[400,128]{1,0:T(8,128)(2,1)S(1)}, u32[]{:S(2)}, u32[]{:S(2)}) collective-permute-start(bf16[400,128]{1,0:T(8,128)(2,1)S(1)} %get-tuple-element.74), channel_id=1, source_target_pairs={{0,8},{4,12},{8,0},{12,4},{16,24},{20,28},{24,16},{28,20},{1,9},{5... | collective-permute-start | bytes 307208 | tf_op jit(solution)/shard_map/ppermute | solution.py:119
  38.7 0.9 %hidden_step.1 = bf16[256,128]{1,0:T(8,128)(2,1)} custom-call(bf16[128,128]{1,0:T(8,128)(2,1)S(1)} %get-tuple-element.53.turned_ref, f32[128,128]{1,0:T(8,128)S(1)} %get-tuple-element.54.bias_ref, bf16[128,256]{1,0:T(8,128)(2,1)S(1)} %get-tuple-element.62.aggregate_ref), custom_call_target="tpu_custom_call" | custom-call | tf_op jit(solution)/shard_map/hidden_step/pallas_call | solution.py:345
  39.5 1.4 %collective-permute-done.14.refs_1_ = bf16[400,128]{1,0:T(8,128)(2,1)S(1)} collective-permute-done((bf16[400,128]{1,0:T(8,128)(2,1)S(1)}, bf16[400,128]{1,0:T(8,128)(2,1)S(1)}, u32[]{:S(2)}, u32[]{:S(2)}) %collective-permute-start.14) | collective-permute-done | bytes 102432 | tf_op jit(solution)/shard_map/ppermute | solution.py:119
  40.9 2.1 %collective-permute-done.15.refs_2_ = bf16[400,128]{1,0:T(8,128)(2,1)S(1)} collective-permute-done((bf16[400,128]{1,0:T(8,128)(2,1)S(1)}, bf16[400,128]{1,0:T(8,128)(2,1)S(1)}, u32[]{:S(2)}, u32[]{:S(2)}) %collective-permute-start.15) | collective-permute-done | bytes 102432 | tf_op jit(solution)/shard_map/ppermute | solution.py:119
  43.1 0.7 %finish.1 = (bf16[256,128]{1,0:T(8,128)(2,1)}, f32[128,128]{1,0:T(8,128)}, f32[1,128]{1,0:T(1,128)}) custom-call(f32[256,128]{1,0:T(8,128)S(1)} %get-tuple-element.63.root_ref, bf16[400,128]{1,0:T(8,128)(2,1)S(1)} %get-tuple-element.71.refs_0_, bf16[400,128]{1,0:T(8,128)(2,1)S(1)} %collective-permute-done.14.refs_1_, ...), custom_call_target="tpu_custom_call" | custom-call | tf_op jit(solution)/shard_map/finish/pallas_call | solution.py:435
  (36 shorter events, 5.2 us)
Async XLA Ops:
  1.7 7.9 %collective-permute-start = (bf16[128,256]{1,0:T(8,128)(2,1)S(1)}, bf16[128,256]{1,0:T(8,128)(2,1)S(1)}, u32[]{:S(2)}, u32[]{:S(2)}) collective-permute-start(bf16[128,256]{1,0:T(8,128)(2,1)S(1)} %get-tuple-element.43.refs_0_), channel_id=1, source_target_pairs={{0,24},{4,28},{8,16},{12,20},{16,8},{20,12},{24,0},{28,4},{1,25},{... | collective-permute-start | bytes 196616 | tf_op jit(solution)/shard_map/ppermute | solution.py:119
  5.6 4.3 %collective-permute-start.1 = (bf16[128,256]{1,0:T(8,128)(2,1)S(1)}, bf16[128,256]{1,0:T(8,128)(2,1)S(1)}, u32[]{:S(2)}, u32[]{:S(2)}) collective-permute-start(bf16[128,256]{1,0:T(8,128)(2,1)S(1)} %get-tuple-element.43.refs_0_), channel_id=1, source_target_pairs={{0,16},{4,20},{8,24},{12,28},{16,0},{20,4},{24,8},{28,12},{1,17},{... | collective-permute-start | bytes 196616 | tf_op jit(solution)/shard_map/ppermute | solution.py:119
  6.1 4.3 %collective-permute-start.2 = (bf16[128,256]{1,0:T(8,128)(2,1)S(1)}, bf16[128,256]{1,0:T(8,128)(2,1)S(1)}, u32[]{:S(2)}, u32[]{:S(2)}) collective-permute-start(bf16[128,256]{1,0:T(8,128)(2,1)S(1)} %get-tuple-element.43.refs_0_), channel_id=1, source_target_pairs={{0,8},{4,12},{8,0},{12,4},{16,24},{20,28},{24,16},{28,20},{1,9},{5... | collective-permute-start | bytes 196616 | tf_op jit(solution)/shard_map/ppermute | solution.py:119
  10.4 1.9 %collective-permute-start.4 = (bf16[384,256]{1,0:T(8,128)(2,1)S(1)}, bf16[384,256]{1,0:T(8,128)(2,1)S(1)}, u32[]{:S(2)}, u32[]{:S(2)}) collective-permute-start(bf16[384,256]{1,0:T(8,128)(2,1)S(1)} %stack.1), channel_id=1, source_target_pairs={{0,4},{4,0},{8,12},{12,8},{16,20},{20,16},{24,28},{28,24},{1,5},{5... | collective-permute-start | bytes 589832 | tf_op jit(solution)/shard_map/ppermute | solution.py:119
  10.5 1.8 %collective-permute-start.3 = (bf16[128,256]{1,0:T(8,128)(2,1)S(1)}, bf16[128,256]{1,0:T(8,128)(2,1)S(1)}, u32[]{:S(2)}, u32[]{:S(2)}) collective-permute-start(bf16[128,256]{1,0:T(8,128)(2,1)S(1)} %get-tuple-element.43.refs_0_), channel_id=1, source_target_pairs={{0,4},{4,0},{8,12},{12,8},{16,20},{20,16},{24,28},{28,24},{1,5},{5... | collective-permute-start | bytes 196616 | tf_op jit(solution)/shard_map/ppermute | solution.py:119
  12.3 5.6 %copy-start = (bf16[128,128]{1,0:T(8,128)(2,1)S(1)}, bf16[128,128]{1,0:T(8,128)(2,1)}, u32[]{:S(2)}) copy-start(bf16[128,128]{1,0:T(8,128)(2,1)} %weight_ref.2) | copy-start | bytes 98308
  12.3 5.6 %copy-start.1 = (bf16[256,128]{1,0:T(8,128)(2,1)S(1)}, bf16[256,128]{1,0:T(8,128)(2,1)}, u32[]{:S(2)}) copy-start(bf16[256,128]{1,0:T(8,128)(2,1)} %cot_ref) | copy-start | bytes 196612
  12.3 5.5 %copy-start.2 = (s32[256]{0:T(256)S(1)}, s32[256]{0:T(256)}, u32[]{:S(2)}) copy-start(s32[256]{0:T(256)} %param.10) | copy-start | bytes 3076
  12.3 5.5 %copy-start.3 = (f32[128]{0:T(128)S(1)}, f32[128]{0:T(128)}, u32[]{:S(2)}) copy-start(f32[128]{0:T(128)} %param.12) | copy-start | bytes 1540
  12.8 6.4 %collective-permute-start.5 = (bf16[128,256]{1,0:T(8,128)(2,1)S(1)}, bf16[128,256]{1,0:T(8,128)(2,1)S(1)}, u32[]{:S(2)}, u32[]{:S(2)}) collective-permute-start(bf16[128,256]{1,0:T(8,128)(2,1)S(1)} %get-tuple-element.57), channel_id=1, source_target_pairs={{0,3},{1,2},{2,1},{3,0},{4,7},{5,6},{6,5},{7,4},{8,11},{9,10},{10,... | collective-permute-start | bytes 196616 | tf_op jit(solution)/shard_map/ppermute | solution.py:119
  16.5 6.0 %collective-permute-start.6 = (bf16[128,256]{1,0:T(8,128)(2,1)S(1)}, bf16[128,256]{1,0:T(8,128)(2,1)S(1)}, u32[]{:S(2)}, u32[]{:S(2)}) collective-permute-start(bf16[128,256]{1,0:T(8,128)(2,1)S(1)} %get-tuple-element.58), channel_id=1, source_target_pairs={{0,2},{1,3},{2,0},{3,1},{4,6},{5,7},{6,4},{7,5},{8,10},{9,11},{10,... | collective-permute-start | bytes 196616 | tf_op jit(solution)/shard_map/ppermute | solution.py:119
  17.0 5.7 %collective-permute-start.7 = (bf16[128,256]{1,0:T(8,128)(2,1)S(1)}, bf16[128,256]{1,0:T(8,128)(2,1)S(1)}, u32[]{:S(2)}, u32[]{:S(2)}) collective-permute-start(bf16[128,256]{1,0:T(8,128)(2,1)S(1)} %get-tuple-element.59), channel_id=1, source_target_pairs={{0,1},{1,0},{2,3},{3,2},{4,5},{5,4},{6,7},{7,6},{8,9},{9,8},{10,11... | collective-permute-start | bytes 196616 | tf_op jit(solution)/shard_map/ppermute | solution.py:119
  23.1 4.9 %collective-permute-start.8 = (bf16[400,128]{1,0:T(8,128)(2,1)S(1)}, bf16[400,128]{1,0:T(8,128)(2,1)S(1)}, u32[]{:S(2)}, u32[]{:S(2)}) collective-permute-start(bf16[400,128]{1,0:T(8,128)(2,1)S(1)} %get-tuple-element.60.refs_0_), channel_id=1, source_target_pairs={{0,1},{1,0},{2,3},{3,2},{4,5},{5,4},{6,7},{7,6},{8,9},{9,8},{10,11... | collective-permute-start | bytes 307208 | tf_op jit(solution)/shard_map/ppermute | solution.py:119
  23.9 6.4 %collective-permute-start.9 = (bf16[256,128]{1,0:T(8,128)(2,1)S(1)}, bf16[256,128]{1,0:T(8,128)(2,1)S(1)}, u32[]{:S(2)}, u32[]{:S(2)}) collective-permute-start(bf16[256,128]{1,0:T(8,128)(2,1)S(1)} %get-tuple-element.64.refs_0_), channel_id=1, source_target_pairs={{0,2},{1,3},{2,0},{3,1},{4,6},{5,7},{6,4},{7,5},{8,10},{9,11},{10,... | collective-permute-start | bytes 196616 | tf_op jit(solution)/shard_map/ppermute | solution.py:119
  25.9 6.1 %collective-permute-start.10 = (bf16[256,128]{1,0:T(8,128)(2,1)S(1)}, bf16[256,128]{1,0:T(8,128)(2,1)S(1)}, u32[]{:S(2)}, u32[]{:S(2)}) collective-permute-start(bf16[256,128]{1,0:T(8,128)(2,1)S(1)} %get-tuple-element.64.refs_0_), channel_id=1, source_target_pairs={{0,3},{1,2},{2,1},{3,0},{4,7},{5,6},{6,5},{7,4},{8,11},{9,10},{10,... | collective-permute-start | bytes 196616 | tf_op jit(solution)/shard_map/ppermute | solution.py:119
  28.0 5.1 %collective-permute-start.11 = (bf16[144,128]{1,0:T(8,128)(2,1)S(1)}, bf16[144,128]{1,0:T(8,128)(2,1)S(1)}, u32[]{:S(2)}, u32[]{:S(2)}) collective-permute-start(bf16[144,128]{1,0:T(8,128)(2,1)S(1)} %terms_col.1.refs_3_), channel_id=1, source_target_pairs={{0,2},{1,3},{2,0},{3,1},{4,6},{5,7},{6,4},{7,5},{8,10},{9,11},{10,... | collective-permute-start | bytes 110600 | tf_op jit(solution)/shard_map/ppermute | solution.py:119
  33.4 1.5 %collective-permute-start.13 = (bf16[656,128]{1,0:T(8,128)(2,1)S(1)}, bf16[656,128]{1,0:T(8,128)(2,1)S(1)}, u32[]{:S(2)}, u32[]{:S(2)}) collective-permute-start(bf16[656,128]{1,0:T(8,128)(2,1)S(1)} %backward_other.1.sent_ref), channel_id=1, source_target_pairs={{0,4},{4,0},{8,12},{12,8},{16,20},{20,16},{24,28},{28,24},{1,5},{5... | collective-permute-start | bytes 503816 | tf_op jit(solution)/shard_map/ppermute | solution.py:119
  33.8 3.8 %collective-permute-start.12 = (bf16[512,128]{1,0:T(8,128)(2,1)S(1)}, bf16[512,128]{1,0:T(8,128)(2,1)S(1)}, u32[]{:S(2)}, u32[]{:S(2)}) collective-permute-start(bf16[512,128]{1,0:T(8,128)(2,1)S(1)} %backward_rest.1), channel_id=1, source_target_pairs={{0,4},{4,0},{8,12},{12,8},{16,20},{20,16},{24,28},{28,24},{1,5},{5... | collective-permute-start | bytes 393224 | tf_op jit(solution)/shard_map/ppermute | solution.py:119
  35.0 5.9 %collective-permute-start.14 = (bf16[400,128]{1,0:T(8,128)(2,1)S(1)}, bf16[400,128]{1,0:T(8,128)(2,1)S(1)}, u32[]{:S(2)}, u32[]{:S(2)}) collective-permute-start(bf16[400,128]{1,0:T(8,128)(2,1)S(1)} %get-tuple-element.72), channel_id=1, source_target_pairs={{0,24},{4,28},{8,16},{12,20},{16,8},{20,12},{24,0},{28,4},{1,25},{... | collective-permute-start | bytes 307208 | tf_op jit(solution)/shard_map/ppermute | solution.py:119
  37.1 5.9 %collective-permute-start.15 = (bf16[400,128]{1,0:T(8,128)(2,1)S(1)}, bf16[400,128]{1,0:T(8,128)(2,1)S(1)}, u32[]{:S(2)}, u32[]{:S(2)}) collective-permute-start(bf16[400,128]{1,0:T(8,128)(2,1)S(1)} %get-tuple-element.73), channel_id=1, source_target_pairs={{0,16},{4,20},{8,24},{12,28},{16,0},{20,4},{24,8},{28,12},{1,17},{... | collective-permute-start | bytes 307208 | tf_op jit(solution)/shard_map/ppermute | solution.py:119
  37.6 5.5 %collective-permute-start.16 = (bf16[400,128]{1,0:T(8,128)(2,1)S(1)}, bf16[400,128]{1,0:T(8,128)(2,1)S(1)}, u32[]{:S(2)}, u32[]{:S(2)}) collective-permute-start(bf16[400,128]{1,0:T(8,128)(2,1)S(1)} %get-tuple-element.74), channel_id=1, source_target_pairs={{0,8},{4,12},{8,0},{12,4},{16,24},{20,28},{24,16},{28,20},{1,9},{5... | collective-permute-start | bytes 307208 | tf_op jit(solution)/shard_map/ppermute | solution.py:119

commit v9 on v7

--- a/solution.py
+++ b/solution.py
@@ -397,7 +397,7 @@
 
 
 def pair_kernel(first, mine_ref, theirs_ref, sent_ref, got_ref, *outs):
-    feat = mine_ref.shape[0] // 4
+    feat = mine_ref.shape[0] // 2
     terms = sum_of((sent_ref.at[2 * feat :], got_ref.at[2 * feat :])).astype(jnp.bfloat16)
     for m, out in enumerate(outs):
         mine = mine_ref[(first + m) * feat : (first + m + 1) * feat, :].astype(jnp.float32)
@@ -408,7 +408,7 @@
 
 def pair_sum(first, mine, theirs, sent, got):
     vmem = pl.BlockSpec(memory_space=pltpu.VMEM)
-    rows = sent.shape[0] - mine.shape[0] // 4
+    rows = sent.shape[0] - mine.shape[0] // 2
     return pl.pallas_call(
         functools.partial(pair_kernel, first),
         out_shape=[jax.ShapeDtypeStruct((rows, mine.shape[1]), jnp.bfloat16)] * 2,
@@ -552,10 +552,11 @@
     sent = backward_parts(block, grads, far, [7, 5], begun, terms, "backward_other")
     got = swap(sent, "row", 1)
     rest = swap(backward_parts(block, grads, far, [3, 1], begun, [], "backward_rest"), "row", 1)
-    mine = backward_parts(block, grads, far, [6, 4, 2, 0], begun, [], "backward_own")
+    mine = backward_parts(block, grads, far, [6, 4], begun, [], "backward_own")
     chunks = pair_sum(0, mine, got, sent, got)
     landed = [swap(chunk, "row", m) for chunk, m in zip(chunks, chips)]
-    chunks = pair_sum(2, mine, rest, sent, got)
+    mine = backward_parts(block, grads, far, [2, 0], begun, [], "backward_last")
+    chunks = pair_sum(0, mine, rest, sent, got)
     landed = [chunks[1], *landed, swap(chunks[0], "row", chips[2])]
     grad_features, grad_weight, grad_bias = finish(root, landed, grad_scale)
     return (hidden, grad_features, grad_weight, grad_bias)

time: 44 us -> 44 us (level)
    pallas_call x4 -> x5, Pallas kernels: 1.72 us -> 1.86 us  [backward_parts(): pl.pallas_call(functools.partial(backward_kernel, pieces, kinds, chunks,...]
  transfers between devices with their start and end apart: 17 -> 17, of which waited for: 12 -> 11; matrix products, arithmetic and copies ran while one was open for 0% -> 0% of each run, Pallas kernels for 16% -> 16%
where the time goes in v9:
time: 44 us; the launch traced here: 43.9 us
  starting transfers between devices  20 us (45%)
  waiting for transfers between devices  12.3 us (28%)
  Pallas kernels  10 us (23%)
  between operations  1.48 us (3%)
    ppermute x17, starting transfers between devices, swap(): return lax.ppermute(value, axis, [(i, i ^ bits) for i in range(size)])  20 us
    ppermute x17, waiting for transfers between devices, swap(): return lax.ppermute(value, axis, [(i, i ^ bits) for i in range(size)])  12.3 us
    pallas_call x2, Pallas kernels, build_block(): pl.pallas_call(functools.partial(build_kernel, first, last), out_shape=pl...  3.9 us
    pallas_call x5, Pallas kernels, backward_parts(): pl.pallas_call(functools.partial(backward_kernel, pieces, kinds, chunks,...  1.86 us
    pallas_call x2, Pallas kernels, forward_parts(): pl.pallas_call(functools.partial(forward_kernel, bits, high), out_shape=[...  1.04 us
    pallas_call x1, Pallas kernels, scale_rows(): pl.pallas_call(scale_kernel, out_shape=[pltpu.VMEM((feat, pieces), jnp.bf...  1.03 us
  transfers between devices with their start and end apart: 17, of which 11 were waited for; matrix products, arithmetic and copies ran while one was open for 0% of the time, Pallas kernels for 16%

profile of v9, /device:TPU:0, one launch (start us, length us, event | category | flops | bytes accessed | tf_op | source)
XLA Modules:
  0.0 43.9 jit_solution(9276651944318321896)
XLA Ops:
  0.6 1.0 %scale_rows.1 = (bf16[128,256]{1,0:T(8,128)(2,1)S(1)}, s32[8,128]{1,0:T(8,128)S(1)}, s32[128,256]{1,0:T(8,128)S(1)}) custom-call(s32[1,256]{1,0:T(1,128)} %bitcast.5, bf16[256,128]{1,0:T(8,128)(2,1)} %features_hbm.1, s32[1,1,128]{2,1,0:T(1,128)} %rows_hbm.1, s32[1,1,128]{2,1,0:T(1,128)} %cols_hbm.1, s32[128,256]{1,0:T(8,128)} %bitcast.9), custom_call_target="tpu_custom_call" | custom-call | tf_op jit(solution)/shard_map/scale_rows/pallas_call | solution.py:475
  1.7 4.0 %collective-permute-start = (bf16[128,256]{1,0:T(8,128)(2,1)S(1)}, bf16[128,256]{1,0:T(8,128)(2,1)S(1)}, u32[]{:S(2)}, u32[]{:S(2)}) collective-permute-start(bf16[128,256]{1,0:T(8,128)(2,1)S(1)} %get-tuple-element.43.refs_0_), channel_id=1, source_target_pairs={{0,24},{4,28},{8,16},{12,20},{16,8},{20,12},{24,0},{28,4},{1,25},{... | collective-permute-start | bytes 196616 | tf_op jit(solution)/shard_map/ppermute | solution.py:119
  6.9 2.6 %build_block.1.refs_0_ = bf16[2048,1024]{1,0:T(8,128)(2,1)S(1)} custom-call(s32[8,128]{1,0:T(8,128)S(1)} %get-tuple-element.41.lists_vmem, s32[1,1,1]{2,1,0:T(1,128)S(6)} %copy.15.count_ref, s32[128,256]{1,0:T(8,128)S(1)} %get-tuple-element.42.codes_ref), custom_call_target="tpu_custom_call" | custom-call | flops 31457280 | bytes 8388608 | tf_op jit(solution)/shard_map/build_block/pallas_call | solution.py:183
  11.0 1.3 %build_rest.1.block_ref = bf16[2048,1024]{1,0:T(8,128)(2,1)S(1)} custom-call(s32[8,128]{1,0:T(8,128)S(1)} %get-tuple-element.41.lists_vmem, s32[1,1,1]{2,1,0:T(1,128)S(6)} %copy.15.count_ref, s32[128,256]{1,0:T(8,128)S(1)} %get-tuple-element.42.codes_ref, bf16[2048,1024]{1,0:T(8,128)(2,1)S(1)} %build_block.1.refs_0_), custom_call_target="tpu_custom_call", output_to_operand_aliasing={{}: (3, {})} | custom-call | flops 10485760 | bytes 8388608 | tf_op jit(solution)/shard_map/build_rest/pallas_call | solution.py:183
  12.3 0.5 %forward_far.1 = (bf16[128,256]{1,0:T(8,128)(2,1)S(1)}, bf16[128,256]{1,0:T(8,128)(2,1)S(1)}) custom-call(bf16[2048,1024]{1,0:T(8,128)(2,1)S(1)} %build_rest.1.block_ref, bf16[128,256]{1,0:T(8,128)(2,1)S(1)} %get-tuple-element.43.refs_0_, bf16[128,256]{1,0:T(8,128)(2,1)S(1)} %collective-permute-done.3.refs_1_, ...), custom_call_target="tpu_custom_call" | custom-call | tf_op jit(solution)/shard_map/forward_far/pallas_call | solution.py:245
  12.9 3.7 %collective-permute-start.5 = (bf16[128,256]{1,0:T(8,128)(2,1)S(1)}, bf16[128,256]{1,0:T(8,128)(2,1)S(1)}, u32[]{:S(2)}, u32[]{:S(2)}) collective-permute-start(bf16[128,256]{1,0:T(8,128)(2,1)S(1)} %get-tuple-element.57), channel_id=1, source_target_pairs={{0,3},{1,2},{2,1},{3,0},{4,7},{5,6},{6,5},{7,4},{8,11},{9,10},{10,... | collective-permute-start | bytes 196616 | tf_op jit(solution)/shard_map/ppermute | solution.py:119
  16.6 0.5 %forward_near.1 = (bf16[128,256]{1,0:T(8,128)(2,1)S(1)}, bf16[128,256]{1,0:T(8,128)(2,1)S(1)}) custom-call(bf16[2048,1024]{1,0:T(8,128)(2,1)S(1)} %build_rest.1.block_ref, bf16[128,256]{1,0:T(8,128)(2,1)S(1)} %get-tuple-element.43.refs_0_, bf16[128,256]{1,0:T(8,128)(2,1)S(1)} %collective-permute-done.3.refs_1_, ...), custom_call_target="tpu_custom_call" | custom-call | tf_op jit(solution)/shard_map/forward_near/pallas_call | solution.py:245
  17.1 0.8 %collective-permute-start.7 = (bf16[128,256]{1,0:T(8,128)(2,1)S(1)}, bf16[128,256]{1,0:T(8,128)(2,1)S(1)}, u32[]{:S(2)}, u32[]{:S(2)}) collective-permute-start(bf16[128,256]{1,0:T(8,128)(2,1)S(1)} %get-tuple-element.59), channel_id=1, source_target_pairs={{0,1},{1,0},{2,3},{3,2},{4,5},{5,4},{6,7},{7,6},{8,9},{9,8},{10,11... | collective-permute-start | bytes 196616 | tf_op jit(solution)/shard_map/ppermute | solution.py:119
  18.1 1.2 %collective-permute-done.5.refs_1_ = bf16[128,256]{1,0:T(8,128)(2,1)S(1)} collective-permute-done((bf16[128,256]{1,0:T(8,128)(2,1)S(1)}, bf16[128,256]{1,0:T(8,128)(2,1)S(1)}, u32[]{:S(2)}, u32[]{:S(2)}) %collective-permute-start.5) | collective-permute-done | bytes 65568 | tf_op jit(solution)/shard_map/ppermute | solution.py:119
  19.3 3.2 %collective-permute-done.6.refs_2_ = bf16[128,256]{1,0:T(8,128)(2,1)S(1)} collective-permute-done((bf16[128,256]{1,0:T(8,128)(2,1)S(1)}, bf16[128,256]{1,0:T(8,128)(2,1)S(1)}, u32[]{:S(2)}, u32[]{:S(2)}) %collective-permute-start.6) | collective-permute-done | bytes 65568 | tf_op jit(solution)/shard_map/ppermute | solution.py:119
  23.1 0.8 %collective-permute-start.8 = (bf16[400,128]{1,0:T(8,128)(2,1)S(1)}, bf16[400,128]{1,0:T(8,128)(2,1)S(1)}, u32[]{:S(2)}, u32[]{:S(2)}) collective-permute-start(bf16[400,128]{1,0:T(8,128)(2,1)S(1)} %get-tuple-element.60.refs_0_), channel_id=1, source_target_pairs={{0,1},{1,0},{2,3},{3,2},{4,5},{5,4},{6,7},{7,6},{8,9},{9,8},{10,11... | collective-permute-start | bytes 307208 | tf_op jit(solution)/shard_map/ppermute | solution.py:119
  24.0 2.0 %collective-permute-start.9 = (bf16[256,128]{1,0:T(8,128)(2,1)S(1)}, bf16[256,128]{1,0:T(8,128)(2,1)S(1)}, u32[]{:S(2)}, u32[]{:S(2)}) collective-permute-start(bf16[256,128]{1,0:T(8,128)(2,1)S(1)} %get-tuple-element.64.refs_0_), channel_id=1, source_target_pairs={{0,2},{1,3},{2,0},{3,1},{4,6},{5,7},{6,4},{7,5},{8,10},{9,11},{10,... | collective-permute-start | bytes 196616 | tf_op jit(solution)/shard_map/ppermute | solution.py:119
  26.0 1.6 %collective-permute-start.10 = (bf16[256,128]{1,0:T(8,128)(2,1)S(1)}, bf16[256,128]{1,0:T(8,128)(2,1)S(1)}, u32[]{:S(2)}, u32[]{:S(2)}) collective-permute-start(bf16[256,128]{1,0:T(8,128)(2,1)S(1)} %get-tuple-element.64.refs_0_), channel_id=1, source_target_pairs={{0,3},{1,2},{2,1},{3,0},{4,7},{5,6},{6,5},{7,4},{8,11},{9,10},{10,... | collective-permute-start | bytes 196616 | tf_op jit(solution)/shard_map/ppermute | solution.py:119
  28.0 1.6 %collective-permute-start.11 = (bf16[144,128]{1,0:T(8,128)(2,1)S(1)}, bf16[144,128]{1,0:T(8,128)(2,1)S(1)}, u32[]{:S(2)}, u32[]{:S(2)}) collective-permute-start(bf16[144,128]{1,0:T(8,128)(2,1)S(1)} %terms_col.1.refs_3_), channel_id=1, source_target_pairs={{0,2},{1,3},{2,0},{3,1},{4,6},{5,7},{6,4},{7,5},{8,10},{9,11},{10,... | collective-permute-start | bytes 110600 | tf_op jit(solution)/shard_map/ppermute | solution.py:119
  29.7 0.7 %backward_near.1.refs_2_ = f32[2048,128]{1,0:T(8,128)S(1)} custom-call(bf16[2048,1024]{1,0:T(8,128)(2,1)S(1)} %build_rest.1.block_ref, bf16[256,128]{1,0:T(8,128)(2,1)S(1)} %get-tuple-element.64.refs_0_, bf16[400,128]{1,0:T(8,128)(2,1)S(1)} %collective-permute-done.8.refs_1_), custom_call_target="tpu_custom_call" | custom-call | tf_op jit(solution)/shard_map/backward_near/pallas_call | solution.py:389
  30.4 1.7 %collective-permute-done.10.refs_1_ = bf16[256,128]{1,0:T(8,128)(2,1)S(1)} collective-permute-done((bf16[256,128]{1,0:T(8,128)(2,1)S(1)}, bf16[256,128]{1,0:T(8,128)(2,1)S(1)}, u32[]{:S(2)}, u32[]{:S(2)}) %collective-permute-start.10) | collective-permute-done | bytes 65568 | tf_op jit(solution)/shard_map/ppermute | solution.py:119
  32.0 1.1 %collective-permute-done.11.refs_4_ = bf16[144,128]{1,0:T(8,128)(2,1)S(1)} collective-permute-done((bf16[144,128]{1,0:T(8,128)(2,1)S(1)}, bf16[144,128]{1,0:T(8,128)(2,1)S(1)}, u32[]{:S(2)}, u32[]{:S(2)}) %collective-permute-start.11) | collective-permute-done | bytes 36896 | tf_op jit(solution)/shard_map/ppermute | solution.py:119
  33.8 0.6 %collective-permute-start.12 = (bf16[512,128]{1,0:T(8,128)(2,1)S(1)}, bf16[512,128]{1,0:T(8,128)(2,1)S(1)}, u32[]{:S(2)}, u32[]{:S(2)}) collective-permute-start(bf16[512,128]{1,0:T(8,128)(2,1)S(1)} %backward_rest.1), channel_id=1, source_target_pairs={{0,4},{4,0},{8,12},{12,8},{16,20},{20,16},{24,28},{28,24},{1,5},{5... | collective-permute-start | bytes 393224 | tf_op jit(solution)/shard_map/ppermute | solution.py:119
  35.0 2.1 %collective-permute-start.14 = (bf16[400,128]{1,0:T(8,128)(2,1)S(1)}, bf16[400,128]{1,0:T(8,128)(2,1)S(1)}, u32[]{:S(2)}, u32[]{:S(2)}) collective-permute-start(bf16[400,128]{1,0:T(8,128)(2,1)S(1)} %get-tuple-element.72), channel_id=1, source_target_pairs={{0,24},{4,28},{8,16},{12,20},{16,8},{20,12},{24,0},{28,4},{1,25},{... | collective-permute-start | bytes 307208 | tf_op jit(solution)/shard_map/ppermute | solution.py:119
  37.7 1.0 %collective-permute-start.16 = (bf16[400,128]{1,0:T(8,128)(2,1)S(1)}, bf16[400,128]{1,0:T(8,128)(2,1)S(1)}, u32[]{:S(2)}, u32[]{:S(2)}) collective-permute-start(bf16[400,128]{1,0:T(8,128)(2,1)S(1)} %get-tuple-element.74), channel_id=1, source_target_pairs={{0,8},{4,12},{8,0},{12,4},{16,24},{20,28},{24,16},{28,20},{1,9},{5... | collective-permute-start | bytes 307208 | tf_op jit(solution)/shard_map/ppermute | solution.py:119
  38.7 0.9 %hidden_step.1 = bf16[256,128]{1,0:T(8,128)(2,1)} custom-call(bf16[128,128]{1,0:T(8,128)(2,1)S(1)} %get-tuple-element.53.turned_ref, f32[128,128]{1,0:T(8,128)S(1)} %get-tuple-element.54.bias_ref, bf16[128,256]{1,0:T(8,128)(2,1)S(1)} %get-tuple-element.62.aggregate_ref), custom_call_target="tpu_custom_call" | custom-call | tf_op jit(solution)/shard_map/hidden_step/pallas_call | solution.py:344
  39.6 1.4 %collective-permute-done.14.refs_1_ = bf16[400,128]{1,0:T(8,128)(2,1)S(1)} collective-permute-done((bf16[400,128]{1,0:T(8,128)(2,1)S(1)}, bf16[400,128]{1,0:T(8,128)(2,1)S(1)}, u32[]{:S(2)}, u32[]{:S(2)}) %collective-permute-start.14) | collective-permute-done | bytes 102432 | tf_op jit(solution)/shard_map/ppermute | solution.py:119
  41.0 2.1 %collective-permute-done.15.refs_2_ = bf16[400,128]{1,0:T(8,128)(2,1)S(1)} collective-permute-done((bf16[400,128]{1,0:T(8,128)(2,1)S(1)}, bf16[400,128]{1,0:T(8,128)(2,1)S(1)}, u32[]{:S(2)}, u32[]{:S(2)}) %collective-permute-start.15) | collective-permute-done | bytes 102432 | tf_op jit(solution)/shard_map/ppermute | solution.py:119
  43.2 0.7 %finish.1 = (bf16[256,128]{1,0:T(8,128)(2,1)}, f32[128,128]{1,0:T(8,128)}, f32[1,128]{1,0:T(1,128)}) custom-call(f32[256,128]{1,0:T(8,128)S(1)} %get-tuple-element.63.root_ref, bf16[400,128]{1,0:T(8,128)(2,1)S(1)} %get-tuple-element.71.refs_0_, bf16[400,128]{1,0:T(8,128)(2,1)S(1)} %collective-permute-done.14.refs_1_, ...), custom_call_target="tpu_custom_call" | custom-call | tf_op jit(solution)/shard_map/finish/pallas_call | solution.py:434
  (36 shorter events, 5.3 us)
Async XLA Ops:
  1.7 7.9 %collective-permute-start = (bf16[128,256]{1,0:T(8,128)(2,1)S(1)}, bf16[128,256]{1,0:T(8,128)(2,1)S(1)}, u32[]{:S(2)}, u32[]{:S(2)}) collective-permute-start(bf16[128,256]{1,0:T(8,128)(2,1)S(1)} %get-tuple-element.43.refs_0_), channel_id=1, source_target_pairs={{0,24},{4,28},{8,16},{12,20},{16,8},{20,12},{24,0},{28,4},{1,25},{... | collective-permute-start | bytes 196616 | tf_op jit(solution)/shard_map/ppermute | solution.py:119
  5.6 4.3 %collective-permute-start.1 = (bf16[128,256]{1,0:T(8,128)(2,1)S(1)}, bf16[128,256]{1,0:T(8,128)(2,1)S(1)}, u32[]{:S(2)}, u32[]{:S(2)}) collective-permute-start(bf16[128,256]{1,0:T(8,128)(2,1)S(1)} %get-tuple-element.43.refs_0_), channel_id=1, source_target_pairs={{0,16},{4,20},{8,24},{12,28},{16,0},{20,4},{24,8},{28,12},{1,17},{... | collective-permute-start | bytes 196616 | tf_op jit(solution)/shard_map/ppermute | solution.py:119
  6.1 4.3 %collective-permute-start.2 = (bf16[128,256]{1,0:T(8,128)(2,1)S(1)}, bf16[128,256]{1,0:T(8,128)(2,1)S(1)}, u32[]{:S(2)}, u32[]{:S(2)}) collective-permute-start(bf16[128,256]{1,0:T(8,128)(2,1)S(1)} %get-tuple-element.43.refs_0_), channel_id=1, source_target_pairs={{0,8},{4,12},{8,0},{12,4},{16,24},{20,28},{24,16},{28,20},{1,9},{5... | collective-permute-start | bytes 196616 | tf_op jit(solution)/shard_map/ppermute | solution.py:119
  10.4 1.9 %collective-permute-start.4 = (bf16[384,256]{1,0:T(8,128)(2,1)S(1)}, bf16[384,256]{1,0:T(8,128)(2,1)S(1)}, u32[]{:S(2)}, u32[]{:S(2)}) collective-permute-start(bf16[384,256]{1,0:T(8,128)(2,1)S(1)} %stack.1), channel_id=1, source_target_pairs={{0,4},{4,0},{8,12},{12,8},{16,20},{20,16},{24,28},{28,24},{1,5},{5... | collective-permute-start | bytes 589832 | tf_op jit(solution)/shard_map/ppermute | solution.py:119
  10.5 1.8 %collective-permute-start.3 = (bf16[128,256]{1,0:T(8,128)(2,1)S(1)}, bf16[128,256]{1,0:T(8,128)(2,1)S(1)}, u32[]{:S(2)}, u32[]{:S(2)}) collective-permute-start(bf16[128,256]{1,0:T(8,128)(2,1)S(1)} %get-tuple-element.43.refs_0_), channel_id=1, source_target_pairs={{0,4},{4,0},{8,12},{12,8},{16,20},{20,16},{24,28},{28,24},{1,5},{5... | collective-permute-start | bytes 196616 | tf_op jit(solution)/shard_map/ppermute | solution.py:119
  12.3 5.6 %copy-start = (bf16[128,128]{1,0:T(8,128)(2,1)S(1)}, bf16[128,128]{1,0:T(8,128)(2,1)}, u32[]{:S(2)}) copy-start(bf16[128,128]{1,0:T(8,128)(2,1)} %weight_ref.2) | copy-start | bytes 98308
  12.3 5.6 %copy-start.1 = (bf16[256,128]{1,0:T(8,128)(2,1)S(1)}, bf16[256,128]{1,0:T(8,128)(2,1)}, u32[]{:S(2)}) copy-start(bf16[256,128]{1,0:T(8,128)(2,1)} %cot_ref) | copy-start | bytes 196612
  12.3 5.6 %copy-start.2 = (s32[256]{0:T(256)S(1)}, s32[256]{0:T(256)}, u32[]{:S(2)}) copy-start(s32[256]{0:T(256)} %param.10) | copy-start | bytes 3076
  12.3 5.6 %copy-start.3 = (f32[128]{0:T(128)S(1)}, f32[128]{0:T(128)}, u32[]{:S(2)}) copy-start(f32[128]{0:T(128)} %param.12) | copy-start | bytes 1540
  12.9 6.4 %collective-permute-start.5 = (bf16[128,256]{1,0:T(8,128)(2,1)S(1)}, bf16[128,256]{1,0:T(8,128)(2,1)S(1)}, u32[]{:S(2)}, u32[]{:S(2)}) collective-permute-start(bf16[128,256]{1,0:T(8,128)(2,1)S(1)} %get-tuple-element.57), channel_id=1, source_target_pairs={{0,3},{1,2},{2,1},{3,0},{4,7},{5,6},{6,5},{7,4},{8,11},{9,10},{10,... | collective-permute-start | bytes 196616 | tf_op jit(solution)/shard_map/ppermute | solution.py:119
  16.6 5.9 %collective-permute-start.6 = (bf16[128,256]{1,0:T(8,128)(2,1)S(1)}, bf16[128,256]{1,0:T(8,128)(2,1)S(1)}, u32[]{:S(2)}, u32[]{:S(2)}) collective-permute-start(bf16[128,256]{1,0:T(8,128)(2,1)S(1)} %get-tuple-element.58), channel_id=1, source_target_pairs={{0,2},{1,3},{2,0},{3,1},{4,6},{5,7},{6,4},{7,5},{8,10},{9,11},{10,... | collective-permute-start | bytes 196616 | tf_op jit(solution)/shard_map/ppermute | solution.py:119
  17.1 5.6 %collective-permute-start.7 = (bf16[128,256]{1,0:T(8,128)(2,1)S(1)}, bf16[128,256]{1,0:T(8,128)(2,1)S(1)}, u32[]{:S(2)}, u32[]{:S(2)}) collective-permute-start(bf16[128,256]{1,0:T(8,128)(2,1)S(1)} %get-tuple-element.59), channel_id=1, source_target_pairs={{0,1},{1,0},{2,3},{3,2},{4,5},{5,4},{6,7},{7,6},{8,9},{9,8},{10,11... | collective-permute-start | bytes 196616 | tf_op jit(solution)/shard_map/ppermute | solution.py:119
  23.1 4.9 %collective-permute-start.8 = (bf16[400,128]{1,0:T(8,128)(2,1)S(1)}, bf16[400,128]{1,0:T(8,128)(2,1)S(1)}, u32[]{:S(2)}, u32[]{:S(2)}) collective-permute-start(bf16[400,128]{1,0:T(8,128)(2,1)S(1)} %get-tuple-element.60.refs_0_), channel_id=1, source_target_pairs={{0,1},{1,0},{2,3},{3,2},{4,5},{5,4},{6,7},{7,6},{8,9},{9,8},{10,11... | collective-permute-start | bytes 307208 | tf_op jit(solution)/shard_map/ppermute | solution.py:119
  24.0 6.4 %collective-permute-start.9 = (bf16[256,128]{1,0:T(8,128)(2,1)S(1)}, bf16[256,128]{1,0:T(8,128)(2,1)S(1)}, u32[]{:S(2)}, u32[]{:S(2)}) collective-permute-start(bf16[256,128]{1,0:T(8,128)(2,1)S(1)} %get-tuple-element.64.refs_0_), channel_id=1, source_target_pairs={{0,2},{1,3},{2,0},{3,1},{4,6},{5,7},{6,4},{7,5},{8,10},{9,11},{10,... | collective-permute-start | bytes 196616 | tf_op jit(solution)/shard_map/ppermute | solution.py:119
  26.0 6.1 %collective-permute-start.10 = (bf16[256,128]{1,0:T(8,128)(2,1)S(1)}, bf16[256,128]{1,0:T(8,128)(2,1)S(1)}, u32[]{:S(2)}, u32[]{:S(2)}) collective-permute-start(bf16[256,128]{1,0:T(8,128)(2,1)S(1)} %get-tuple-element.64.refs_0_), channel_id=1, source_target_pairs={{0,3},{1,2},{2,1},{3,0},{4,7},{5,6},{6,5},{7,4},{8,11},{9,10},{10,... | collective-permute-start | bytes 196616 | tf_op jit(solution)/shard_map/ppermute | solution.py:119
  28.0 5.1 %collective-permute-start.11 = (bf16[144,128]{1,0:T(8,128)(2,1)S(1)}, bf16[144,128]{1,0:T(8,128)(2,1)S(1)}, u32[]{:S(2)}, u32[]{:S(2)}) collective-permute-start(bf16[144,128]{1,0:T(8,128)(2,1)S(1)} %terms_col.1.refs_3_), channel_id=1, source_target_pairs={{0,2},{1,3},{2,0},{3,1},{4,6},{5,7},{6,4},{7,5},{8,10},{9,11},{10,... | collective-permute-start | bytes 110600 | tf_op jit(solution)/shard_map/ppermute | solution.py:119
  33.4 1.5 %collective-permute-start.13 = (bf16[656,128]{1,0:T(8,128)(2,1)S(1)}, bf16[656,128]{1,0:T(8,128)(2,1)S(1)}, u32[]{:S(2)}, u32[]{:S(2)}) collective-permute-start(bf16[656,128]{1,0:T(8,128)(2,1)S(1)} %backward_other.1.sent_ref), channel_id=1, source_target_pairs={{0,4},{4,0},{8,12},{12,8},{16,20},{20,16},{24,28},{28,24},{1,5},{5... | collective-permute-start | bytes 503816 | tf_op jit(solution)/shard_map/ppermute | solution.py:119
  33.8 3.8 %collective-permute-start.12 = (bf16[512,128]{1,0:T(8,128)(2,1)S(1)}, bf16[512,128]{1,0:T(8,128)(2,1)S(1)}, u32[]{:S(2)}, u32[]{:S(2)}) collective-permute-start(bf16[512,128]{1,0:T(8,128)(2,1)S(1)} %backward_rest.1), channel_id=1, source_target_pairs={{0,4},{4,0},{8,12},{12,8},{16,20},{20,16},{24,28},{28,24},{1,5},{5... | collective-permute-start | bytes 393224 | tf_op jit(solution)/shard_map/ppermute | solution.py:119
  35.0 5.9 %collective-permute-start.14 = (bf16[400,128]{1,0:T(8,128)(2,1)S(1)}, bf16[400,128]{1,0:T(8,128)(2,1)S(1)}, u32[]{:S(2)}, u32[]{:S(2)}) collective-permute-start(bf16[400,128]{1,0:T(8,128)(2,1)S(1)} %get-tuple-element.72), channel_id=1, source_target_pairs={{0,24},{4,28},{8,16},{12,20},{16,8},{20,12},{24,0},{28,4},{1,25},{... | collective-permute-start | bytes 307208 | tf_op jit(solution)/shard_map/ppermute | solution.py:119
  37.2 5.9 %collective-permute-start.15 = (bf16[400,128]{1,0:T(8,128)(2,1)S(1)}, bf16[400,128]{1,0:T(8,128)(2,1)S(1)}, u32[]{:S(2)}, u32[]{:S(2)}) collective-permute-start(bf16[400,128]{1,0:T(8,128)(2,1)S(1)} %get-tuple-element.73), channel_id=1, source_target_pairs={{0,16},{4,20},{8,24},{12,28},{16,0},{20,4},{24,8},{28,12},{1,17},{... | collective-permute-start | bytes 307208 | tf_op jit(solution)/shard_map/ppermute | solution.py:119
  37.7 5.5 %collective-permute-start.16 = (bf16[400,128]{1,0:T(8,128)(2,1)S(1)}, bf16[400,128]{1,0:T(8,128)(2,1)S(1)}, u32[]{:S(2)}, u32[]{:S(2)}) collective-permute-start(bf16[400,128]{1,0:T(8,128)(2,1)S(1)} %get-tuple-element.74), channel_id=1, source_target_pairs={{0,8},{4,12},{8,0},{12,4},{16,24},{20,28},{24,16},{28,20},{1,9},{5... | collective-permute-start | bytes 307208 | tf_op jit(solution)/shard_map/ppermute | solution.py:119

commit v10 on v8

--- a/solution.py
+++ b/solution.py
@@ -9,7 +9,7 @@
 from jax.sharding import PartitionSpec as P
 
 BLOCK = 16
-GROUP = 32
+GROUP = 16
 MOD = 4093
 HIT = 64
 DENSE_BYTES = 8 * 2**20
@@ -528,7 +528,7 @@
     landed = [swap(scaled, "row", m) for m in chips]
     sibling = swap(scaled, "row", 1)
     slots = codes.shape[0]
-    middle = slots * 3 // 4 // GROUP * GROUP
+    middle = slots * 7 // 8 // GROUP * GROUP
     size = (pieces * n_col, pieces * n_row)
     block = build_block(lists, tile_count, codes, *size, 0, middle)
     block, landed = lax.optimization_barrier((block, landed))

time: 44 us -> 44 us (level)
  transfers between devices with their start and end apart: 17 -> 17, of which waited for: 11 -> 10; matrix products, arithmetic and copies ran while one was open for 0% -> 0% of each run, Pallas kernels for 16% -> 17%
where the time goes in v10:
time: 44 us; the launch traced here: 43.8 us
  starting transfers between devices  20 us (45%)
  waiting for transfers between devices  12 us (27%)
  Pallas kernels  10.3 us (23%)
  between operations  1.48 us (3%)
    ppermute x17, starting transfers between devices, swap(): return lax.ppermute(value, axis, [(i, i ^ bits) for i in range(size)])  20 us
    ppermute x17, waiting for transfers between devices, swap(): return lax.ppermute(value, axis, [(i, i ^ bits) for i in range(size)])  12 us
    pallas_call x2, Pallas kernels, build_block(): pl.pallas_call(functools.partial(build_kernel, first, last), out_shape=pl...  4.19 us
    pallas_call x5, Pallas kernels, backward_parts(): pl.pallas_call(functools.partial(backward_kernel, pieces, kinds, chunks,...  1.87 us
    pallas_call x1, Pallas kernels, scale_rows(): pl.pallas_call(scale_kernel, out_shape=[pltpu.VMEM((feat, pieces), jnp.bf...  1.03 us
    pallas_call x2, Pallas kernels, forward_parts(): pl.pallas_call(functools.partial(forward_kernel, bits, far), out_shape=[j...  0.96 us
  transfers between devices with their start and end apart: 17, of which 10 were waited for; matrix products, arithmetic and copies ran while one was open for 0% of the time, Pallas kernels for 17%

profile of v10, /device:TPU:0, one launch (start us, length us, event | category | flops | bytes accessed | tf_op | source)
XLA Modules:
  0.0 43.8 jit_solution(13092690329908133483)
XLA Ops:
  0.6 1.0 %scale_rows.1 = (bf16[128,256]{1,0:T(8,128)(2,1)S(1)}, s32[8,128]{1,0:T(8,128)S(1)}, s32[128,256]{1,0:T(8,128)S(1)}) custom-call(s32[1,256]{1,0:T(1,128)} %bitcast.5, bf16[256,128]{1,0:T(8,128)(2,1)} %features_hbm.1, s32[1,1,128]{2,1,0:T(1,128)} %rows_hbm.1, s32[1,1,128]{2,1,0:T(1,128)} %cols_hbm.1, s32[128,256]{1,0:T(8,128)} %bitcast.9), custom_call_target="tpu_custom_call" | custom-call | tf_op jit(solution)/shard_map/scale_rows/pallas_call | solution.py:476
  1.7 4.0 %collective-permute-start = (bf16[128,256]{1,0:T(8,128)(2,1)S(1)}, bf16[128,256]{1,0:T(8,128)(2,1)S(1)}, u32[]{:S(2)}, u32[]{:S(2)}) collective-permute-start(bf16[128,256]{1,0:T(8,128)(2,1)S(1)} %get-tuple-element.43.refs_0_), channel_id=1, source_target_pairs={{0,24},{4,28},{8,16},{12,20},{16,8},{20,12},{24,0},{28,4},{1,25},{... | collective-permute-start | bytes 196616 | tf_op jit(solution)/shard_map/ppermute | solution.py:119
  6.9 3.2 %build_block.1.refs_0_ = bf16[2048,1024]{1,0:T(8,128)(2,1)S(1)} custom-call(s32[8,128]{1,0:T(8,128)S(1)} %get-tuple-element.41.lists_vmem, s32[1,1,1]{2,1,0:T(1,128)S(6)} %copy.15.count_ref, s32[128,256]{1,0:T(8,128)S(1)} %get-tuple-element.42.codes_ref), custom_call_target="tpu_custom_call" | custom-call | flops 36700160 | bytes 8388608 | tf_op jit(solution)/shard_map/build_block/pallas_call | solution.py:183
  11.0 1.0 %build_rest.1.block_ref = bf16[2048,1024]{1,0:T(8,128)(2,1)S(1)} custom-call(s32[8,128]{1,0:T(8,128)S(1)} %get-tuple-element.41.lists_vmem, s32[1,1,1]{2,1,0:T(1,128)S(6)} %copy.15.count_ref, s32[128,256]{1,0:T(8,128)S(1)} %get-tuple-element.42.codes_ref, bf16[2048,1024]{1,0:T(8,128)(2,1)S(1)} %build_block.1.refs_0_), custom_call_target="tpu_custom_call", output_to_operand_aliasing={{}: (3, {})} | custom-call | flops 5242880 | bytes 8388608 | tf_op jit(solution)/shard_map/build_rest/pallas_call | solution.py:183
  12.5 3.9 %collective-permute-start.5 = (bf16[128,256]{1,0:T(8,128)(2,1)S(1)}, bf16[128,256]{1,0:T(8,128)(2,1)S(1)}, u32[]{:S(2)}, u32[]{:S(2)}) collective-permute-start(bf16[128,256]{1,0:T(8,128)(2,1)S(1)} %get-tuple-element.57), channel_id=1, source_target_pairs={{0,3},{1,2},{2,1},{3,0},{4,7},{5,6},{6,5},{7,4},{8,11},{9,10},{10,... | collective-permute-start | bytes 196616 | tf_op jit(solution)/shard_map/ppermute | solution.py:119
  16.9 0.7 %collective-permute-start.7 = (bf16[128,256]{1,0:T(8,128)(2,1)S(1)}, bf16[128,256]{1,0:T(8,128)(2,1)S(1)}, u32[]{:S(2)}, u32[]{:S(2)}) collective-permute-start(bf16[128,256]{1,0:T(8,128)(2,1)S(1)} %get-tuple-element.59), channel_id=1, source_target_pairs={{0,1},{1,0},{2,3},{3,2},{4,5},{5,4},{6,7},{7,6},{8,9},{9,8},{10,11... | collective-permute-start | bytes 196616 | tf_op jit(solution)/shard_map/ppermute | solution.py:119
  17.8 1.3 %collective-permute-done.5.refs_1_ = bf16[128,256]{1,0:T(8,128)(2,1)S(1)} collective-permute-done((bf16[128,256]{1,0:T(8,128)(2,1)S(1)}, bf16[128,256]{1,0:T(8,128)(2,1)S(1)}, u32[]{:S(2)}, u32[]{:S(2)}) %collective-permute-start.5) | collective-permute-done | bytes 65568 | tf_op jit(solution)/shard_map/ppermute | solution.py:119
  19.1 3.4 %collective-permute-done.6.refs_2_ = bf16[128,256]{1,0:T(8,128)(2,1)S(1)} collective-permute-done((bf16[128,256]{1,0:T(8,128)(2,1)S(1)}, bf16[128,256]{1,0:T(8,128)(2,1)S(1)}, u32[]{:S(2)}, u32[]{:S(2)}) %collective-permute-start.6) | collective-permute-done | bytes 65568 | tf_op jit(solution)/shard_map/ppermute | solution.py:119
  23.0 0.9 %collective-permute-start.8 = (bf16[400,128]{1,0:T(8,128)(2,1)S(1)}, bf16[400,128]{1,0:T(8,128)(2,1)S(1)}, u32[]{:S(2)}, u32[]{:S(2)}) collective-permute-start(bf16[400,128]{1,0:T(8,128)(2,1)S(1)} %get-tuple-element.60.refs_0_), channel_id=1, source_target_pairs={{0,1},{1,0},{2,3},{3,2},{4,5},{5,4},{6,7},{7,6},{8,9},{9,8},{10,11... | collective-permute-start | bytes 307208 | tf_op jit(solution)/shard_map/ppermute | solution.py:119
  23.9 1.9 %collective-permute-start.9 = (bf16[256,128]{1,0:T(8,128)(2,1)S(1)}, bf16[256,128]{1,0:T(8,128)(2,1)S(1)}, u32[]{:S(2)}, u32[]{:S(2)}) collective-permute-start(bf16[256,128]{1,0:T(8,128)(2,1)S(1)} %get-tuple-element.64.refs_0_), channel_id=1, source_target_pairs={{0,2},{1,3},{2,0},{3,1},{4,6},{5,7},{6,4},{7,5},{8,10},{9,11},{10,... | collective-permute-start | bytes 196616 | tf_op jit(solution)/shard_map/ppermute | solution.py:119
  25.8 1.6 %collective-permute-start.10 = (bf16[256,128]{1,0:T(8,128)(2,1)S(1)}, bf16[256,128]{1,0:T(8,128)(2,1)S(1)}, u32[]{:S(2)}, u32[]{:S(2)}) collective-permute-start(bf16[256,128]{1,0:T(8,128)(2,1)S(1)} %get-tuple-element.64.refs_0_), channel_id=1, source_target_pairs={{0,3},{1,2},{2,1},{3,0},{4,7},{5,6},{6,5},{7,4},{8,11},{9,10},{10,... | collective-permute-start | bytes 196616 | tf_op jit(solution)/shard_map/ppermute | solution.py:119
  27.5 0.5 %collective-permute-done.8.refs_1_ = bf16[400,128]{1,0:T(8,128)(2,1)S(1)} collective-permute-done((bf16[400,128]{1,0:T(8,128)(2,1)S(1)}, bf16[400,128]{1,0:T(8,128)(2,1)S(1)}, u32[]{:S(2)}, u32[]{:S(2)}) %collective-permute-start.8) | collective-permute-done | bytes 102432 | tf_op jit(solution)/shard_map/ppermute | solution.py:119
  28.0 1.6 %collective-permute-start.11 = (bf16[144,128]{1,0:T(8,128)(2,1)S(1)}, bf16[144,128]{1,0:T(8,128)(2,1)S(1)}, u32[]{:S(2)}, u32[]{:S(2)}) collective-permute-start(bf16[144,128]{1,0:T(8,128)(2,1)S(1)} %terms_col.1.refs_3_), channel_id=1, source_target_pairs={{0,2},{1,3},{2,0},{3,1},{4,6},{5,7},{6,4},{7,5},{8,10},{9,11},{10,... | collective-permute-start | bytes 110600 | tf_op jit(solution)/shard_map/ppermute | solution.py:119
  29.6 0.7 %backward_near.1.refs_2_ = f32[2048,128]{1,0:T(8,128)S(1)} custom-call(bf16[2048,1024]{1,0:T(8,128)(2,1)S(1)} %build_rest.1.block_ref, bf16[256,128]{1,0:T(8,128)(2,1)S(1)} %get-tuple-element.64.refs_0_, bf16[400,128]{1,0:T(8,128)(2,1)S(1)} %collective-permute-done.8.refs_1_), custom_call_target="tpu_custom_call" | custom-call | tf_op jit(solution)/shard_map/backward_near/pallas_call | solution.py:390
  30.3 0.8 %collective-permute-done.9.refs_0_ = bf16[256,128]{1,0:T(8,128)(2,1)S(1)} collective-permute-done((bf16[256,128]{1,0:T(8,128)(2,1)S(1)}, bf16[256,128]{1,0:T(8,128)(2,1)S(1)}, u32[]{:S(2)}, u32[]{:S(2)}) %collective-permute-start.9) | collective-permute-done | bytes 65568 | tf_op jit(solution)/shard_map/ppermute | solution.py:119
  31.2 0.7 %collective-permute-done.10.refs_1_ = bf16[256,128]{1,0:T(8,128)(2,1)S(1)} collective-permute-done((bf16[256,128]{1,0:T(8,128)(2,1)S(1)}, bf16[256,128]{1,0:T(8,128)(2,1)S(1)}, u32[]{:S(2)}, u32[]{:S(2)}) %collective-permute-start.10) | collective-permute-done | bytes 65568 | tf_op jit(solution)/shard_map/ppermute | solution.py:119
  31.9 1.3 %collective-permute-done.11.refs_4_ = bf16[144,128]{1,0:T(8,128)(2,1)S(1)} collective-permute-done((bf16[144,128]{1,0:T(8,128)(2,1)S(1)}, bf16[144,128]{1,0:T(8,128)(2,1)S(1)}, u32[]{:S(2)}, u32[]{:S(2)}) %collective-permute-start.11) | collective-permute-done | bytes 36896 | tf_op jit(solution)/shard_map/ppermute | solution.py:119
  33.9 0.6 %collective-permute-start.12 = (bf16[512,128]{1,0:T(8,128)(2,1)S(1)}, bf16[512,128]{1,0:T(8,128)(2,1)S(1)}, u32[]{:S(2)}, u32[]{:S(2)}) collective-permute-start(bf16[512,128]{1,0:T(8,128)(2,1)S(1)} %backward_rest.1), channel_id=1, source_target_pairs={{0,4},{4,0},{8,12},{12,8},{16,20},{20,16},{24,28},{28,24},{1,5},{5... | collective-permute-start | bytes 393224 | tf_op jit(solution)/shard_map/ppermute | solution.py:119
  35.1 2.3 %collective-permute-start.14 = (bf16[400,128]{1,0:T(8,128)(2,1)S(1)}, bf16[400,128]{1,0:T(8,128)(2,1)S(1)}, u32[]{:S(2)}, u32[]{:S(2)}) collective-permute-start(bf16[400,128]{1,0:T(8,128)(2,1)S(1)} %get-tuple-element.72), channel_id=1, source_target_pairs={{0,24},{4,28},{8,16},{12,20},{16,8},{20,12},{24,0},{28,4},{1,25},{... | collective-permute-start | bytes 307208 | tf_op jit(solution)/shard_map/ppermute | solution.py:119
  38.0 0.8 %collective-permute-start.16 = (bf16[400,128]{1,0:T(8,128)(2,1)S(1)}, bf16[400,128]{1,0:T(8,128)(2,1)S(1)}, u32[]{:S(2)}, u32[]{:S(2)}) collective-permute-start(bf16[400,128]{1,0:T(8,128)(2,1)S(1)} %get-tuple-element.74), channel_id=1, source_target_pairs={{0,8},{4,12},{8,0},{12,4},{16,24},{20,28},{24,16},{28,20},{1,9},{5... | collective-permute-start | bytes 307208 | tf_op jit(solution)/shard_map/ppermute | solution.py:119
  38.8 0.9 %hidden_step.1 = bf16[256,128]{1,0:T(8,128)(2,1)} custom-call(bf16[128,128]{1,0:T(8,128)(2,1)S(1)} %get-tuple-element.53.turned_ref, f32[128,128]{1,0:T(8,128)S(1)} %get-tuple-element.54.bias_ref, bf16[128,256]{1,0:T(8,128)(2,1)S(1)} %get-tuple-element.62.aggregate_ref), custom_call_target="tpu_custom_call" | custom-call | tf_op jit(solution)/shard_map/hidden_step/pallas_call | solution.py:345
  39.7 1.4 %collective-permute-done.14.refs_1_ = bf16[400,128]{1,0:T(8,128)(2,1)S(1)} collective-permute-done((bf16[400,128]{1,0:T(8,128)(2,1)S(1)}, bf16[400,128]{1,0:T(8,128)(2,1)S(1)}, u32[]{:S(2)}, u32[]{:S(2)}) %collective-permute-start.14) | collective-permute-done | bytes 102432 | tf_op jit(solution)/shard_map/ppermute | solution.py:119
  41.1 2.1 %collective-permute-done.15.refs_2_ = bf16[400,128]{1,0:T(8,128)(2,1)S(1)} collective-permute-done((bf16[400,128]{1,0:T(8,128)(2,1)S(1)}, bf16[400,128]{1,0:T(8,128)(2,1)S(1)}, u32[]{:S(2)}, u32[]{:S(2)}) %collective-permute-start.15) | collective-permute-done | bytes 102432 | tf_op jit(solution)/shard_map/ppermute | solution.py:119
  43.1 0.7 %finish.1 = (bf16[256,128]{1,0:T(8,128)(2,1)}, f32[128,128]{1,0:T(8,128)}, f32[1,128]{1,0:T(1,128)}) custom-call(f32[256,128]{1,0:T(8,128)S(1)} %get-tuple-element.63.root_ref, bf16[400,128]{1,0:T(8,128)(2,1)S(1)} %get-tuple-element.71.refs_0_, bf16[400,128]{1,0:T(8,128)(2,1)S(1)} %collective-permute-done.14.refs_1_, ...), custom_call_target="tpu_custom_call" | custom-call | tf_op jit(solution)/shard_map/finish/pallas_call | solution.py:435
  (36 shorter events, 5.0 us)
Async XLA Ops:
  1.7 8.5 %collective-permute-start = (bf16[128,256]{1,0:T(8,128)(2,1)S(1)}, bf16[128,256]{1,0:T(8,128)(2,1)S(1)}, u32[]{:S(2)}, u32[]{:S(2)}) collective-permute-start(bf16[128,256]{1,0:T(8,128)(2,1)S(1)} %get-tuple-element.43.refs_0_), channel_id=1, source_target_pairs={{0,24},{4,28},{8,16},{12,20},{16,8},{20,12},{24,0},{28,4},{1,25},{... | collective-permute-start | bytes 196616 | tf_op jit(solution)/shard_map/ppermute | solution.py:119
  5.6 4.5 %collective-permute-start.1 = (bf16[128,256]{1,0:T(8,128)(2,1)S(1)}, bf16[128,256]{1,0:T(8,128)(2,1)S(1)}, u32[]{:S(2)}, u32[]{:S(2)}) collective-permute-start(bf16[128,256]{1,0:T(8,128)(2,1)S(1)} %get-tuple-element.43.refs_0_), channel_id=1, source_target_pairs={{0,16},{4,20},{8,24},{12,28},{16,0},{20,4},{24,8},{28,12},{1,17},{... | collective-permute-start | bytes 196616 | tf_op jit(solution)/shard_map/ppermute | solution.py:119
  6.1 4.3 %collective-permute-start.2 = (bf16[128,256]{1,0:T(8,128)(2,1)S(1)}, bf16[128,256]{1,0:T(8,128)(2,1)S(1)}, u32[]{:S(2)}, u32[]{:S(2)}) collective-permute-start(bf16[128,256]{1,0:T(8,128)(2,1)S(1)} %get-tuple-element.43.refs_0_), channel_id=1, source_target_pairs={{0,8},{4,12},{8,0},{12,4},{16,24},{20,28},{24,16},{28,20},{1,9},{5... | collective-permute-start | bytes 196616 | tf_op jit(solution)/shard_map/ppermute | solution.py:119
  10.4 1.6 %collective-permute-start.4 = (bf16[384,256]{1,0:T(8,128)(2,1)S(1)}, bf16[384,256]{1,0:T(8,128)(2,1)S(1)}, u32[]{:S(2)}, u32[]{:S(2)}) collective-permute-start(bf16[384,256]{1,0:T(8,128)(2,1)S(1)} %stack.1), channel_id=1, source_target_pairs={{0,4},{4,0},{8,12},{12,8},{16,20},{20,16},{24,28},{28,24},{1,5},{5... | collective-permute-start | bytes 589832 | tf_op jit(solution)/shard_map/ppermute | solution.py:119
  10.5 1.5 %collective-permute-start.3 = (bf16[128,256]{1,0:T(8,128)(2,1)S(1)}, bf16[128,256]{1,0:T(8,128)(2,1)S(1)}, u32[]{:S(2)}, u32[]{:S(2)}) collective-permute-start(bf16[128,256]{1,0:T(8,128)(2,1)S(1)} %get-tuple-element.43.refs_0_), channel_id=1, source_target_pairs={{0,4},{4,0},{8,12},{12,8},{16,20},{20,16},{24,28},{28,24},{1,5},{5... | collective-permute-start | bytes 196616 | tf_op jit(solution)/shard_map/ppermute | solution.py:119
  12.0 5.6 %copy-start = (bf16[128,128]{1,0:T(8,128)(2,1)S(1)}, bf16[128,128]{1,0:T(8,128)(2,1)}, u32[]{:S(2)}) copy-start(bf16[128,128]{1,0:T(8,128)(2,1)} %weight_ref.2) | copy-start | bytes 98308
  12.0 5.6 %copy-start.1 = (bf16[256,128]{1,0:T(8,128)(2,1)S(1)}, bf16[256,128]{1,0:T(8,128)(2,1)}, u32[]{:S(2)}) copy-start(bf16[256,128]{1,0:T(8,128)(2,1)} %cot_ref) | copy-start | bytes 196612
  12.0 5.6 %copy-start.2 = (s32[256]{0:T(256)S(1)}, s32[256]{0:T(256)}, u32[]{:S(2)}) copy-start(s32[256]{0:T(256)} %param.10) | copy-start | bytes 3076
  12.0 5.6 %copy-start.3 = (f32[128]{0:T(128)S(1)}, f32[128]{0:T(128)}, u32[]{:S(2)}) copy-start(f32[128]{0:T(128)} %param.12) | copy-start | bytes 1540
  12.5 6.5 %collective-permute-start.5 = (bf16[128,256]{1,0:T(8,128)(2,1)S(1)}, bf16[128,256]{1,0:T(8,128)(2,1)S(1)}, u32[]{:S(2)}, u32[]{:S(2)}) collective-permute-start(bf16[128,256]{1,0:T(8,128)(2,1)S(1)} %get-tuple-element.57), channel_id=1, source_target_pairs={{0,3},{1,2},{2,1},{3,0},{4,7},{5,6},{6,5},{7,4},{8,11},{9,10},{10,... | collective-permute-start | bytes 196616 | tf_op jit(solution)/shard_map/ppermute | solution.py:119
  16.4 6.0 %collective-permute-start.6 = (bf16[128,256]{1,0:T(8,128)(2,1)S(1)}, bf16[128,256]{1,0:T(8,128)(2,1)S(1)}, u32[]{:S(2)}, u32[]{:S(2)}) collective-permute-start(bf16[128,256]{1,0:T(8,128)(2,1)S(1)} %get-tuple-element.58), channel_id=1, source_target_pairs={{0,2},{1,3},{2,0},{3,1},{4,6},{5,7},{6,4},{7,5},{8,10},{9,11},{10,... | collective-permute-start | bytes 196616 | tf_op jit(solution)/shard_map/ppermute | solution.py:119
  16.9 5.7 %collective-permute-start.7 = (bf16[128,256]{1,0:T(8,128)(2,1)S(1)}, bf16[128,256]{1,0:T(8,128)(2,1)S(1)}, u32[]{:S(2)}, u32[]{:S(2)}) collective-permute-start(bf16[128,256]{1,0:T(8,128)(2,1)S(1)} %get-tuple-element.59), channel_id=1, source_target_pairs={{0,1},{1,0},{2,3},{3,2},{4,5},{5,4},{6,7},{7,6},{8,9},{9,8},{10,11... | collective-permute-start | bytes 196616 | tf_op jit(solution)/shard_map/ppermute | solution.py:119
  23.0 5.0 %collective-permute-start.8 = (bf16[400,128]{1,0:T(8,128)(2,1)S(1)}, bf16[400,128]{1,0:T(8,128)(2,1)S(1)}, u32[]{:S(2)}, u32[]{:S(2)}) collective-permute-start(bf16[400,128]{1,0:T(8,128)(2,1)S(1)} %get-tuple-element.60.refs_0_), channel_id=1, source_target_pairs={{0,1},{1,0},{2,3},{3,2},{4,5},{5,4},{6,7},{7,6},{8,9},{9,8},{10,11... | collective-permute-start | bytes 307208 | tf_op jit(solution)/shard_map/ppermute | solution.py:119
  23.9 7.2 %collective-permute-start.9 = (bf16[256,128]{1,0:T(8,128)(2,1)S(1)}, bf16[256,128]{1,0:T(8,128)(2,1)S(1)}, u32[]{:S(2)}, u32[]{:S(2)}) collective-permute-start(bf16[256,128]{1,0:T(8,128)(2,1)S(1)} %get-tuple-element.64.refs_0_), channel_id=1, source_target_pairs={{0,2},{1,3},{2,0},{3,1},{4,6},{5,7},{6,4},{7,5},{8,10},{9,11},{10,... | collective-permute-start | bytes 196616 | tf_op jit(solution)/shard_map/ppermute | solution.py:119
  25.8 6.1 %collective-permute-start.10 = (bf16[256,128]{1,0:T(8,128)(2,1)S(1)}, bf16[256,128]{1,0:T(8,128)(2,1)S(1)}, u32[]{:S(2)}, u32[]{:S(2)}) collective-permute-start(bf16[256,128]{1,0:T(8,128)(2,1)S(1)} %get-tuple-element.64.refs_0_), channel_id=1, source_target_pairs={{0,3},{1,2},{2,1},{3,0},{4,7},{5,6},{6,5},{7,4},{8,11},{9,10},{10,... | collective-permute-start | bytes 196616 | tf_op jit(solution)/shard_map/ppermute | solution.py:119
  28.0 5.2 %collective-permute-start.11 = (bf16[144,128]{1,0:T(8,128)(2,1)S(1)}, bf16[144,128]{1,0:T(8,128)(2,1)S(1)}, u32[]{:S(2)}, u32[]{:S(2)}) collective-permute-start(bf16[144,128]{1,0:T(8,128)(2,1)S(1)} %terms_col.1.refs_3_), channel_id=1, source_target_pairs={{0,2},{1,3},{2,0},{3,1},{4,6},{5,7},{6,4},{7,5},{8,10},{9,11},{10,... | collective-permute-start | bytes 110600 | tf_op jit(solution)/shard_map/ppermute | solution.py:119
  33.5 1.5 %collective-permute-start.13 = (bf16[656,128]{1,0:T(8,128)(2,1)S(1)}, bf16[656,128]{1,0:T(8,128)(2,1)S(1)}, u32[]{:S(2)}, u32[]{:S(2)}) collective-permute-start(bf16[656,128]{1,0:T(8,128)(2,1)S(1)} %backward_other.1.sent_ref), channel_id=1, source_target_pairs={{0,4},{4,0},{8,12},{12,8},{16,20},{20,16},{24,28},{28,24},{1,5},{5... | collective-permute-start | bytes 503816 | tf_op jit(solution)/shard_map/ppermute | solution.py:119
  33.9 4.1 %collective-permute-start.12 = (bf16[512,128]{1,0:T(8,128)(2,1)S(1)}, bf16[512,128]{1,0:T(8,128)(2,1)S(1)}, u32[]{:S(2)}, u32[]{:S(2)}) collective-permute-start(bf16[512,128]{1,0:T(8,128)(2,1)S(1)} %backward_rest.1), channel_id=1, source_target_pairs={{0,4},{4,0},{8,12},{12,8},{16,20},{20,16},{24,28},{28,24},{1,5},{5... | collective-permute-start | bytes 393224 | tf_op jit(solution)/shard_map/ppermute | solution.py:119
  35.1 5.9 %collective-permute-start.14 = (bf16[400,128]{1,0:T(8,128)(2,1)S(1)}, bf16[400,128]{1,0:T(8,128)(2,1)S(1)}, u32[]{:S(2)}, u32[]{:S(2)}) collective-permute-start(bf16[400,128]{1,0:T(8,128)(2,1)S(1)} %get-tuple-element.72), channel_id=1, source_target_pairs={{0,24},{4,28},{8,16},{12,20},{16,8},{20,12},{24,0},{28,4},{1,25},{... | collective-permute-start | bytes 307208 | tf_op jit(solution)/shard_map/ppermute | solution.py:119
  37.5 5.7 %collective-permute-start.15 = (bf16[400,128]{1,0:T(8,128)(2,1)S(1)}, bf16[400,128]{1,0:T(8,128)(2,1)S(1)}, u32[]{:S(2)}, u32[]{:S(2)}) collective-permute-start(bf16[400,128]{1,0:T(8,128)(2,1)S(1)} %get-tuple-element.73), channel_id=1, source_target_pairs={{0,16},{4,20},{8,24},{12,28},{16,0},{20,4},{24,8},{28,12},{1,17},{... | collective-permute-start | bytes 307208 | tf_op jit(solution)/shard_map/ppermute | solution.py:119
  38.0 5.1 %collective-permute-start.16 = (bf16[400,128]{1,0:T(8,128)(2,1)S(1)}, bf16[400,128]{1,0:T(8,128)(2,1)S(1)}, u32[]{:S(2)}, u32[]{:S(2)}) collective-permute-start(bf16[400,128]{1,0:T(8,128)(2,1)S(1)} %get-tuple-element.74), channel_id=1, source_target_pairs={{0,8},{4,12},{8,0},{12,4},{16,24},{20,28},{24,16},{28,20},{1,9},{5... | collective-permute-start | bytes 307208 | tf_op jit(solution)/shard_map/ppermute | solution.py:119
